TPU v7x, 512 devices: a whole 4x8x8 slice. The times are simulated.
512 devices in a mesh: idx: 64 (over z, y), mdl: 8 (over x, core).
Axes of the slice: x: 4, y: 8, z: 8, core: 2. Of those that a mesh axis runs over, the one named last changes fastest.
Arguments:
- index_emb: bfloat16 [8192, 768], P('idx'), may hold values from -6 to 6
- query_emb: bfloat16 [128, 768], P('idx'), may hold values from -6 to 6
- passage_owner: int32 [2560, 1], P('idx'), may hold values from 0 to 63; in each aligned block of 40 rows (0 to 39, 40 to 79, ...) at most 3 rows name the same one
- passage_row: int32 [2560], P('idx'), may hold values from 0 to 127
- token_ids: int32 [2560, 4], P('idx'), may hold values from 0 to 16383
- vocab_table: bfloat16 [16384, 2048], P('idx', 'mdl'), may hold values from -3 to 3
- w_query: bfloat16 [2048, 1024], P(None, 'mdl'), may hold values from -0.125 to 0.125
- w_key: bfloat16 [2048, 1024], P(None, 'mdl'), may hold values from -0.125 to 0.125
- w_value: bfloat16 [2048, 1024], P(None, 'mdl'), may hold values from -0.125 to 0.125
- w_out: bfloat16 [1024, 2048], P('mdl'), may hold values from -0.1875 to 0.1875
- out_grad: bfloat16 [10240, 2048], P('idx', 'mdl'), may hold values from -6 to 6
- slab_emb: bfloat16 [4096, 768], P('idx'), may hold values from -6 to 6
- slab_ids: int32 [4096], P('idx'), may hold values from 0 to 8191, as said below
Outputs:
- relevance: float32 [128, 20], P('idx')
- grad_query: float32 [2048, 1024], P('idx', 'mdl')
- grad_key: float32 [2048, 1024], P('idx', 'mdl')
- grad_value: float32 [2048, 1024], P('idx', 'mdl')
- grad_out: float32 [1024, 2048], P('mdl', 'idx')
- refreshed_index: bfloat16 [8192, 768], P('idx')
Inputs may be any that keep to these rules, and one draw needn't show every extreme that they name: `passage_owner`: among the 40 passages of one device's queries no owner appears more than 3 times. `slab_ids`: the ids are distinct; the 64 ids of one device name exactly 2 passages of each of 32 owners, the owner of an id being id // 128.
All inputs are finite; a program needn't handle non-finite values.
Results may differ from a plain program's by a relative error of at most 0.009.
The roundings to bfloat16 on the way count: a program that leaves them out, or rounds other values in their place, can miss the bound.
Values may be sent and summed in bfloat16 or wider, within the bound.
No kernel may reach another device: no remote copies, remote signals or barrier semaphores. Data moves between devices by JAX's collectives and lax.ppermute only.
A program may use at most 64 MiB of HBM per device.

v0:
```python
import jax
import jax.numpy as jnp
from jax import lax
from jax.sharding import PartitionSpec as P

HEAD_DIM = 64
K = 20
CAPS = 2


def owner_ranks(target, owners):
    marks = (target[:, None] == jnp.arange(owners, dtype=jnp.int32)[None, :]).astype(jnp.int32)
    return jnp.sum((jnp.cumsum(marks, axis=0) - 1) * marks, axis=1)


def slot_table(target, ranks, values, owners, capacity):
    select = (target[:, None, None] == jnp.arange(owners, dtype=jnp.int32)[None, :, None]) & (
        ranks[:, None, None] == jnp.arange(capacity, dtype=jnp.int32)[None, None, :]
    )
    return jnp.sum(jnp.where(select, values[:, None, None] + 1, 0), axis=0) - 1


def lookup_rows(index_emb, asked):
    rows = jnp.take(index_emb, jnp.clip(asked, 0, index_emb.shape[0] - 1), axis=0)
    return jnp.where(asked[..., None] >= 0, rows, jnp.zeros_like(rows))


def shards(
    index_emb,
    query_emb,
    passage_owner,
    passage_row,
    token_ids,
    vocab_table,
    w_query,
    w_key,
    w_value,
    w_out,
    out_grad,
    slab_emb,
    slab_ids,
):
    owners = lax.axis_size("idx")
    pass_rows = index_emb.shape[0]
    width = index_emb.shape[1]
    count = passage_row.shape[0]
    capacity = max(3, count // owners + 2)
    target = passage_owner[:, 0]
    ranks = owner_ranks(target, owners)
    table = slot_table(target, ranks, passage_row, owners, capacity)
    replies = lax.all_to_all(
        lookup_rows(
            index_emb, lax.all_to_all(table, "idx", split_axis=0, concat_axis=0, tiled=True)
        ),
        "idx",
        split_axis=0,
        concat_axis=0,
        tiled=True,
    )
    fetched = replies[target, ranks]
    scores = jnp.einsum(
        "qke,qe->qk", fetched.reshape(-1, K, width), query_emb, preferred_element_type=jnp.float32
    )
    relevance = jax.nn.softmax(scores, axis=-1)
    flat_tokens = token_ids.reshape(-1)
    blank = jnp.zeros((flat_tokens.shape[0], vocab_table.shape[1]), jnp.bfloat16)
    piece = lax.all_gather(vocab_table, "idx", axis=0, tiled=True)
    inside = (flat_tokens >= 0) & (flat_tokens < piece.shape[0])
    rows = jnp.take(piece, jnp.clip(flat_tokens, 0, piece.shape[0] - 1), axis=0)
    token_part = jnp.where(inside[:, None], rows, blank)
    tokens, full_grad = (
        lax.all_gather(token_part, "mdl", axis=1, tiled=True),
        lax.all_gather(out_grad, "mdl", axis=1, tiled=True),
    )
    npass = token_ids.shape[0]
    plen = token_ids.shape[1]
    heads = w_query.shape[1] // HEAD_DIM
    local_inner = w_query.shape[1]

    def project(weight):
        states = jnp.dot(tokens, weight, preferred_element_type=jnp.float32).astype(jnp.bfloat16)
        return states.reshape(npass, plen, heads, HEAD_DIM)

    query_states = project(w_query)
    key_states = project(w_key)
    value_states = project(w_value)
    logits = jnp.einsum(
        "pihd,pjhd->phij", query_states, key_states, preferred_element_type=jnp.float32
    )
    probs = jax.nn.softmax(logits, axis=-1)
    attn = probs.astype(jnp.bfloat16)
    context = jnp.einsum(
        "phij,pjhd->pihd", attn, value_states, preferred_element_type=jnp.float32
    ).astype(jnp.bfloat16)
    flat_context = context.reshape(npass * plen, local_inner)
    weighted = (
        (full_grad.reshape(npass, plen, -1).astype(jnp.float32) * relevance.reshape(npass, 1, 1))
        .astype(jnp.bfloat16)
        .reshape(npass * plen, -1)
    )
    contract_rows = (((0,), (0,)), ((), ()))
    context_grad = lax.dot_general(
        weighted, w_out, (((1,), (1,)), ((), ())), preferred_element_type=jnp.float32
    )
    context_grad = context_grad.astype(jnp.bfloat16).reshape(npass, plen, heads, HEAD_DIM)
    attn_grad = jnp.einsum(
        "pihd,pjhd->phij", context_grad, value_states, preferred_element_type=jnp.float32
    )
    value_grad = jnp.einsum(
        "phij,pihd->pjhd", attn, context_grad, preferred_element_type=jnp.float32
    ).astype(jnp.bfloat16)
    score_grad = (probs * (attn_grad - jnp.sum(attn_grad * probs, axis=-1, keepdims=True))).astype(
        jnp.bfloat16
    )
    query_grad = jnp.einsum(
        "phij,pjhd->pihd", score_grad, key_states, preferred_element_type=jnp.float32
    ).astype(jnp.bfloat16)
    key_grad = jnp.einsum(
        "phij,pihd->pjhd", score_grad, query_states, preferred_element_type=jnp.float32
    ).astype(jnp.bfloat16)

    def weight_grad(states):
        return lax.dot_general(
            tokens,
            states.reshape(npass * plen, -1),
            contract_rows,
            preferred_element_type=jnp.float32,
        )

    grad_out_term = lax.dot_general(
        flat_context, weighted, contract_rows, preferred_element_type=jnp.float32
    )
    grad_query, grad_key, grad_value, grad_out = (
        lax.psum_scatter(weight_grad(query_grad), "idx", scatter_dimension=0, tiled=True),
        lax.psum_scatter(weight_grad(key_grad), "idx", scatter_dimension=0, tiled=True),
        lax.psum_scatter(weight_grad(value_grad), "idx", scatter_dimension=0, tiled=True),
        lax.psum_scatter(grad_out_term, "idx", scatter_dimension=1, tiled=True),
    )
    slab_owner = slab_ids // pass_rows
    slab_row = slab_ids % pass_rows
    slab_ranks = owner_ranks(slab_owner, owners)
    row_table = slot_table(slab_owner, slab_ranks, slab_row, owners, CAPS)
    source_table = slot_table(
        slab_owner, slab_ranks, jnp.arange(slab_ids.shape[0], dtype=jnp.int32), owners, CAPS
    )
    emb_table = lookup_rows(slab_emb, source_table)
    got_emb, got_row = (
        lax.all_to_all(emb_table, "idx", split_axis=0, concat_axis=0, tiled=True),
        lax.all_to_all(row_table, "idx", split_axis=0, concat_axis=0, tiled=True),
    )
    flat_row = got_row.reshape(-1)
    placed = jnp.where(flat_row >= 0, flat_row, pass_rows)
    refreshed_index = index_emb.at[placed].set(got_emb.reshape(-1, width), mode="drop")
    return (relevance, grad_query, grad_key, grad_value, grad_out, refreshed_index)


def solution(mesh):
    return jax.shard_map(
        shards,
        mesh=mesh,
        in_specs=(
            P("idx", None),
            P("idx", None),
            P("idx", None),
            P("idx"),
            P("idx", None),
            P("idx", "mdl"),
            P(None, "mdl"),
            P(None, "mdl"),
            P(None, "mdl"),
            P("mdl", None),
            P("idx", "mdl"),
            P("idx", None),
            P("idx"),
        ),
        out_specs=(
            P("idx", None),
            P("idx", "mdl"),
            P("idx", "mdl"),
            P("idx", "mdl"),
            P("mdl", "idx"),
            P("idx", None),
        ),
        check_vma=False,
    )
```

profile of v0, /device:TPU:6, one launch (start us, length us, event | category | flops | bytes accessed | tf_op | source)
XLA Modules:
  0.0 1127.2 jit_solution(15189134375063383699)
XLA Ops:
  7.2 1.0 copy.181
  8.2 0.7 iota_compare_fusion.1
  9.0 0.8 select_reduce_fusion.2
  9.9 0.7 broadcast_add_fusion
  10.7 0.7 copy.104
  11.4 16.6 %all-to-all-start = ((s32[64,1,3]{2,1,0:T(1,128)}), s32[64,1,3]{2,1,0:T(1,128)S(1)}, u32[]{:S(2)}, u32[]{:S(2)}) async-start(s32[64,1,3]{2,1,0:T(1,128)} %copy.104), calls=%async_computation | async-start | bytes 65536 | tf_op jit(solution)/shard_map/all_to_all | solution.py:53
  28.0 0.7 broadcast_clamp_fusion.1
  28.9 0.7 compare_and_fusion.3
  29.5 0.7 fusion.35
  30.4 0.1 and.79
  30.5 9.3 all-to-all-done
  40.0 0.1 copy.106
  40.2 0.1 reshape.355
  40.4 1.0 gather_fusion
  41.4 0.1 reshape.354
  41.6 1.2 select_select_fusion
  42.7 4.8 all-to-all-start.1
  47.6 13.2 %all_gather.11 = bf16[160,2048]{1,0:T(8,128)(2,1)S(1)} all-gather(bf16[160,256]{1,0:T(8,128)(2,1)S(1)} %copy-done.5), channel_id=1, replica_groups=mesh['idx'=64,'mdl'=8] {'mdl'}, dimensions={1}, use_global_device_ids=true | all-gather | bytes 737280 | tf_op jit(solution)/shard_map/all_gather | solution.py:73
  60.8 4.1 all-to-all-done.1
  64.9 1.1 gather_fusion.1
  66.1 0.1 fusion.24
  66.2 0.1 reduce_max.18
  66.3 0.2 fusion.27
  66.8 0.1 mul.30
  66.9 52.0 %all-gather.2.cloned.1.call-done = bf16[16384,256]{1,0:T(8,128)(2,1)} async-done(((bf16[256,256]{1,0:T(8,128)(2,1)}), bf16[16384,256]{1,0:T(8,128)(2,1)}) %all-gather.2.cloned.1.call-update) | async-done | bytes 8388624 | tf_op jit(solution)/shard_map/all_gather | solution.py:67
  118.9 5.3 gather_fusion.2
  124.1 0.1 select_select_fusion.1
  124.3 13.2 %all_gather.10 = bf16[160,2048]{1,0:T(8,128)(2,1)S(1)} all-gather(bf16[160,256]{1,0:T(8,128)(2,1)S(1)} %select_select_fusion.1), channel_id=1, replica_groups=mesh['idx'=64,'mdl'=8] {'mdl'}, dimensions={1}, use_global_device_ids=true | all-gather | bytes 737280 | tf_op jit(solution)/shard_map/all_gather | solution.py:72
  137.5 0.3 convolution_convert_fusion.4
  137.9 0.3 convolution_convert_fusion.6
  138.4 0.2 copy-done.4
  138.6 0.3 convolution_convert_fusion.7
  139.0 0.4 fusion.56
  139.4 0.5 fusion.6
  140.1 1.6 fusion.7
  141.8 0.4 convolution_convert_fusion.5
  142.3 0.3 multiply_reduce_fusion
  142.7 0.2 fusion.4
  143.1 1.5 fusion.62
  144.7 0.2 reduce-scatter.5.cloned.1.call-start
  144.9 0.3 fusion.3
  145.4 1.5 fusion.61
  146.9 0.4 fusion.5
  147.6 1.5 fusion.63
  149.3 0.2 select_reduce_fusion.1
  149.5 0.1 fusion.9
  149.6 0.7 copy.125
  150.3 10.0 all-to-all-start.2
  160.4 0.1 copy.127
  160.5 0.1 copy.126
  160.7 0.1 reshape.377
  160.9 0.9 gather_fusion.3
  161.8 1.1 broadcast_select_fusion.1
  162.9 9.4 all-to-all-done.2
  172.3 4.6 all-to-all-start.3
  177.0 0.5 broadcast.429
  177.5 0.7 reduce.3
  178.2 0.1 reshape.351
  178.3 12.0 %all-to-all-done.3 = bf16[64,2,768]{2,1,0:T(2,128)(2,1)S(1)} async-done(((bf16[64,2,768]{2,1,0:T(2,128)(2,1)}), bf16[64,2,768]{2,1,0:T(2,128)(2,1)S(1)}, u32[]{:S(2)}, u32[]{:S(2)}) %all-to-all-start.3) | async-done | bytes 196640 | tf_op jit(solution)/shard_map/all_to_all | solution.py:148
  190.4 1.2 scatter_fusion
  191.7 192.3 %reduce-scatter.11.cloned.1.call-done = f32[128,32]{0,1:T(8,128)} async-done(((f32[128,2048]{0,1:T(8,128)}), f32[128,32]{0,1:T(8,128)}) %reduce-scatter.11.cloned.1.call-update) | async-done | bytes 16400 | tf_op jit(solution)/shard_map/reduce_scatter | solution.py:137
  384.0 245.8 %reduce-scatter.7.cloned.1.call-done = f32[32,128]{1,0:T(8,128)} async-done(((f32[2048,128]{1,0:T(8,128)}), f32[32,128]{1,0:T(8,128)}) %reduce-scatter.7.cloned.1.call-update) | async-done | bytes 16400 | tf_op jit(solution)/shard_map/reduce_scatter | solution.py:135
  629.8 245.1 %reduce-scatter.5.cloned.1.call-done = f32[32,128]{1,0:T(8,128)} async-done(((f32[2048,128]{1,0:T(8,128)}), f32[32,128]{1,0:T(8,128)}) %reduce-scatter.5.cloned.1.call-update) | async-done | bytes 16400 | tf_op jit(solution)/shard_map/reduce_scatter | solution.py:134
  874.9 245.7 %reduce-scatter.9.cloned.1.call-done = f32[32,128]{1,0:T(8,128)} async-done(((f32[2048,128]{1,0:T(8,128)}), f32[32,128]{1,0:T(8,128)}) %reduce-scatter.9.cloned.1.call-update) | async-done | bytes 16400 | tf_op jit(solution)/shard_map/reduce_scatter | solution.py:136
  (75 shorter events, 3.0 us)
Async XLA Ops:
  7.2 130.3 %copy-start = (bf16[2048,128]{1,0:T(8,128)(2,1)S(1)}, bf16[2048,128]{1,0:T(8,128)(2,1)}, u32[]{:S(2)}) copy-start(bf16[2048,128]{1,0:T(8,128)(2,1)} %param.21) | copy-start | bytes 1572868
  7.2 111.7 %all-gather.2.cloned.1.call-start = ((), (), s32[]{:S(2)}) async-start(), calls=%async_computation.8 | async-start | bytes 8519680 | tf_op jit(solution)/shard_map/all_gather | solution.py:67
  11.4 28.5 %all-to-all-start = ((s32[64,1,3]{2,1,0:T(1,128)}), s32[64,1,3]{2,1,0:T(1,128)S(1)}, u32[]{:S(2)}, u32[]{:S(2)}) async-start(s32[64,1,3]{2,1,0:T(1,128)} %copy.104), calls=%async_computation | async-start | bytes 65536 | tf_op jit(solution)/shard_map/all_to_all | solution.py:53
  41.4 6.2 copy-start.5
  42.7 23.3 %copy-start.9 = (bf16[2,768]{1,0:T(2,128)(2,1)S(1)}, bf16[2,768]{1,0:T(2,128)(2,1)}, u32[]{:S(2)}) copy-start(bf16[2,768]{1,0:T(2,128)(2,1)} %param.14) | copy-start | bytes 9220
  42.7 22.2 %all-to-all-start.1 = ((bf16[64,3,768]{2,1,0:T(4,128)(2,1)}), bf16[64,3,768]{2,1,0:T(4,128)(2,1)S(1)}, u32[]{:S(2)}, u32[]{:S(2)}) async-start(bf16[64,3,768]{2,1,0:T(4,128)(2,1)} %select_select_fusion), calls=%async_computation.1 | async-start | bytes 786432 | tf_op jit(solution)/shard_map/all_to_all | solution.py:51
  47.5 336.5 %reduce-scatter.11.cloned.1.call-start = ((), (), s32[]{:S(2)}) async-start(), calls=%async_computation.12 | async-start | bytes 1064960 | tf_op jit(solution)/shard_map/reduce_scatter | solution.py:137
  66.6 71.2 %copy-start.6 = (f32[2,20]{1,0:T(2,128)}, f32[2,20]{1,0:T(2,128)S(1)}, u32[]{:S(2)}) copy-start(f32[2,20]{1,0:T(2,128)S(1)} %fusion.26) | copy-start | bytes 484
  66.9 71.0 %copy-start.3 = (bf16[2048,128]{1,0:T(8,128)(2,1)S(1)}, bf16[2048,128]{1,0:T(8,128)(2,1)}, u32[]{:S(2)}) copy-start(bf16[2048,128]{1,0:T(8,128)(2,1)} %param.19) | copy-start | bytes 1572868
  137.5 1.0 copy-start.4
  140.1 1.7 copy-start.8
  141.8 488.0 %reduce-scatter.7.cloned.1.call-start = ((), (), s32[]{:S(2)}) async-start(), calls=%async_computation.10 | async-start | bytes 1064960 | tf_op jit(solution)/shard_map/reduce_scatter | solution.py:135
  144.7 730.3 %reduce-scatter.5.cloned.1.call-start = ((), (), s32[]{:S(2)}) async-start(), calls=%async_computation.9 | async-start | bytes 1064960 | tf_op jit(solution)/shard_map/reduce_scatter | solution.py:134
  146.9 973.8 %reduce-scatter.9.cloned.1.call-start = ((), (), s32[]{:S(2)}) async-start(), calls=%async_computation.11 | async-start | bytes 1064960 | tf_op jit(solution)/shard_map/reduce_scatter | solution.py:136
  147.6 1.5 copy-start.7
  147.6 13.3 %copy-start.2 = (bf16[64,768]{1,0:T(8,128)(2,1)S(1)}, bf16[64,768]{1,0:T(8,128)(2,1)}, u32[]{:S(2)}) copy-start(bf16[64,768]{1,0:T(8,128)(2,1)} %param.24) | copy-start | bytes 294916
  150.3 22.0 %all-to-all-start.2 = ((s32[64,1,2]{2,1,0:T(1,128)}), s32[64,1,2]{2,1,0:T(1,128)S(1)}, u32[]{:S(2)}, u32[]{:S(2)}) async-start(s32[64,1,2]{2,1,0:T(1,128)} %copy.125), calls=%async_computation.6 | async-start | bytes 65536 | tf_op jit(solution)/shard_map/all_to_all | solution.py:149
  172.3 18.0 %all-to-all-start.3 = ((bf16[64,2,768]{2,1,0:T(2,128)(2,1)}), bf16[64,2,768]{2,1,0:T(2,128)(2,1)S(1)}, u32[]{:S(2)}, u32[]{:S(2)}) async-start(bf16[64,2,768]{2,1,0:T(2,128)(2,1)} %broadcast_select_fusion.1), calls=%async_computation.7 | async-start | bytes 393216 | tf_op jit(solution)/shard_map/all_to_all | solution.py:148
  191.7 929.0 %copy-start.1 = (bf16[128,768]{1,0:T(8,128)(2,1)}, bf16[128,768]{1,0:T(8,128)(2,1)S(1)}, u32[]{:S(2)}) copy-start(bf16[128,768]{1,0:T(8,128)(2,1)S(1)} %scatter_fusion) | copy-start | bytes 589828
Sparse Core Ops, SparseCore 0:
  11.1 107.7 all-gather.1
  141.9 242.0 reduce-scatter.10
  389.1 240.6 reduce-scatter.6
  634.3 240.5 reduce-scatter.4
  880.0 240.6 reduce-scatter.8
where the time goes:
time: 1130 us
  waiting for transfers between devices  1020 us (90%)
  starting transfers between devices  36.4 us (3%)
  blocking collectives  26.5 us (2%)
  local copies, waits for them, and re-layouts  15.8 us (1%)
  between operations  14.2 us (1%)
    reduce_scatter x1, waiting for transfers between devices, shards(): lax.psum_scatter(weight_grad(key_grad), 'idx', scatter_dimension=0, tiled...  246 us
    reduce_scatter x1, waiting for transfers between devices, shards(): lax.psum_scatter(weight_grad(value_grad), 'idx', scatter_dimension=0, til...  246 us
    reduce_scatter x1, waiting for transfers between devices, shards(): lax.psum_scatter(weight_grad(query_grad), 'idx', scatter_dimension=0, til...  245 us
    reduce_scatter x1, waiting for transfers between devices, shards(): lax.psum_scatter(grad_out_term, 'idx', scatter_dimension=1, tiled=True)  192 us
    all_gather x1, waiting for transfers between devices, shards(): piece = lax.all_gather(vocab_table, 'idx', axis=0, tiled=True)  52 us
  transfers between devices with their start and end apart: 9, of which 9 were waited for; matrix products, arithmetic and copies ran while one was open for 2% of the time, Pallas kernels for 0%

commit v1 on v0

v1 whole, which is shorter than its diff:
```python
import jax
import jax.numpy as jnp
from jax import lax
from jax.experimental import pallas as pl
from jax.experimental.pallas import tpu as pltpu
from jax.sharding import Mesh
from jax.sharding import PartitionSpec as P

HEAD_DIM = 64
K = 20
PLEN = 4
CAPS = 2
LANES = 128
IDX = ("z", "y")
F32 = jnp.float32
BF16 = jnp.bfloat16
ROWS = (((0,), (0,)), ((), ()))
COLS = (((1,), (1,)), ((), ()))


def dot(a, b, dims=None):
    if dims is None:
        return jnp.dot(a, b, preferred_element_type=F32)
    return lax.dot_general(a, b, dims, preferred_element_type=F32)


def reader_kernel(tokens_ref, grad_ref, rel_ref, wq_ref, wk_ref, wv_ref, wo_ref, out_ref):
    tokens = tokens_ref[...]
    count, inner = tokens.shape[0], wq_ref.shape[1]
    owners = out_ref.shape[0]
    rows = out_ref.shape[1] // 4
    query = dot(tokens, wq_ref[...]).astype(BF16)
    key = dot(tokens, wk_ref[...]).astype(BF16)
    value = dot(tokens, wv_ref[...]).astype(BF16)
    weighted = (grad_ref[...].astype(F32) * rel_ref[...]).astype(BF16)
    context_grad = dot(weighted, wo_ref[...], COLS).astype(BF16)
    passage_i = lax.broadcasted_iota(jnp.int32, (count, count), 0) // PLEN
    passage_j = lax.broadcasted_iota(jnp.int32, (count, count), 1) // PLEN
    same = passage_i == passage_j
    parts = [], [], [], []
    for head in range(inner // HEAD_DIM):
        cols = slice(head * HEAD_DIM, (head + 1) * HEAD_DIM)
        q, k, v, c = query[:, cols], key[:, cols], value[:, cols], context_grad[:, cols]
        logits = jnp.where(same, dot(q, k, COLS), -jnp.inf)
        exps = jnp.exp(logits - jnp.max(logits, axis=1, keepdims=True))
        probs = exps / jnp.sum(exps, axis=1, keepdims=True)
        attn = probs.astype(BF16)
        attn_grad = dot(c, v, COLS)
        mean = jnp.sum(attn_grad * probs, axis=1, keepdims=True)
        score_grad = (probs * (attn_grad - mean)).astype(BF16)
        parts[0].append(dot(score_grad, k).astype(BF16))
        parts[1].append(dot(score_grad, q, ROWS).astype(BF16))
        parts[2].append(dot(attn, c, ROWS).astype(BF16))
        parts[3].append(dot(attn, v).astype(BF16))
    query_grad, key_grad, value_grad, context = (jnp.concatenate(p, axis=1) for p in parts)
    for place, (left, right) in enumerate(
        ((tokens, query_grad), (tokens, key_grad), (tokens, value_grad), (weighted, context))
    ):
        term = dot(left, right, ROWS).astype(BF16)
        out_ref[:, place * rows : (place + 1) * rows, :] = term.reshape(owners, rows, inner)


def reader(tokens, out_grad, rel, w_query, w_key, w_value, w_out, owners):
    width, inner = w_query.shape
    return pl.pallas_call(
        reader_kernel,
        out_shape=jax.ShapeDtypeStruct((owners, 4 * width // owners, inner), BF16),
        compiler_params=pltpu.CompilerParams(vmem_limit_bytes=40 * 1024 * 1024),
        name="reader",
    )(tokens, out_grad, rel, w_query, w_key, w_value, w_out)


def shards(
    index_emb,
    query_emb,
    passage_owner,
    passage_row,
    token_ids,
    vocab_table,
    w_query,
    w_key,
    w_value,
    w_out,
    out_grad,
    slab_emb,
    slab_ids,
):
    nz, ny = lax.axis_size("z"), lax.axis_size("y")
    owners = nz * ny
    my_z, my_y = lax.axis_index("z"), lax.axis_index("y")
    pass_rows, width = index_emb.shape
    queries = query_emb.shape[0]
    npass = token_ids.shape[0]
    count = npass * PLEN
    vocab_rows = vocab_table.shape[0]
    slab = slab_ids.shape[0]

    vocab = lax.all_gather(vocab_table, "z", axis=0, tiled=True)
    full_grad = lax.all_gather(out_grad, "m", axis=1, tiled=True)

    flat_ids = token_ids.reshape(-1)
    slab_owner, slab_row = slab_ids // pass_rows, slab_ids % pass_rows
    earlier = (slab_owner[:, None] == slab_owner[None, :]) & (
        jnp.arange(slab)[:, None] > jnp.arange(slab)[None, :]
    )
    slot = slab_owner * CAPS + jnp.sum(earlier.astype(jnp.int32), axis=1)
    select = (jnp.arange(owners * CAPS)[:, None] == slot[None, :]).astype(BF16)
    slab_wide = jnp.concatenate(
        [slab_emb, jnp.broadcast_to((slab_row + 1).astype(BF16)[:, None], (slab, LANES))], axis=1
    )
    slab_out = dot(select, slab_wide).astype(BF16).reshape(owners, CAPS, width + LANES)
    ids_part = jnp.stack([flat_ids // LANES, flat_ids % LANES]).astype(BF16)
    common = jnp.concatenate([query_emb, ids_part], axis=1)
    message = jnp.concatenate(
        [slab_out, jnp.broadcast_to(common[None], (owners, *common.shape))], axis=2
    )
    got = lax.all_to_all(message, IDX, 0, 0, tiled=True)

    all_queries = got[:, :, width + LANES : 2 * width + LANES].reshape(-1, width)
    scores_out = dot(all_queries, index_emb, COLS).reshape(owners, queries, pass_rows)
    scores_in = lax.all_to_all(scores_out, IDX, 0, 0, tiled=True)

    got_rows = got[:, :, :width].reshape(-1, width)
    got_place = got[:, :, width].reshape(-1).astype(jnp.int32) - 1
    put = jnp.arange(pass_rows)[:, None] == got_place[None, :]
    refreshed = jnp.where(
        jnp.any(put, axis=1)[:, None], dot(put.astype(BF16), got_rows).astype(BF16), index_emb
    )

    ids_all = got[:, :, 2 * width + LANES :].astype(jnp.int32)
    ids_all = ids_all[:, 0] * LANES + ids_all[:, 1]
    ids = lax.dynamic_slice_in_dim(ids_all, my_z * ny, ny, axis=0).reshape(-1)
    id_owner = ids // vocab_rows
    local = jnp.where(id_owner % ny == my_y, (id_owner // ny) * vocab_rows + ids % vocab_rows, -1)
    one_hot = (local[:, None] == jnp.arange(nz * vocab_rows)[None, :]).astype(BF16)
    served = dot(one_hot, vocab).astype(BF16).reshape(ny, count, -1)
    token_in = lax.all_to_all(served, "y", 0, 0, tiled=True)
    token_part = jnp.sum(token_in.astype(F32), axis=0).astype(BF16)
    tokens = lax.all_gather(token_part, "m", axis=1, tiled=True)

    at = (passage_owner[:, 0][:, None, None] == jnp.arange(owners)[None, :, None]) & (
        passage_row[:, None, None] == jnp.arange(pass_rows)[None, None, :]
    )
    table = jnp.repeat(scores_in.transpose(1, 0, 2), K, axis=0)
    scores = jnp.sum(jnp.where(at, table, 0.0), axis=(1, 2)).reshape(queries, K)
    relevance = jax.nn.softmax(scores, axis=-1)
    rel = jnp.repeat(relevance.reshape(-1), PLEN)[:, None]

    terms = reader(tokens, full_grad, rel, w_query, w_key, w_value, w_out, owners)
    sums = jnp.sum(lax.all_to_all(terms, IDX, 0, 0, tiled=True).astype(F32), axis=0)
    rows = sums.shape[0] // 4
    grad_query, grad_key, grad_value = (sums[i * rows : (i + 1) * rows] for i in range(3))
    grad_out = sums[3 * rows :].T
    return (relevance, grad_query, grad_key, grad_value, grad_out, refreshed)


def solution(mesh):
    owners, columns = mesh.devices.shape
    side = 1
    while side * side < owners:
        side *= 2
    fine = Mesh(mesh.devices.reshape(owners // side, side, columns), ("z", "y", "m"))
    return jax.shard_map(
        shards,
        mesh=fine,
        in_specs=(
            P(IDX, None),
            P(IDX, None),
            P(IDX, None),
            P(IDX),
            P(IDX, None),
            P(IDX, "m"),
            P(None, "m"),
            P(None, "m"),
            P(None, "m"),
            P("m", None),
            P(IDX, "m"),
            P(IDX, None),
            P(IDX),
        ),
        out_specs=(
            P(IDX, None),
            P(IDX, "m"),
            P(IDX, "m"),
            P(IDX, "m"),
            P("m", IDX),
            P(IDX, None),
        ),
        check_vma=False,
    )
```

time: 1130 us -> 193 us (0.17)
  waiting for transfers between devices: 1020 us -> 88.4 us
    reduce_scatter x4 -> x0, waiting for transfers between devices: 929 us -> none  [the longest x1 246 us: shards(): lax.psum_scatter(weight_grad(key_grad), 'idx', scatter_dimension=0, tiled...]
    all_to_all x4, waiting for transfers between devices: 34.9 us -> 68 us  [the longest x1 50.3 us: shards(): lax.all_to_all(terms, IDX, 0, 0, tiled=True).astype(F32)]
    all_gather x1, waiting for transfers between devices: 52 us -> 19.7 us  [shards(): vocab = lax.all_gather(vocab_table, 'z', axis=0, tiled=True)]
  transfers between devices with their start and end apart: 9 -> 5, of which waited for: 9 -> 4; matrix products, arithmetic and copies ran while one was open for 2% -> 6% of each run, Pallas kernels for 0% -> 0%
where the time goes in v1:
time: 193 us; the launch traced here: 192 us
  waiting for transfers between devices  88.4 us (46%)
  starting transfers between devices  38 us (20%)
  blocking collectives  26.9 us (14%)
  between operations  14.3 us (7%)
  other arithmetic  8.19 us (4%)
  matrix products  6.22 us (3%)
  local copies, waits for them, and re-layouts  4.78 us (2%)
  Pallas kernels  4.72 us (2%)
    all_to_all x1, waiting for transfers between devices, shards(): lax.all_to_all(terms, IDX, 0, 0, tiled=True).astype(F32)  50.3 us
    all_gather x1, waiting for transfers between devices, shards(): vocab = lax.all_gather(vocab_table, 'z', axis=0, tiled=True)  19.7 us
    all_to_all x1, waiting for transfers between devices, shards(): got = lax.all_to_all(message, IDX, 0, 0, tiled=True)  16.9 us
    all_to_all x1, starting transfers between devices, shards(): got = lax.all_to_all(message, IDX, 0, 0, tiled=True)  16.6 us
    all_gather x1, blocking collectives, shards(): full_grad = lax.all_gather(out_grad, 'm', axis=1, tiled=True)  13.4 us
    all_gather x1, blocking collectives, shards(): tokens = lax.all_gather(token_part, 'm', axis=1, tiled=True)  13.4 us
    all_to_all x1, starting transfers between devices, shards(): lax.all_to_all(terms, IDX, 0, 0, tiled=True).astype(F32)  9.49 us
    all_to_all x1, starting transfers between devices, shards(): token_in = lax.all_to_all(served, 'y', 0, 0, tiled=True)  6.87 us
  transfers between devices with their start and end apart: 5, of which 4 were waited for; matrix products, arithmetic and copies ran while one was open for 6% of the time, Pallas kernels for 0%

profile of v1, /device:TPU:6, one launch (start us, length us, event | category | flops | bytes accessed | tf_op | source)
XLA Modules:
  0.0 191.5 jit_solution(14795550222648992330)
XLA Ops:
  7.2 0.0 copy-start.9
  7.2 0.0 copy-start.10
  7.2 0.0 copy-start.5
  7.2 0.7 and_select_fusion.3
  7.9 0.2 convert_reduce_fusion.1
  8.1 0.8 copy.31
  8.9 0.1 reshape.297
  9.0 0.1 broadcast_in_dim.17
  9.1 1.1 convolution_convert_fusion
  10.2 0.1 reshape.296
  10.3 0.7 maximum_maximum_fusion
  11.0 0.1 broadcast_in_dim.18
  11.1 1.3 pad_maximum_fusion
  12.4 16.6 %all-to-all-start = ((bf16[64,2,1824]{2,1,0:T(2,128)(2,1)}), bf16[64,2,1824]{2,1,0:T(2,128)(2,1)S(1)}, u32[]{:S(2)}, u32[]{:S(2)}) async-start(bf16[64,2,1824]{2,1,0:T(2,128)(2,1)} %pad_maximum_fusion), calls=%async_computation | async-start | bytes 983040 | tf_op jit(solution)/shard_map/all_to_all | solution.py:117
  29.0 0.0 all-gather.2.cloned.1.call-start
  29.0 0.7 all-gather.2.cloned.1.call-update
  29.7 0.5 broadcast.309
  30.2 0.0 copy-done.9
  30.2 0.7 reduce.9
  30.9 0.1 eq.109
  31.0 0.0 copy-done.10
  31.0 0.1 eq.113
  31.1 16.9 %all-to-all-done = bf16[64,2,1824]{2,1,0:T(2,128)(2,1)S(1)} async-done(((bf16[64,2,1824]{2,1,0:T(2,128)(2,1)}), bf16[64,2,1824]{2,1,0:T(2,128)(2,1)S(1)}, u32[]{:S(2)}, u32[]{:S(2)}) %all-to-all-start) | async-done | bytes 466976 | tf_op jit(solution)/shard_map/all_to_all | solution.py:117
  47.9 0.9 fusion.29
  48.9 0.0 copy-done.5
  48.9 0.2 fusion.4
  49.1 0.7 copy.33
  49.8 0.1 slice_convert_fusion
  49.8 0.1 fusion.30
  50.0 0.1 reshape.298
  50.1 5.0 %all-to-all-start.1 = ((f32[64,2,128]{2,1,0:T(2,128)}), f32[64,2,128]{2,1,0:T(2,128)S(1)}, u32[]{:S(2)}, u32[]{:S(2)}) async-start(f32[64,2,128]{2,1,0:T(2,128)} %copy.33), calls=%async_computation.1 | async-start | bytes 131072 | tf_op jit(solution)/shard_map/all_to_all | solution.py:121
  55.1 19.7 %all-gather.2.cloned.1.call-done = bf16[2048,256]{1,0:T(8,128)(2,1)} async-done(((bf16[256,256]{1,0:T(8,128)(2,1)}), bf16[2048,256]{1,0:T(8,128)(2,1)}) %all-gather.2.cloned.1.call-update) | async-done | bytes 1048592 | tf_op jit(solution)/shard_map/all_gather | solution.py:98
  74.9 4.0 %fusion.2 = bf16[1280,256]{1,0:T(8,128)(2,1)} fusion(bf16[2048,256]{1,0:T(8,128)(2,1)} %all-gather.2.cloned.1.call-done, s32[1280]{0:T(1024)S(1)} %fusion.17), kind=kOutput, calls=%fused_computation.4 | convolution fusion | flops 1345126400 | bytes 1709056 | tf_op jit(solution)/shard_map/dot_general | solution.py:23
  78.9 0.0 copy-done.4
  78.9 0.0 copy-start.3
  78.9 0.0 all-to-all-done.1
  78.9 6.9 %all-to-all-start.2 = ((bf16[8,160,256]{2,1,0:T(8,128)(2,1)}), bf16[8,160,256]{2,1,0:T(8,128)(2,1)S(1)}, u32[]{:S(2)}, u32[]{:S(2)}) async-start(bf16[8,160,256]{2,1,0:T(8,128)(2,1)} %bitcast.2), calls=%async_computation.2 | async-start | bytes 1310720 | tf_op jit(solution)/shard_map/all_to_all | solution.py:137
  85.8 0.1 iota_compare_fusion.9
  85.9 0.1 iota_compare_fusion.10
  85.9 13.4 %all_gather.11.grad_ref = bf16[160,2048]{1,0:T(8,128)(2,1)S(1)} all-gather(bf16[160,256]{1,0:T(8,128)(2,1)} %param.23), channel_id=1, replica_groups=mesh['z'=8,'y'=8,'m'=8] {'m'}, dimensions={1}, use_global_device_ids=true | all-gather | bytes 737280 | tf_op jit(solution)/shard_map/all_gather | solution.py:99
  99.4 1.0 select_reduce_fusion
  100.4 0.1 reduce_max.9
  100.5 0.2 fusion.25
  100.7 0.1 fusion.24
  100.8 0.1 div.76
  100.8 0.1 broadcast_in_dim.25
  100.9 0.1 broadcast_in_dim_reshape.4.rel_ref
  101.0 0.8 all-to-all-done.2
  101.8 0.7 reduce_sum.51
  102.5 13.4 %all_gather.10.tokens_ref = bf16[160,2048]{1,0:T(8,128)(2,1)S(1)} all-gather(bf16[160,256]{1,0:T(8,128)(2,1)} %reduce_sum.51), channel_id=1, replica_groups=mesh['z'=8,'y'=8,'m'=8] {'m'}, dimensions={1}, use_global_device_ids=true | all-gather | bytes 737280 | tf_op jit(solution)/shard_map/all_gather | solution.py:139
  116.0 0.0 copy-done
  116.0 0.0 copy-done.1
  116.0 0.0 copy-done.2
  116.0 4.7 %reader.1 = bf16[64,128,128]{2,1,0:T(8,128)(2,1)} custom-call(bf16[160,2048]{1,0:T(8,128)(2,1)S(1)} %all_gather.10.tokens_ref, bf16[160,2048]{1,0:T(8,128)(2,1)S(1)} %all_gather.11.grad_ref, f32[160,1]{1,0:T(8,128)S(1)} %broadcast_in_dim_reshape.4.rel_ref, bf16[2048,128]{1,0:T(8,128)(2,1)S(1)} %copy-done, bf16[2048,128]{1,0:T(8,128)(2,1)S(1)} %copy-done.1, ...), custom_call_target="tpu_custom_call" | custom-call | tf_op jit(solution)/shard_map/reader/pallas_call | solution.py:65
  120.7 9.5 %all-to-all-start.3 = ((bf16[64,128,128]{2,1,0:T(8,128)(2,1)}), bf16[64,128,128]{2,1,0:T(8,128)(2,1)S(1)}, u32[]{:S(2)}, u32[]{:S(2)}) async-start(bf16[64,128,128]{2,1,0:T(8,128)(2,1)} %reader.1), calls=%async_computation.3 | async-start | bytes 4194304 | tf_op jit(solution)/shard_map/all_to_all | solution.py:150
  130.2 1.9 add_reduce_fusion
  132.1 0.1 sub.45
  132.3 0.1 reshape.300
  132.4 0.1 fusion.10
  132.5 0.0 copy-done.6
  132.5 0.9 fusion.3
  133.4 50.3 %all-to-all-done.3 = bf16[64,128,128]{2,1,0:T(8,128)(2,1)S(1)} async-done(((bf16[64,128,128]{2,1,0:T(8,128)(2,1)}), bf16[64,128,128]{2,1,0:T(8,128)(2,1)S(1)}, u32[]{:S(2)}, u32[]{:S(2)}) %all-to-all-start.3) | async-done | bytes 2097184 | tf_op jit(solution)/shard_map/all_to_all | solution.py:150
  183.7 0.3 convert_reduce_fusion
  184.0 0.6 slice_bitcast_fusion
  (16 shorter events, 0.1 us)
Async XLA Ops:
  7.2 23.1 %copy-start.9 = (s32[40,1]{0,1:T(1,128)S(1)}, s32[40,1]{0,1:T(1,128)}, u32[]{:S(2)}) copy-start(s32[40,1]{0,1:T(1,128)} %param.15) | copy-start | bytes 484
  7.2 23.8 %copy-start.10 = (s32[40]{0:T(128)S(1)}, s32[40]{0:T(128)}, u32[]{:S(2)}) copy-start(s32[40]{0:T(128)} %param.16) | copy-start | bytes 484
  7.2 41.7 %copy-start.5 = (bf16[128,768]{1,0:T(8,128)(2,1)S(1)}, bf16[128,768]{1,0:T(8,128)(2,1)}, u32[]{:S(2)}) copy-start(bf16[128,768]{1,0:T(8,128)(2,1)} %param.13) | copy-start | bytes 589828
  12.4 35.6 %all-to-all-start = ((bf16[64,2,1824]{2,1,0:T(2,128)(2,1)}), bf16[64,2,1824]{2,1,0:T(2,128)(2,1)S(1)}, u32[]{:S(2)}, u32[]{:S(2)}) async-start(bf16[64,2,1824]{2,1,0:T(2,128)(2,1)} %pad_maximum_fusion), calls=%async_computation | async-start | bytes 983040 | tf_op jit(solution)/shard_map/all_to_all | solution.py:117
  29.0 45.9 %all-gather.2.cloned.1.call-start = ((), (), s32[]{:S(2)}) async-start(), calls=%async_computation.4 | async-start | bytes 1179648 | tf_op jit(solution)/shard_map/all_gather | solution.py:98
  47.9 31.0 %copy-start.4 = (bf16[64,2,1824]{2,1,0:T(2,128)(2,1)}, bf16[64,2,1824]{2,1,0:T(2,128)(2,1)S(1)}, u32[]{:S(2)}) copy-start(bf16[64,2,1824]{2,1,0:T(2,128)(2,1)S(1)} %all-to-all-done) | copy-start | bytes 1400836
  50.1 28.9 %all-to-all-start.1 = ((f32[64,2,128]{2,1,0:T(2,128)}), f32[64,2,128]{2,1,0:T(2,128)S(1)}, u32[]{:S(2)}, u32[]{:S(2)}) async-start(f32[64,2,128]{2,1,0:T(2,128)} %copy.33), calls=%async_computation.1 | async-start | bytes 131072 | tf_op jit(solution)/shard_map/all_to_all | solution.py:121
  78.9 37.1 %copy-start = (bf16[2048,128]{1,0:T(8,128)(2,1)S(1)}, bf16[2048,128]{1,0:T(8,128)(2,1)}, u32[]{:S(2)}) copy-start(bf16[2048,128]{1,0:T(8,128)(2,1)} %wq_ref.1) | copy-start | bytes 1572868
  78.9 37.1 %copy-start.1 = (bf16[2048,128]{1,0:T(8,128)(2,1)S(1)}, bf16[2048,128]{1,0:T(8,128)(2,1)}, u32[]{:S(2)}) copy-start(bf16[2048,128]{1,0:T(8,128)(2,1)} %wk_ref.1) | copy-start | bytes 1572868
  78.9 37.1 %copy-start.2 = (bf16[2048,128]{1,0:T(8,128)(2,1)S(1)}, bf16[2048,128]{1,0:T(8,128)(2,1)}, u32[]{:S(2)}) copy-start(bf16[2048,128]{1,0:T(8,128)(2,1)} %wv_ref.1) | copy-start | bytes 1572868
  78.9 37.1 %copy-start.3 = (bf16[128,2048]{1,0:T(8,128)(2,1)S(1)}, bf16[128,2048]{1,0:T(8,128)(2,1)}, u32[]{:S(2)}) copy-start(bf16[128,2048]{1,0:T(8,128)(2,1)} %wo_ref.1) | copy-start | bytes 1572868
  78.9 22.9 %all-to-all-start.2 = ((bf16[8,160,256]{2,1,0:T(8,128)(2,1)}), bf16[8,160,256]{2,1,0:T(8,128)(2,1)S(1)}, u32[]{:S(2)}, u32[]{:S(2)}) async-start(bf16[8,160,256]{2,1,0:T(8,128)(2,1)} %bitcast.2), calls=%async_computation.2 | async-start | bytes 1310720 | tf_op jit(solution)/shard_map/all_to_all | solution.py:137
  100.8 20.0 %copy-start.8 = (f32[2,20]{1,0:T(2,128)}, f32[2,20]{1,0:T(2,128)S(1)}, u32[]{:S(2)}) copy-start(f32[2,20]{1,0:T(2,128)S(1)} %fusion.24) | copy-start | bytes 484
  120.7 11.6 %copy-start.7 = (bf16[64,2,768]{2,1,0:T(2,128)(2,1)S(1)}, bf16[64,2,768]{2,1,0:T(2,128)(2,1)}, u32[]{:S(2)}) copy-start(bf16[64,2,768]{2,1,0:T(2,128)(2,1)} %get-tuple-element.8) | copy-start | bytes 589828
  120.7 11.8 %copy-start.6 = (bf16[128,768]{1,0:T(8,128)(2,1)S(1)}, bf16[128,768]{1,0:T(8,128)(2,1)}, u32[]{:S(2)}) copy-start(bf16[128,768]{1,0:T(8,128)(2,1)} %param.13) | copy-start | bytes 589828
  120.7 63.0 %all-to-all-start.3 = ((bf16[64,128,128]{2,1,0:T(8,128)(2,1)}), bf16[64,128,128]{2,1,0:T(8,128)(2,1)S(1)}, u32[]{:S(2)}, u32[]{:S(2)}) async-start(bf16[64,128,128]{2,1,0:T(8,128)(2,1)} %reader.1), calls=%async_computation.3 | async-start | bytes 4194304 | tf_op jit(solution)/shard_map/all_to_all | solution.py:150
Sparse Core Ops, SparseCore 0:
  31.9 42.9 all-gather.1

commit v2 on v1

v2 whole, which is shorter than its diff:
```python
import functools

import jax
import jax.numpy as jnp
from jax import lax
from jax.experimental import pallas as pl
from jax.experimental.pallas import tpu as pltpu
from jax.sharding import Mesh
from jax.sharding import PartitionSpec as P

HEAD_DIM = 64
K = 20
PLEN = 4
CAPS = 2
LANES = 128
IDX = ("z", "h", "p", "q")
F32 = jnp.float32
BF16 = jnp.bfloat16
ROWS = (((0,), (0,)), ((), ()))
COLS = (((1,), (1,)), ((), ()))


def dot(a, b, dims=None):
    if dims is None:
        return jnp.dot(a, b, preferred_element_type=F32)
    return lax.dot_general(a, b, dims, preferred_element_type=F32)


def reader_kernel(
    heads, half_ref, tokens_ref, grad_ref, rel_ref, wq_ref, wk_ref, wv_ref, wo_ref, out_ref
):
    blocks, count, deep = tokens_ref.shape
    rows = out_ref.shape[1] // 2
    mine = half_ref[0]
    rel = rel_ref[...]

    def projected(weight_ref):
        total = dot(tokens_ref[0], weight_ref[:deep])
        for b in range(1, blocks):
            total += dot(tokens_ref[b], weight_ref[b * deep : (b + 1) * deep])
        return total.astype(BF16)

    def own(states):
        kept = states[:, :HEAD_DIM]
        for head in range(1, heads):
            kept = jnp.where(mine == head, states[:, head * HEAD_DIM : (head + 1) * HEAD_DIM], kept)
        return kept

    q, k, v = own(projected(wq_ref)), own(projected(wk_ref)), own(projected(wv_ref))
    weighted = [(grad_ref[b].astype(F32) * rel).astype(BF16) for b in range(blocks)]
    total = dot(weighted[0], wo_ref[:, :deep], COLS)
    for b in range(1, blocks):
        total += dot(weighted[b], wo_ref[:, b * deep : (b + 1) * deep], COLS)
    c = own(total.astype(BF16))
    passage_i = lax.broadcasted_iota(jnp.int32, (count, count), 0) // PLEN
    passage_j = lax.broadcasted_iota(jnp.int32, (count, count), 1) // PLEN
    logits = jnp.where(passage_i == passage_j, dot(q, k, COLS), -jnp.inf)
    exps = jnp.exp(logits - jnp.max(logits, axis=1, keepdims=True))
    probs = exps / jnp.sum(exps, axis=1, keepdims=True)
    attn = probs.astype(BF16)
    attn_grad = dot(c, v, COLS)
    mean = jnp.sum(attn_grad * probs, axis=1, keepdims=True)
    score_grad = (probs * (attn_grad - mean)).astype(BF16)
    query_grad = dot(score_grad, k).astype(BF16)
    key_grad = dot(score_grad, q, ROWS).astype(BF16)
    value_grad = dot(attn, c, ROWS).astype(BF16)
    context = dot(attn, v).astype(BF16)
    query_key = jnp.concatenate([query_grad, key_grad], axis=1)
    each = deep // rows
    for b in range(blocks):
        first = dot(tokens_ref[b], query_key, ROWS).astype(BF16)
        second = jnp.concatenate(
            [dot(tokens_ref[b], value_grad, ROWS), dot(weighted[b], context, ROWS)], axis=1
        ).astype(BF16)
        out_ref[b * each : (b + 1) * each, :rows, :] = first.reshape(each, rows, -1)
        out_ref[b * each : (b + 1) * each, rows:, :] = second.reshape(each, rows, -1)


def reader(half, tokens, out_grad, rel, w_query, w_key, w_value, w_out, owners):
    width, inner = w_query.shape
    vmem = pl.BlockSpec(memory_space=pltpu.VMEM)
    return pl.pallas_call(
        functools.partial(reader_kernel, inner // HEAD_DIM),
        out_shape=jax.ShapeDtypeStruct((owners, 2 * width // owners, 2 * HEAD_DIM), BF16),
        in_specs=[pl.BlockSpec(memory_space=pltpu.SMEM)] + [vmem] * 7,
        out_specs=vmem,
        compiler_params=pltpu.CompilerParams(vmem_limit_bytes=40 * 1024 * 1024),
        name="reader",
    )(half, tokens, out_grad, rel, w_query, w_key, w_value, w_out)


def all_features(part):
    along_x = lax.all_gather(part, "x", axis=0)
    count = part.shape[0]
    halves = [
        lax.all_gather(along_x[:, i * count // 2 : (i + 1) * count // 2], "c", axis=1)
        for i in range(2)
    ]
    whole = jnp.concatenate(halves, axis=2)
    return whole.reshape(-1, *part.shape)


def shards(
    index_emb,
    query_emb,
    passage_owner,
    passage_row,
    token_ids,
    vocab_table,
    w_query,
    w_key,
    w_value,
    w_out,
    out_grad,
    slab_emb,
    slab_ids,
):
    nq = lax.axis_size("q")
    group = lax.axis_size("p") * nq
    outer = lax.axis_size("z") * lax.axis_size("h")
    owners = outer * group
    my_outer = lax.axis_index(("z", "h"))
    my_inner = lax.axis_index(("p", "q"))
    my_pair = lax.axis_index(("z", "h", "p"))
    my_half = lax.axis_index("q")
    pass_rows, width = index_emb.shape
    queries = query_emb.shape[0]
    npass, plen = token_ids.shape
    count = npass * plen
    vocab_rows = vocab_table.shape[0]
    slab = slab_ids.shape[0]

    vocab = lax.all_gather(vocab_table, ("z", "h"), axis=0, tiled=True)
    full_grad = all_features(lax.all_gather(out_grad, "q", axis=0, tiled=True))

    slab_owner, slab_row = slab_ids // pass_rows, slab_ids % pass_rows
    earlier = (slab_owner[:, None] == slab_owner[None, :]) & (
        jnp.arange(slab)[:, None] > jnp.arange(slab)[None, :]
    )
    slot = slab_owner * CAPS + jnp.sum(earlier.astype(jnp.int32), axis=1)
    select = (jnp.arange(owners * CAPS)[:, None] == slot[None, :]).astype(BF16)
    slab_wide = jnp.concatenate(
        [slab_emb, jnp.broadcast_to((slab_row + 1).astype(BF16)[:, None], (slab, LANES))], axis=1
    )
    slab_out = dot(select, slab_wide).astype(BF16).reshape(owners, CAPS, width + LANES)
    flat_ids = token_ids.reshape(-1)
    ids_part = jnp.stack([flat_ids // LANES, flat_ids % LANES]).astype(BF16)
    place_part = jnp.stack([passage_owner[:, 0], passage_row]).astype(BF16)
    common = jnp.concatenate([query_emb, ids_part, place_part], axis=1)
    message = jnp.concatenate(
        [slab_out, jnp.broadcast_to(common[None], (owners, *common.shape))], axis=2
    )
    got = lax.all_to_all(message, IDX, 0, 0, tiled=True)
    got_slab, got_common = got[:, :, : width + LANES], got[:, :, width + LANES :]

    scores_out = dot(got_common[:, :, :width].reshape(-1, width), index_emb, COLS)
    scores_out = jnp.repeat(
        scores_out.reshape(owners // nq, nq * queries, pass_rows), nq, axis=0
    )
    scores_in = lax.all_to_all(scores_out, IDX, 0, 0, tiled=True)

    got_rows = got_slab[:, :, :width].reshape(-1, width)
    got_place = got_slab[:, :, width].reshape(-1).astype(jnp.int32) - 1
    put = jnp.arange(pass_rows)[:, None] == got_place[None, :]
    refreshed = jnp.where(
        jnp.any(put, axis=1)[:, None], dot(put.astype(BF16), got_rows).astype(BF16), index_emb
    )

    ids = lax.dynamic_slice_in_dim(
        got_common[:, :, width : width + count], my_outer * group, group, axis=0
    ).astype(jnp.int32)
    ids = (ids[:, 0] * LANES + ids[:, 1]).reshape(-1)
    id_owner = ids // vocab_rows
    local = jnp.where(
        id_owner % group == my_inner, (id_owner // group) * vocab_rows + ids % vocab_rows, -1
    )
    one_hot = (local[:, None] == jnp.arange(outer * vocab_rows)[None, :]).astype(BF16)
    served = dot(one_hot, vocab).astype(BF16).reshape(group // nq, nq * count, -1)
    token_in = lax.all_to_all(jnp.repeat(served, nq, axis=0), ("p", "q"), 0, 0, tiled=True)
    token_part = jnp.sum(token_in.astype(F32), axis=0).astype(BF16)
    tokens = all_features(token_part)

    places = lax.dynamic_slice_in_dim(
        got_common[:, :, width + count :], my_pair * nq, nq, axis=0
    ).astype(jnp.int32)
    pair_owner, pair_row = places[:, 0].reshape(-1), places[:, 1].reshape(-1)
    at = (pair_owner[:, None, None] == jnp.arange(owners)[None, :, None]) & (
        pair_row[:, None, None] == jnp.arange(pass_rows)[None, None, :]
    )
    table = jnp.repeat(scores_in.transpose(1, 0, 2), K, axis=0)
    scores = jnp.sum(jnp.where(at, table, 0.0), axis=(1, 2)).reshape(nq * queries, K)
    pair_relevance = jax.nn.softmax(scores, axis=-1)
    relevance = lax.dynamic_slice_in_dim(pair_relevance, my_half * queries, queries, axis=0)
    rel = jnp.repeat(pair_relevance.reshape(-1), plen)[:, None]

    terms = reader(
        my_half.reshape(1), tokens, full_grad, rel, w_query, w_key, w_value, w_out, owners
    )
    terms = lax.all_to_all(terms, IDX, 0, 0, tiled=True)
    rows = terms.shape[1] // 2
    sums = jnp.sum(terms.astype(F32).reshape(owners // nq, nq, 2, rows, 2, HEAD_DIM), axis=0)
    parts = sums.transpose(1, 3, 2, 0, 4).reshape(2, 2, rows, nq * HEAD_DIM)
    return (relevance, parts[0, 0], parts[0, 1], parts[1, 0], parts[1, 1].T, refreshed)


def solution(mesh):
    devices = mesh.devices
    owners, columns = devices.shape
    fine = Mesh(
        devices.reshape(owners // 8, 2, 2, 2, columns // 2, 2), ("z", "h", "p", "q", "x", "c")
    )
    m = ("x", "c")
    return jax.shard_map(
        shards,
        mesh=fine,
        in_specs=(
            P(IDX, None),
            P(IDX, None),
            P(IDX, None),
            P(IDX),
            P(IDX, None),
            P(IDX, m),
            P(None, m),
            P(None, m),
            P(None, m),
            P(m, None),
            P(IDX, m),
            P(IDX, None),
            P(IDX),
        ),
        out_specs=(
            P(IDX, None),
            P(IDX, m),
            P(IDX, m),
            P(IDX, m),
            P(m, IDX),
            P(IDX, None),
        ),
        check_vma=False,
    )
```

time: 193 us -> 225 us (1.17)
  blocking collectives: 26.9 us -> 53.2 us
  other arithmetic: 8.19 us -> 12.7 us
  local copies, waits for them, and re-layouts: 4.78 us -> 9.16 us
  waiting for transfers between devices: 88.4 us -> 85.2 us
    all_gather x1, waiting for transfers between devices: 19.7 us -> 48.1 us  [shards(): vocab = lax.all_gather(vocab_table, ('z', 'h'), axis=0, tiled=True)]
    all_gather x2 -> x7, blocking collectives: 26.9 us -> 53.2 us  [the longest x2 27.2 us: all_features(): along_x = lax.all_gather(part, 'x', axis=0)]
    all_to_all x1, waiting for transfers between devices: 16.9 us -> 0.01 us  [shards(): got = lax.all_to_all(message, IDX, 0, 0, tiled=True)]
    all_to_all x2, waiting for transfers between devices: 51.2 us -> 36.4 us  [the longest x1 26.9 us: shards(): terms = lax.all_to_all(terms, IDX, 0, 0, tiled=True)]
    all_to_all x1, starting transfers between devices: 5.04 us -> 11.6 us  [shards(): scores_in = lax.all_to_all(scores_out, IDX, 0, 0, tiled=True)]
    all_to_all x2, starting transfers between devices: 16.4 us -> 10.9 us  [the longest x1 7.46 us: shards(): terms = lax.all_to_all(terms, IDX, 0, 0, tiled=True)]
    reduce_sum x3, other arithmetic: 1.47 us -> 6.5 us  [the longest x1 4.36 us: shards(): jnp.sum(terms.astype(F32).reshape(owners // nq, nq, 2, rows, 2, HEAD_DIM)...]
    reshape x2 -> x3, local copies, waits for them, and re-layouts: 0.15 us -> 3.79 us  [the longest x1 3.58 us: shards(): terms.astype(F32).reshape(owners // nq, nq, 2, rows, 2, HEAD_DIM)]
  transfers between devices with their start and end apart: 5 -> 5, of which waited for: 4 -> 3; matrix products, arithmetic and copies ran while one was open for 6% -> 8% of each run, Pallas kernels for 0% -> 0%
where the time goes in v2:
time: 225 us; the launch traced here: 224 us
  waiting for transfers between devices  85.2 us (38%)
  blocking collectives  53.2 us (24%)
  starting transfers between devices  39.2 us (17%)
  between operations  14.4 us (6%)
  other arithmetic  12.7 us (6%)
  local copies, waits for them, and re-layouts  9.16 us (4%)
  matrix products  5.61 us (2%)
  Pallas kernels  4.86 us (2%)
    all_gather x1, waiting for transfers between devices, shards(): vocab = lax.all_gather(vocab_table, ('z', 'h'), axis=0, tiled=True)  48.1 us
    all_gather x2, blocking collectives, all_features(): along_x = lax.all_gather(part, 'x', axis=0)  27.2 us
    all_to_all x1, waiting for transfers between devices, shards(): terms = lax.all_to_all(terms, IDX, 0, 0, tiled=True)  26.9 us
    all_gather x1, blocking collectives, shards(): full_grad = all_features(lax.all_gather(out_grad, 'q', axis=0, tiled=True))  16.6 us
    all_to_all x1, starting transfers between devices, shards(): got = lax.all_to_all(message, IDX, 0, 0, tiled=True)  16.6 us
    all_to_all x1, starting transfers between devices, shards(): scores_in = lax.all_to_all(scores_out, IDX, 0, 0, tiled=True)  11.6 us
    all_to_all x1, waiting for transfers between devices, shards(): lax.all_to_all(jnp.repeat(served, nq, axis=0), ('p', 'q'), 0, 0, tiled=True)  9.45 us
    all_gather x4, blocking collectives, all_features(): lax.all_gather(along_x[:, i * count // 2:(i + 1) * count // 2], 'c', axis=1)  9.34 us
  transfers between devices with their start and end apart: 5, of which 3 were waited for; matrix products, arithmetic and copies ran while one was open for 8% of the time, Pallas kernels for 0%

profile of v2, /device:TPU:6, one launch (start us, length us, event | category | flops | bytes accessed | tf_op | source)
XLA Modules:
  0.0 224.2 jit_solution(17829632544533516081)
XLA Ops:
  7.2 0.0 all-gather.8.cloned.1.call-start
  7.2 0.7 all-gather.8.cloned.1.call-update
  7.9 0.7 and_select_fusion.3
  8.6 0.8 copy.37
  9.3 0.1 reshape.310
  9.5 0.2 convert_reduce_fusion
  9.6 0.1 broadcast_in_dim.24
  9.7 1.1 convolution_convert_fusion
  10.8 0.1 reshape.309
  10.9 0.7 convert_bitcast_fusion.1
  11.6 0.7 convert_bitcast_fusion
  12.3 0.8 maximum_maximum_fusion
  13.0 0.1 broadcast_in_dim.26
  13.2 1.2 pad_maximum_fusion.2
  14.4 16.6 %all-to-all-start = ((bf16[64,2,1864]{2,1,0:T(2,128)(2,1)}), bf16[64,2,1864]{2,1,0:T(2,128)(2,1)S(1)}, u32[]{:S(2)}, u32[]{:S(2)}) async-start(bf16[64,2,1864]{2,1,0:T(2,128)(2,1)} %pad_maximum_fusion.2), calls=%async_computation | async-start | bytes 983040 | tf_op jit(solution)/shard_map/all_to_all | solution.py:153
  31.0 16.6 %all_gather.49 = bf16[320,256]{1,0:T(8,128)(2,1)S(1)} all-gather(bf16[160,256]{1,0:T(8,128)(2,1)S(1)} %copy-done.5), channel_id=1, replica_groups=mesh['z'=8,'h'=2,'p'=2,'q'=2,'x'=4,'c'=2] {'q'}, dimensions={0}, use_global_device_ids=true | all-gather | bytes 245760 | tf_op jit(solution)/shard_map/all_gather | solution.py:134
  47.6 13.9 %all-gather.3 = bf16[1280,256]{1,0:T(8,128)(2,1)S(1)} all-gather(bf16[320,256]{1,0:T(8,128)(2,1)S(1)} %all_gather.49), channel_id=5, replica_groups=mesh['z'=8,'h'=2,'p'=2,'q'=2,'x'=4,'c'=2] {'x'}, dimensions={0}, use_global_device_ids=true | all-gather | bytes 819200 | tf_op jit(solution)/shard_map/all_gather | solution.py:93
  61.6 2.3 %all-gather.4 = bf16[4,320,256]{2,1,0:T(8,128)(2,1)S(1)} all-gather(bf16[4,160,256]{2,1,0:T(8,128)(2,1)S(1)} %get-tuple-element.10), channel_id=6, replica_groups=mesh['z'=8,'h'=2,'p'=2,'q'=2,'x'=4,'c'=2] {'c'}, dimensions={1}, use_global_device_ids=true | all-gather | bytes 983040 | tf_op jit(solution)/shard_map/all_gather | solution.py:96
  63.9 2.4 %all-gather.5 = bf16[4,320,256]{2,1,0:T(8,128)(2,1)S(1)} all-gather(bf16[4,160,256]{2,1,0:T(8,128)(2,1)S(1)} %get-tuple-element.11), channel_id=7, replica_groups=mesh['z'=8,'h'=2,'p'=2,'q'=2,'x'=4,'c'=2] {'c'}, dimensions={1}, use_global_device_ids=true | all-gather | bytes 983040 | tf_op jit(solution)/shard_map/all_gather | solution.py:96
  66.3 0.1 pad_maximum_fusion.1
  66.5 0.1 add.119
  66.6 0.3 fusion.31
  66.8 0.1 dot_general.15
  66.9 0.2 fusion.4
  67.2 0.7 broadcast_in_dim.27
  67.9 11.6 %all-to-all-start.1 = ((f32[64,4,128]{2,1,0:T(4,128)}), f32[64,4,128]{2,1,0:T(4,128)S(1)}, u32[]{:S(2)}, u32[]{:S(2)}) async-start(f32[64,4,128]{2,1,0:T(4,128)} %bitcast.3), calls=%async_computation.1 | async-start | bytes 262144 | tf_op jit(solution)/shard_map/all_to_all | solution.py:160
  79.5 0.1 slice.75
  79.7 48.1 %all-gather.8.cloned.1.call-done = bf16[4096,256]{1,0:T(8,128)(2,1)} async-done(((bf16[256,256]{1,0:T(8,128)(2,1)}), bf16[4096,256]{1,0:T(8,128)(2,1)}) %all-gather.8.cloned.1.call-update) | async-done | bytes 2097168 | tf_op jit(solution)/shard_map/all_gather | solution.py:133
  127.7 3.4 %fusion.2 = bf16[640,256]{1,0:T(8,128)(2,1)S(1)} fusion(bf16[4096,256]{1,0:T(8,128)(2,1)} %all-gather.8.cloned.1.call-done, s32[640]{0:T(1024)S(1)} %fusion.17), kind=kOutput, calls=%fused_computation.6 | convolution fusion | flops 1344962560 | bytes 2427392 | tf_op jit(solution)/shard_map/dot_general | solution.py:25
  131.2 0.9 broadcast_in_dim.30
  132.0 3.5 %all-to-all-start.2 = ((bf16[4,320,256]{2,1,0:T(8,128)(2,1)}), bf16[4,320,256]{2,1,0:T(8,128)(2,1)S(1)}, u32[]{:S(2)}, u32[]{:S(2)}) async-start(bf16[4,320,256]{2,1,0:T(8,128)(2,1)} %bitcast.7), calls=%async_computation.2 | async-start | bytes 1310720 | tf_op jit(solution)/shard_map/all_to_all | solution.py:179
  135.5 0.1 eq.115
  135.6 0.1 eq.119
  135.7 0.1 iota_compare_fusion.8
  135.8 0.1 iota_compare_fusion.9
  135.9 2.0 select_reduce_fusion
  137.9 0.1 reduce_max.9
  138.0 0.2 fusion.23
  138.2 0.1 fusion.22
  138.3 0.1 div.76
  138.3 0.1 broadcast_in_dim.31
  138.4 0.1 broadcast_in_dim_reshape.4.rel_ref
  138.5 9.5 %all-to-all-done.2 = bf16[4,320,256]{2,1,0:T(8,128)(2,1)S(1)} async-done(((bf16[4,320,256]{2,1,0:T(8,128)(2,1)}), bf16[4,320,256]{2,1,0:T(8,128)(2,1)S(1)}, u32[]{:S(2)}, u32[]{:S(2)}) %all-to-all-start.2) | async-done | bytes 655392 | tf_op jit(solution)/shard_map/all_to_all | solution.py:179
  148.0 0.1 reduce_sum.51
  148.1 13.3 %all-gather = bf16[1280,256]{1,0:T(8,128)(2,1)S(1)} all-gather(bf16[320,256]{1,0:T(8,128)(2,1)S(1)} %reduce_sum.51), channel_id=2, replica_groups=mesh['z'=8,'h'=2,'p'=2,'q'=2,'x'=4,'c'=2] {'x'}, dimensions={0}, use_global_device_ids=true | all-gather | bytes 819200 | tf_op jit(solution)/shard_map/all_gather | solution.py:93
  161.5 0.0 copy-start.2
  161.5 0.0 copy-start.3
  161.5 2.4 %all-gather.1 = bf16[4,320,256]{2,1,0:T(8,128)(2,1)S(1)} all-gather(bf16[4,160,256]{2,1,0:T(8,128)(2,1)S(1)} %get-tuple-element.12), channel_id=3, replica_groups=mesh['z'=8,'h'=2,'p'=2,'q'=2,'x'=4,'c'=2] {'c'}, dimensions={1}, use_global_device_ids=true | all-gather | bytes 983040 | tf_op jit(solution)/shard_map/all_gather | solution.py:96
  163.9 2.3 %all-gather.2 = bf16[4,320,256]{2,1,0:T(8,128)(2,1)S(1)} all-gather(bf16[4,160,256]{2,1,0:T(8,128)(2,1)S(1)} %get-tuple-element.13), channel_id=4, replica_groups=mesh['z'=8,'h'=2,'p'=2,'q'=2,'x'=4,'c'=2] {'c'}, dimensions={1}, use_global_device_ids=true | all-gather | bytes 983040 | tf_op jit(solution)/shard_map/all_gather | solution.py:96
  166.2 0.1 pad_maximum_fusion
  166.3 4.9 %reader.1 = bf16[64,64,128]{2,1,0:T(8,128)(2,1)} custom-call(s32[1]{0:T(128)} %bitcast.5.half_ref, bf16[8,320,256]{2,1,0:T(8,128)(2,1)S(1)} %bitcast.34, bf16[8,320,256]{2,1,0:T(8,128)(2,1)S(1)} %bitcast.33, f32[320,1]{1,0:T(8,128)S(1)} %broadcast_in_dim_reshape.4.rel_ref, bf16[2048,128]{1,0:T(8,128)(2,1)S(1)} %copy-done, bf16[2048,128]{1,0:T(8,128)(2,1)S(1)} %copy-done.1, ...), custom_call_target="tpu_custom_call" | custom-call | tf_op jit(solution)/shard_map/reader/pallas_call | solution.py:82
  171.2 7.5 %all-to-all-start.3 = ((bf16[64,64,128]{2,1,0:T(8,128)(2,1)}), bf16[64,64,128]{2,1,0:T(8,128)(2,1)S(1)}, u32[]{:S(2)}, u32[]{:S(2)}) async-start(bf16[64,64,128]{2,1,0:T(8,128)(2,1)} %reader.1), calls=%async_computation.3 | async-start | bytes 2097152 | tf_op jit(solution)/shard_map/all_to_all | solution.py:199
  178.6 1.2 add_reduce_fusion
  179.8 0.1 sub.45
  179.9 0.1 reshape.320
  180.0 0.1 fusion.10
  180.1 0.9 fusion.3
  181.0 0.6 constant_dynamic-slice_fusion
  181.6 26.9 %all-to-all-done.3 = bf16[64,64,128]{2,1,0:T(8,128)(2,1)S(1)} async-done(((bf16[64,64,128]{2,1,0:T(8,128)(2,1)}), bf16[64,64,128]{2,1,0:T(8,128)(2,1)S(1)}, u32[]{:S(2)}, u32[]{:S(2)}) %all-to-all-start.3) | async-done | bytes 1048608 | tf_op jit(solution)/shard_map/all_to_all | solution.py:199
  208.5 3.6 %reshape.322 = f32[32,2,2,32,2,64]{5,4,3,2,1,0:T(2,128)} reshape(bf16[64,64,128]{2,1,0:T(8,128)(2,1)S(1)} %all-to-all-done.3) | data formatting | bytes 3145728 | tf_op jit(solution)/shard_map/reshape | solution.py:201
  212.1 4.4 %reduce_sum.52 = f32[2,2,32,2,64]{4,3,2,1,0:T(2,128)S(1)} reduce(f32[32,2,2,32,2,64]{5,4,3,2,1,0:T(2,128)} %reshape.322, f32[]{:T(128)} %constant.120.clone.1), dimensions={0}, to_apply=%region_5.6 | reduce | flops 507904 | bytes 2162692 | tf_op jit(solution)/shard_map/reduce_sum | solution.py:201
  216.5 0.1 copy.42
  216.6 0.1 reshape.319
  216.7 0.6 slice_bitcast_fusion
  (25 shorter events, 0.3 us)
Async XLA Ops:
  7.2 23.9 %copy-start.5 = (bf16[160,256]{1,0:T(8,128)(2,1)S(1)}, bf16[160,256]{1,0:T(8,128)(2,1)}, u32[]{:S(2)}) copy-start(bf16[160,256]{1,0:T(8,128)(2,1)} %param.23) | copy-start | bytes 245764
  7.2 120.5 %all-gather.8.cloned.1.call-start = ((), (), s32[]{:S(2)}) async-start(), calls=%async_computation.4 | async-start | bytes 2228224 | tf_op jit(solution)/shard_map/all_gather | solution.py:133
  14.4 51.9 %all-to-all-start = ((bf16[64,2,1864]{2,1,0:T(2,128)(2,1)}), bf16[64,2,1864]{2,1,0:T(2,128)(2,1)S(1)}, u32[]{:S(2)}, u32[]{:S(2)}) async-start(bf16[64,2,1864]{2,1,0:T(2,128)(2,1)} %pad_maximum_fusion.2), calls=%async_computation | async-start | bytes 983040 | tf_op jit(solution)/shard_map/all_to_all | solution.py:153
  63.9 3.0 %copy-start.4 = (bf16[128,768]{1,0:T(8,128)(2,1)S(1)}, bf16[128,768]{1,0:T(8,128)(2,1)}, u32[]{:S(2)}) copy-start(bf16[128,768]{1,0:T(8,128)(2,1)} %param.13) | copy-start | bytes 589828
  67.9 63.3 %all-to-all-start.1 = ((f32[64,4,128]{2,1,0:T(4,128)}), f32[64,4,128]{2,1,0:T(4,128)S(1)}, u32[]{:S(2)}, u32[]{:S(2)}) async-start(f32[64,4,128]{2,1,0:T(4,128)} %bitcast.3), calls=%async_computation.1 | async-start | bytes 262144 | tf_op jit(solution)/shard_map/all_to_all | solution.py:160
  132.0 15.9 %all-to-all-start.2 = ((bf16[4,320,256]{2,1,0:T(8,128)(2,1)}), bf16[4,320,256]{2,1,0:T(8,128)(2,1)S(1)}, u32[]{:S(2)}, u32[]{:S(2)}) async-start(bf16[4,320,256]{2,1,0:T(8,128)(2,1)} %bitcast.7), calls=%async_computation.2 | async-start | bytes 1310720 | tf_op jit(solution)/shard_map/all_to_all | solution.py:179
  161.5 4.8 %copy-start = (bf16[2048,128]{1,0:T(8,128)(2,1)S(1)}, bf16[2048,128]{1,0:T(8,128)(2,1)}, u32[]{:S(2)}) copy-start(bf16[2048,128]{1,0:T(8,128)(2,1)} %wq_ref.1) | copy-start | bytes 1572868
  161.5 4.8 %copy-start.1 = (bf16[2048,128]{1,0:T(8,128)(2,1)S(1)}, bf16[2048,128]{1,0:T(8,128)(2,1)}, u32[]{:S(2)}) copy-start(bf16[2048,128]{1,0:T(8,128)(2,1)} %wk_ref.1) | copy-start | bytes 1572868
  161.5 4.8 %copy-start.2 = (bf16[2048,128]{1,0:T(8,128)(2,1)S(1)}, bf16[2048,128]{1,0:T(8,128)(2,1)}, u32[]{:S(2)}) copy-start(bf16[2048,128]{1,0:T(8,128)(2,1)} %wv_ref.1) | copy-start | bytes 1572868
  161.5 4.8 %copy-start.3 = (bf16[128,2048]{1,0:T(8,128)(2,1)S(1)}, bf16[128,2048]{1,0:T(8,128)(2,1)}, u32[]{:S(2)}) copy-start(bf16[128,2048]{1,0:T(8,128)(2,1)} %wo_ref.1) | copy-start | bytes 1572868
  171.2 37.4 %all-to-all-start.3 = ((bf16[64,64,128]{2,1,0:T(8,128)(2,1)}), bf16[64,64,128]{2,1,0:T(8,128)(2,1)S(1)}, u32[]{:S(2)}, u32[]{:S(2)}) async-start(bf16[64,64,128]{2,1,0:T(8,128)(2,1)} %reader.1), calls=%async_computation.3 | async-start | bytes 2097152 | tf_op jit(solution)/shard_map/all_to_all | solution.py:199
Sparse Core Ops, SparseCore 0:
  11.2 116.4 all-gather.7

commit v3 on v2

--- a/solution.py
+++ b/solution.py
@@ -13,7 +13,8 @@
 PLEN = 4
 CAPS = 2
 LANES = 128
-IDX = ("z", "h", "p", "q")
+IDX = ("z", "p", "q")
+M = ("x", "c")
 F32 = jnp.float32
 BF16 = jnp.bfloat16
 ROWS = (((0,), (0,)), ((), ()))
@@ -115,13 +116,13 @@
     slab_emb,
     slab_ids,
 ):
-    nq = lax.axis_size("q")
-    group = lax.axis_size("p") * nq
-    outer = lax.axis_size("z") * lax.axis_size("h")
-    owners = outer * group
-    my_outer = lax.axis_index(("z", "h"))
-    my_inner = lax.axis_index(("p", "q"))
-    my_pair = lax.axis_index(("z", "h", "p"))
+    nz, nq = lax.axis_size("z"), lax.axis_size("q")
+    ny = lax.axis_size("p") * nq
+    owners = nz * ny
+    swap = [(0, 1), (1, 0)]
+    my_z = lax.axis_index("z")
+    my_y = lax.axis_index(("p", "q"))
+    my_idx = lax.axis_index(IDX)
     my_half = lax.axis_index("q")
     pass_rows, width = index_emb.shape
     queries = query_emb.shape[0]
@@ -129,9 +130,15 @@
     count = npass * plen
     vocab_rows = vocab_table.shape[0]
     slab = slab_ids.shape[0]
-
-    vocab = lax.all_gather(vocab_table, ("z", "h"), axis=0, tiled=True)
-    full_grad = all_features(lax.all_gather(out_grad, "q", axis=0, tiled=True))
+    strips = width // LANES
+    strip = lax.rem(lax.axis_index(M), strips)
+
+    def my_strip(array):
+        return lax.dynamic_slice_in_dim(array, strip * LANES, LANES, axis=1)
+
+    vocab = lax.all_gather(vocab_table, "z", axis=0, tiled=True)
+    pair_grad = jnp.concatenate([out_grad, lax.ppermute(out_grad, "q", swap)], axis=0)
+    full_grad = lax.all_gather(pair_grad, M, axis=0)
 
     slab_owner, slab_row = slab_ids // pass_rows, slab_ids % pass_rows
     earlier = (slab_owner[:, None] == slab_owner[None, :]) & (
@@ -140,9 +147,13 @@
     slot = slab_owner * CAPS + jnp.sum(earlier.astype(jnp.int32), axis=1)
     select = (jnp.arange(owners * CAPS)[:, None] == slot[None, :]).astype(BF16)
     slab_wide = jnp.concatenate(
-        [slab_emb, jnp.broadcast_to((slab_row + 1).astype(BF16)[:, None], (slab, LANES))], axis=1
-    )
-    slab_out = dot(select, slab_wide).astype(BF16).reshape(owners, CAPS, width + LANES)
+        [
+            my_strip(slab_emb),
+            jnp.broadcast_to((slab_row + 1).astype(BF16)[:, None], (slab, LANES)),
+        ],
+        axis=1,
+    )
+    slab_out = dot(select, slab_wide).astype(BF16).reshape(owners, CAPS, 2 * LANES)
     flat_ids = token_ids.reshape(-1)
     ids_part = jnp.stack([flat_ids // LANES, flat_ids % LANES]).astype(BF16)
     place_part = jnp.stack([passage_owner[:, 0], passage_row]).astype(BF16)
@@ -151,46 +162,48 @@
         [slab_out, jnp.broadcast_to(common[None], (owners, *common.shape))], axis=2
     )
     got = lax.all_to_all(message, IDX, 0, 0, tiled=True)
-    got_slab, got_common = got[:, :, : width + LANES], got[:, :, width + LANES :]
+    got_slab, got_common = got[:, :, : 2 * LANES], got[:, :, 2 * LANES :]
 
     scores_out = dot(got_common[:, :, :width].reshape(-1, width), index_emb, COLS)
-    scores_out = jnp.repeat(
-        scores_out.reshape(owners // nq, nq * queries, pass_rows), nq, axis=0
-    )
-    scores_in = lax.all_to_all(scores_out, IDX, 0, 0, tiled=True)
-
-    got_rows = got_slab[:, :, :width].reshape(-1, width)
-    got_place = got_slab[:, :, width].reshape(-1).astype(jnp.int32) - 1
+    scores_out = scores_out.reshape(owners // nq, nq, queries, pass_rows)
+    scores_out = jnp.concatenate([scores_out, scores_out[:, ::-1]], axis=2)
+    scores_in = lax.all_to_all(
+        scores_out.reshape(owners, nq * queries, pass_rows), IDX, 0, 0, tiled=True
+    )
+
+    got_place = got_slab[:, :, LANES].reshape(-1).astype(jnp.int32) - 1
     put = jnp.arange(pass_rows)[:, None] == got_place[None, :]
-    refreshed = jnp.where(
-        jnp.any(put, axis=1)[:, None], dot(put.astype(BF16), got_rows).astype(BF16), index_emb
-    )
+    placed = dot(put.astype(BF16), got_slab[:, :, :LANES].reshape(-1, LANES)).astype(BF16)
+    refreshed = jnp.where(jnp.any(put, axis=1)[:, None], placed, my_strip(index_emb))
+    refreshed = lax.all_gather(refreshed, M, axis=0)
+    refreshed = jnp.concatenate([refreshed[i] for i in range(strips)], axis=1)
 
     ids = lax.dynamic_slice_in_dim(
-        got_common[:, :, width : width + count], my_outer * group, group, axis=0
+        got_common[:, :, width : width + count], my_z * ny, ny, axis=0
     ).astype(jnp.int32)
     ids = (ids[:, 0] * LANES + ids[:, 1]).reshape(-1)
     id_owner = ids // vocab_rows
-    local = jnp.where(
-        id_owner % group == my_inner, (id_owner // group) * vocab_rows + ids % vocab_rows, -1
-    )
-    one_hot = (local[:, None] == jnp.arange(outer * vocab_rows)[None, :]).astype(BF16)
-    served = dot(one_hot, vocab).astype(BF16).reshape(group // nq, nq * count, -1)
-    token_in = lax.all_to_all(jnp.repeat(served, nq, axis=0), ("p", "q"), 0, 0, tiled=True)
+    local = jnp.where(id_owner % ny == my_y, (id_owner // ny) * vocab_rows + ids % vocab_rows, -1)
+    one_hot = (local[:, None] == jnp.arange(nz * vocab_rows)[None, :]).astype(BF16)
+    served = dot(one_hot, vocab).astype(BF16).reshape(ny, count, -1)
+    token_in = lax.all_to_all(served, ("p", "q"), 0, 0, tiled=True)
     token_part = jnp.sum(token_in.astype(F32), axis=0).astype(BF16)
-    tokens = all_features(token_part)
-
-    places = lax.dynamic_slice_in_dim(
-        got_common[:, :, width + count :], my_pair * nq, nq, axis=0
+    tokens = all_features(
+        jnp.concatenate([token_part, lax.ppermute(token_part, "q", swap)], axis=0)
+    )
+
+    other = my_idx + 1 - 2 * my_half
+    other_place = lax.dynamic_index_in_dim(
+        got_common[:, :, width + count :], other, axis=0, keepdims=False
     ).astype(jnp.int32)
-    pair_owner, pair_row = places[:, 0].reshape(-1), places[:, 1].reshape(-1)
+    pair_owner = jnp.concatenate([passage_owner[:, 0], other_place[0]])
+    pair_row = jnp.concatenate([passage_row, other_place[1]])
     at = (pair_owner[:, None, None] == jnp.arange(owners)[None, :, None]) & (
         pair_row[:, None, None] == jnp.arange(pass_rows)[None, None, :]
     )
     table = jnp.repeat(scores_in.transpose(1, 0, 2), K, axis=0)
     scores = jnp.sum(jnp.where(at, table, 0.0), axis=(1, 2)).reshape(nq * queries, K)
     pair_relevance = jax.nn.softmax(scores, axis=-1)
-    relevance = lax.dynamic_slice_in_dim(pair_relevance, my_half * queries, queries, axis=0)
     rel = jnp.repeat(pair_relevance.reshape(-1), plen)[:, None]
 
     terms = reader(
@@ -198,18 +211,31 @@
     )
     terms = lax.all_to_all(terms, IDX, 0, 0, tiled=True)
     rows = terms.shape[1] // 2
-    sums = jnp.sum(terms.astype(F32).reshape(owners // nq, nq, 2, rows, 2, HEAD_DIM), axis=0)
-    parts = sums.transpose(1, 3, 2, 0, 4).reshape(2, 2, rows, nq * HEAD_DIM)
-    return (relevance, parts[0, 0], parts[0, 1], parts[1, 0], parts[1, 1].T, refreshed)
+    sums = jnp.sum(terms.reshape(owners // nq, nq, *terms.shape[1:]).astype(F32), axis=0)
+
+    def whole(top, left):
+        return jnp.concatenate(
+            [
+                sums[h, top * rows : (top + 1) * rows, left * HEAD_DIM : (left + 1) * HEAD_DIM]
+                for h in range(nq)
+            ],
+            axis=1,
+        )
+
+    return (
+        pair_relevance[:queries],
+        whole(0, 0),
+        whole(0, 1),
+        whole(1, 0),
+        whole(1, 1).T,
+        refreshed,
+    )
 
 
 def solution(mesh):
     devices = mesh.devices
     owners, columns = devices.shape
-    fine = Mesh(
-        devices.reshape(owners // 8, 2, 2, 2, columns // 2, 2), ("z", "h", "p", "q", "x", "c")
-    )
-    m = ("x", "c")
+    fine = Mesh(devices.reshape(owners // 8, 4, 2, columns // 2, 2), (*IDX, *M))
     return jax.shard_map(
         shards,
         mesh=fine,
@@ -219,21 +245,21 @@
             P(IDX, None),
             P(IDX),
             P(IDX, None),
-            P(IDX, m),
-            P(None, m),
-            P(None, m),
-            P(None, m),
-            P(m, None),
-            P(IDX, m),
+            P(IDX, M),
+            P(None, M),
+            P(None, M),
+            P(None, M),
+            P(M, None),
+            P(IDX, M),
             P(IDX, None),
             P(IDX),
         ),
         out_specs=(
             P(IDX, None),
-            P(IDX, m),
-            P(IDX, m),
-            P(IDX, m),
-            P(m, IDX),
+            P(IDX, M),
+            P(IDX, M),
+            P(IDX, M),
+            P(M, IDX),
             P(IDX, None),
         ),
         check_vma=False,

time: 225 us -> 169 us (0.75)
  waiting for transfers between devices: 85.2 us -> 54.7 us
  blocking collectives: 53.2 us -> 31.2 us
    all_gather x1 -> x2, waiting for transfers between devices: 48.1 us -> 4.98 us  [the longest x1 4.96 us: shards(): vocab = lax.all_gather(vocab_table, 'z', axis=0, tiled=True)]
    all_gather x2 -> x1, blocking collectives: 27.2 us -> 13.9 us  [all_features(): along_x = lax.all_gather(part, 'x', axis=0)]
    all_to_all x1, waiting for transfers between devices: 26.9 us -> 14 us  [shards(): terms = lax.all_to_all(terms, IDX, 0, 0, tiled=True)]
    ppermute x0 -> x2, waiting for transfers between devices: none -> 10.2 us  [the longest x1 6.58 us: shards(): lax.ppermute(out_grad, 'q', swap)]
    all_to_all x2, waiting for transfers between devices: 9.45 us -> 19 us  [the longest x1 15.3 us: shards(): token_in = lax.all_to_all(served, ('p', 'q'), 0, 0, tiled=True)]
    ppermute x0 -> x2, starting transfers between devices: none -> 5.81 us  [the longest x1 3.48 us: shards(): lax.ppermute(out_grad, 'q', swap)]
    all_to_all x1, waiting for transfers between devices: 0.01 us -> 5.8 us  [shards(): got = lax.all_to_all(message, IDX, 0, 0, tiled=True)]
    all_to_all x2, starting transfers between devices: 15.1 us -> 10.2 us  [the longest x1 5.9 us: shards(): lax.all_to_all(scores_out.reshape(owners, nq * queries, pass_rows), IDX,...]
  transfers between devices with their start and end apart: 5 -> 8, of which waited for: 3 -> 7; matrix products, arithmetic and copies ran while one was open for 8% -> 11% of each run, Pallas kernels for 0% -> 0%
where the time goes in v3:
time: 169 us
  waiting for transfers between devices  54.7 us (32%)
  starting transfers between devices  39 us (23%)
  blocking collectives  31.2 us (18%)
  between operations  14.4 us (9%)
  other arithmetic  11 us (7%)
  local copies, waits for them, and re-layouts  8.06 us (5%)
  matrix products  5.27 us (3%)
  Pallas kernels  4.88 us (3%)
    all_to_all x1, starting transfers between devices, shards(): got = lax.all_to_all(message, IDX, 0, 0, tiled=True)  16.6 us
    all_to_all x1, waiting for transfers between devices, shards(): token_in = lax.all_to_all(served, ('p', 'q'), 0, 0, tiled=True)  15.3 us
    all_to_all x1, waiting for transfers between devices, shards(): terms = lax.all_to_all(terms, IDX, 0, 0, tiled=True)  14 us
    all_gather x1, blocking collectives, all_features(): along_x = lax.all_gather(part, 'x', axis=0)  13.9 us
    all_gather x1, blocking collectives, shards(): refreshed = lax.all_gather(refreshed, M, axis=0)  12.8 us
    ppermute x1, waiting for transfers between devices, shards(): lax.ppermute(out_grad, 'q', swap)  6.58 us
    all_to_all x1, starting transfers between devices, shards(): terms = lax.all_to_all(terms, IDX, 0, 0, tiled=True)  6.37 us
    all_to_all x1, starting transfers between devices, shards(): lax.all_to_all(scores_out.reshape(owners, nq * queries, pass_rows), IDX,...  5.9 us
  transfers between devices with their start and end apart: 8, of which 7 were waited for; matrix products, arithmetic and copies ran while one was open for 11% of the time, Pallas kernels for 0%

profile of v3, /device:TPU:6, one launch (start us, length us, event | category | flops | bytes accessed | tf_op | source)
XLA Modules:
  0.0 168.6 jit_solution(16915855851267309844)
XLA Ops:
  7.3 0.7 all-gather.8.cloned.1.call-update
  8.0 0.7 and_select_fusion.3
  8.6 0.2 convert_reduce_fusion.1
  8.9 0.1 convolution_convert_fusion
  9.1 0.8 copy.31
  9.9 0.1 reshape.306
  10.0 0.7 convert_bitcast_fusion
  10.6 0.5 broadcast.321
  11.2 1.4 fusion.31
  12.6 0.8 maximum_maximum_fusion
  13.4 0.1 broadcast_in_dim.18
  13.5 1.0 pad_maximum_fusion.1
  14.5 16.6 %all-to-all-start = ((bf16[64,2,1224]{2,1,0:T(2,128)(2,1)}), bf16[64,2,1224]{2,1,0:T(2,128)(2,1)S(1)}, u32[]{:S(2)}, u32[]{:S(2)}) async-start(bf16[64,2,1224]{2,1,0:T(2,128)(2,1)} %pad_maximum_fusion.1), calls=%async_computation | async-start | bytes 655360 | tf_op jit(solution)/shard_map/all_to_all | solution.py:164
  31.2 3.5 %collective-permute-start.1 = (bf16[160,256]{1,0:T(8,128)(2,1)S(1)}, bf16[160,256]{1,0:T(8,128)(2,1)S(1)}, u32[]{:S(2)}, u32[]{:S(2)}) collective-permute-start(bf16[160,256]{1,0:T(8,128)(2,1)S(1)} %copy-done.7), channel_id=1, source_target_pairs={{0,8},{8,0},{1,9},{9,1},{2,10},{10,2},{3,11},{11,3},{4,12},{12,4},... | collective-permute-start | bytes 245768 | tf_op jit(solution)/shard_map/ppermute | solution.py:140
  34.7 0.1 concatenate.58
  34.8 0.1 concatenate.52
  34.9 6.6 %collective-permute-done.1 = bf16[160,256]{1,0:T(8,128)(2,1)S(1)} collective-permute-done((bf16[160,256]{1,0:T(8,128)(2,1)S(1)}, bf16[160,256]{1,0:T(8,128)(2,1)S(1)}, u32[]{:S(2)}, u32[]{:S(2)}) %collective-permute-start.1) | collective-permute-done | bytes 81952 | tf_op jit(solution)/shard_map/ppermute | solution.py:140
  41.4 0.7 pad_maximum_fusion.3
  42.1 5.8 %all-to-all-done = bf16[64,2,1224]{2,1,0:T(2,128)(2,1)S(1)} async-done(((bf16[64,2,1224]{2,1,0:T(2,128)(2,1)}), bf16[64,2,1224]{2,1,0:T(2,128)(2,1)S(1)}, u32[]{:S(2)}, u32[]{:S(2)}) %all-to-all-start) | async-done | bytes 313376 | tf_op jit(solution)/shard_map/all_to_all | solution.py:164
  48.2 0.1 slice.120
  48.3 0.2 fusion.4
  48.6 0.1 copy.33
  48.7 0.7 copy.34
  49.4 5.9 %all-to-all-start.1 = ((f32[64,4,128]{2,1,0:T(4,128)}), f32[64,4,128]{2,1,0:T(4,128)S(1)}, u32[]{:S(2)}, u32[]{:S(2)}) async-start(f32[64,4,128]{2,1,0:T(4,128)} %copy.34), calls=%async_computation.1 | async-start | bytes 262144 | tf_op jit(solution)/shard_map/all_to_all | solution.py:170
  55.3 0.1 slice.119
  55.4 5.0 %all-gather.8.cloned.1.call-done = bf16[2048,256]{1,0:T(8,128)(2,1)} async-done(((bf16[256,256]{1,0:T(8,128)(2,1)}), bf16[2048,256]{1,0:T(8,128)(2,1)}) %all-gather.8.cloned.1.call-update) | async-done | bytes 1048592 | tf_op jit(solution)/shard_map/all_gather | solution.py:139
  60.4 4.0 %fusion.2 = bf16[1280,256]{1,0:T(8,128)(2,1)} fusion(bf16[2048,256]{1,0:T(8,128)(2,1)} %all-gather.8.cloned.1.call-done, s32[1280]{0:T(1024)S(1)} %fusion.17), kind=kOutput, calls=%fused_computation.4 | convolution fusion | flops 1345126400 | bytes 1709056 | tf_op jit(solution)/shard_map/dot_general | solution.py:26
  64.4 3.7 %all-to-all-done.1 = f32[64,4,128]{2,1,0:T(4,128)S(1)} async-done(((f32[64,4,128]{2,1,0:T(4,128)}), f32[64,4,128]{2,1,0:T(4,128)S(1)}, u32[]{:S(2)}, u32[]{:S(2)}) %all-to-all-start.1) | async-done | bytes 131104 | tf_op jit(solution)/shard_map/all_to_all | solution.py:170
  68.1 4.3 %all-to-all-start.2 = ((bf16[8,160,256]{2,1,0:T(8,128)(2,1)}), bf16[8,160,256]{2,1,0:T(8,128)(2,1)S(1)}, u32[]{:S(2)}, u32[]{:S(2)}) async-start(bf16[8,160,256]{2,1,0:T(8,128)(2,1)} %bitcast.8), calls=%async_computation.2 | async-start | bytes 1310720 | tf_op jit(solution)/shard_map/all_to_all | solution.py:189
  72.4 0.1 concatenate.56
  72.5 0.1 concatenate.59
  72.6 0.1 iota_compare_fusion.9
  72.7 0.1 iota_compare_fusion.8
  72.8 2.0 %select_reduce_fusion = f32[4,20]{1,0:T(4,128)S(1)} fusion(f32[4,64,128]{2,1,0:T(8,128)S(1)} %copy.35, pred[4,20,128]{2,1,0:T(8,128)(4,1)S(1)} %iota_compare_fusion.8, pred[4,20,64]{2,1,0:T(8,128)(4,1)S(1)} %iota_compare_fusion.9), kind=kLoop, calls=%fused_computation.3 | loop fusion | flops 1966000 | bytes 146752 | tf_op jit(solution)/shard_map/reduce_sum | solution.py:205
  74.7 0.1 reduce_max.9
  74.8 0.2 fusion.23
  75.0 15.3 %all-to-all-done.2 = bf16[8,160,256]{2,1,0:T(8,128)(2,1)S(1)} async-done(((bf16[8,160,256]{2,1,0:T(8,128)(2,1)}), bf16[8,160,256]{2,1,0:T(8,128)(2,1)S(1)}, u32[]{:S(2)}, u32[]{:S(2)}) %all-to-all-start.2) | async-done | bytes 655392 | tf_op jit(solution)/shard_map/all_to_all | solution.py:189
  90.3 0.1 reduce_sum.51
  90.4 2.3 %collective-permute-start = (bf16[160,256]{1,0:T(8,128)(2,1)S(1)}, bf16[160,256]{1,0:T(8,128)(2,1)S(1)}, u32[]{:S(2)}, u32[]{:S(2)}) collective-permute-start(bf16[160,256]{1,0:T(8,128)(2,1)S(1)} %reduce_sum.51), channel_id=1, source_target_pairs={{0,8},{8,0},{1,9},{9,1},{2,10},{10,2},{3,11},{11,3},{4,12},{12,4},... | collective-permute-start | bytes 245768 | tf_op jit(solution)/shard_map/ppermute | solution.py:192
  92.8 0.1 div.76
  93.0 0.1 broadcast_in_dim_reshape.4.rel_ref
  93.1 3.7 %collective-permute-done = bf16[160,256]{1,0:T(8,128)(2,1)S(1)} collective-permute-done((bf16[160,256]{1,0:T(8,128)(2,1)S(1)}, bf16[160,256]{1,0:T(8,128)(2,1)S(1)}, u32[]{:S(2)}, u32[]{:S(2)}) %collective-permute-start) | collective-permute-done | bytes 81952 | tf_op jit(solution)/shard_map/ppermute | solution.py:192
  96.8 13.9 %all-gather = bf16[1280,256]{1,0:T(8,128)(2,1)S(1)} all-gather(bf16[320,256]{1,0:T(8,128)(2,1)S(1)} %pad_maximum_fusion.2), channel_id=2, replica_groups=mesh['z'=8,'p'=4,'q'=2,'x'=4,'c'=2] {'x'}, dimensions={0}, use_global_device_ids=true | all-gather | bytes 819200 | tf_op jit(solution)/shard_map/all_gather | solution.py:94
  110.7 2.3 %all-gather.1 = bf16[4,320,256]{2,1,0:T(8,128)(2,1)S(1)} all-gather(bf16[4,160,256]{2,1,0:T(8,128)(2,1)S(1)} %get-tuple-element.10), channel_id=3, replica_groups=mesh['z'=8,'p'=4,'q'=2,'x'=4,'c'=2] {'c'}, dimensions={1}, use_global_device_ids=true | all-gather | bytes 983040 | tf_op jit(solution)/shard_map/all_gather | solution.py:97
  112.9 2.3 %all-gather.2 = bf16[4,320,256]{2,1,0:T(8,128)(2,1)S(1)} all-gather(bf16[4,160,256]{2,1,0:T(8,128)(2,1)S(1)} %get-tuple-element.11), channel_id=4, replica_groups=mesh['z'=8,'p'=4,'q'=2,'x'=4,'c'=2] {'c'}, dimensions={1}, use_global_device_ids=true | all-gather | bytes 983040 | tf_op jit(solution)/shard_map/all_gather | solution.py:97
  115.2 0.1 pad_maximum_fusion
  115.3 0.9 copy-done.2
  116.3 0.2 copy-done.3
  116.4 0.2 copy-done.4
  116.6 1.3 copy-done.1
  117.9 1.0 copy-done.5
  118.9 4.9 %reader.1 = bf16[64,64,128]{2,1,0:T(8,128)(2,1)} custom-call(s32[1]{0:T(128)} %bitcast.7.half_ref, bf16[8,320,256]{2,1,0:T(8,128)(2,1)S(1)} %bitcast.43, bf16[8,320,256]{2,1,0:T(8,128)(2,1)S(1)} %bitcast.44, f32[320,1]{1,0:T(8,128)S(1)} %broadcast_in_dim_reshape.4.rel_ref, bf16[2048,128]{1,0:T(8,128)(2,1)S(1)} %copy-done.2, bf16[2048,128]{1,0:T(8,128)(2,1)S(1)} %copy-done.3, ...), custom_call_target="tpu_custom_call" | custom-call | tf_op jit(solution)/shard_map/reader/pallas_call | solution.py:83
  123.8 6.4 %all-to-all-start.3 = ((bf16[64,64,128]{2,1,0:T(8,128)(2,1)}), bf16[64,64,128]{2,1,0:T(8,128)(2,1)S(1)}, u32[]{:S(2)}, u32[]{:S(2)}) async-start(bf16[64,64,128]{2,1,0:T(8,128)(2,1)} %reader.1), calls=%async_computation.3 | async-start | bytes 2097152 | tf_op jit(solution)/shard_map/all_to_all | solution.py:212
  130.2 1.2 add_reduce_fusion
  131.3 0.1 sub.49
  131.5 0.1 fusion.7
  131.6 0.9 fusion.3
  132.5 12.8 %all-gather.4 = bf16[1024,128]{1,0:T(8,128)(2,1)S(1)} all-gather(bf16[128,128]{1,0:T(8,128)(2,1)S(1)} %fusion.3), channel_id=6, replica_groups=mesh['z'=8,'p'=4,'q'=2,'x'=4,'c'=2] {'x','c'}, dimensions={0}, use_global_device_ids=true | all-gather | bytes 294912 | tf_op jit(solution)/shard_map/all_gather | solution.py:178
  145.5 0.6 slice.91
  146.1 14.0 %all-to-all-done.3 = bf16[64,64,128]{2,1,0:T(8,128)(2,1)S(1)} async-done(((bf16[64,64,128]{2,1,0:T(8,128)(2,1)}), bf16[64,64,128]{2,1,0:T(8,128)(2,1)S(1)}, u32[]{:S(2)}, u32[]{:S(2)}) %all-to-all-start.3) | async-done | bytes 1048608 | tf_op jit(solution)/shard_map/all_to_all | solution.py:212
  160.1 0.2 convert_reduce_fusion
  160.3 0.1 slice_bitcast_fusion.1
  160.3 0.7 pad_maximum_fusion.7
  161.0 0.7 pad_maximum_fusion.5
  (48 shorter events, 0.9 us)
Async XLA Ops:
  7.2 1.7 copy-start
  7.2 27.5 %copy-start.9 = (s32[40]{0:T(128)S(1)}, s32[40]{0:T(128)}, u32[]{:S(2)}) copy-start(s32[40]{0:T(128)} %param.16) | copy-start | bytes 484
  7.2 24.0 %copy-start.7 = (bf16[160,256]{1,0:T(8,128)(2,1)S(1)}, bf16[160,256]{1,0:T(8,128)(2,1)}, u32[]{:S(2)}) copy-start(bf16[160,256]{1,0:T(8,128)(2,1)} %param.23) | copy-start | bytes 245764
  7.2 53.2 %all-gather.8.cloned.1.call-start = ((), (), s32[]{:S(2)}) async-start(), calls=%async_computation.4 | async-start | bytes 1179648 | tf_op jit(solution)/shard_map/all_gather | solution.py:139
  13.4 35.0 %copy-start.6 = (bf16[128,768]{1,0:T(8,128)(2,1)S(1)}, bf16[128,768]{1,0:T(8,128)(2,1)}, u32[]{:S(2)}) copy-start(bf16[128,768]{1,0:T(8,128)(2,1)} %param.13) | copy-start | bytes 589828
  14.5 33.4 %all-to-all-start = ((bf16[64,2,1224]{2,1,0:T(2,128)(2,1)}), bf16[64,2,1224]{2,1,0:T(2,128)(2,1)S(1)}, u32[]{:S(2)}, u32[]{:S(2)}) async-start(bf16[64,2,1224]{2,1,0:T(2,128)(2,1)} %pad_maximum_fusion.1), calls=%async_computation | async-start | bytes 655360 | tf_op jit(solution)/shard_map/all_to_all | solution.py:164
  31.1 84.2 %all-gather.10.cloned.1.call-start = ((), (), s32[]{:S(2)}) async-start(), calls=%async_computation.5 | async-start | bytes 1474560 | tf_op jit(solution)/shard_map/all_gather | solution.py:141
  31.2 10.3 %collective-permute-start.1 = (bf16[160,256]{1,0:T(8,128)(2,1)S(1)}, bf16[160,256]{1,0:T(8,128)(2,1)S(1)}, u32[]{:S(2)}, u32[]{:S(2)}) collective-permute-start(bf16[160,256]{1,0:T(8,128)(2,1)S(1)} %copy-done.7), channel_id=1, source_target_pairs={{0,8},{8,0},{1,9},{9,1},{2,10},{10,2},{3,11},{11,3},{4,12},{12,4},... | collective-permute-start | bytes 245768 | tf_op jit(solution)/shard_map/ppermute | solution.py:140
  49.4 18.7 %all-to-all-start.1 = ((f32[64,4,128]{2,1,0:T(4,128)}), f32[64,4,128]{2,1,0:T(4,128)S(1)}, u32[]{:S(2)}, u32[]{:S(2)}) async-start(f32[64,4,128]{2,1,0:T(4,128)} %copy.34), calls=%async_computation.1 | async-start | bytes 262144 | tf_op jit(solution)/shard_map/all_to_all | solution.py:170
  68.1 22.2 %all-to-all-start.2 = ((bf16[8,160,256]{2,1,0:T(8,128)(2,1)}), bf16[8,160,256]{2,1,0:T(8,128)(2,1)S(1)}, u32[]{:S(2)}, u32[]{:S(2)}) async-start(bf16[8,160,256]{2,1,0:T(8,128)(2,1)} %bitcast.8), calls=%async_computation.2 | async-start | bytes 1310720 | tf_op jit(solution)/shard_map/all_to_all | solution.py:189
  90.4 6.3 %collective-permute-start = (bf16[160,256]{1,0:T(8,128)(2,1)S(1)}, bf16[160,256]{1,0:T(8,128)(2,1)S(1)}, u32[]{:S(2)}, u32[]{:S(2)}) collective-permute-start(bf16[160,256]{1,0:T(8,128)(2,1)S(1)} %reduce_sum.51), channel_id=1, source_target_pairs={{0,8},{8,0},{1,9},{9,1},{2,10},{10,2},{3,11},{11,3},{4,12},{12,4},... | collective-permute-start | bytes 245768 | tf_op jit(solution)/shard_map/ppermute | solution.py:192
  115.2 1.0 copy-start.2
  115.2 1.2 copy-start.3
  115.2 1.4 copy-start.4
  116.6 1.3 copy-start.1
  117.9 1.0 copy-start.5
  123.8 36.3 %all-to-all-start.3 = ((bf16[64,64,128]{2,1,0:T(8,128)(2,1)}), bf16[64,64,128]{2,1,0:T(8,128)(2,1)S(1)}, u32[]{:S(2)}, u32[]{:S(2)}) async-start(bf16[64,64,128]{2,1,0:T(8,128)(2,1)} %reader.1), calls=%async_computation.3 | async-start | bytes 2097152 | tf_op jit(solution)/shard_map/all_to_all | solution.py:212
  145.5 16.3 %copy-start.8 = (bf16[128,768]{1,0:T(8,128)(2,1)}, bf16[128,768]{1,0:T(8,128)(2,1)S(1)}, u32[]{:S(2)}) copy-start(bf16[128,768]{1,0:T(8,128)(2,1)S(1)} %slice_dynamic-update-slice_fusion) | copy-start | bytes 589828
Sparse Core Ops, SparseCore 0:
  10.1 50.2 all-gather.7
  63.1 27.8 all-gather.9

commit v4 on v3

--- a/solution.py
+++ b/solution.py
@@ -27,9 +27,12 @@
     return lax.dot_general(a, b, dims, preferred_element_type=F32)
 
 
-def reader_kernel(
-    heads, half_ref, tokens_ref, grad_ref, rel_ref, wq_ref, wk_ref, wv_ref, wo_ref, out_ref
-):
+def reader_kernel(heads, half_ref, tokens_ref, grad_ref, rel_ref, *refs):
+    hbm, out_ref, vmem, sems = refs[:4], refs[4], refs[5:9], refs[9]
+    copies = [pltpu.make_async_copy(hbm[i], vmem[i], sems.at[i]) for i in range(4)]
+    for copy in copies:
+        copy.start()
+    wq_ref, wk_ref, wv_ref, wo_ref = vmem
     blocks, count, deep = tokens_ref.shape
     rows = out_ref.shape[1] // 2
     mine = half_ref[0]
@@ -47,8 +50,10 @@
             kept = jnp.where(mine == head, states[:, head * HEAD_DIM : (head + 1) * HEAD_DIM], kept)
         return kept
 
+    weighted = [(grad_ref[b].astype(F32) * rel).astype(BF16) for b in range(blocks)]
+    for copy in copies:
+        copy.wait()
     q, k, v = own(projected(wq_ref)), own(projected(wk_ref)), own(projected(wv_ref))
-    weighted = [(grad_ref[b].astype(F32) * rel).astype(BF16) for b in range(blocks)]
     total = dot(weighted[0], wo_ref[:, :deep], COLS)
     for b in range(1, blocks):
         total += dot(weighted[b], wo_ref[:, b * deep : (b + 1) * deep], COLS)
@@ -83,8 +88,12 @@
     return pl.pallas_call(
         functools.partial(reader_kernel, inner // HEAD_DIM),
         out_shape=jax.ShapeDtypeStruct((owners, 2 * width // owners, 2 * HEAD_DIM), BF16),
-        in_specs=[pl.BlockSpec(memory_space=pltpu.SMEM)] + [vmem] * 7,
+        in_specs=[pl.BlockSpec(memory_space=pltpu.SMEM)]
+        + [vmem] * 3
+        + [pl.BlockSpec(memory_space=pl.ANY)] * 4,
         out_specs=vmem,
+        scratch_shapes=[pltpu.VMEM((width, inner), BF16)] * 3
+        + [pltpu.VMEM((inner, width), BF16), pltpu.SemaphoreType.DMA((4,))],
         compiler_params=pltpu.CompilerParams(vmem_limit_bytes=40 * 1024 * 1024),
         name="reader",
     )(half, tokens, out_grad, rel, w_query, w_key, w_value, w_out)
@@ -120,9 +129,7 @@
     ny = lax.axis_size("p") * nq
     owners = nz * ny
     swap = [(0, 1), (1, 0)]
-    my_z = lax.axis_index("z")
     my_y = lax.axis_index(("p", "q"))
-    my_idx = lax.axis_index(IDX)
     my_half = lax.axis_index("q")
     pass_rows, width = index_emb.shape
     queries = query_emb.shape[0]
@@ -136,9 +143,43 @@
     def my_strip(array):
         return lax.dynamic_slice_in_dim(array, strip * LANES, LANES, axis=1)
 
-    vocab = lax.all_gather(vocab_table, "z", axis=0, tiled=True)
-    pair_grad = jnp.concatenate([out_grad, lax.ppermute(out_grad, "q", swap)], axis=0)
-    full_grad = lax.all_gather(pair_grad, M, axis=0)
+    deep = vocab_table.shape[1]
+    query_rows = queries * width // deep
+    pad = jnp.zeros((-query_rows % 8, deep), BF16)
+    message = jnp.concatenate([vocab_table, query_emb.reshape(query_rows, deep), pad], axis=0)
+    stride = message.shape[0]
+    got_z = lax.all_to_all(
+        jnp.broadcast_to(message[None], (nz, *message.shape)), "z", 0, 0, tiled=True
+    )
+    ids = jnp.pad(token_ids.reshape(1, -1), ((0, 0), (0, -count % LANES)))
+    ids = lax.all_gather(ids, ("p", "q"), axis=0, tiled=True)[:, :count].reshape(-1)
+
+    places = jnp.concatenate([passage_owner[:, 0], passage_row]).astype(BF16)
+    places = jnp.pad(places[None], ((0, 15), (0, deep - 2 * npass)))
+    other = lax.ppermute(jnp.concatenate([out_grad, places], axis=0), "q", swap)
+    full_grad = lax.all_gather(jnp.concatenate([out_grad, other[:count]], axis=0), M, axis=0)
+    other_place = other[count, : 2 * npass].astype(jnp.int32)
+    pair_owner = jnp.concatenate([passage_owner[:, 0], other_place[:npass]])
+    pair_row = jnp.concatenate([passage_row, other_place[npass:]])
+
+    id_owner = ids // vocab_rows
+    local = jnp.where(id_owner % ny == my_y, (id_owner // ny) * stride + ids % vocab_rows, -1)
+    one_hot = (local[:, None] == jnp.arange(nz * stride)[None, :]).astype(BF16)
+    served = dot(one_hot, got_z.reshape(nz * stride, deep)).astype(BF16).reshape(ny, count, deep)
+    z_queries = got_z[:, vocab_rows : vocab_rows + query_rows].reshape(1, nz * query_rows, deep)
+    got_y = lax.all_to_all(
+        jnp.concatenate(
+            [served, jnp.broadcast_to(z_queries, (ny, nz * query_rows, deep))], axis=1
+        ),
+        ("p", "q"),
+        0,
+        0,
+        tiled=True,
+    )
+    token_part = jnp.sum(got_y[:, :count].astype(F32), axis=0).astype(BF16)
+    tokens = all_features(
+        jnp.concatenate([token_part, lax.ppermute(token_part, "q", swap)], axis=0)
+    )
 
     slab_owner, slab_row = slab_ids // pass_rows, slab_ids % pass_rows
     earlier = (slab_owner[:, None] == slab_owner[None, :]) & (
@@ -146,58 +187,30 @@
     )
     slot = slab_owner * CAPS + jnp.sum(earlier.astype(jnp.int32), axis=1)
     select = (jnp.arange(owners * CAPS)[:, None] == slot[None, :]).astype(BF16)
-    slab_wide = jnp.concatenate(
-        [
-            my_strip(slab_emb),
-            jnp.broadcast_to((slab_row + 1).astype(BF16)[:, None], (slab, LANES)),
-        ],
-        axis=1,
-    )
-    slab_out = dot(select, slab_wide).astype(BF16).reshape(owners, CAPS, 2 * LANES)
-    flat_ids = token_ids.reshape(-1)
-    ids_part = jnp.stack([flat_ids // LANES, flat_ids % LANES]).astype(BF16)
-    place_part = jnp.stack([passage_owner[:, 0], passage_row]).astype(BF16)
-    common = jnp.concatenate([query_emb, ids_part, place_part], axis=1)
-    message = jnp.concatenate(
-        [slab_out, jnp.broadcast_to(common[None], (owners, *common.shape))], axis=2
-    )
-    got = lax.all_to_all(message, IDX, 0, 0, tiled=True)
-    got_slab, got_common = got[:, :, : 2 * LANES], got[:, :, 2 * LANES :]
-
-    scores_out = dot(got_common[:, :, :width].reshape(-1, width), index_emb, COLS)
+    slab_out = dot(select, my_strip(slab_emb)).reshape(owners, CAPS, LANES)
+    place_out = jnp.sum(jnp.where(select > 0, (slab_row + 1)[None, :], 0), axis=1)
+    place_out = jnp.broadcast_to(
+        place_out.astype(F32).reshape(owners, CAPS, 1), (owners, CAPS, LANES)
+    )
+
+    all_queries = got_y[:, count:].reshape(ny, nz, queries, width).transpose(1, 0, 2, 3)
+    scores_out = dot(all_queries.reshape(-1, width), index_emb, COLS)
     scores_out = scores_out.reshape(owners // nq, nq, queries, pass_rows)
     scores_out = jnp.concatenate([scores_out, scores_out[:, ::-1]], axis=2)
-    scores_in = lax.all_to_all(
-        scores_out.reshape(owners, nq * queries, pass_rows), IDX, 0, 0, tiled=True
-    )
-
-    got_place = got_slab[:, :, LANES].reshape(-1).astype(jnp.int32) - 1
+    back = jnp.concatenate(
+        [scores_out.reshape(owners, nq * queries, pass_rows), slab_out, place_out], axis=1
+    )
+    got = lax.all_to_all(back, IDX, 0, 0, tiled=True)
+    scores_in = got[:, : nq * queries]
+    got_slab = got[:, nq * queries : nq * queries + CAPS].reshape(-1, LANES).astype(BF16)
+    got_place = got[:, nq * queries + CAPS :, 0].reshape(-1).astype(jnp.int32) - 1
+
     put = jnp.arange(pass_rows)[:, None] == got_place[None, :]
-    placed = dot(put.astype(BF16), got_slab[:, :, :LANES].reshape(-1, LANES)).astype(BF16)
+    placed = dot(put.astype(BF16), got_slab).astype(BF16)
     refreshed = jnp.where(jnp.any(put, axis=1)[:, None], placed, my_strip(index_emb))
     refreshed = lax.all_gather(refreshed, M, axis=0)
     refreshed = jnp.concatenate([refreshed[i] for i in range(strips)], axis=1)
 
-    ids = lax.dynamic_slice_in_dim(
-        got_common[:, :, width : width + count], my_z * ny, ny, axis=0
-    ).astype(jnp.int32)
-    ids = (ids[:, 0] * LANES + ids[:, 1]).reshape(-1)
-    id_owner = ids // vocab_rows
-    local = jnp.where(id_owner % ny == my_y, (id_owner // ny) * vocab_rows + ids % vocab_rows, -1)
-    one_hot = (local[:, None] == jnp.arange(nz * vocab_rows)[None, :]).astype(BF16)
-    served = dot(one_hot, vocab).astype(BF16).reshape(ny, count, -1)
-    token_in = lax.all_to_all(served, ("p", "q"), 0, 0, tiled=True)
-    token_part = jnp.sum(token_in.astype(F32), axis=0).astype(BF16)
-    tokens = all_features(
-        jnp.concatenate([token_part, lax.ppermute(token_part, "q", swap)], axis=0)
-    )
-
-    other = my_idx + 1 - 2 * my_half
-    other_place = lax.dynamic_index_in_dim(
-        got_common[:, :, width + count :], other, axis=0, keepdims=False
-    ).astype(jnp.int32)
-    pair_owner = jnp.concatenate([passage_owner[:, 0], other_place[0]])
-    pair_row = jnp.concatenate([passage_row, other_place[1]])
     at = (pair_owner[:, None, None] == jnp.arange(owners)[None, :, None]) & (
         pair_row[:, None, None] == jnp.arange(pass_rows)[None, None, :]
     )

time: 169 us -> 175 us (1.036)
  blocking collectives: 31.2 us -> 47.8 us
  waiting for transfers between devices: 54.7 us -> 44.3 us
  starting transfers between devices: 39 us -> 40.8 us
  matrix products: 5.27 us -> 3.48 us
    all_gather x0 -> x1, blocking collectives: none -> 16.5 us  [shards(): lax.all_gather(ids, ('p', 'q'), axis=0, tiled=True)[:, :count].reshape(-1)]
    ppermute x1, waiting for transfers between devices: 6.58 us -> 0.01 us  [shards(): other = lax.ppermute(jnp.concatenate([out_grad, places], axis=0), 'q', swap)]
    all_to_all x1, starting transfers between devices: 6.37 us -> 12.6 us  [shards(): terms = lax.all_to_all(terms, IDX, 0, 0, tiled=True)]
    all_to_all x3, waiting for transfers between devices: 24.8 us -> 30.3 us  [the longest x1 22.7 us: shards(): lax.all_to_all(jnp.concatenate([served, jnp.broadcast_to(z_queries, (ny,...]
    all_gather x2 -> x1, waiting for transfers between devices: 4.98 us -> 0.02 us  [shards(): lax.all_gather(jnp.concatenate([out_grad, other[:count]], axis=0), M, axi...]
    all_to_all x3, starting transfers between devices: 26.8 us -> 22.2 us  [the longest x1 10.5 us: shards(): lax.all_to_all(jnp.broadcast_to(message[None], (nz, *message.shape)), 'z'...]
    ppermute x1, waiting for transfers between devices: 3.65 us -> 0.01 us  [shards(): lax.ppermute(token_part, 'q', swap)]
    unnamed x27 -> x35, local copies, waits for them, and re-layouts: 4.96 us -> 3.07 us
  transfers between devices with their start and end apart: 8 -> 7, of which waited for: 7 -> 3; matrix products, arithmetic and copies ran while one was open for 11% -> 8% of each run, Pallas kernels for 0% -> 0%
where the time goes in v4:
time: 175 us; the launch traced here: 174 us
  blocking collectives  47.8 us (27%)
  waiting for transfers between devices  44.3 us (25%)
  starting transfers between devices  40.8 us (23%)
  between operations  14.5 us (8%)
  other arithmetic  9.31 us (5%)
  local copies, waits for them, and re-layouts  8.29 us (5%)
  Pallas kernels  5.3 us (3%)
  matrix products  3.48 us (2%)
    all_to_all x1, waiting for transfers between devices, shards(): lax.all_to_all(jnp.concatenate([served, jnp.broadcast_to(z_queries, (ny,...  22.7 us
    all_gather x1, blocking collectives, shards(): lax.all_gather(ids, ('p', 'q'), axis=0, tiled=True)[:, :count].reshape(-1)  16.5 us
    all_to_all x1, waiting for transfers between devices, shards(): terms = lax.all_to_all(terms, IDX, 0, 0, tiled=True)  14 us
    all_gather x1, blocking collectives, all_features(): along_x = lax.all_gather(part, 'x', axis=0)  13.9 us
    all_gather x1, blocking collectives, shards(): refreshed = lax.all_gather(refreshed, M, axis=0)  12.8 us
    all_to_all x1, starting transfers between devices, shards(): terms = lax.all_to_all(terms, IDX, 0, 0, tiled=True)  12.6 us
    all_to_all x1, starting transfers between devices, shards(): lax.all_to_all(jnp.broadcast_to(message[None], (nz, *message.shape)), 'z'...  10.5 us
    all_to_all x1, waiting for transfers between devices, shards(): lax.all_to_all(jnp.broadcast_to(message[None], (nz, *message.shape)), 'z'...  7.61 us
  transfers between devices with their start and end apart: 7, of which 3 were waited for; matrix products, arithmetic and copies ran while one was open for 8% of the time, Pallas kernels for 0%

profile of v4, /device:TPU:6, one launch (start us, length us, event | category | flops | bytes accessed | tf_op | source)
XLA Modules:
  0.0 173.8 jit_solution(3876934486116153345)
XLA Ops:
  7.2 0.7 reshape.267
  7.9 0.1 pad.33.clone
  8.0 1.0 maximum_maximum_fusion
  9.0 1.1 broadcast_in_dim.40
  10.1 10.5 %all-to-all-start = ((bf16[8,264,256]{2,1,0:T(8,128)(2,1)}), bf16[8,264,256]{2,1,0:T(8,128)(2,1)S(1)}, u32[]{:S(2)}, u32[]{:S(2)}) async-start(bf16[8,264,256]{2,1,0:T(8,128)(2,1)} %broadcast_in_dim.40), calls=%async_computation | async-start | bytes 2162688 | tf_op jit(solution)/shard_map/all_to_all | solution.py:151
  20.6 0.5 broadcast.235
  21.1 0.7 fusion.34
  21.8 0.1 fusion.25
  21.8 3.5 %collective-permute-start = (bf16[176,256]{1,0:T(8,128)(2,1)S(1)}, bf16[176,256]{1,0:T(8,128)(2,1)S(1)}, u32[]{:S(2)}, u32[]{:S(2)}) collective-permute-start(bf16[176,256]{1,0:T(8,128)(2,1)S(1)} %pad_maximum_fusion.6), channel_id=1, source_target_pairs={{0,8},{8,0},{1,9},{9,1},{2,10},{10,2},{3,11},{11,3},{4,12},{12,4},... | collective-permute-start | bytes 270344 | tf_op jit(solution)/shard_map/ppermute | solution.py:159
  25.4 0.1 copy.47
  25.4 0.1 reshape.265
  25.6 16.5 %all-gather.5 = s32[8,1,256]{2,1,0:T(1,128)S(1)} all-gather(s32[1,1,256]{2,1,0:T(1,128)S(1)} %pad_bitcast_fusion), channel_id=1, replica_groups=mesh['z'=8,'p'=4,'q'=2,'x'=4,'c'=2] {'p','q'}, dimensions={0}, use_global_device_ids=true | all-gather | bytes 9216 | tf_op jit(solution)/shard_map/all_gather | solution.py:155
  42.1 0.1 reshape.266
  42.2 0.2 convert_reduce_fusion.1
  42.4 7.6 %all-to-all-done = bf16[8,264,256]{2,1,0:T(8,128)(2,1)S(1)} async-done(((bf16[8,264,256]{2,1,0:T(8,128)(2,1)}), bf16[8,264,256]{2,1,0:T(8,128)(2,1)S(1)}, u32[]{:S(2)}, u32[]{:S(2)}) %all-to-all-start) | async-done | bytes 1081376 | tf_op jit(solution)/shard_map/all_to_all | solution.py:151
  50.0 2.1 %fusion.2 = bf16[1280,256]{1,0:T(8,128)(2,1)S(1)} fusion(bf16[2112,256]{1,0:T(8,128)(2,1)S(1)} %bitcast.59, s32[1280]{0:T(1024)S(1)} %fusion.24), kind=kOutput, calls=%fused_computation.4 | convolution fusion | flops 1387151360 | bytes 1741824 | tf_op jit(solution)/shard_map/dot_general | solution.py:26
  52.1 1.0 pad_maximum_fusion.1
  53.1 7.1 %all-to-all-start.1 = ((bf16[8,208,256]{2,1,0:T(8,128)(2,1)}), bf16[8,208,256]{2,1,0:T(8,128)(2,1)S(1)}, u32[]{:S(2)}, u32[]{:S(2)}) async-start(bf16[8,208,256]{2,1,0:T(8,128)(2,1)} %pad_maximum_fusion.1), calls=%async_computation.1 | async-start | bytes 1703936 | tf_op jit(solution)/shard_map/all_to_all | solution.py:170
  60.3 0.1 concatenate.72
  60.4 0.3 fusion.12
  60.7 0.1 select_reduce_fusion.1
  60.8 0.1 convert_element_type.65
  61.0 0.1 concatenate.66
  61.1 0.1 slice_reduce_fusion.2
  61.2 0.1 slice.99
  61.3 0.1 slice.101
  61.4 0.7 pad_maximum_fusion.4
  62.1 0.1 iota_compare_fusion.7
  62.2 0.1 iota_compare_fusion.6
  62.3 22.7 %all-to-all-done.1 = bf16[8,208,256]{2,1,0:T(8,128)(2,1)S(1)} async-done(((bf16[8,208,256]{2,1,0:T(8,128)(2,1)}), bf16[8,208,256]{2,1,0:T(8,128)(2,1)S(1)}, u32[]{:S(2)}, u32[]{:S(2)}) %all-to-all-start.1) | async-done | bytes 852000 | tf_op jit(solution)/shard_map/all_to_all | solution.py:170
  85.0 0.1 reshape.270
  85.1 0.1 copy.48
  85.2 0.2 fusion.4
  85.5 0.1 copy.50
  85.6 0.1 slice_reduce_fusion
  85.7 2.5 %collective-permute-start.1 = (bf16[160,256]{1,0:T(8,128)(2,1)S(1)}, bf16[160,256]{1,0:T(8,128)(2,1)S(1)}, u32[]{:S(2)}, u32[]{:S(2)}) collective-permute-start(bf16[160,256]{1,0:T(8,128)(2,1)S(1)} %slice_reduce_fusion), channel_id=1, source_target_pairs={{0,8},{8,0},{1,9},{9,1},{2,10},{10,2},{3,11},{11,3},{4,12},{12,4},... | collective-permute-start | bytes 245768 | tf_op jit(solution)/shard_map/ppermute | solution.py:181
  88.3 0.9 copy.53
  89.1 4.6 %all-to-all-start.2 = ((f32[64,8,128]{2,1,0:T(8,128)}), f32[64,8,128]{2,1,0:T(8,128)S(1)}, u32[]{:S(2)}, u32[]{:S(2)}) async-start(f32[64,8,128]{2,1,0:T(8,128)} %copy.53), calls=%async_computation.2 | async-start | bytes 524288 | tf_op jit(solution)/shard_map/all_to_all | solution.py:203
  93.8 13.9 %all-gather = bf16[1280,256]{1,0:T(8,128)(2,1)S(1)} all-gather(bf16[320,256]{1,0:T(8,128)(2,1)S(1)} %pad_maximum_fusion.3), channel_id=2, replica_groups=mesh['z'=8,'p'=4,'q'=2,'x'=4,'c'=2] {'x'}, dimensions={0}, use_global_device_ids=true | all-gather | bytes 819200 | tf_op jit(solution)/shard_map/all_gather | solution.py:103
  107.7 2.3 %all-gather.1 = bf16[4,320,256]{2,1,0:T(8,128)(2,1)S(1)} all-gather(bf16[4,160,256]{2,1,0:T(8,128)(2,1)S(1)} %get-tuple-element.8), channel_id=3, replica_groups=mesh['z'=8,'p'=4,'q'=2,'x'=4,'c'=2] {'c'}, dimensions={1}, use_global_device_ids=true | all-gather | bytes 983040 | tf_op jit(solution)/shard_map/all_gather | solution.py:106
  110.0 2.3 %all-gather.2 = bf16[4,320,256]{2,1,0:T(8,128)(2,1)S(1)} all-gather(bf16[4,160,256]{2,1,0:T(8,128)(2,1)S(1)} %get-tuple-element.9), channel_id=4, replica_groups=mesh['z'=8,'p'=4,'q'=2,'x'=4,'c'=2] {'c'}, dimensions={1}, use_global_device_ids=true | all-gather | bytes 983040 | tf_op jit(solution)/shard_map/all_gather | solution.py:106
  112.3 0.1 pad_maximum_fusion
  112.4 2.0 %select_reduce_fusion = f32[4,20]{1,0:T(4,128)S(1)} fusion(f32[4,64,128]{2,1,0:T(8,128)S(1)} %copy.54, pred[4,20,128]{2,1,0:T(8,128)(4,1)S(1)} %iota_compare_fusion.6, pred[4,20,64]{2,1,0:T(8,128)(4,1)S(1)} %iota_compare_fusion.7), kind=kLoop, calls=%fused_computation.3 | loop fusion | flops 1966000 | bytes 146752 | tf_op jit(solution)/shard_map/reduce_sum | solution.py:218
  114.4 0.1 reduce_max.9
  114.5 0.2 fusion.30
  114.7 0.1 fusion.29
  114.8 0.1 div.60
  114.8 0.1 broadcast_in_dim.49
  114.9 0.1 broadcast_in_dim_reshape.4.rel_ref
  115.1 1.3 copy-done.1
  116.4 1.0 copy-done.5
  117.5 5.3 %reader.1 = bf16[64,64,128]{2,1,0:T(8,128)(2,1)} custom-call(s32[1]{0:T(128)} %bitcast.12.half_ref, bf16[8,320,256]{2,1,0:T(8,128)(2,1)S(1)} %bitcast.53, bf16[8,320,256]{2,1,0:T(8,128)(2,1)S(1)} %bitcast.54, f32[320,1]{1,0:T(8,128)S(1)} %broadcast_in_dim_reshape.4.rel_ref, bf16[2048,128]{1,0:T(8,128)(2,1)S(1)} %copy-done.2, ...), custom_call_target="tpu_custom_call" | custom-call | tf_op jit(solution)/shard_map/reader/pallas_call | solution.py:88
  122.8 12.6 %all-to-all-start.3 = ((bf16[64,64,128]{2,1,0:T(8,128)(2,1)}), bf16[64,64,128]{2,1,0:T(8,128)(2,1)S(1)}, u32[]{:S(2)}, u32[]{:S(2)}) async-start(bf16[64,64,128]{2,1,0:T(8,128)(2,1)} %reader.1), calls=%async_computation.3 | async-start | bytes 2097152 | tf_op jit(solution)/shard_map/all_to_all | solution.py:225
  135.4 0.6 slice.106
  136.0 1.2 fusion.8
  137.1 0.1 sub.38
  137.3 0.1 fusion.9
  137.4 0.9 fusion.3
  138.3 12.8 %all-gather.4 = bf16[1024,128]{1,0:T(8,128)(2,1)S(1)} all-gather(bf16[128,128]{1,0:T(8,128)(2,1)S(1)} %fusion.3), channel_id=6, replica_groups=mesh['z'=8,'p'=4,'q'=2,'x'=4,'c'=2] {'x','c'}, dimensions={0}, use_global_device_ids=true | all-gather | bytes 294912 | tf_op jit(solution)/shard_map/all_gather | solution.py:211
  151.3 14.0 %all-to-all-done.3 = bf16[64,64,128]{2,1,0:T(8,128)(2,1)S(1)} async-done(((bf16[64,64,128]{2,1,0:T(8,128)(2,1)}), bf16[64,64,128]{2,1,0:T(8,128)(2,1)S(1)}, u32[]{:S(2)}, u32[]{:S(2)}) %all-to-all-start.3) | async-done | bytes 1048608 | tf_op jit(solution)/shard_map/all_to_all | solution.py:225
  165.3 0.2 convert_reduce_fusion
  165.5 0.1 slice_bitcast_fusion.2
  165.5 0.7 pad_maximum_fusion.9
  166.2 0.7 pad_maximum_fusion.7
  (64 shorter events, 0.7 us)
Async XLA Ops:
  7.2 53.2 %copy-start = (bf16[64,768]{1,0:T(8,128)(2,1)S(1)}, bf16[64,768]{1,0:T(8,128)(2,1)}, u32[]{:S(2)}) copy-start(bf16[64,768]{1,0:T(8,128)(2,1)} %param.24) | copy-start | bytes 294916
  10.1 10.5 %copy-start.12 = (s32[40]{0:T(128)S(1)}, s32[40]{0:T(128)}, u32[]{:S(2)}) copy-start(s32[40]{0:T(128)} %param.16) | copy-start | bytes 484
  10.1 11.0 %copy-start.10 = (s32[40,1]{0,1:T(1,128)S(1)}, s32[40,1]{0,1:T(1,128)}, u32[]{:S(2)}) copy-start(s32[40,1]{0,1:T(1,128)} %param.15) | copy-start | bytes 484
  10.1 11.8 %copy-start.6 = (bf16[160,256]{1,0:T(8,128)(2,1)S(1)}, bf16[160,256]{1,0:T(8,128)(2,1)}, u32[]{:S(2)}) copy-start(bf16[160,256]{1,0:T(8,128)(2,1)} %param.23) | copy-start | bytes 245764
  10.1 15.3 %copy-start.9 = (s32[40,4]{0,1:T(4,128)S(1)}, s32[40,4]{0,1:T(4,128)}, u32[]{:S(2)}) copy-start(s32[40,4]{0,1:T(4,128)} %param.17) | copy-start | bytes 1924
  10.1 32.1 %copy-start.11 = (s32[64]{0:T(128)S(1)}, s32[64]{0:T(128)}, u32[]{:S(2)}) copy-start(s32[64]{0:T(128)} %param.25) | copy-start | bytes 772
  10.1 39.9 %all-to-all-start = ((bf16[8,264,256]{2,1,0:T(8,128)(2,1)}), bf16[8,264,256]{2,1,0:T(8,128)(2,1)S(1)}, u32[]{:S(2)}, u32[]{:S(2)}) async-start(bf16[8,264,256]{2,1,0:T(8,128)(2,1)} %broadcast_in_dim.40), calls=%async_computation | async-start | bytes 2162688 | tf_op jit(solution)/shard_map/all_to_all | solution.py:151
  21.8 39.2 %collective-permute-start = (bf16[176,256]{1,0:T(8,128)(2,1)S(1)}, bf16[176,256]{1,0:T(8,128)(2,1)S(1)}, u32[]{:S(2)}, u32[]{:S(2)}) collective-permute-start(bf16[176,256]{1,0:T(8,128)(2,1)S(1)} %pad_maximum_fusion.6), channel_id=1, source_target_pairs={{0,8},{8,0},{1,9},{9,1},{2,10},{10,2},{3,11},{11,3},{4,12},{12,4},... | collective-permute-start | bytes 270344 | tf_op jit(solution)/shard_map/ppermute | solution.py:159
  53.1 31.8 %all-to-all-start.1 = ((bf16[8,208,256]{2,1,0:T(8,128)(2,1)}), bf16[8,208,256]{2,1,0:T(8,128)(2,1)S(1)}, u32[]{:S(2)}, u32[]{:S(2)}) async-start(bf16[8,208,256]{2,1,0:T(8,128)(2,1)} %pad_maximum_fusion.1), calls=%async_computation.1 | async-start | bytes 1703936 | tf_op jit(solution)/shard_map/all_to_all | solution.py:170
  60.2 25.0 %copy-start.7 = (bf16[128,768]{1,0:T(8,128)(2,1)S(1)}, bf16[128,768]{1,0:T(8,128)(2,1)}, u32[]{:S(2)}) copy-start(bf16[128,768]{1,0:T(8,128)(2,1)} %param.13) | copy-start | bytes 589828
  60.2 54.8 %all-gather.8.cloned.1.call-start = ((), (), s32[]{:S(2)}) async-start(), calls=%async_computation.4 | async-start | bytes 1474560 | tf_op jit(solution)/shard_map/all_gather | solution.py:160
  85.7 8.1 %collective-permute-start.1 = (bf16[160,256]{1,0:T(8,128)(2,1)S(1)}, bf16[160,256]{1,0:T(8,128)(2,1)S(1)}, u32[]{:S(2)}, u32[]{:S(2)}) collective-permute-start(bf16[160,256]{1,0:T(8,128)(2,1)S(1)} %slice_reduce_fusion), channel_id=1, source_target_pairs={{0,8},{8,0},{1,9},{9,1},{2,10},{10,2},{3,11},{11,3},{4,12},{12,4},... | collective-permute-start | bytes 245768 | tf_op jit(solution)/shard_map/ppermute | solution.py:181
  89.1 23.2 %all-to-all-start.2 = ((f32[64,8,128]{2,1,0:T(8,128)}), f32[64,8,128]{2,1,0:T(8,128)S(1)}, u32[]{:S(2)}, u32[]{:S(2)}) async-start(f32[64,8,128]{2,1,0:T(8,128)} %copy.53), calls=%async_computation.2 | async-start | bytes 524288 | tf_op jit(solution)/shard_map/all_to_all | solution.py:203
  112.3 2.8 %copy-start.2 = (bf16[2048,128]{1,0:T(8,128)(2,1)S(1)}, bf16[2048,128]{1,0:T(8,128)(2,1)}, u32[]{:S(2)}) copy-start(bf16[2048,128]{1,0:T(8,128)(2,1)} %refs_0_.1) | copy-start | bytes 1572868
  112.3 2.8 %copy-start.3 = (bf16[2048,128]{1,0:T(8,128)(2,1)S(1)}, bf16[2048,128]{1,0:T(8,128)(2,1)}, u32[]{:S(2)}) copy-start(bf16[2048,128]{1,0:T(8,128)(2,1)} %refs_1_.1) | copy-start | bytes 1572868
  112.3 2.8 %copy-start.4 = (bf16[2048,128]{1,0:T(8,128)(2,1)S(1)}, bf16[2048,128]{1,0:T(8,128)(2,1)}, u32[]{:S(2)}) copy-start(bf16[2048,128]{1,0:T(8,128)(2,1)} %refs_2_.1) | copy-start | bytes 1572868
  115.1 1.3 copy-start.1
  116.4 1.0 copy-start.5
  122.8 42.5 %all-to-all-start.3 = ((bf16[64,64,128]{2,1,0:T(8,128)(2,1)}), bf16[64,64,128]{2,1,0:T(8,128)(2,1)S(1)}, u32[]{:S(2)}, u32[]{:S(2)}) async-start(bf16[64,64,128]{2,1,0:T(8,128)(2,1)} %reader.1), calls=%async_computation.3 | async-start | bytes 2097152 | tf_op jit(solution)/shard_map/all_to_all | solution.py:225
  151.3 15.7 %copy-start.8 = (bf16[128,768]{1,0:T(8,128)(2,1)}, bf16[128,768]{1,0:T(8,128)(2,1)S(1)}, u32[]{:S(2)}) copy-start(bf16[128,768]{1,0:T(8,128)(2,1)S(1)} %slice_dynamic-update-slice_fusion) | copy-start | bytes 589828
Sparse Core Ops, SparseCore 0:
  63.8 24.0 all-gather.7

commit v5 on v4

v5 whole, which is shorter than its diff:
```python
import functools

import jax
import jax.numpy as jnp
from jax import lax
from jax.experimental import pallas as pl
from jax.experimental.pallas import tpu as pltpu
from jax.sharding import Mesh
from jax.sharding import PartitionSpec as P

HEAD_DIM = 64
K = 20
PLEN = 4
LANES = 128
IDX = ("z", "p", "q")
M = ("x", "c")
F32 = jnp.float32
BF16 = jnp.bfloat16
ROWS = (((0,), (0,)), ((), ()))
COLS = (((1,), (1,)), ((), ()))


def dot(a, b, dims=None):
    if dims is None:
        return jnp.dot(a, b, preferred_element_type=F32)
    return lax.dot_general(a, b, dims, preferred_element_type=F32)


def reader_kernel(heads, half_ref, high_ref, query_ref, *refs):
    token_refs, grad_refs, hbm = refs[:2], refs[2:4], refs[4:8]
    out_ref, rel_ref, vmem, sems = refs[8], refs[9], refs[10:14], refs[14]
    copies = [pltpu.make_async_copy(hbm[i], vmem[i], sems.at[i]) for i in range(4)]
    for copy in copies:
        copy.start()
    wq_ref, wk_ref, wv_ref, wo_ref = vmem
    nc, nx, count, deep = grad_refs[0].shape
    blocks = 2 * nx * nc
    strips, passages = query_ref.shape[:2]
    rows = out_ref.shape[1] // 2
    mine = half_ref[0]

    def block(pair, b, low, high):
        x, c = divmod(b, nc)
        return pair[x // nx][c, x % nx, low:high, :]

    acc = jnp.zeros((passages, deep), F32)
    for s in range(strips):
        fetched = block(token_refs, s, count, count + passages)
        acc += fetched.astype(F32) * query_ref[s].astype(F32)
    low = jnp.sum(acc[:, :LANES], axis=1, keepdims=True)
    high = jnp.sum(acc[:, LANES:], axis=1, keepdims=True)
    scores = jnp.where(high_ref[...] > 0, high, low)
    queries = passages // K
    p = lax.broadcasted_iota(jnp.int32, (passages, queries), 0)
    first = lax.broadcasted_iota(jnp.int32, (passages, queries), 1) * K
    group = (p >= first) & (p < first + K)
    top = jnp.max(jnp.where(group, scores, -jnp.inf), axis=0, keepdims=True)
    exps = jnp.where(group, jnp.exp(scores - top), 0.0)
    rel_column = jnp.sum(exps / jnp.sum(exps, axis=0, keepdims=True), axis=1, keepdims=True)
    same = lax.broadcasted_iota(jnp.int32, (passages, passages), 0) == lax.broadcasted_iota(
        jnp.int32, (passages, passages), 1
    )
    rel_row = jnp.sum(jnp.where(same, rel_column, 0.0), axis=0, keepdims=True)
    rel_ref[...] = rel_row
    token = lax.broadcasted_iota(jnp.int32, (count, passages), 0)
    begin = lax.broadcasted_iota(jnp.int32, (count, passages), 1) * PLEN
    of_token = (token >= begin) & (token < begin + PLEN)
    rel = jnp.sum(jnp.where(of_token, rel_row, 0.0), axis=1, keepdims=True)

    tokens = [block(token_refs, b, 0, count) for b in range(blocks)]
    weighted = [
        (block(grad_refs, b, 0, count).astype(F32) * rel).astype(BF16) for b in range(blocks)
    ]
    for copy in copies:
        copy.wait()

    def projected(weight_ref):
        total = dot(tokens[0], weight_ref[:deep])
        for b in range(1, blocks):
            total += dot(tokens[b], weight_ref[b * deep : (b + 1) * deep])
        return total.astype(BF16)

    def own(states):
        kept = states[:, :HEAD_DIM]
        for head in range(1, heads):
            kept = jnp.where(mine == head, states[:, head * HEAD_DIM : (head + 1) * HEAD_DIM], kept)
        return kept

    q, k, v = own(projected(wq_ref)), own(projected(wk_ref)), own(projected(wv_ref))
    total = dot(weighted[0], wo_ref[:, :deep], COLS)
    for b in range(1, blocks):
        total += dot(weighted[b], wo_ref[:, b * deep : (b + 1) * deep], COLS)
    c = own(total.astype(BF16))
    passage_i = lax.broadcasted_iota(jnp.int32, (count, count), 0) // PLEN
    passage_j = lax.broadcasted_iota(jnp.int32, (count, count), 1) // PLEN
    logits = jnp.where(passage_i == passage_j, dot(q, k, COLS), -jnp.inf)
    exps = jnp.exp(logits - jnp.max(logits, axis=1, keepdims=True))
    probs = exps / jnp.sum(exps, axis=1, keepdims=True)
    attn = probs.astype(BF16)
    attn_grad = dot(c, v, COLS)
    mean = jnp.sum(attn_grad * probs, axis=1, keepdims=True)
    score_grad = (probs * (attn_grad - mean)).astype(BF16)
    query_grad = dot(score_grad, k).astype(BF16)
    key_grad = dot(score_grad, q, ROWS).astype(BF16)
    value_grad = dot(attn, c, ROWS).astype(BF16)
    context = dot(attn, v).astype(BF16)
    query_key = jnp.concatenate([query_grad, key_grad], axis=1)
    each = deep // rows
    for b in range(blocks):
        upper = dot(tokens[b], query_key, ROWS).astype(BF16)
        lower = jnp.concatenate(
            [dot(tokens[b], value_grad, ROWS), dot(weighted[b], context, ROWS)], axis=1
        ).astype(BF16)
        out_ref[b * each : (b + 1) * each, :rows, :] = upper.reshape(each, rows, -1)
        out_ref[b * each : (b + 1) * each, rows:, :] = lower.reshape(each, rows, -1)


def reader(half, high, query, tokens, out_grad, weights, owners):
    width, inner = weights[0].shape
    passages = query.shape[1]
    vmem = pl.BlockSpec(memory_space=pltpu.VMEM)
    return pl.pallas_call(
        functools.partial(reader_kernel, inner // HEAD_DIM),
        out_shape=(
            jax.ShapeDtypeStruct((owners, 2 * width // owners, 2 * HEAD_DIM), BF16),
            jax.ShapeDtypeStruct((1, passages), F32),
        ),
        in_specs=[pl.BlockSpec(memory_space=pltpu.SMEM)]
        + [vmem] * 6
        + [pl.BlockSpec(memory_space=pl.ANY)] * 4,
        out_specs=(vmem, vmem),
        scratch_shapes=[pltpu.VMEM((width, inner), BF16)] * 3
        + [pltpu.VMEM((inner, width), BF16), pltpu.SemaphoreType.DMA((4,))],
        compiler_params=pltpu.CompilerParams(vmem_limit_bytes=40 * 1024 * 1024),
        name="reader",
    )(half, high, query, *tokens, *out_grad, *weights)


def all_features(part):
    along_x = lax.all_gather(part, "x", axis=0)
    half = along_x.shape[0] // 2
    return [lax.all_gather(along_x[i * half : (i + 1) * half], "c", axis=0) for i in range(2)]


def shards(
    index_emb,
    query_emb,
    passage_owner,
    passage_row,
    token_ids,
    vocab_table,
    w_query,
    w_key,
    w_value,
    w_out,
    out_grad,
    slab_emb,
    slab_ids,
):
    nz, nq = lax.axis_size("z"), lax.axis_size("q")
    ny = lax.axis_size("p") * nq
    owners = nz * ny
    swap = [(0, 1), (1, 0)]
    my_y = lax.axis_index(("p", "q"))
    my_idx = lax.axis_index(IDX)
    my_half = lax.axis_index("q")
    pass_rows, width = index_emb.shape
    queries = query_emb.shape[0]
    npass, plen = token_ids.shape
    count = npass * plen
    vocab_rows = vocab_table.shape[0]
    slab = slab_ids.shape[0]
    strips = width // LANES
    strip = lax.rem(lax.axis_index(M), strips)

    def my_strip(array):
        return lax.dynamic_slice_in_dim(array, strip * LANES, LANES, axis=1)

    deep = vocab_table.shape[1]
    index_strip = my_strip(index_emb)
    folded = pass_rows // 2
    message = jnp.concatenate(
        [vocab_table, jnp.concatenate([index_strip[:folded], index_strip[folded:]], axis=1)], axis=0
    )
    stride = message.shape[0]
    got_z = lax.all_to_all(
        jnp.broadcast_to(message[None], (nz, *message.shape)), "z", 0, 0, tiled=True
    )
    wanted = jnp.concatenate([token_ids.reshape(-1), passage_owner[:, 0], passage_row])
    wanted = jnp.pad(wanted[None], ((0, 0), (0, -wanted.shape[0] % LANES)))
    wanted = lax.all_gather(wanted, ("p", "q"), axis=0, tiled=True)

    query_strips = query_emb.reshape(queries, strips, LANES).transpose(1, 0, 2)
    extra = jnp.concatenate(
        [
            query_strips.reshape(strips, queries * LANES),
            jnp.pad(passage_row.astype(BF16)[None], ((0, 0), (0, deep - npass))),
        ],
        axis=0,
    )
    extra = jnp.pad(extra, ((0, -extra.shape[0] % 16), (0, 0)))
    other = lax.ppermute(jnp.concatenate([out_grad, extra], axis=0), "q", swap)
    grads = all_features(jnp.concatenate([out_grad, other[:count]], axis=0))
    other_strips = other[count : count + strips].reshape(strips, queries, LANES)
    pair_query = jnp.concatenate([query_strips, other_strips], axis=1)
    pair_query = jnp.repeat(jnp.concatenate([pair_query, pair_query], axis=2), K, axis=1)
    other_row = other[count + strips, :npass].astype(jnp.int32)
    high = (jnp.concatenate([passage_row, other_row])[:, None] >= folded).astype(jnp.int32)

    ids, place_owner, place_row = (
        wanted[:, :count],
        wanted[:, count : count + npass],
        wanted[:, count + npass : count + 2 * npass],
    )
    id_owner = ids // vocab_rows
    token_at = jnp.where(id_owner % ny == my_y, id_owner // ny * stride + ids % vocab_rows, -1)
    place_at = jnp.where(
        place_owner % ny == my_y,
        place_owner // ny * stride + vocab_rows + place_row % folded,
        -1,
    )
    at = jnp.concatenate([token_at, place_at], axis=1).reshape(-1)
    one_hot = (at[:, None] == jnp.arange(nz * stride)[None, :]).astype(BF16)
    served = dot(one_hot, got_z.reshape(nz * stride, deep)).astype(BF16)
    got_y = lax.all_to_all(
        served.reshape(ny, count + npass, deep), ("p", "q"), 0, 0, tiled=True
    )
    got_y, grads = lax.optimization_barrier((got_y, grads))
    part = jnp.sum(got_y.astype(F32), axis=0).astype(BF16)
    other_part = lax.ppermute(part, "q", swap)
    tokens = all_features(
        jnp.concatenate(
            [part[:count], other_part[:count], part[count:], other_part[count:]], axis=0
        )
    )

    slab_ids_row = jnp.concatenate([slab_ids // pass_rows, slab_ids % pass_rows]).astype(BF16)
    slab_part = jnp.concatenate(
        [my_strip(slab_emb), jnp.pad(slab_ids_row[None], ((0, 15), (0, 0)))], axis=0
    )
    slabs = lax.all_gather(slab_part, IDX, axis=0)
    slab_at = slabs[:, slab].astype(jnp.int32)
    slab_at = jnp.where(slab_at[:, :slab] == my_idx, slab_at[:, slab:], -1)
    slab_at = jnp.pad(slab_at, ((0, 0), (0, 16)), constant_values=-1).reshape(-1)
    put = jnp.arange(pass_rows)[:, None] == slab_at[None, :]
    placed = dot(put.astype(BF16), slabs.reshape(-1, LANES)).astype(BF16)
    refreshed = jnp.where(jnp.any(put, axis=1)[:, None], placed, index_strip)
    refreshed = lax.all_gather(refreshed, M, axis=0)
    refreshed = jnp.concatenate([refreshed[i] for i in range(strips)], axis=1)

    terms, pair_relevance = reader(
        my_half.reshape(1), high, pair_query, tokens, grads, (w_query, w_key, w_value, w_out), owners
    )
    relevance = pair_relevance[0, :npass].reshape(queries, K)
    terms = lax.all_to_all(terms, IDX, 0, 0, tiled=True)
    rows = terms.shape[1] // 2
    sums = jnp.sum(terms.reshape(owners // nq, nq, *terms.shape[1:]).astype(F32), axis=0)

    def whole(top, left):
        return jnp.concatenate(
            [
                sums[h, top * rows : (top + 1) * rows, left * HEAD_DIM : (left + 1) * HEAD_DIM]
                for h in range(nq)
            ],
            axis=1,
        )

    return (
        relevance,
        whole(0, 0),
        whole(0, 1),
        whole(1, 0),
        whole(1, 1).T,
        refreshed,
    )


def solution(mesh):
    devices = mesh.devices
    owners, columns = devices.shape
    fine = Mesh(devices.reshape(owners // 8, 4, 2, columns // 2, 2), (*IDX, *M))
    return jax.shard_map(
        shards,
        mesh=fine,
        in_specs=(
            P(IDX, None),
            P(IDX, None),
            P(IDX, None),
            P(IDX),
            P(IDX, None),
            P(IDX, M),
            P(None, M),
            P(None, M),
            P(None, M),
            P(M, None),
            P(IDX, M),
            P(IDX, None),
            P(IDX),
        ),
        out_specs=(
            P(IDX, None),
            P(IDX, M),
            P(IDX, M),
            P(IDX, M),
            P(M, IDX),
            P(IDX, None),
        ),
        check_vma=False,
    )
```

time: 175 us -> 187 us (1.069)
  blocking collectives: 47.8 us -> 66.4 us
  waiting for transfers between devices: 44.3 us -> 53.4 us
  starting transfers between devices: 40.8 us -> 32.4 us
  local copies, waits for them, and re-layouts: 8.29 us -> 3.52 us
  other arithmetic: 9.31 us -> 5.11 us
    all_gather x1, waiting for transfers between devices: 0.02 us -> 20.5 us  [shards(): slabs = lax.all_gather(slab_part, IDX, axis=0)]
    all_to_all x2 -> x1, waiting for transfers between devices: 22.7 us -> 5.34 us  [shards(): lax.all_to_all(served.reshape(ny, count + npass, deep), ('p', 'q'), 0, 0,...]
    all_gather x1 -> x2, blocking collectives: 13.9 us -> 27.6 us  [all_features(): along_x = lax.all_gather(part, 'x', axis=0)]
    all_to_all x1, waiting for transfers between devices: 7.61 us -> 13.2 us  [shards(): lax.all_to_all(jnp.broadcast_to(message[None], (nz, *message.shape)), 'z'...]
    all_gather x3 -> x5, blocking collectives: 21.1 us -> 26 us  [the longest x1 16.5 us: shards(): wanted = lax.all_gather(wanted, ('p', 'q'), axis=0, tiled=True)]
    all_to_all x2 -> x1, starting transfers between devices: 11.7 us -> 7.18 us  [shards(): lax.all_to_all(served.reshape(ny, count + npass, deep), ('p', 'q'), 0, 0,...]
    all_to_all x1, starting transfers between devices: 12.6 us -> 8.88 us  [shards(): terms = lax.all_to_all(terms, IDX, 0, 0, tiled=True)]
    unnamed x35 -> x34, local copies, waits for them, and re-layouts: 3.07 us -> 0.23 us
  transfers between devices with their start and end apart: 7 -> 6, of which waited for: 3 -> 4; matrix products, arithmetic and copies ran while one was open for 8% -> 5% of each run, Pallas kernels for 0% -> 0%
where the time goes in v5:
time: 187 us; the launch traced here: 186 us
  blocking collectives  66.4 us (36%)
  waiting for transfers between devices  53.4 us (29%)
  starting transfers between devices  32.4 us (17%)
  between operations  14.5 us (8%)
  Pallas kernels  5.72 us (3%)
  matrix products  5.27 us (3%)
  other arithmetic  5.11 us (3%)
  local copies, waits for them, and re-layouts  3.52 us (2%)
    all_gather x2, blocking collectives, all_features(): along_x = lax.all_gather(part, 'x', axis=0)  27.6 us
    all_gather x1, waiting for transfers between devices, shards(): slabs = lax.all_gather(slab_part, IDX, axis=0)  20.5 us
    all_gather x1, blocking collectives, shards(): wanted = lax.all_gather(wanted, ('p', 'q'), axis=0, tiled=True)  16.5 us
    all_to_all x1, waiting for transfers between devices, shards(): terms = lax.all_to_all(terms, IDX, 0, 0, tiled=True)  14.3 us
    all_to_all x1, waiting for transfers between devices, shards(): lax.all_to_all(jnp.broadcast_to(message[None], (nz, *message.shape)), 'z'...  13.2 us
    all_gather x1, blocking collectives, shards(): refreshed = lax.all_gather(refreshed, M, axis=0)  12.8 us
    all_to_all x1, starting transfers between devices, shards(): lax.all_to_all(jnp.broadcast_to(message[None], (nz, *message.shape)), 'z'...  10.5 us
    all_gather x4, blocking collectives, all_features(): lax.all_gather(along_x[i * half:(i + 1) * half], 'c', axis=0)  9.44 us
  transfers between devices with their start and end apart: 6, of which 4 were waited for; matrix products, arithmetic and copies ran while one was open for 5% of the time, Pallas kernels for 0%

profile of v5, /device:TPU:6, one launch (start us, length us, event | category | flops | bytes accessed | tf_op | source)
XLA Modules:
  0.0 186.3 jit_solution(16406099864919589842)
XLA Ops:
  7.2 0.0 copy-start
  7.2 0.8 constant_dynamic-slice_fusion
  8.0 0.9 maximum_maximum_fusion
  8.9 1.1 broadcast_in_dim.39
  10.1 0.0 copy-start.8
  10.1 0.0 copy-start.10
  10.1 10.5 %all-to-all-start = ((bf16[8,320,256]{2,1,0:T(8,128)(2,1)}), bf16[8,320,256]{2,1,0:T(8,128)(2,1)S(1)}, u32[]{:S(2)}, u32[]{:S(2)}) async-start(bf16[8,320,256]{2,1,0:T(8,128)(2,1)} %broadcast_in_dim.39), calls=%async_computation | async-start | bytes 2621440 | tf_op jit(solution)/shard_map/all_to_all | solution.py:186
  20.5 0.0 all-gather.11.cloned.1.call-start
  20.6 0.0 copy-done.7
  20.6 0.0 copy-done.11
  20.6 0.0 copy-done.5
  20.7 3.5 %collective-permute-start = (bf16[176,256]{1,0:T(8,128)(2,1)S(1)}, bf16[176,256]{1,0:T(8,128)(2,1)S(1)}, u32[]{:S(2)}, u32[]{:S(2)}) collective-permute-start(bf16[176,256]{1,0:T(8,128)(2,1)S(1)} %fusion.9), channel_id=1, source_target_pairs={{0,8},{8,0},{1,9},{9,1},{2,10},{10,2},{3,11},{11,3},{4,12},{12,4},... | collective-permute-start | bytes 270344 | tf_op jit(solution)/shard_map/ppermute | solution.py:202
  24.2 0.0 copy-done.12
  24.2 0.1 fusion.27
  24.3 0.0 copy-done
  24.3 0.6 pad_maximum_fusion.2
  24.9 0.0 all-gather.11.cloned.1.call-update
  24.9 0.1 copy.35
  25.0 0.1 reshape.121
  25.1 0.1 pad_add_fusion.1
  25.2 16.5 %all-gather.8 = s32[8,1,256]{2,1,0:T(1,128)S(1)} all-gather(s32[1,1,256]{2,1,0:T(1,128)S(1)} %pad_bitcast_fusion), channel_id=1, replica_groups=mesh['z'=8,'p'=4,'q'=2,'x'=4,'c'=2] {'p','q'}, dimensions={0}, use_global_device_ids=true | all-gather | bytes 9216 | tf_op jit(solution)/shard_map/all_gather | solution.py:191
  41.7 0.1 fusion.24
  41.9 0.1 pad_add_fusion
  41.9 0.1 eq.60
  42.0 13.2 %all-to-all-done = bf16[8,320,256]{2,1,0:T(8,128)(2,1)S(1)} async-done(((bf16[8,320,256]{2,1,0:T(8,128)(2,1)}), bf16[8,320,256]{2,1,0:T(8,128)(2,1)S(1)}, u32[]{:S(2)}, u32[]{:S(2)}) %all-to-all-start) | async-done | bytes 1310752 | tf_op jit(solution)/shard_map/all_to_all | solution.py:186
  55.2 3.9 %fusion.4 = bf16[1600,256]{1,0:T(8,128)(2,1)} fusion(bf16[2560,256]{1,0:T(8,128)(2,1)S(1)} %bitcast.66, s32[1600]{0:T(1024)S(1)} %eq.60), kind=kOutput, calls=%fused_computation.6 | convolution fusion | flops 2101657600 | bytes 2136320 | tf_op jit(solution)/shard_map/dot_general | solution.py:25
  59.1 7.2 %all-to-all-start.1 = ((bf16[8,200,256]{2,1,0:T(8,128)(2,1)}), bf16[8,200,256]{2,1,0:T(8,128)(2,1)S(1)}, u32[]{:S(2)}, u32[]{:S(2)}) async-start(bf16[8,200,256]{2,1,0:T(8,128)(2,1)} %bitcast.11), calls=%async_computation.1 | async-start | bytes 1638400 | tf_op jit(solution)/shard_map/all_to_all | solution.py:225
  66.3 0.0 collective-permute-done
  66.4 0.1 reshape.120.query_ref
  66.4 0.1 compare_convert_fusion
  66.5 0.1 copy.36.high_ref
  66.7 13.8 %all-gather = bf16[1280,256]{1,0:T(8,128)(2,1)S(1)} all-gather(bf16[320,256]{1,0:T(8,128)(2,1)S(1)} %pad_maximum_fusion.1), channel_id=2, replica_groups=mesh['z'=8,'p'=4,'q'=2,'x'=4,'c'=2] {'x'}, dimensions={0}, use_global_device_ids=true | all-gather | bytes 819200 | tf_op jit(solution)/shard_map/all_gather | solution.py:140
  80.5 2.3 %all-gather.1 = bf16[4,320,256]{2,1,0:T(8,128)(2,1)S(1)} all-gather(bf16[2,320,256]{2,1,0:T(8,128)(2,1)S(1)} %bitcast.68), channel_id=3, replica_groups=mesh['z'=8,'p'=4,'q'=2,'x'=4,'c'=2] {'c'}, dimensions={0}, use_global_device_ids=true | all-gather | bytes 983040 | tf_op jit(solution)/shard_map/all_gather | solution.py:142
  82.8 2.3 %all-gather.2 = bf16[4,320,256]{2,1,0:T(8,128)(2,1)S(1)} all-gather(bf16[2,320,256]{2,1,0:T(8,128)(2,1)S(1)} %bitcast.67), channel_id=4, replica_groups=mesh['z'=8,'p'=4,'q'=2,'x'=4,'c'=2] {'c'}, dimensions={0}, use_global_device_ids=true | all-gather | bytes 983040 | tf_op jit(solution)/shard_map/all_gather | solution.py:142
  85.0 5.3 %all-to-all-done.1 = bf16[8,200,256]{2,1,0:T(8,128)(2,1)S(1)} async-done(((bf16[8,200,256]{2,1,0:T(8,128)(2,1)}), bf16[8,200,256]{2,1,0:T(8,128)(2,1)S(1)}, u32[]{:S(2)}, u32[]{:S(2)}) %all-to-all-start.1) | async-done | bytes 819232 | tf_op jit(solution)/shard_map/all_to_all | solution.py:225
  90.4 0.1 reduce_sum.21
  90.5 2.4 %collective-permute-start.1 = (bf16[200,256]{1,0:T(8,128)(2,1)S(1)}, bf16[200,256]{1,0:T(8,128)(2,1)S(1)}, u32[]{:S(2)}, u32[]{:S(2)}) collective-permute-start(bf16[200,256]{1,0:T(8,128)(2,1)S(1)} %reduce_sum.21), channel_id=1, source_target_pairs={{0,8},{8,0},{1,9},{9,1},{2,10},{10,2},{3,11},{11,3},{4,12},{12,4},... | collective-permute-start | bytes 307208 | tf_op jit(solution)/shard_map/ppermute | solution.py:230
  92.9 20.5 %all-gather.11.cloned.1.call-done = bf16[5120,128]{1,0:T(8,128)(2,1)} async-done(((bf16[80,128]{1,0:T(8,128)(2,1)}), bf16[5120,128]{1,0:T(8,128)(2,1)}) %all-gather.11.cloned.1.call-update) | async-done | bytes 1310736 | tf_op jit(solution)/shard_map/all_gather | solution.py:241
  113.4 0.9 slice_convert_fusion
  114.4 0.0 collective-permute-done.1
  114.4 13.9 %all-gather.3 = bf16[1600,256]{1,0:T(8,128)(2,1)S(1)} all-gather(bf16[400,256]{1,0:T(8,128)(2,1)S(1)} %pad_maximum_fusion), channel_id=5, replica_groups=mesh['z'=8,'p'=4,'q'=2,'x'=4,'c'=2] {'x'}, dimensions={0}, use_global_device_ids=true | all-gather | bytes 1024000 | tf_op jit(solution)/shard_map/all_gather | solution.py:140
  128.3 0.1 fusion.33
  128.4 0.0 copy-start.1
  128.4 0.0 copy-start.2
  128.4 0.0 copy-start.3
  128.4 0.0 copy-start.4
  128.4 2.5 %all-gather.4 = bf16[4,400,256]{2,1,0:T(8,128)(2,1)S(1)} all-gather(bf16[2,400,256]{2,1,0:T(8,128)(2,1)S(1)} %bitcast.65), channel_id=6, replica_groups=mesh['z'=8,'p'=4,'q'=2,'x'=4,'c'=2] {'c'}, dimensions={0}, use_global_device_ids=true | all-gather | bytes 1228800 | tf_op jit(solution)/shard_map/all_gather | solution.py:142
  130.9 2.4 %all-gather.5 = bf16[4,400,256]{2,1,0:T(8,128)(2,1)S(1)} all-gather(bf16[2,400,256]{2,1,0:T(8,128)(2,1)S(1)} %bitcast.64), channel_id=7, replica_groups=mesh['z'=8,'p'=4,'q'=2,'x'=4,'c'=2] {'c'}, dimensions={0}, use_global_device_ids=true | all-gather | bytes 1228800 | tf_op jit(solution)/shard_map/all_gather | solution.py:142
  133.3 0.0 copy-done.2
  133.3 5.7 %reader.1 = (bf16[64,64,128]{2,1,0:T(8,128)(2,1)}, f32[1,80]{1,0:T(1,128)S(1)}) custom-call(s32[1]{0:T(128)} %bitcast.half_ref, s32[80,1]{1,0:T(8,128)S(1)} %copy.36.high_ref, bf16[6,80,256]{2,1,0:T(8,128)(2,1)S(1)} %reshape.120.query_ref, bf16[2,2,400,256]{3,2,1,0:T(8,128)(2,1)S(1)} %bitcast.59, bf16[2,2,400,256]{3,2,1,0:T(8,128)(2,1)S(1)} %bitcast.60, ...), custom_call_target="tpu_custom_call" | custom-call | tf_op jit(solution)/shard_map/reader/pallas_call | solution.py:122
  139.1 0.0 copy-start.9
  139.1 8.9 %all-to-all-start.2 = ((bf16[64,64,128]{2,1,0:T(8,128)(2,1)}), bf16[64,64,128]{2,1,0:T(8,128)(2,1)S(1)}, u32[]{:S(2)}, u32[]{:S(2)}) async-start(bf16[64,64,128]{2,1,0:T(8,128)(2,1)} %get-tuple-element.15), calls=%async_computation.2 | async-start | bytes 2097152 | tf_op jit(solution)/shard_map/all_to_all | solution.py:255
  148.0 0.1 slice_select_fusion
  148.1 0.1 eq.67
  148.1 0.4 fusion.3
  148.6 1.3 fusion.7
  149.9 12.8 %all-gather.7 = bf16[1024,128]{1,0:T(8,128)(2,1)S(1)} all-gather(bf16[128,128]{1,0:T(8,128)(2,1)S(1)} %fusion.7), channel_id=9, replica_groups=mesh['z'=8,'p'=4,'q'=2,'x'=4,'c'=2] {'x','c'}, dimensions={0}, use_global_device_ids=true | all-gather | bytes 294912 | tf_op jit(solution)/shard_map/all_gather | solution.py:248
  162.8 0.0 copy-start.6
  162.9 0.6 reshape_squeeze.3
  163.5 14.3 %all-to-all-done.2 = bf16[64,64,128]{2,1,0:T(8,128)(2,1)S(1)} async-done(((bf16[64,64,128]{2,1,0:T(8,128)(2,1)}), bf16[64,64,128]{2,1,0:T(8,128)(2,1)S(1)}, u32[]{:S(2)}, u32[]{:S(2)}) %all-to-all-start.2) | async-done | bytes 1048608 | tf_op jit(solution)/shard_map/all_to_all | solution.py:255
  177.9 0.2 convert_reduce_fusion
  178.0 0.1 slice_bitcast_fusion.1
  178.1 0.7 pad_maximum_fusion.5
  178.8 0.7 pad_maximum_fusion.3
  (41 shorter events, 0.4 us)
Async XLA Ops:
  7.2 17.1 %copy-start = (bf16[64,768]{1,0:T(8,128)(2,1)S(1)}, bf16[64,768]{1,0:T(8,128)(2,1)}, u32[]{:S(2)}) copy-start(bf16[64,768]{1,0:T(8,128)(2,1)} %param.24) | copy-start | bytes 294916
  10.0 10.5 %copy-start.7 = (bf16[2,768]{1,0:T(2,128)(2,1)S(1)}, bf16[2,768]{1,0:T(2,128)(2,1)}, u32[]{:S(2)}) copy-start(bf16[2,768]{1,0:T(2,128)(2,1)} %param.14) | copy-start | bytes 9220
  10.0 10.6 %copy-start.11 = (s32[40]{0:T(128)S(1)}, s32[40]{0:T(128)}, u32[]{:S(2)}) copy-start(s32[40]{0:T(128)} %param.16) | copy-start | bytes 484
  10.0 10.6 %copy-start.5 = (bf16[160,256]{1,0:T(8,128)(2,1)S(1)}, bf16[160,256]{1,0:T(8,128)(2,1)}, u32[]{:S(2)}) copy-start(bf16[160,256]{1,0:T(8,128)(2,1)} %param.23) | copy-start | bytes 245764
  10.0 14.1 %copy-start.12 = (s32[64]{0:T(128)S(1)}, s32[64]{0:T(128)}, u32[]{:S(2)}) copy-start(s32[64]{0:T(128)} %param.25) | copy-start | bytes 772
  10.1 14.9 %copy-start.8 = (s32[40,4]{0,1:T(4,128)S(1)}, s32[40,4]{0,1:T(4,128)}, u32[]{:S(2)}) copy-start(s32[40,4]{0,1:T(4,128)} %param.17) | copy-start | bytes 1924
  10.1 15.1 %copy-start.10 = (s32[40,1]{0,1:T(1,128)S(1)}, s32[40,1]{0,1:T(1,128)}, u32[]{:S(2)}) copy-start(s32[40,1]{0,1:T(1,128)} %param.15) | copy-start | bytes 484
  10.1 45.1 %all-to-all-start = ((bf16[8,320,256]{2,1,0:T(8,128)(2,1)}), bf16[8,320,256]{2,1,0:T(8,128)(2,1)S(1)}, u32[]{:S(2)}, u32[]{:S(2)}) async-start(bf16[8,320,256]{2,1,0:T(8,128)(2,1)} %broadcast_in_dim.39), calls=%async_computation | async-start | bytes 2621440 | tf_op jit(solution)/shard_map/all_to_all | solution.py:186
  20.5 92.9 %all-gather.11.cloned.1.call-start = ((), (), s32[]{:S(2)}) async-start(), calls=%async_computation.3 | async-start | bytes 1331200 | tf_op jit(solution)/shard_map/all_gather | solution.py:241
  20.7 45.6 %collective-permute-start = (bf16[176,256]{1,0:T(8,128)(2,1)S(1)}, bf16[176,256]{1,0:T(8,128)(2,1)S(1)}, u32[]{:S(2)}, u32[]{:S(2)}) collective-permute-start(bf16[176,256]{1,0:T(8,128)(2,1)S(1)} %fusion.9), channel_id=1, source_target_pairs={{0,8},{8,0},{1,9},{9,1},{2,10},{10,2},{3,11},{11,3},{4,12},{12,4},... | collective-permute-start | bytes 270344 | tf_op jit(solution)/shard_map/ppermute | solution.py:202
  59.1 31.3 %all-to-all-start.1 = ((bf16[8,200,256]{2,1,0:T(8,128)(2,1)}), bf16[8,200,256]{2,1,0:T(8,128)(2,1)S(1)}, u32[]{:S(2)}, u32[]{:S(2)}) async-start(bf16[8,200,256]{2,1,0:T(8,128)(2,1)} %bitcast.11), calls=%async_computation.1 | async-start | bytes 1638400 | tf_op jit(solution)/shard_map/all_to_all | solution.py:225
  90.5 23.9 %collective-permute-start.1 = (bf16[200,256]{1,0:T(8,128)(2,1)S(1)}, bf16[200,256]{1,0:T(8,128)(2,1)S(1)}, u32[]{:S(2)}, u32[]{:S(2)}) collective-permute-start(bf16[200,256]{1,0:T(8,128)(2,1)S(1)} %reduce_sum.21), channel_id=1, source_target_pairs={{0,8},{8,0},{1,9},{9,1},{2,10},{10,2},{3,11},{11,3},{4,12},{12,4},... | collective-permute-start | bytes 307208 | tf_op jit(solution)/shard_map/ppermute | solution.py:230
  128.4 5.0 %copy-start.1 = (bf16[2048,128]{1,0:T(8,128)(2,1)S(1)}, bf16[2048,128]{1,0:T(8,128)(2,1)}, u32[]{:S(2)}) copy-start(bf16[2048,128]{1,0:T(8,128)(2,1)} %refs_4_.1) | copy-start | bytes 1572868
  128.4 4.9 %copy-start.2 = (bf16[2048,128]{1,0:T(8,128)(2,1)S(1)}, bf16[2048,128]{1,0:T(8,128)(2,1)}, u32[]{:S(2)}) copy-start(bf16[2048,128]{1,0:T(8,128)(2,1)} %refs_5_.1) | copy-start | bytes 1572868
  128.4 4.9 %copy-start.3 = (bf16[2048,128]{1,0:T(8,128)(2,1)S(1)}, bf16[2048,128]{1,0:T(8,128)(2,1)}, u32[]{:S(2)}) copy-start(bf16[2048,128]{1,0:T(8,128)(2,1)} %refs_6_.1) | copy-start | bytes 1572868
  128.4 4.9 %copy-start.4 = (bf16[128,2048]{1,0:T(8,128)(2,1)S(1)}, bf16[128,2048]{1,0:T(8,128)(2,1)}, u32[]{:S(2)}) copy-start(bf16[128,2048]{1,0:T(8,128)(2,1)} %refs_7_.1) | copy-start | bytes 1572868
  139.1 9.5 %copy-start.9 = (bf16[5120,128]{1,0:T(8,128)(2,1)S(1)}, bf16[5120,128]{1,0:T(8,128)(2,1)}, u32[]{:S(2)}) copy-start(bf16[5120,128]{1,0:T(8,128)(2,1)} %all-gather.11.cloned.1.call-done) | copy-start | bytes 3932164
  139.1 38.8 %all-to-all-start.2 = ((bf16[64,64,128]{2,1,0:T(8,128)(2,1)}), bf16[64,64,128]{2,1,0:T(8,128)(2,1)S(1)}, u32[]{:S(2)}, u32[]{:S(2)}) async-start(bf16[64,64,128]{2,1,0:T(8,128)(2,1)} %get-tuple-element.15), calls=%async_computation.2 | async-start | bytes 2097152 | tf_op jit(solution)/shard_map/all_to_all | solution.py:255
  162.8 16.6 %copy-start.6 = (bf16[128,768]{1,0:T(8,128)(2,1)}, bf16[128,768]{1,0:T(8,128)(2,1)S(1)}, u32[]{:S(2)}) copy-start(bf16[128,768]{1,0:T(8,128)(2,1)S(1)} %slice_dynamic-update-slice_fusion) | copy-start | bytes 589828
Sparse Core Ops, SparseCore 0:
  25.0 88.3 all-gather.10

commit v6 on v5

--- a/solution.py
+++ b/solution.py
@@ -11,6 +11,7 @@
 HEAD_DIM = 64
 K = 20
 PLEN = 4
+CAPS = 2
 LANES = 128
 IDX = ("z", "p", "q")
 M = ("x", "c")
@@ -162,7 +163,6 @@
     owners = nz * ny
     swap = [(0, 1), (1, 0)]
     my_y = lax.axis_index(("p", "q"))
-    my_idx = lax.axis_index(IDX)
     my_half = lax.axis_index("q")
     pass_rows, width = index_emb.shape
     queries = query_emb.shape[0]
@@ -234,24 +234,33 @@
         )
     )
 
-    slab_ids_row = jnp.concatenate([slab_ids // pass_rows, slab_ids % pass_rows]).astype(BF16)
-    slab_part = jnp.concatenate(
-        [my_strip(slab_emb), jnp.pad(slab_ids_row[None], ((0, 15), (0, 0)))], axis=0
-    )
-    slabs = lax.all_gather(slab_part, IDX, axis=0)
-    slab_at = slabs[:, slab].astype(jnp.int32)
-    slab_at = jnp.where(slab_at[:, :slab] == my_idx, slab_at[:, slab:], -1)
-    slab_at = jnp.pad(slab_at, ((0, 0), (0, 16)), constant_values=-1).reshape(-1)
-    put = jnp.arange(pass_rows)[:, None] == slab_at[None, :]
-    placed = dot(put.astype(BF16), slabs.reshape(-1, LANES)).astype(BF16)
+    slab_owner, slab_row = slab_ids // pass_rows, slab_ids % pass_rows
+    earlier = (slab_owner[:, None] == slab_owner[None, :]) & (
+        jnp.arange(slab)[:, None] > jnp.arange(slab)[None, :]
+    )
+    slot = slab_owner * CAPS + jnp.sum(earlier.astype(jnp.int32), axis=1)
+    select = (jnp.arange(owners * CAPS)[:, None] == slot[None, :]).astype(BF16)
+    slab_wide = jnp.concatenate(
+        [
+            my_strip(slab_emb),
+            jnp.broadcast_to((slab_row + 1).astype(BF16)[:, None], (slab, LANES)),
+        ],
+        axis=1,
+    )
+    slab_out = dot(select, slab_wide).astype(BF16).reshape(owners, CAPS, 2 * LANES)
+    slab_out, _ = lax.optimization_barrier((slab_out, part))
+    got_slab = lax.all_to_all(slab_out, IDX, 0, 0, tiled=True).reshape(-1, 2 * LANES)
+    got_place = got_slab[:, LANES].astype(jnp.int32) - 1
+    put = jnp.arange(pass_rows)[:, None] == got_place[None, :]
+    placed = dot(put.astype(BF16), got_slab[:, :LANES]).astype(BF16)
     refreshed = jnp.where(jnp.any(put, axis=1)[:, None], placed, index_strip)
+    terms, pair_relevance = reader(
+        my_half.reshape(1), high, pair_query, tokens, grads, (w_query, w_key, w_value, w_out), owners
+    )
+    relevance = pair_relevance[0, :npass].reshape(queries, K)
+    refreshed, terms = lax.optimization_barrier((refreshed, terms))
     refreshed = lax.all_gather(refreshed, M, axis=0)
     refreshed = jnp.concatenate([refreshed[i] for i in range(strips)], axis=1)
-
-    terms, pair_relevance = reader(
-        my_half.reshape(1), high, pair_query, tokens, grads, (w_query, w_key, w_value, w_out), owners
-    )
-    relevance = pair_relevance[0, :npass].reshape(queries, K)
     terms = lax.all_to_all(terms, IDX, 0, 0, tiled=True)
     rows = terms.shape[1] // 2
     sums = jnp.sum(terms.reshape(owners // nq, nq, *terms.shape[1:]).astype(F32), axis=0)

time: 187 us -> 164 us (0.88)
  waiting for transfers between devices: 53.4 us -> 34.4 us
  between operations: 14.5 us -> 1.04 us
  starting transfers between devices: 32.4 us -> 41 us
    all_gather x1 -> x0, waiting for transfers between devices: 20.5 us -> none  [shards(): slabs = lax.all_gather(slab_part, IDX, axis=0)]
    all_to_all x0 -> x1, starting transfers between devices: none -> 4.63 us  [shards(): lax.all_to_all(slab_out, IDX, 0, 0, tiled=True).reshape(-1, 2 * LANES)]
    all_to_all x1, starting transfers between devices: 8.88 us -> 12.9 us  [shards(): terms = lax.all_to_all(terms, IDX, 0, 0, tiled=True)]
    all_to_all x1, waiting for transfers between devices: 14.3 us -> 16.3 us  [shards(): terms = lax.all_to_all(terms, IDX, 0, 0, tiled=True)]
    dot_general x2 -> x3, matrix products: 5.27 us -> 4.97 us  [dot(): return jnp.dot(a, b, preferred_element_type=F32)]
  transfers between devices with their start and end apart: 6 -> 6, of which waited for: 4 -> 3; matrix products, arithmetic and copies ran while one was open for 5% -> 4% of each run, Pallas kernels for 0% -> 4%
where the time goes in v6:
time: 164 us; the launch traced here: 163 us
  blocking collectives  67 us (41%)
  starting transfers between devices  41 us (25%)
  waiting for transfers between devices  34.4 us (21%)
  Pallas kernels  5.74 us (4%)
  matrix products  4.97 us (3%)
  other arithmetic  4.74 us (3%)
  local copies, waits for them, and re-layouts  4.21 us (3%)
    all_gather x2, blocking collectives, all_features(): along_x = lax.all_gather(part, 'x', axis=0)  28.2 us
    all_gather x1, blocking collectives, shards(): wanted = lax.all_gather(wanted, ('p', 'q'), axis=0, tiled=True)  16.5 us
    all_to_all x1, waiting for transfers between devices, shards(): terms = lax.all_to_all(terms, IDX, 0, 0, tiled=True)  16.3 us
    all_to_all x1, starting transfers between devices, shards(): terms = lax.all_to_all(terms, IDX, 0, 0, tiled=True)  12.9 us
    all_gather x1, blocking collectives, shards(): refreshed = lax.all_gather(refreshed, M, axis=0)  12.8 us
    all_to_all x1, waiting for transfers between devices, shards(): lax.all_to_all(jnp.broadcast_to(message[None], (nz, *message.shape)), 'z'...  12.6 us
    all_to_all x1, starting transfers between devices, shards(): lax.all_to_all(jnp.broadcast_to(message[None], (nz, *message.shape)), 'z'...  10.5 us
    all_gather x4, blocking collectives, all_features(): lax.all_gather(along_x[i * half:(i + 1) * half], 'c', axis=0)  9.44 us
  transfers between devices with their start and end apart: 6, of which 3 were waited for; matrix products, arithmetic and copies ran while one was open for 4% of the time, Pallas kernels for 4%

profile of v6, /device:TPU:6, one launch (start us, length us, event | category | flops | bytes accessed | tf_op | source)
XLA Modules:
  0.0 163.1 jit_solution(7602135315599036415)
XLA Ops:
  0.6 0.8 constant_dynamic-slice_fusion
  1.4 0.9 maximum_maximum_fusion
  2.3 1.2 broadcast_in_dim.22
  3.5 0.0 copy-start.8
  3.5 0.0 copy-start.10
  3.5 10.5 %all-to-all-start = ((bf16[8,320,256]{2,1,0:T(8,128)(2,1)}), bf16[8,320,256]{2,1,0:T(8,128)(2,1)S(1)}, u32[]{:S(2)}, u32[]{:S(2)}) async-start(bf16[8,320,256]{2,1,0:T(8,128)(2,1)} %broadcast_in_dim.22), calls=%async_computation | async-start | bytes 2621440 | tf_op jit(solution)/shard_map/all_to_all | solution.py:186
  14.0 0.0 copy-done.6
  14.0 0.0 copy-done.9
  14.1 0.0 copy-done.4
  14.1 3.5 %collective-permute-start = (bf16[176,256]{1,0:T(8,128)(2,1)S(1)}, bf16[176,256]{1,0:T(8,128)(2,1)S(1)}, u32[]{:S(2)}, u32[]{:S(2)}) collective-permute-start(bf16[176,256]{1,0:T(8,128)(2,1)S(1)} %fusion.5), channel_id=1, source_target_pairs={{0,8},{8,0},{1,9},{9,1},{2,10},{10,2},{3,11},{11,3},{4,12},{12,4},... | collective-permute-start | bytes 270344 | tf_op jit(solution)/shard_map/ppermute | solution.py:202
  17.6 0.0 copy-done.7
  17.6 0.1 copy.40
  17.7 0.1 reshape.103
  17.8 0.0 copy-done.8
  17.8 0.1 pad_add_fusion.1
  17.9 16.5 %all-gather.7 = s32[8,1,256]{2,1,0:T(1,128)S(1)} all-gather(s32[1,1,256]{2,1,0:T(1,128)S(1)} %pad_bitcast_fusion), channel_id=1, replica_groups=mesh['z'=8,'p'=4,'q'=2,'x'=4,'c'=2] {'p','q'}, dimensions={0}, use_global_device_ids=true | all-gather | bytes 9216 | tf_op jit(solution)/shard_map/all_gather | solution.py:191
  34.4 0.1 fusion.26
  34.5 0.1 pad_add_fusion
  34.6 0.1 eq.78
  34.7 0.2 convert_reduce_fusion.1
  34.9 0.1 broadcast_in_dim.23
  35.0 0.1 convolution_convert_fusion
  35.1 0.7 reshape.106
  35.8 12.6 %all-to-all-done = bf16[8,320,256]{2,1,0:T(8,128)(2,1)S(1)} async-done(((bf16[8,320,256]{2,1,0:T(8,128)(2,1)}), bf16[8,320,256]{2,1,0:T(8,128)(2,1)S(1)}, u32[]{:S(2)}, u32[]{:S(2)}) %all-to-all-start) | async-done | bytes 1310752 | tf_op jit(solution)/shard_map/all_to_all | solution.py:186
  48.4 3.9 %fusion.2 = bf16[1600,256]{1,0:T(8,128)(2,1)} fusion(bf16[2560,256]{1,0:T(8,128)(2,1)S(1)} %bitcast.59, s32[1600]{0:T(1024)S(1)} %eq.78), kind=kOutput, calls=%fused_computation.3 | convolution fusion | flops 2101657600 | bytes 2136320 | tf_op jit(solution)/shard_map/dot_general | solution.py:26
  52.3 7.1 %all-to-all-start.1 = ((bf16[8,200,256]{2,1,0:T(8,128)(2,1)}), bf16[8,200,256]{2,1,0:T(8,128)(2,1)S(1)}, u32[]{:S(2)}, u32[]{:S(2)}) async-start(bf16[8,200,256]{2,1,0:T(8,128)(2,1)} %bitcast.11), calls=%async_computation.1 | async-start | bytes 1638400 | tf_op jit(solution)/shard_map/all_to_all | solution.py:225
  59.4 0.0 collective-permute-done
  59.5 13.9 %all-gather = bf16[1280,256]{1,0:T(8,128)(2,1)S(1)} all-gather(bf16[320,256]{1,0:T(8,128)(2,1)S(1)} %pad_maximum_fusion.1), channel_id=2, replica_groups=mesh['z'=8,'p'=4,'q'=2,'x'=4,'c'=2] {'x'}, dimensions={0}, use_global_device_ids=true | all-gather | bytes 819200 | tf_op jit(solution)/shard_map/all_gather | solution.py:141
  73.4 2.3 %all-gather.1 = bf16[4,320,256]{2,1,0:T(8,128)(2,1)S(1)} all-gather(bf16[2,320,256]{2,1,0:T(8,128)(2,1)S(1)} %bitcast.61), channel_id=3, replica_groups=mesh['z'=8,'p'=4,'q'=2,'x'=4,'c'=2] {'c'}, dimensions={0}, use_global_device_ids=true | all-gather | bytes 983040 | tf_op jit(solution)/shard_map/all_gather | solution.py:143
  75.7 2.3 %all-gather.2 = bf16[4,320,256]{2,1,0:T(8,128)(2,1)S(1)} all-gather(bf16[2,320,256]{2,1,0:T(8,128)(2,1)S(1)} %bitcast.60), channel_id=4, replica_groups=mesh['z'=8,'p'=4,'q'=2,'x'=4,'c'=2] {'c'}, dimensions={0}, use_global_device_ids=true | all-gather | bytes 983040 | tf_op jit(solution)/shard_map/all_gather | solution.py:143
  78.0 5.5 %all-to-all-done.1 = bf16[8,200,256]{2,1,0:T(8,128)(2,1)S(1)} async-done(((bf16[8,200,256]{2,1,0:T(8,128)(2,1)}), bf16[8,200,256]{2,1,0:T(8,128)(2,1)S(1)}, u32[]{:S(2)}, u32[]{:S(2)}) %all-to-all-start.1) | async-done | bytes 819232 | tf_op jit(solution)/shard_map/all_to_all | solution.py:225
  83.4 0.1 reduce_sum.30
  83.6 2.5 %collective-permute-start.1 = (bf16[200,256]{1,0:T(8,128)(2,1)S(1)}, bf16[200,256]{1,0:T(8,128)(2,1)S(1)}, u32[]{:S(2)}, u32[]{:S(2)}) collective-permute-start(bf16[200,256]{1,0:T(8,128)(2,1)S(1)} %reduce_sum.30), channel_id=1, source_target_pairs={{0,8},{8,0},{1,9},{9,1},{2,10},{10,2},{3,11},{11,3},{4,12},{12,4},... | collective-permute-start | bytes 307208 | tf_op jit(solution)/shard_map/ppermute | solution.py:230
  86.0 0.1 compare_convert_fusion
  86.1 0.1 copy.41.high_ref
  86.3 0.1 reshape.102.query_ref
  86.3 4.6 %all-to-all-start.2 = ((bf16[64,2,256]{2,1,0:T(2,128)(2,1)}), bf16[64,2,256]{2,1,0:T(2,128)(2,1)S(1)}, u32[]{:S(2)}, u32[]{:S(2)}) async-start(bf16[64,2,256]{2,1,0:T(2,128)(2,1)} %reshape.106), calls=%async_computation.2 | async-start | bytes 131072 | tf_op jit(solution)/shard_map/all_to_all | solution.py:252
  91.0 0.0 collective-permute-done.1
  91.0 14.3 %all-gather.3 = bf16[1600,256]{1,0:T(8,128)(2,1)S(1)} all-gather(bf16[400,256]{1,0:T(8,128)(2,1)S(1)} %pad_maximum_fusion), channel_id=5, replica_groups=mesh['z'=8,'p'=4,'q'=2,'x'=4,'c'=2] {'x'}, dimensions={0}, use_global_device_ids=true | all-gather | bytes 1024000 | tf_op jit(solution)/shard_map/all_gather | solution.py:141
  105.4 0.1 fusion.35
  105.4 0.0 copy-start
  105.4 0.0 copy-start.1
  105.4 0.0 copy-start.2
  105.4 0.0 copy-start.3
  105.5 2.5 %all-gather.4 = bf16[4,400,256]{2,1,0:T(8,128)(2,1)S(1)} all-gather(bf16[2,400,256]{2,1,0:T(8,128)(2,1)S(1)} %bitcast.58), channel_id=6, replica_groups=mesh['z'=8,'p'=4,'q'=2,'x'=4,'c'=2] {'c'}, dimensions={0}, use_global_device_ids=true | all-gather | bytes 1228800 | tf_op jit(solution)/shard_map/all_gather | solution.py:143
  108.0 2.4 %all-gather.5 = bf16[4,400,256]{2,1,0:T(8,128)(2,1)S(1)} all-gather(bf16[2,400,256]{2,1,0:T(8,128)(2,1)S(1)} %bitcast.57), channel_id=7, replica_groups=mesh['z'=8,'p'=4,'q'=2,'x'=4,'c'=2] {'c'}, dimensions={0}, use_global_device_ids=true | all-gather | bytes 1228800 | tf_op jit(solution)/shard_map/all_gather | solution.py:143
  110.4 0.0 copy-done.3
  110.4 5.7 %reader.1 = (bf16[64,64,128]{2,1,0:T(8,128)(2,1)}, f32[1,80]{1,0:T(1,128)S(1)}) custom-call(s32[1]{0:T(128)} %bitcast.half_ref, s32[80,1]{1,0:T(8,128)S(1)} %copy.41.high_ref, bf16[6,80,256]{2,1,0:T(8,128)(2,1)S(1)} %reshape.102.query_ref, bf16[2,2,400,256]{3,2,1,0:T(8,128)(2,1)S(1)} %bitcast.52, bf16[2,2,400,256]{3,2,1,0:T(8,128)(2,1)S(1)} %bitcast.53, ...), custom_call_target="tpu_custom_call" | custom-call | tf_op jit(solution)/shard_map/reader/pallas_call | solution.py:123
  116.1 0.0 all-to-all-done.2
  116.2 0.1 add_reduce_fusion
  116.3 0.1 fusion.6
  116.4 0.9 fusion.3
  117.3 12.9 %all-to-all-start.3 = ((bf16[64,64,128]{2,1,0:T(8,128)(2,1)}), bf16[64,64,128]{2,1,0:T(8,128)(2,1)S(1)}, u32[]{:S(2)}, u32[]{:S(2)}) async-start(bf16[64,64,128]{2,1,0:T(8,128)(2,1)} %get-tuple-element.20), calls=%async_computation.3 | async-start | bytes 2097152 | tf_op jit(solution)/shard_map/all_to_all | solution.py:264
  130.2 0.6 reshape_squeeze.3
  130.9 12.8 %all-gather.6 = bf16[1024,128]{1,0:T(8,128)(2,1)S(1)} all-gather(bf16[128,128]{1,0:T(8,128)(2,1)S(1)} %fusion.3), channel_id=8, replica_groups=mesh['z'=8,'p'=4,'q'=2,'x'=4,'c'=2] {'x','c'}, dimensions={0}, use_global_device_ids=true | all-gather | bytes 294912 | tf_op jit(solution)/shard_map/all_gather | solution.py:262
  143.8 0.0 copy-start.5
  143.8 16.3 %all-to-all-done.3 = bf16[64,64,128]{2,1,0:T(8,128)(2,1)S(1)} async-done(((bf16[64,64,128]{2,1,0:T(8,128)(2,1)}), bf16[64,64,128]{2,1,0:T(8,128)(2,1)S(1)}, u32[]{:S(2)}, u32[]{:S(2)}) %all-to-all-start.3) | async-done | bytes 1048608 | tf_op jit(solution)/shard_map/all_to_all | solution.py:264
  160.1 0.2 convert_reduce_fusion
  160.3 0.1 slice_bitcast_fusion.1
  160.3 0.7 maximum_bitcast_fusion
  161.0 0.7 pad_maximum_fusion.4
  161.7 0.7 pad_maximum_fusion.3
  162.4 0.7 pad_maximum_fusion.2
  163.1 0.0 copy-done.5
  (38 shorter events, 0.4 us)
Async XLA Ops:
  3.5 10.5 %copy-start.6 = (bf16[2,768]{1,0:T(2,128)(2,1)S(1)}, bf16[2,768]{1,0:T(2,128)(2,1)}, u32[]{:S(2)}) copy-start(bf16[2,768]{1,0:T(2,128)(2,1)} %param.14) | copy-start | bytes 9220
  3.5 10.5 %copy-start.9 = (s32[40]{0:T(128)S(1)}, s32[40]{0:T(128)}, u32[]{:S(2)}) copy-start(s32[40]{0:T(128)} %param.16) | copy-start | bytes 484
  3.5 10.6 %copy-start.4 = (bf16[160,256]{1,0:T(8,128)(2,1)S(1)}, bf16[160,256]{1,0:T(8,128)(2,1)}, u32[]{:S(2)}) copy-start(bf16[160,256]{1,0:T(8,128)(2,1)} %param.23) | copy-start | bytes 245764
  3.5 14.1 %copy-start.7 = (s32[40,4]{0,1:T(4,128)S(1)}, s32[40,4]{0,1:T(4,128)}, u32[]{:S(2)}) copy-start(s32[40,4]{0,1:T(4,128)} %param.17) | copy-start | bytes 1924
  3.5 14.3 %copy-start.8 = (s32[40,1]{0,1:T(1,128)S(1)}, s32[40,1]{0,1:T(1,128)}, u32[]{:S(2)}) copy-start(s32[40,1]{0,1:T(1,128)} %param.15) | copy-start | bytes 484
  3.5 31.2 %copy-start.10 = (s32[64]{0:T(128)S(1)}, s32[64]{0:T(128)}, u32[]{:S(2)}) copy-start(s32[64]{0:T(128)} %param.25) | copy-start | bytes 772
  3.5 44.9 %all-to-all-start = ((bf16[8,320,256]{2,1,0:T(8,128)(2,1)}), bf16[8,320,256]{2,1,0:T(8,128)(2,1)S(1)}, u32[]{:S(2)}, u32[]{:S(2)}) async-start(bf16[8,320,256]{2,1,0:T(8,128)(2,1)} %broadcast_in_dim.22), calls=%async_computation | async-start | bytes 2621440 | tf_op jit(solution)/shard_map/all_to_all | solution.py:186
  14.1 45.4 %collective-permute-start = (bf16[176,256]{1,0:T(8,128)(2,1)S(1)}, bf16[176,256]{1,0:T(8,128)(2,1)S(1)}, u32[]{:S(2)}, u32[]{:S(2)}) collective-permute-start(bf16[176,256]{1,0:T(8,128)(2,1)S(1)} %fusion.5), channel_id=1, source_target_pairs={{0,8},{8,0},{1,9},{9,1},{2,10},{10,2},{3,11},{11,3},{4,12},{12,4},... | collective-permute-start | bytes 270344 | tf_op jit(solution)/shard_map/ppermute | solution.py:202
  52.3 31.1 %all-to-all-start.1 = ((bf16[8,200,256]{2,1,0:T(8,128)(2,1)}), bf16[8,200,256]{2,1,0:T(8,128)(2,1)S(1)}, u32[]{:S(2)}, u32[]{:S(2)}) async-start(bf16[8,200,256]{2,1,0:T(8,128)(2,1)} %bitcast.11), calls=%async_computation.1 | async-start | bytes 1638400 | tf_op jit(solution)/shard_map/all_to_all | solution.py:225
  83.6 7.4 %collective-permute-start.1 = (bf16[200,256]{1,0:T(8,128)(2,1)S(1)}, bf16[200,256]{1,0:T(8,128)(2,1)S(1)}, u32[]{:S(2)}, u32[]{:S(2)}) collective-permute-start(bf16[200,256]{1,0:T(8,128)(2,1)S(1)} %reduce_sum.30), channel_id=1, source_target_pairs={{0,8},{8,0},{1,9},{9,1},{2,10},{10,2},{3,11},{11,3},{4,12},{12,4},... | collective-permute-start | bytes 307208 | tf_op jit(solution)/shard_map/ppermute | solution.py:230
  86.3 29.8 %all-to-all-start.2 = ((bf16[64,2,256]{2,1,0:T(2,128)(2,1)}), bf16[64,2,256]{2,1,0:T(2,128)(2,1)S(1)}, u32[]{:S(2)}, u32[]{:S(2)}) async-start(bf16[64,2,256]{2,1,0:T(2,128)(2,1)} %reshape.106), calls=%async_computation.2 | async-start | bytes 131072 | tf_op jit(solution)/shard_map/all_to_all | solution.py:252
  105.4 5.0 %copy-start = (bf16[2048,128]{1,0:T(8,128)(2,1)S(1)}, bf16[2048,128]{1,0:T(8,128)(2,1)}, u32[]{:S(2)}) copy-start(bf16[2048,128]{1,0:T(8,128)(2,1)} %refs_4_.1) | copy-start | bytes 1572868
  105.4 4.9 %copy-start.1 = (bf16[2048,128]{1,0:T(8,128)(2,1)S(1)}, bf16[2048,128]{1,0:T(8,128)(2,1)}, u32[]{:S(2)}) copy-start(bf16[2048,128]{1,0:T(8,128)(2,1)} %refs_5_.1) | copy-start | bytes 1572868
  105.4 4.9 %copy-start.2 = (bf16[2048,128]{1,0:T(8,128)(2,1)S(1)}, bf16[2048,128]{1,0:T(8,128)(2,1)}, u32[]{:S(2)}) copy-start(bf16[2048,128]{1,0:T(8,128)(2,1)} %refs_6_.1) | copy-start | bytes 1572868
  105.4 4.9 %copy-start.3 = (bf16[128,2048]{1,0:T(8,128)(2,1)S(1)}, bf16[128,2048]{1,0:T(8,128)(2,1)}, u32[]{:S(2)}) copy-start(bf16[128,2048]{1,0:T(8,128)(2,1)} %refs_7_.1) | copy-start | bytes 1572868
  117.3 42.8 %all-to-all-start.3 = ((bf16[64,64,128]{2,1,0:T(8,128)(2,1)}), bf16[64,64,128]{2,1,0:T(8,128)(2,1)S(1)}, u32[]{:S(2)}, u32[]{:S(2)}) async-start(bf16[64,64,128]{2,1,0:T(8,128)(2,1)} %get-tuple-element.20), calls=%async_computation.3 | async-start | bytes 2097152 | tf_op jit(solution)/shard_map/all_to_all | solution.py:264
  143.8 19.3 %copy-start.5 = (bf16[128,768]{1,0:T(8,128)(2,1)}, bf16[128,768]{1,0:T(8,128)(2,1)S(1)}, u32[]{:S(2)}) copy-start(bf16[128,768]{1,0:T(8,128)(2,1)S(1)} %slice_dynamic-update-slice_fusion) | copy-start | bytes 589828

commit v7 on v5

--- a/solution.py
+++ b/solution.py
@@ -11,6 +11,7 @@
 HEAD_DIM = 64
 K = 20
 PLEN = 4
+CAPS = 2
 LANES = 128
 IDX = ("z", "p", "q")
 M = ("x", "c")
@@ -39,20 +40,28 @@
     rows = out_ref.shape[1] // 2
     mine = half_ref[0]
 
-    def block(pair, b, low, high):
+    def grad_block(b):
         x, c = divmod(b, nc)
-        return pair[x // nx][c, x % nx, low:high, :]
+        return grad_refs[x // nx][c, x % nx]
+
+    def token_block(b, low, high):
+        x, c = divmod(b, nc)
+        both = [ref[c, x, low:high, :] for ref in token_refs]
+        ordered = [jnp.where(mine == 0, both[0], both[1]), jnp.where(mine == 0, both[1], both[0])]
+        return jnp.concatenate(ordered, axis=0)
 
     acc = jnp.zeros((passages, deep), F32)
     for s in range(strips):
-        fetched = block(token_refs, s, count, count + passages)
+        fetched = token_block(s, count // 2, (count + passages) // 2)
         acc += fetched.astype(F32) * query_ref[s].astype(F32)
     low = jnp.sum(acc[:, :LANES], axis=1, keepdims=True)
     high = jnp.sum(acc[:, LANES:], axis=1, keepdims=True)
     scores = jnp.where(high_ref[...] > 0, high, low)
-    queries = passages // K
-    p = lax.broadcasted_iota(jnp.int32, (passages, queries), 0)
-    first = lax.broadcasted_iota(jnp.int32, (passages, queries), 1) * K
+    each, valid = passages // 2, count // 2 // PLEN
+    queries = valid // K
+    p = lax.broadcasted_iota(jnp.int32, (passages, 2 * queries), 0)
+    g = lax.broadcasted_iota(jnp.int32, (passages, 2 * queries), 1)
+    first = jnp.where(g >= queries, each + (g - queries) * K, g * K)
     group = (p >= first) & (p < first + K)
     top = jnp.max(jnp.where(group, scores, -jnp.inf), axis=0, keepdims=True)
     exps = jnp.where(group, jnp.exp(scores - top), 0.0)
@@ -63,13 +72,16 @@
     rel_row = jnp.sum(jnp.where(same, rel_column, 0.0), axis=0, keepdims=True)
     rel_ref[...] = rel_row
     token = lax.broadcasted_iota(jnp.int32, (count, passages), 0)
-    begin = lax.broadcasted_iota(jnp.int32, (count, passages), 1) * PLEN
+    p = lax.broadcasted_iota(jnp.int32, (count, passages), 1)
+    at = jnp.where(p >= each, p - each, p)
+    begin = jnp.where(p >= each, count // 2, 0) + at * PLEN
+    begin = jnp.where(at < valid, begin, count)
     of_token = (token >= begin) & (token < begin + PLEN)
     rel = jnp.sum(jnp.where(of_token, rel_row, 0.0), axis=1, keepdims=True)
 
-    tokens = [block(token_refs, b, 0, count) for b in range(blocks)]
+    tokens = [token_block(b, 0, count // 2) for b in range(blocks)]
     weighted = [
-        (block(grad_refs, b, 0, count).astype(F32) * rel).astype(BF16) for b in range(blocks)
+        (grad_block(b).astype(F32) * rel).astype(BF16) for b in range(blocks)
     ]
     for copy in copies:
         copy.wait()
@@ -105,14 +117,14 @@
     value_grad = dot(attn, c, ROWS).astype(BF16)
     context = dot(attn, v).astype(BF16)
     query_key = jnp.concatenate([query_grad, key_grad], axis=1)
-    each = deep // rows
+    span = deep // rows
     for b in range(blocks):
         upper = dot(tokens[b], query_key, ROWS).astype(BF16)
         lower = jnp.concatenate(
             [dot(tokens[b], value_grad, ROWS), dot(weighted[b], context, ROWS)], axis=1
         ).astype(BF16)
-        out_ref[b * each : (b + 1) * each, :rows, :] = upper.reshape(each, rows, -1)
-        out_ref[b * each : (b + 1) * each, rows:, :] = lower.reshape(each, rows, -1)
+        out_ref[b * span : (b + 1) * span, :rows, :] = upper.reshape(span, rows, -1)
+        out_ref[b * span : (b + 1) * span, rows:, :] = lower.reshape(span, rows, -1)
 
 
 def reader(half, high, query, tokens, out_grad, weights, owners):
@@ -134,12 +146,6 @@
         compiler_params=pltpu.CompilerParams(vmem_limit_bytes=40 * 1024 * 1024),
         name="reader",
     )(half, high, query, *tokens, *out_grad, *weights)
-
-
-def all_features(part):
-    along_x = lax.all_gather(part, "x", axis=0)
-    half = along_x.shape[0] // 2
-    return [lax.all_gather(along_x[i * half : (i + 1) * half], "c", axis=0) for i in range(2)]
 
 
 def shards(
@@ -162,7 +168,6 @@
     owners = nz * ny
     swap = [(0, 1), (1, 0)]
     my_y = lax.axis_index(("p", "q"))
-    my_idx = lax.axis_index(IDX)
     my_half = lax.axis_index("q")
     pass_rows, width = index_emb.shape
     queries = query_emb.shape[0]
@@ -177,18 +182,56 @@
         return lax.dynamic_slice_in_dim(array, strip * LANES, LANES, axis=1)
 
     deep = vocab_table.shape[1]
+    flat_ids = token_ids.reshape(-1)
+    upper = jnp.concatenate([flat_ids // LANES, passage_owner[:, 0], passage_row])
+    lower = jnp.pad(flat_ids % LANES, (0, 2 * npass))
+    wanted = jnp.stack([upper, lower]).astype(BF16)
+    wanted = jnp.pad(wanted, ((0, 6), (0, deep - wanted.shape[1])))
+    slab_owner, slab_row = slab_ids // pass_rows, slab_ids % pass_rows
+    earlier = (slab_owner[:, None] == slab_owner[None, :]) & (
+        jnp.arange(slab)[:, None] > jnp.arange(slab)[None, :]
+    )
+    rank = jnp.sum(earlier.astype(jnp.int32), axis=1)
+    slot = ((slab_owner % ny) * nz + slab_owner // ny) * CAPS + rank
+    select = (jnp.arange(owners * CAPS)[:, None] == slot[None, :]).astype(BF16)
+    slab_wide = jnp.concatenate(
+        [
+            my_strip(slab_emb),
+            jnp.broadcast_to((slab_row + 1).astype(BF16)[:, None], (slab, deep - LANES)),
+        ],
+        axis=1,
+    )
+    slab_out = dot(select, slab_wide).astype(BF16).reshape(ny, nz * CAPS, deep)
+    got_first = lax.all_to_all(
+        jnp.concatenate([jnp.broadcast_to(wanted[None], (ny, *wanted.shape)), slab_out], axis=1),
+        ("p", "q"),
+        0,
+        0,
+        tiled=True,
+    )
+    got_wanted = got_first[:, :2].astype(jnp.int32)
+    slab_out = got_first[:, wanted.shape[0] :].reshape(ny, nz, CAPS, deep).transpose(1, 0, 2, 3)
+
     index_strip = my_strip(index_emb)
     folded = pass_rows // 2
     message = jnp.concatenate(
         [vocab_table, jnp.concatenate([index_strip[:folded], index_strip[folded:]], axis=1)], axis=0
     )
-    stride = message.shape[0]
+    held = message.shape[0]
+    stride = held + ny * CAPS
     got_z = lax.all_to_all(
-        jnp.broadcast_to(message[None], (nz, *message.shape)), "z", 0, 0, tiled=True
-    )
-    wanted = jnp.concatenate([token_ids.reshape(-1), passage_owner[:, 0], passage_row])
-    wanted = jnp.pad(wanted[None], ((0, 0), (0, -wanted.shape[0] % LANES)))
-    wanted = lax.all_gather(wanted, ("p", "q"), axis=0, tiled=True)
+        jnp.concatenate(
+            [
+                jnp.broadcast_to(message[None], (nz, *message.shape)),
+                slab_out.reshape(nz, ny * CAPS, deep),
+            ],
+            axis=1,
+        ),
+        "z",
+        0,
+        0,
+        tiled=True,
+    )
 
     query_strips = query_emb.reshape(queries, strips, LANES).transpose(1, 0, 2)
     extra = jnp.concatenate(
@@ -198,20 +241,32 @@
         ],
         axis=0,
     )
-    extra = jnp.pad(extra, ((0, -extra.shape[0] % 16), (0, 0)))
-    other = lax.ppermute(jnp.concatenate([out_grad, extra], axis=0), "q", swap)
-    grads = all_features(jnp.concatenate([out_grad, other[:count]], axis=0))
+    extra = jnp.pad(extra, ((0, -extra.shape[0] % 8), (0, 0)))
+    pair_message, _ = lax.optimization_barrier(
+        (jnp.concatenate([out_grad, extra], axis=0), got_wanted)
+    )
+    other = lax.ppermute(pair_message, "q", swap)
+    grads = lax.all_gather(jnp.concatenate([out_grad, other[:count]], axis=0), "x", axis=0)
+    grads = [
+        lax.all_gather(grads[i * grads.shape[0] // 2 : (i + 1) * grads.shape[0] // 2], "c", axis=0)
+        for i in range(2)
+    ]
+    got_z, grads = lax.optimization_barrier((got_z, grads))
     other_strips = other[count : count + strips].reshape(strips, queries, LANES)
-    pair_query = jnp.concatenate([query_strips, other_strips], axis=1)
-    pair_query = jnp.repeat(jnp.concatenate([pair_query, pair_query], axis=2), K, axis=1)
+    spare = -npass % 16
+
+    def per_passage(some):
+        some = jnp.repeat(jnp.concatenate([some, some], axis=2), K, axis=1)
+        return jnp.pad(some, ((0, 0), (0, spare), (0, 0)))
+
+    pair_query = jnp.concatenate([per_passage(query_strips), per_passage(other_strips)], axis=1)
     other_row = other[count + strips, :npass].astype(jnp.int32)
-    high = (jnp.concatenate([passage_row, other_row])[:, None] >= folded).astype(jnp.int32)
-
-    ids, place_owner, place_row = (
-        wanted[:, :count],
-        wanted[:, count : count + npass],
-        wanted[:, count + npass : count + 2 * npass],
-    )
+    high = jnp.concatenate([jnp.pad(passage_row, (0, spare)), jnp.pad(other_row, (0, spare))])
+    high = (high[:, None] >= folded).astype(jnp.int32)
+
+    ids = got_wanted[:, 0, :count] * LANES + got_wanted[:, 1, :count]
+    place_owner = got_wanted[:, 0, count : count + npass]
+    place_row = got_wanted[:, 0, count + npass : count + 2 * npass]
     id_owner = ids // vocab_rows
     token_at = jnp.where(id_owner % ny == my_y, id_owner // ny * stride + ids % vocab_rows, -1)
     place_at = jnp.where(
@@ -219,32 +274,27 @@
         place_owner // ny * stride + vocab_rows + place_row % folded,
         -1,
     )
-    at = jnp.concatenate([token_at, place_at], axis=1).reshape(-1)
+    at = jnp.concatenate([token_at, place_at, jnp.full((ny, spare), -1, jnp.int32)], axis=1)
+    at = at.reshape(-1)
     one_hot = (at[:, None] == jnp.arange(nz * stride)[None, :]).astype(BF16)
     served = dot(one_hot, got_z.reshape(nz * stride, deep)).astype(BF16)
     got_y = lax.all_to_all(
-        served.reshape(ny, count + npass, deep), ("p", "q"), 0, 0, tiled=True
-    )
-    got_y, grads = lax.optimization_barrier((got_y, grads))
+        served.reshape(ny, count + npass + spare, deep), ("p", "q"), 0, 0, tiled=True
+    )
     part = jnp.sum(got_y.astype(F32), axis=0).astype(BF16)
-    other_part = lax.ppermute(part, "q", swap)
-    tokens = all_features(
-        jnp.concatenate(
-            [part[:count], other_part[:count], part[count:], other_part[count:]], axis=0
-        )
-    )
-
-    slab_ids_row = jnp.concatenate([slab_ids // pass_rows, slab_ids % pass_rows]).astype(BF16)
-    slab_part = jnp.concatenate(
-        [my_strip(slab_emb), jnp.pad(slab_ids_row[None], ((0, 15), (0, 0)))], axis=0
-    )
-    slabs = lax.all_gather(slab_part, IDX, axis=0)
-    slab_at = slabs[:, slab].astype(jnp.int32)
-    slab_at = jnp.where(slab_at[:, :slab] == my_idx, slab_at[:, slab:], -1)
-    slab_at = jnp.pad(slab_at, ((0, 0), (0, 16)), constant_values=-1).reshape(-1)
-    put = jnp.arange(pass_rows)[:, None] == slab_at[None, :]
-    placed = dot(put.astype(BF16), slabs.reshape(-1, LANES)).astype(BF16)
+
+    nx = lax.axis_size("x")
+    near = lax.all_to_all(
+        jnp.broadcast_to(part[None], (nq * nx, *part.shape)), ("q", "x"), 0, 0, tiled=True
+    )
+    tokens = [lax.all_gather(near[i * nx : (i + 1) * nx], "c", axis=0) for i in range(nq)]
+
+    got_slab = got_z[:, held:].reshape(-1, deep)
+    got_place = got_slab[:, LANES].astype(jnp.int32) - 1
+    put = jnp.arange(pass_rows)[:, None] == got_place[None, :]
+    placed = dot(put.astype(BF16), got_slab[:, :LANES]).astype(BF16)
     refreshed = jnp.where(jnp.any(put, axis=1)[:, None], placed, index_strip)
+    refreshed, _ = lax.optimization_barrier((refreshed, served))
     refreshed = lax.all_gather(refreshed, M, axis=0)
     refreshed = jnp.concatenate([refreshed[i] for i in range(strips)], axis=1)
 

time: 187 us -> 165 us (0.88)
  between operations: 14.5 us -> 1.03 us
  waiting for transfers between devices: 53.4 us -> 45.6 us
  blocking collectives: 66.4 us -> 62.7 us
  other arithmetic: 5.11 us -> 8.56 us
  starting transfers between devices: 32.4 us -> 29.3 us
  local copies, waits for them, and re-layouts: 3.52 us -> 5.85 us
    all_gather x7 -> x5, blocking collectives: 53.6 us -> 22.5 us  [the longest x1 13 us: shards(): lax.all_gather(jnp.concatenate([out_grad, other[:count]], axis=0), 'x', a...]
    all_to_all x0 -> x1, blocking collectives: none -> 27.4 us  [shards(): lax.all_to_all(served.reshape(ny, count + npass + spare, deep), ('p', 'q'...]
    all_gather x1 -> x0, waiting for transfers between devices: 20.5 us -> none  [shards(): slabs = lax.all_gather(slab_part, IDX, axis=0)]
    all_to_all x2 -> x3, waiting for transfers between devices: 18.5 us -> 27.3 us  [the longest x1 10.2 us: shards(): lax.all_to_all(jnp.concatenate([jnp.broadcast_to(message[None], (nz, *mes...]
    all_to_all x2 -> x3, starting transfers between devices: 17.6 us -> 22.3 us  [the longest x1 10.4 us: shards(): lax.all_to_all(jnp.concatenate([jnp.broadcast_to(message[None], (nz, *mes...]
    all_to_all x1, starting transfers between devices: 8.88 us -> 4.66 us  [shards(): terms = lax.all_to_all(terms, IDX, 0, 0, tiled=True)]
    ppermute x2 -> x1, waiting for transfers between devices: 0.01 us -> 3.71 us  [shards(): other = lax.ppermute(pair_message, 'q', swap)]
    ppermute x2 -> x1, starting transfers between devices: 5.88 us -> 2.34 us  [shards(): other = lax.ppermute(pair_message, 'q', swap)]
  transfers between devices with their start and end apart: 6 -> 5, of which waited for: 4 -> 5; matrix products, arithmetic and copies ran while one was open for 5% -> 3% of each run, Pallas kernels for 0% -> 0%
where the time goes in v7:
time: 165 us; the launch traced here: 163 us
  blocking collectives  62.7 us (38%)
  waiting for transfers between devices  45.6 us (28%)
  starting transfers between devices  29.3 us (18%)
  other arithmetic  8.56 us (5%)
  local copies, waits for them, and re-layouts  5.85 us (4%)
  Pallas kernels  5.84 us (4%)
  matrix products  4.34 us (3%)
    all_to_all x1, blocking collectives, shards(): lax.all_to_all(served.reshape(ny, count + npass + spare, deep), ('p', 'q'...  27.4 us
    all_to_all x1, waiting for transfers between devices, shards(): terms = lax.all_to_all(terms, IDX, 0, 0, tiled=True)  14.5 us
    all_gather x1, blocking collectives, shards(): lax.all_gather(jnp.concatenate([out_grad, other[:count]], axis=0), 'x', a...  13 us
    all_gather x1, blocking collectives, shards(): refreshed = lax.all_gather(refreshed, M, axis=0)  12.8 us
    all_to_all x1, starting transfers between devices, shards(): lax.all_to_all(jnp.concatenate([jnp.broadcast_to(message[None], (nz, *mes...  10.4 us
    all_to_all x1, waiting for transfers between devices, shards(): lax.all_to_all(jnp.concatenate([jnp.broadcast_to(message[None], (nz, *mes...  10.2 us
    all_to_all x1, waiting for transfers between devices, shards(): lax.all_to_all(jnp.broadcast_to(part[None], (nq * nx, *part.shape)), ('q'...  10 us
    all_to_all x1, waiting for transfers between devices, shards(): lax.all_to_all(jnp.concatenate([jnp.broadcast_to(wanted[None], (ny, *want...  7.11 us
  transfers between devices with their start and end apart: 5, of which 5 were waited for; matrix products, arithmetic and copies ran while one was open for 3% of the time, Pallas kernels for 0%

profile of v7, /device:TPU:6, one launch (start us, length us, event | category | flops | bytes accessed | tf_op | source)
XLA Modules:
  0.0 163.3 jit_solution(5789519729147145584)
XLA Ops:
  0.6 0.7 convert_bitcast_fusion
  1.3 0.7 and_select_fusion.3
  2.0 0.2 convert_reduce_fusion.1
  2.2 0.7 fusion.51
  2.8 0.8 copy.54
  3.6 0.1 reshape.115
  3.7 0.1 pad_maximum_fusion.8
  3.8 0.8 constant_dynamic-slice_fusion
  4.6 0.1 broadcast_in_dim.27
  4.7 0.1 convolution_convert_fusion
  4.8 0.7 pad_maximum_fusion.2
  5.5 7.1 %all-to-all-start = ((bf16[8,24,256]{2,1,0:T(8,128)(2,1)}), bf16[8,24,256]{2,1,0:T(8,128)(2,1)S(1)}, u32[]{:S(2)}, u32[]{:S(2)}) async-start(bf16[8,24,256]{2,1,0:T(8,128)(2,1)} %pad_maximum_fusion.2), calls=%async_computation | async-start | bytes 196608 | tf_op jit(solution)/shard_map/all_to_all | solution.py:205
  12.6 0.7 reshape.113
  13.3 0.9 maximum_maximum_fusion
  14.2 7.1 %all-to-all-done = bf16[8,24,256]{2,1,0:T(8,128)(2,1)S(1)} async-done(((bf16[8,24,256]{2,1,0:T(8,128)(2,1)}), bf16[8,24,256]{2,1,0:T(8,128)(2,1)S(1)}, u32[]{:S(2)}, u32[]{:S(2)}) %all-to-all-start) | async-done | bytes 98336 | tf_op jit(solution)/shard_map/all_to_all | solution.py:205
  21.4 0.1 broadcast_in_dim.31
  21.5 1.2 pad_maximum_fusion
  22.7 10.4 %all-to-all-start.1 = ((bf16[8,336,256]{2,1,0:T(8,128)(2,1)}), bf16[8,336,256]{2,1,0:T(8,128)(2,1)S(1)}, u32[]{:S(2)}, u32[]{:S(2)}) async-start(bf16[8,336,256]{2,1,0:T(8,128)(2,1)} %pad_maximum_fusion), calls=%async_computation.1 | async-start | bytes 2752512 | tf_op jit(solution)/shard_map/all_to_all | solution.py:222
  33.2 0.1 pad.57.clone
  33.3 0.0 copy-done.5
  33.3 2.3 %collective-permute-start = (bf16[168,256]{1,0:T(8,128)(2,1)S(1)}, bf16[168,256]{1,0:T(8,128)(2,1)S(1)}, u32[]{:S(2)}, u32[]{:S(2)}) collective-permute-start(bf16[168,256]{1,0:T(8,128)(2,1)S(1)} %fusion.8), channel_id=1, source_target_pairs={{0,8},{8,0},{1,9},{9,1},{2,10},{10,2},{3,11},{11,3},{4,12},{12,4},... | collective-permute-start | bytes 258056 | tf_op jit(solution)/shard_map/ppermute | solution.py:248
  35.6 0.1 fusion.50
  35.8 0.1 add_add_fusion
  35.9 0.1 eq.87
  36.0 3.7 %collective-permute-done = bf16[168,256]{1,0:T(8,128)(2,1)S(1)} collective-permute-done((bf16[168,256]{1,0:T(8,128)(2,1)S(1)}, bf16[168,256]{1,0:T(8,128)(2,1)S(1)}, u32[]{:S(2)}, u32[]{:S(2)}) %collective-permute-start) | collective-permute-done | bytes 86048 | tf_op jit(solution)/shard_map/ppermute | solution.py:248
  39.7 13.0 %all-gather = bf16[1280,256]{1,0:T(8,128)(2,1)S(1)} all-gather(bf16[320,256]{1,0:T(8,128)(2,1)S(1)} %pad_maximum_fusion.1), channel_id=2, replica_groups=mesh['z'=8,'p'=4,'q'=2,'x'=4,'c'=2] {'x'}, dimensions={0}, use_global_device_ids=true | all-gather | bytes 819200 | tf_op jit(solution)/shard_map/all_gather | solution.py:249
  52.8 2.3 %all-gather.1 = bf16[4,320,256]{2,1,0:T(8,128)(2,1)S(1)} all-gather(bf16[2,320,256]{2,1,0:T(8,128)(2,1)S(1)} %bitcast.79), channel_id=3, replica_groups=mesh['z'=8,'p'=4,'q'=2,'x'=4,'c'=2] {'c'}, dimensions={0}, use_global_device_ids=true | all-gather | bytes 983040 | tf_op jit(solution)/shard_map/all_gather | solution.py:251
  55.1 2.3 %all-gather.2 = bf16[4,320,256]{2,1,0:T(8,128)(2,1)S(1)} all-gather(bf16[2,320,256]{2,1,0:T(8,128)(2,1)S(1)} %bitcast.78), channel_id=4, replica_groups=mesh['z'=8,'p'=4,'q'=2,'x'=4,'c'=2] {'c'}, dimensions={0}, use_global_device_ids=true | all-gather | bytes 983040 | tf_op jit(solution)/shard_map/all_gather | solution.py:251
  57.3 10.2 %all-to-all-done.1 = bf16[8,336,256]{2,1,0:T(8,128)(2,1)S(1)} async-done(((bf16[8,336,256]{2,1,0:T(8,128)(2,1)}), bf16[8,336,256]{2,1,0:T(8,128)(2,1)S(1)}, u32[]{:S(2)}, u32[]{:S(2)}) %all-to-all-start.1) | async-done | bytes 1376288 | tf_op jit(solution)/shard_map/all_to_all | solution.py:222
  67.5 3.3 %fusion.2 = bf16[1664,256]{1,0:T(8,128)(2,1)S(1)} fusion(bf16[2688,256]{1,0:T(8,128)(2,1)S(1)} %bitcast.77, s32[1664]{0:T(1024)S(1)} %eq.87), kind=kOutput, calls=%fused_computation.3 | convolution fusion | flops 2294988800 | bytes 2234880 | tf_op jit(solution)/shard_map/dot_general | solution.py:26
  70.8 0.0 copy-done.4
  70.8 27.4 %all_to_all.25 = bf16[8,208,256]{2,1,0:T(8,128)(2,1)S(1)} all-to-all(bf16[8,208,256]{2,1,0:T(8,128)(2,1)S(1)} %bitcast.80), channel_id=1, replica_groups=mesh['z'=8,'p'=4,'q'=2,'x'=4,'c'=2] {'p','q'}, dimensions={0} | all-to-all | bytes 1703936 | tf_op jit(solution)/shard_map/all_to_all | solution.py:281
  98.2 0.1 reduce_sum.31
  98.3 0.0 copy-start.7
  98.3 1.0 broadcast_in_dim.32
  99.3 4.8 %all-to-all-start.3 = ((bf16[8,208,256]{2,1,0:T(8,128)(2,1)}), bf16[8,208,256]{2,1,0:T(8,128)(2,1)S(1)}, u32[]{:S(2)}, u32[]{:S(2)}) async-start(bf16[8,208,256]{2,1,0:T(8,128)(2,1)} %broadcast_in_dim.32), calls=%async_computation.3 | async-start | bytes 1703936 | tf_op jit(solution)/shard_map/all_to_all | solution.py:287
  104.2 0.0 copy-done.7
  104.2 0.1 compare_convert_fusion
  104.3 0.1 copy.60.high_ref
  104.5 10.0 %all-to-all-done.3 = bf16[8,208,256]{2,1,0:T(8,128)(2,1)S(1)} async-done(((bf16[8,208,256]{2,1,0:T(8,128)(2,1)}), bf16[8,208,256]{2,1,0:T(8,128)(2,1)S(1)}, u32[]{:S(2)}, u32[]{:S(2)}) %all-to-all-start.3) | async-done | bytes 852000 | tf_op jit(solution)/shard_map/all_to_all | solution.py:287
  114.6 0.1 fusion.48
  114.6 0.0 copy-start
  114.6 0.0 copy-start.1
  114.6 0.0 copy-start.2
  114.7 0.0 copy-start.3
  114.7 2.5 %all-gather.4 = bf16[8,208,256]{2,1,0:T(8,128)(2,1)S(1)} all-gather(bf16[4,208,256]{2,1,0:T(8,128)(2,1)S(1)} %get-tuple-element.20), channel_id=6, replica_groups=mesh['z'=8,'p'=4,'q'=2,'x'=4,'c'=2] {'c'}, dimensions={0}, use_global_device_ids=true | all-gather | bytes 1277952 | tf_op jit(solution)/shard_map/all_gather | solution.py:290
  117.2 2.4 %all-gather.3 = bf16[8,208,256]{2,1,0:T(8,128)(2,1)S(1)} all-gather(bf16[4,208,256]{2,1,0:T(8,128)(2,1)S(1)} %get-tuple-element.21), channel_id=5, replica_groups=mesh['z'=8,'p'=4,'q'=2,'x'=4,'c'=2] {'c'}, dimensions={0}, use_global_device_ids=true | all-gather | bytes 1277952 | tf_op jit(solution)/shard_map/all_gather | solution.py:290
  119.6 0.0 copy-done
  119.6 5.8 %reader.1 = (bf16[64,64,128]{2,1,0:T(8,128)(2,1)}, f32[1,96]{1,0:T(1,128)S(1)}) custom-call(s32[1]{0:T(128)} %bitcast.half_ref, s32[96,1]{1,0:T(8,128)S(1)} %copy.60.high_ref, bf16[6,96,256]{2,1,0:T(8,128)(2,1)S(1)} %fusion.6.query_ref, bf16[2,4,208,256]{3,2,1,0:T(8,128)(2,1)S(1)} %bitcast.73, bf16[2,4,208,256]{3,2,1,0:T(8,128)(2,1)S(1)} %bitcast.72, ...), custom_call_target="tpu_custom_call" | custom-call | tf_op jit(solution)/shard_map/reader/pallas_call | solution.py:134
  125.5 4.7 %all-to-all-start.4 = ((bf16[64,64,128]{2,1,0:T(8,128)(2,1)}), bf16[64,64,128]{2,1,0:T(8,128)(2,1)S(1)}, u32[]{:S(2)}, u32[]{:S(2)}) async-start(bf16[64,64,128]{2,1,0:T(8,128)(2,1)} %get-tuple-element.18), calls=%async_computation.4 | async-start | bytes 2097152 | tf_op jit(solution)/shard_map/all_to_all | solution.py:305
  130.2 0.9 slice.123
  131.0 0.1 add_reduce_fusion
  131.1 0.1 fusion.9
  131.2 0.9 fusion.3
  132.1 12.8 %all-gather.5 = bf16[1024,128]{1,0:T(8,128)(2,1)S(1)} all-gather(bf16[128,128]{1,0:T(8,128)(2,1)S(1)} %fusion.3), channel_id=7, replica_groups=mesh['z'=8,'p'=4,'q'=2,'x'=4,'c'=2] {'x','c'}, dimensions={0}, use_global_device_ids=true | all-gather | bytes 294912 | tf_op jit(solution)/shard_map/all_gather | solution.py:298
  145.1 0.0 copy-start.6
  145.1 0.6 reshape_squeeze.3
  145.8 14.5 %all-to-all-done.4 = bf16[64,64,128]{2,1,0:T(8,128)(2,1)S(1)} async-done(((bf16[64,64,128]{2,1,0:T(8,128)(2,1)}), bf16[64,64,128]{2,1,0:T(8,128)(2,1)S(1)}, u32[]{:S(2)}, u32[]{:S(2)}) %all-to-all-start.4) | async-done | bytes 1048608 | tf_op jit(solution)/shard_map/all_to_all | solution.py:305
  160.3 0.2 convert_reduce_fusion
  160.4 0.1 slice_bitcast_fusion.1
  160.5 0.7 maximum_bitcast_fusion
  161.2 0.7 pad_maximum_fusion.5
  161.9 0.7 pad_maximum_fusion.4
  162.6 0.7 pad_maximum_fusion.3
  (47 shorter events, 0.6 us)
Async XLA Ops:
  5.5 15.8 %all-to-all-start = ((bf16[8,24,256]{2,1,0:T(8,128)(2,1)}), bf16[8,24,256]{2,1,0:T(8,128)(2,1)S(1)}, u32[]{:S(2)}, u32[]{:S(2)}) async-start(bf16[8,24,256]{2,1,0:T(8,128)(2,1)} %pad_maximum_fusion.2), calls=%async_computation | async-start | bytes 196608 | tf_op jit(solution)/shard_map/all_to_all | solution.py:205
  22.7 10.6 %copy-start.5 = (bf16[160,256]{1,0:T(8,128)(2,1)S(1)}, bf16[160,256]{1,0:T(8,128)(2,1)}, u32[]{:S(2)}) copy-start(bf16[160,256]{1,0:T(8,128)(2,1)} %param.23) | copy-start | bytes 245764
  22.7 44.8 %all-to-all-start.1 = ((bf16[8,336,256]{2,1,0:T(8,128)(2,1)}), bf16[8,336,256]{2,1,0:T(8,128)(2,1)S(1)}, u32[]{:S(2)}, u32[]{:S(2)}) async-start(bf16[8,336,256]{2,1,0:T(8,128)(2,1)} %pad_maximum_fusion), calls=%async_computation.1 | async-start | bytes 2752512 | tf_op jit(solution)/shard_map/all_to_all | solution.py:222
  33.3 6.4 %collective-permute-start = (bf16[168,256]{1,0:T(8,128)(2,1)S(1)}, bf16[168,256]{1,0:T(8,128)(2,1)S(1)}, u32[]{:S(2)}, u32[]{:S(2)}) collective-permute-start(bf16[168,256]{1,0:T(8,128)(2,1)S(1)} %fusion.8), channel_id=1, source_target_pairs={{0,8},{8,0},{1,9},{9,1},{2,10},{10,2},{3,11},{11,3},{4,12},{12,4},... | collective-permute-start | bytes 258056 | tf_op jit(solution)/shard_map/ppermute | solution.py:248
  67.5 3.3 %copy-start.4 = (bf16[8,336,256]{2,1,0:T(8,128)(2,1)}, bf16[8,336,256]{2,1,0:T(8,128)(2,1)S(1)}, u32[]{:S(2)}) copy-start(bf16[8,336,256]{2,1,0:T(8,128)(2,1)S(1)} %all-to-all-done.1) | copy-start | bytes 4128772
  98.3 5.9 %copy-start.7 = (s32[40]{0:T(128)S(1)}, s32[40]{0:T(128)}, u32[]{:S(2)}) copy-start(s32[40]{0:T(128)} %param.16) | copy-start | bytes 484
  99.3 15.3 %all-to-all-start.3 = ((bf16[8,208,256]{2,1,0:T(8,128)(2,1)}), bf16[8,208,256]{2,1,0:T(8,128)(2,1)S(1)}, u32[]{:S(2)}, u32[]{:S(2)}) async-start(bf16[8,208,256]{2,1,0:T(8,128)(2,1)} %broadcast_in_dim.32), calls=%async_computation.3 | async-start | bytes 1703936 | tf_op jit(solution)/shard_map/all_to_all | solution.py:287
  114.6 5.0 %copy-start = (bf16[2048,128]{1,0:T(8,128)(2,1)S(1)}, bf16[2048,128]{1,0:T(8,128)(2,1)}, u32[]{:S(2)}) copy-start(bf16[2048,128]{1,0:T(8,128)(2,1)} %refs_4_.1) | copy-start | bytes 1572868
  114.6 5.0 %copy-start.1 = (bf16[2048,128]{1,0:T(8,128)(2,1)S(1)}, bf16[2048,128]{1,0:T(8,128)(2,1)}, u32[]{:S(2)}) copy-start(bf16[2048,128]{1,0:T(8,128)(2,1)} %refs_5_.1) | copy-start | bytes 1572868
  114.6 5.0 %copy-start.2 = (bf16[2048,128]{1,0:T(8,128)(2,1)S(1)}, bf16[2048,128]{1,0:T(8,128)(2,1)}, u32[]{:S(2)}) copy-start(bf16[2048,128]{1,0:T(8,128)(2,1)} %refs_6_.1) | copy-start | bytes 1572868
  114.7 5.0 %copy-start.3 = (bf16[128,2048]{1,0:T(8,128)(2,1)S(1)}, bf16[128,2048]{1,0:T(8,128)(2,1)}, u32[]{:S(2)}) copy-start(bf16[128,2048]{1,0:T(8,128)(2,1)} %refs_7_.1) | copy-start | bytes 1572868
  125.5 34.8 %all-to-all-start.4 = ((bf16[64,64,128]{2,1,0:T(8,128)(2,1)}), bf16[64,64,128]{2,1,0:T(8,128)(2,1)S(1)}, u32[]{:S(2)}, u32[]{:S(2)}) async-start(bf16[64,64,128]{2,1,0:T(8,128)(2,1)} %get-tuple-element.18), calls=%async_computation.4 | async-start | bytes 2097152 | tf_op jit(solution)/shard_map/all_to_all | solution.py:305
  145.1 18.2 %copy-start.6 = (bf16[128,768]{1,0:T(8,128)(2,1)}, bf16[128,768]{1,0:T(8,128)(2,1)S(1)}, u32[]{:S(2)}) copy-start(bf16[128,768]{1,0:T(8,128)(2,1)S(1)} %slice_dynamic-update-slice_fusion) | copy-start | bytes 589828

commit v8 on v7

--- a/solution.py
+++ b/solution.py
@@ -15,6 +15,7 @@
 LANES = 128
 IDX = ("z", "p", "q")
 M = ("x", "c")
+ALONG = ("z", "p", "q", "c")
 F32 = jnp.float32
 BF16 = jnp.bfloat16
 ROWS = (((0,), (0,)), ((), ()))
@@ -167,6 +168,7 @@
     ny = lax.axis_size("p") * nq
     owners = nz * ny
     swap = [(0, 1), (1, 0)]
+    my_z = lax.axis_index("z")
     my_y = lax.axis_index(("p", "q"))
     my_half = lax.axis_index("q")
     pass_rows, width = index_emb.shape
@@ -181,18 +183,33 @@
     def my_strip(array):
         return lax.dynamic_slice_in_dim(array, strip * LANES, LANES, axis=1)
 
+    cores = lax.axis_size("c")
+    my_core = lax.axis_index("c")
+    at_z = [[(z * ny + y) * cores for z in range(nz)] for y in range(ny)]
+    at_y = [[(z * ny + y) * cores for y in range(ny)] for z in range(nz)]
+    first_groups = at_z + [[i + 1 for i in group] for group in at_y]
+    second_groups = at_y + [[i + 1 for i in group] for group in at_z]
+    second = jnp.where(my_core == 0, my_y, my_z)
+
+    def places(owner):
+        z, y = owner // ny, owner % ny
+        return jnp.where(my_core == 0, z, y), jnp.where(my_core == 0, y, z)
+
     deep = vocab_table.shape[1]
-    flat_ids = token_ids.reshape(-1)
-    upper = jnp.concatenate([flat_ids // LANES, passage_owner[:, 0], passage_row])
-    lower = jnp.pad(flat_ids % LANES, (0, 2 * npass))
-    wanted = jnp.stack([upper, lower]).astype(BF16)
-    wanted = jnp.pad(wanted, ((0, 6), (0, deep - wanted.shape[1])))
+    index_strip = my_strip(index_emb)
+    folded = pass_rows // 2
+    message = jnp.concatenate(
+        [vocab_table, jnp.concatenate([index_strip[:folded], index_strip[folded:]], axis=1)], axis=0
+    )
+    held = message.shape[0]
+    stride = held + ny * CAPS
     slab_owner, slab_row = slab_ids // pass_rows, slab_ids % pass_rows
     earlier = (slab_owner[:, None] == slab_owner[None, :]) & (
         jnp.arange(slab)[:, None] > jnp.arange(slab)[None, :]
     )
     rank = jnp.sum(earlier.astype(jnp.int32), axis=1)
-    slot = ((slab_owner % ny) * nz + slab_owner // ny) * CAPS + rank
+    slab_first, slab_second = places(slab_owner)
+    slot = (slab_first * ny + slab_second) * CAPS + rank
     select = (jnp.arange(owners * CAPS)[:, None] == slot[None, :]).astype(BF16)
     slab_wide = jnp.concatenate(
         [
@@ -201,36 +218,19 @@
         ],
         axis=1,
     )
-    slab_out = dot(select, slab_wide).astype(BF16).reshape(ny, nz * CAPS, deep)
+    slab_out = dot(select, slab_wide).astype(BF16).reshape(nz, ny * CAPS, deep)
     got_first = lax.all_to_all(
-        jnp.concatenate([jnp.broadcast_to(wanted[None], (ny, *wanted.shape)), slab_out], axis=1),
-        ("p", "q"),
+        jnp.concatenate([jnp.broadcast_to(message[None], (nz, *message.shape)), slab_out], axis=1),
+        ALONG,
         0,
         0,
+        axis_index_groups=first_groups,
         tiled=True,
     )
-    got_wanted = got_first[:, :2].astype(jnp.int32)
-    slab_out = got_first[:, wanted.shape[0] :].reshape(ny, nz, CAPS, deep).transpose(1, 0, 2, 3)
-
-    index_strip = my_strip(index_emb)
-    folded = pass_rows // 2
-    message = jnp.concatenate(
-        [vocab_table, jnp.concatenate([index_strip[:folded], index_strip[folded:]], axis=1)], axis=0
-    )
-    held = message.shape[0]
-    stride = held + ny * CAPS
-    got_z = lax.all_to_all(
-        jnp.concatenate(
-            [
-                jnp.broadcast_to(message[None], (nz, *message.shape)),
-                slab_out.reshape(nz, ny * CAPS, deep),
-            ],
-            axis=1,
-        ),
-        "z",
-        0,
-        0,
-        tiled=True,
+    wanted = jnp.concatenate([token_ids.reshape(-1), passage_owner[:, 0], passage_row])
+    wanted = jnp.pad(wanted[None], ((0, 0), (0, -wanted.shape[0] % LANES)))
+    wanted = lax.all_gather(
+        wanted, ALONG, axis=0, axis_index_groups=second_groups, tiled=True
     )
 
     query_strips = query_emb.reshape(queries, strips, LANES).transpose(1, 0, 2)
@@ -242,16 +242,12 @@
         axis=0,
     )
     extra = jnp.pad(extra, ((0, -extra.shape[0] % 8), (0, 0)))
-    pair_message, _ = lax.optimization_barrier(
-        (jnp.concatenate([out_grad, extra], axis=0), got_wanted)
-    )
-    other = lax.ppermute(pair_message, "q", swap)
+    other = lax.ppermute(jnp.concatenate([out_grad, extra], axis=0), "q", swap)
     grads = lax.all_gather(jnp.concatenate([out_grad, other[:count]], axis=0), "x", axis=0)
     grads = [
         lax.all_gather(grads[i * grads.shape[0] // 2 : (i + 1) * grads.shape[0] // 2], "c", axis=0)
         for i in range(2)
     ]
-    got_z, grads = lax.optimization_barrier((got_z, grads))
     other_strips = other[count : count + strips].reshape(strips, queries, LANES)
     spare = -npass % 16
 
@@ -264,24 +260,39 @@
     high = jnp.concatenate([jnp.pad(passage_row, (0, spare)), jnp.pad(other_row, (0, spare))])
     high = (high[:, None] >= folded).astype(jnp.int32)
 
-    ids = got_wanted[:, 0, :count] * LANES + got_wanted[:, 1, :count]
-    place_owner = got_wanted[:, 0, count : count + npass]
-    place_row = got_wanted[:, 0, count + npass : count + 2 * npass]
-    id_owner = ids // vocab_rows
-    token_at = jnp.where(id_owner % ny == my_y, id_owner // ny * stride + ids % vocab_rows, -1)
+    ids, place_owner, place_row = (
+        wanted[:, :count],
+        wanted[:, count : count + npass],
+        wanted[:, count + npass : count + 2 * npass],
+    )
+    token_first, token_second = places(ids // vocab_rows)
+    token_at = jnp.where(token_second == second, token_first * stride + ids % vocab_rows, -1)
+    place_first, place_second = places(place_owner)
     place_at = jnp.where(
-        place_owner % ny == my_y,
-        place_owner // ny * stride + vocab_rows + place_row % folded,
-        -1,
-    )
-    at = jnp.concatenate([token_at, place_at, jnp.full((ny, spare), -1, jnp.int32)], axis=1)
-    at = at.reshape(-1)
-    one_hot = (at[:, None] == jnp.arange(nz * stride)[None, :]).astype(BF16)
-    served = dot(one_hot, got_z.reshape(nz * stride, deep)).astype(BF16)
-    got_y = lax.all_to_all(
-        served.reshape(ny, count + npass + spare, deep), ("p", "q"), 0, 0, tiled=True
-    )
-    part = jnp.sum(got_y.astype(F32), axis=0).astype(BF16)
+        place_second == second, place_first * stride + vocab_rows + place_row % folded, -1
+    )
+    slab_at = (
+        held
+        + jnp.arange(ny)[:, None, None] * CAPS
+        + jnp.arange(nz)[None, :, None] * stride
+        + jnp.arange(CAPS)[None, None, :]
+    ).reshape(ny, nz * CAPS)
+    at = jnp.concatenate(
+        [token_at, place_at, jnp.full((ny, spare), -1, jnp.int32), slab_at], axis=1
+    )
+    one_hot = (at.reshape(-1)[:, None] == jnp.arange(nz * stride)[None, :]).astype(BF16)
+    served = dot(one_hot, got_first.reshape(nz * stride, deep)).astype(BF16)
+    got_second = lax.all_to_all(
+        served.reshape(*at.shape, deep),
+        ALONG,
+        0,
+        0,
+        axis_index_groups=second_groups,
+        tiled=True,
+    )
+    got_second, grads = lax.optimization_barrier((got_second, grads))
+    rows_here = count + npass + spare
+    part = jnp.sum(got_second[:, :rows_here].astype(F32), axis=0).astype(BF16)
 
     nx = lax.axis_size("x")
     near = lax.all_to_all(
@@ -289,19 +300,19 @@
     )
     tokens = [lax.all_gather(near[i * nx : (i + 1) * nx], "c", axis=0) for i in range(nq)]
 
-    got_slab = got_z[:, held:].reshape(-1, deep)
+    got_slab = got_second[:, rows_here:].reshape(-1, deep)
     got_place = got_slab[:, LANES].astype(jnp.int32) - 1
     put = jnp.arange(pass_rows)[:, None] == got_place[None, :]
     placed = dot(put.astype(BF16), got_slab[:, :LANES]).astype(BF16)
     refreshed = jnp.where(jnp.any(put, axis=1)[:, None], placed, index_strip)
-    refreshed, _ = lax.optimization_barrier((refreshed, served))
+
+    terms, pair_relevance = reader(
+        my_half.reshape(1), high, pair_query, tokens, grads, (w_query, w_key, w_value, w_out), owners
+    )
+    relevance = pair_relevance[0, :npass].reshape(queries, K)
+    refreshed, terms = lax.optimization_barrier((refreshed, terms))
     refreshed = lax.all_gather(refreshed, M, axis=0)
     refreshed = jnp.concatenate([refreshed[i] for i in range(strips)], axis=1)
-
-    terms, pair_relevance = reader(
-        my_half.reshape(1), high, pair_query, tokens, grads, (w_query, w_key, w_value, w_out), owners
-    )
-    relevance = pair_relevance[0, :npass].reshape(queries, K)
     terms = lax.all_to_all(terms, IDX, 0, 0, tiled=True)
     rows = terms.shape[1] // 2
     sums = jnp.sum(terms.reshape(owners // nq, nq, *terms.shape[1:]).astype(F32), axis=0)

time: 165 us -> 153 us (0.927)
  waiting for transfers between devices: 45.6 us -> 36.5 us
  blocking collectives: 62.7 us -> 55.4 us
  starting transfers between devices: 29.3 us -> 35.4 us
    all_to_all x1 -> x0, blocking collectives: 27.4 us -> none  [shards(): lax.all_to_all(served.reshape(ny, count + npass + spare, deep), ('p', 'q'...]
    all_gather x0 -> x1, blocking collectives: none -> 20.1 us  [shards(): lax.all_gather(wanted, ALONG, axis=0, axis_index_groups=second_groups, ti...]
    all_to_all x1, waiting for transfers between devices: 10.2 us -> 1.48 us  [shards(): lax.all_to_all(jnp.concatenate([jnp.broadcast_to(message[None], (nz, *mes...]
    all_to_all x1, waiting for transfers between devices: 7.11 us -> 0.01 us  [shards(): lax.all_to_all(served.reshape(*at.shape, deep), ALONG, 0, 0, axis_index_g...]
    ppermute x1, waiting for transfers between devices: 3.71 us -> 10.5 us  [shards(): other = lax.ppermute(jnp.concatenate([out_grad, extra], axis=0), 'q', swap)]
    all_to_all x1, starting transfers between devices: 4.66 us -> 9.3 us  [shards(): terms = lax.all_to_all(terms, IDX, 0, 0, tiled=True)]
    all_to_all x1, waiting for transfers between devices: 10 us -> 8.23 us  [shards(): lax.all_to_all(jnp.broadcast_to(part[None], (nq * nx, *part.shape)), ('q'...]
    all_to_all x1, waiting for transfers between devices: 14.5 us -> 16.3 us  [shards(): terms = lax.all_to_all(terms, IDX, 0, 0, tiled=True)]
  transfers between devices with their start and end apart: 5 -> 5, of which waited for: 5 -> 4; matrix products, arithmetic and copies ran while one was open for 3% -> 3% of each run, Pallas kernels for 0% -> 0%
where the time goes in v8:
time: 153 us; the launch traced here: 152 us
  blocking collectives  55.4 us (36%)
  waiting for transfers between devices  36.5 us (24%)
  starting transfers between devices  35.4 us (23%)
  other arithmetic  7.67 us (5%)
  Pallas kernels  5.84 us (4%)
  matrix products  5.55 us (4%)
  local copies, waits for them, and re-layouts  4.29 us (3%)
    all_gather x1, blocking collectives, shards(): lax.all_gather(wanted, ALONG, axis=0, axis_index_groups=second_groups, ti...  20.1 us
    all_to_all x1, waiting for transfers between devices, shards(): terms = lax.all_to_all(terms, IDX, 0, 0, tiled=True)  16.3 us
    all_gather x1, blocking collectives, shards(): lax.all_gather(jnp.concatenate([out_grad, other[:count]], axis=0), 'x', a...  13 us
    all_gather x1, blocking collectives, shards(): refreshed = lax.all_gather(refreshed, M, axis=0)  12.8 us
    ppermute x1, waiting for transfers between devices, shards(): other = lax.ppermute(jnp.concatenate([out_grad, extra], axis=0), 'q', swap)  10.5 us
    all_to_all x1, starting transfers between devices, shards(): lax.all_to_all(jnp.concatenate([jnp.broadcast_to(message[None], (nz, *mes...  10.4 us
    all_to_all x1, starting transfers between devices, shards(): terms = lax.all_to_all(terms, IDX, 0, 0, tiled=True)  9.3 us
    all_to_all x1, waiting for transfers between devices, shards(): lax.all_to_all(jnp.broadcast_to(part[None], (nq * nx, *part.shape)), ('q'...  8.23 us
  transfers between devices with their start and end apart: 5, of which 4 were waited for; matrix products, arithmetic and copies ran while one was open for 3% of the time, Pallas kernels for 0%

profile of v8, /device:TPU:6, one launch (start us, length us, event | category | flops | bytes accessed | tf_op | source)
XLA Modules:
  0.0 151.6 jit_solution(10897428056668336685)
XLA Ops:
  0.7 0.7 and_select_fusion.3
  1.3 0.2 convert_reduce_fusion.1
  1.5 0.8 constant_dynamic-slice_fusion
  2.3 0.1 broadcast_in_dim.31
  2.4 0.1 convolution_convert_fusion
  2.5 0.9 maximum_maximum_fusion
  3.4 0.1 broadcast_in_dim.30
  3.5 1.2 pad_maximum_fusion
  4.7 10.4 %all-to-all-start = ((bf16[8,336,256]{2,1,0:T(8,128)(2,1)}), bf16[8,336,256]{2,1,0:T(8,128)(2,1)S(1)}, u32[]{:S(2)}, u32[]{:S(2)}) async-start(bf16[8,336,256]{2,1,0:T(8,128)(2,1)} %pad_maximum_fusion), calls=%async_computation | async-start | bytes 2752512 | tf_op jit(solution)/shard_map/all_to_all | solution.py:222
  15.2 0.1 pad.53.clone
  15.3 0.1 add.149
  15.3 0.1 broadcast_add_fusion.1
  15.4 0.1 broadcast_add_fusion
  15.5 0.1 copy.46
  15.6 0.0 copy-done.7
  15.6 0.1 copy.45
  15.7 0.1 reshape.155
  15.8 0.0 copy-done.8
  15.8 0.1 pad_add_fusion.1
  15.9 20.1 %all-gather.6 = s32[8,1,256]{2,1,0:T(1,128)S(1)} all-gather(s32[1,1,256]{2,1,0:T(1,128)S(1)} %pad_bitcast_fusion), channel_id=1, replica_groups={{0,8,16,24,32,40,48,56},{64,72,80,88,96,104,112,120},{128,136,144,152,1..., dimensions={0}, use_global_device_ids=true | all-gather | bytes 9216 | tf_op jit(solution)/shard_map/all_gather | solution.py:232
  35.9 0.1 fusion.28
  36.1 0.1 pad_add_fusion
  36.1 0.1 eq.89
  36.2 1.5 all-to-all-done
  37.7 4.5 %fusion.2 = bf16[1792,256]{1,0:T(8,128)(2,1)} fusion(bf16[2688,256]{1,0:T(8,128)(2,1)S(1)} %bitcast.57, s32[1792]{0:T(1024)S(1)} %eq.89), kind=kOutput, calls=%fused_computation.3 | convolution fusion | flops 2471526400 | bytes 2300928 | tf_op jit(solution)/shard_map/dot_general | solution.py:27
  42.2 7.2 %all-to-all-start.1 = ((bf16[8,224,256]{2,1,0:T(8,128)(2,1)}), bf16[8,224,256]{2,1,0:T(8,128)(2,1)S(1)}, u32[]{:S(2)}, u32[]{:S(2)}) async-start(bf16[8,224,256]{2,1,0:T(8,128)(2,1)} %bitcast.13), calls=%async_computation.1 | async-start | bytes 1835008 | tf_op jit(solution)/shard_map/all_to_all | solution.py:285
  49.5 3.9 %collective-permute-start = (bf16[168,256]{1,0:T(8,128)(2,1)S(1)}, bf16[168,256]{1,0:T(8,128)(2,1)S(1)}, u32[]{:S(2)}, u32[]{:S(2)}) collective-permute-start(bf16[168,256]{1,0:T(8,128)(2,1)S(1)} %fusion.8), channel_id=1, source_target_pairs={{0,8},{8,0},{1,9},{9,1},{2,10},{10,2},{3,11},{11,3},{4,12},{12,4},... | collective-permute-start | bytes 258056 | tf_op jit(solution)/shard_map/ppermute | solution.py:245
  53.4 10.5 %collective-permute-done = bf16[168,256]{1,0:T(8,128)(2,1)S(1)} collective-permute-done((bf16[168,256]{1,0:T(8,128)(2,1)S(1)}, bf16[168,256]{1,0:T(8,128)(2,1)S(1)}, u32[]{:S(2)}, u32[]{:S(2)}) %collective-permute-start) | collective-permute-done | bytes 86048 | tf_op jit(solution)/shard_map/ppermute | solution.py:245
  64.0 13.0 %all-gather = bf16[1280,256]{1,0:T(8,128)(2,1)S(1)} all-gather(bf16[320,256]{1,0:T(8,128)(2,1)S(1)} %pad_maximum_fusion.1), channel_id=2, replica_groups=mesh['z'=8,'p'=4,'q'=2,'x'=4,'c'=2] {'x'}, dimensions={0}, use_global_device_ids=true | all-gather | bytes 819200 | tf_op jit(solution)/shard_map/all_gather | solution.py:246
  77.1 2.3 %all-gather.1 = bf16[4,320,256]{2,1,0:T(8,128)(2,1)S(1)} all-gather(bf16[2,320,256]{2,1,0:T(8,128)(2,1)S(1)} %bitcast.59), channel_id=3, replica_groups=mesh['z'=8,'p'=4,'q'=2,'x'=4,'c'=2] {'c'}, dimensions={0}, use_global_device_ids=true | all-gather | bytes 983040 | tf_op jit(solution)/shard_map/all_gather | solution.py:248
  79.3 2.3 %all-gather.2 = bf16[4,320,256]{2,1,0:T(8,128)(2,1)S(1)} all-gather(bf16[2,320,256]{2,1,0:T(8,128)(2,1)S(1)} %bitcast.58), channel_id=4, replica_groups=mesh['z'=8,'p'=4,'q'=2,'x'=4,'c'=2] {'c'}, dimensions={0}, use_global_device_ids=true | all-gather | bytes 983040 | tf_op jit(solution)/shard_map/all_gather | solution.py:248
  81.6 0.0 all-to-all-done.1
  81.6 0.1 slice_reduce_fusion
  81.7 1.0 broadcast_in_dim.32
  82.7 4.5 %all-to-all-start.2 = ((bf16[8,208,256]{2,1,0:T(8,128)(2,1)}), bf16[8,208,256]{2,1,0:T(8,128)(2,1)S(1)}, u32[]{:S(2)}, u32[]{:S(2)}) async-start(bf16[8,208,256]{2,1,0:T(8,128)(2,1)} %broadcast_in_dim.32), calls=%async_computation.2 | async-start | bytes 1703936 | tf_op jit(solution)/shard_map/all_to_all | solution.py:298
  87.3 0.1 compare_convert_fusion
  87.4 0.1 copy.47.high_ref
  87.6 0.7 reshape.154
  88.2 0.9 fusion.6.query_ref
  89.2 0.1 add_reduce_fusion
  89.3 0.1 fusion.9
  89.4 0.9 fusion.3
  90.3 8.2 %all-to-all-done.2 = bf16[8,208,256]{2,1,0:T(8,128)(2,1)S(1)} async-done(((bf16[8,208,256]{2,1,0:T(8,128)(2,1)}), bf16[8,208,256]{2,1,0:T(8,128)(2,1)S(1)}, u32[]{:S(2)}, u32[]{:S(2)}) %all-to-all-start.2) | async-done | bytes 852000 | tf_op jit(solution)/shard_map/all_to_all | solution.py:298
  98.5 0.1 fusion.39
  98.6 0.0 copy-start
  98.6 0.0 copy-start.1
  98.6 0.0 copy-start.2
  98.6 0.0 copy-start.3
  98.7 2.5 %all-gather.4 = bf16[8,208,256]{2,1,0:T(8,128)(2,1)S(1)} all-gather(bf16[4,208,256]{2,1,0:T(8,128)(2,1)S(1)} %get-tuple-element.20), channel_id=6, replica_groups=mesh['z'=8,'p'=4,'q'=2,'x'=4,'c'=2] {'c'}, dimensions={0}, use_global_device_ids=true | all-gather | bytes 1277952 | tf_op jit(solution)/shard_map/all_gather | solution.py:301
  101.2 2.4 %all-gather.3 = bf16[8,208,256]{2,1,0:T(8,128)(2,1)S(1)} all-gather(bf16[4,208,256]{2,1,0:T(8,128)(2,1)S(1)} %get-tuple-element.21), channel_id=5, replica_groups=mesh['z'=8,'p'=4,'q'=2,'x'=4,'c'=2] {'c'}, dimensions={0}, use_global_device_ids=true | all-gather | bytes 1277952 | tf_op jit(solution)/shard_map/all_gather | solution.py:301
  103.6 0.0 copy-done.3
  103.6 5.8 %reader.1 = (bf16[64,64,128]{2,1,0:T(8,128)(2,1)}, f32[1,96]{1,0:T(1,128)S(1)}) custom-call(s32[1]{0:T(128)} %bitcast.half_ref, s32[96,1]{1,0:T(8,128)S(1)} %copy.47.high_ref, bf16[6,96,256]{2,1,0:T(8,128)(2,1)S(1)} %fusion.6.query_ref, bf16[2,4,208,256]{3,2,1,0:T(8,128)(2,1)S(1)} %bitcast.53, bf16[2,4,208,256]{3,2,1,0:T(8,128)(2,1)S(1)} %bitcast.52, ...), custom_call_target="tpu_custom_call" | custom-call | tf_op jit(solution)/shard_map/reader/pallas_call | solution.py:135
  109.5 9.3 %all-to-all-start.3 = ((bf16[64,64,128]{2,1,0:T(8,128)(2,1)}), bf16[64,64,128]{2,1,0:T(8,128)(2,1)S(1)}, u32[]{:S(2)}, u32[]{:S(2)}) async-start(bf16[64,64,128]{2,1,0:T(8,128)(2,1)} %get-tuple-element.18), calls=%async_computation.3 | async-start | bytes 2097152 | tf_op jit(solution)/shard_map/all_to_all | solution.py:316
  118.8 0.6 reshape_squeeze.3
  119.4 12.8 %all-gather.5 = bf16[1024,128]{1,0:T(8,128)(2,1)S(1)} all-gather(bf16[128,128]{1,0:T(8,128)(2,1)S(1)} %fusion.3), channel_id=7, replica_groups=mesh['z'=8,'p'=4,'q'=2,'x'=4,'c'=2] {'x','c'}, dimensions={0}, use_global_device_ids=true | all-gather | bytes 294912 | tf_op jit(solution)/shard_map/all_gather | solution.py:314
  132.4 0.0 copy-start.5
  132.4 16.3 %all-to-all-done.3 = bf16[64,64,128]{2,1,0:T(8,128)(2,1)S(1)} async-done(((bf16[64,64,128]{2,1,0:T(8,128)(2,1)}), bf16[64,64,128]{2,1,0:T(8,128)(2,1)S(1)}, u32[]{:S(2)}, u32[]{:S(2)}) %all-to-all-start.3) | async-done | bytes 1048608 | tf_op jit(solution)/shard_map/all_to_all | solution.py:316
  148.7 0.2 convert_reduce_fusion
  148.8 0.1 slice_bitcast_fusion.1
  148.9 0.7 maximum_bitcast_fusion
  149.6 0.7 pad_maximum_fusion.4
  150.3 0.7 pad_maximum_fusion.3
  151.0 0.7 pad_maximum_fusion.2
  151.6 0.0 copy-done.5
  (45 shorter events, 0.4 us)
Async XLA Ops:
  4.7 10.9 %copy-start.7 = (s32[40,4]{0,1:T(4,128)S(1)}, s32[40,4]{0,1:T(4,128)}, u32[]{:S(2)}) copy-start(s32[40,4]{0,1:T(4,128)} %param.17) | copy-start | bytes 1924
  4.7 11.1 %copy-start.8 = (s32[40,1]{0,1:T(1,128)S(1)}, s32[40,1]{0,1:T(1,128)}, u32[]{:S(2)}) copy-start(s32[40,1]{0,1:T(1,128)} %param.15) | copy-start | bytes 484
  4.7 11.1 %copy-start.9 = (s32[40]{0:T(128)S(1)}, s32[40]{0:T(128)}, u32[]{:S(2)}) copy-start(s32[40]{0:T(128)} %param.16) | copy-start | bytes 484
  4.7 33.0 %all-to-all-start = ((bf16[8,336,256]{2,1,0:T(8,128)(2,1)}), bf16[8,336,256]{2,1,0:T(8,128)(2,1)S(1)}, u32[]{:S(2)}, u32[]{:S(2)}) async-start(bf16[8,336,256]{2,1,0:T(8,128)(2,1)} %pad_maximum_fusion), calls=%async_computation | async-start | bytes 2752512 | tf_op jit(solution)/shard_map/all_to_all | solution.py:222
  42.2 7.2 %copy-start.6 = (bf16[2,768]{1,0:T(2,128)(2,1)S(1)}, bf16[2,768]{1,0:T(2,128)(2,1)}, u32[]{:S(2)}) copy-start(bf16[2,768]{1,0:T(2,128)(2,1)} %param.14) | copy-start | bytes 9220
  42.2 7.3 %copy-start.4 = (bf16[160,256]{1,0:T(8,128)(2,1)S(1)}, bf16[160,256]{1,0:T(8,128)(2,1)}, u32[]{:S(2)}) copy-start(bf16[160,256]{1,0:T(8,128)(2,1)} %param.23) | copy-start | bytes 245764
  42.2 39.4 %all-to-all-start.1 = ((bf16[8,224,256]{2,1,0:T(8,128)(2,1)}), bf16[8,224,256]{2,1,0:T(8,128)(2,1)S(1)}, u32[]{:S(2)}, u32[]{:S(2)}) async-start(bf16[8,224,256]{2,1,0:T(8,128)(2,1)} %bitcast.13), calls=%async_computation.1 | async-start | bytes 1835008 | tf_op jit(solution)/shard_map/all_to_all | solution.py:285
  49.5 14.4 %collective-permute-start = (bf16[168,256]{1,0:T(8,128)(2,1)S(1)}, bf16[168,256]{1,0:T(8,128)(2,1)S(1)}, u32[]{:S(2)}, u32[]{:S(2)}) collective-permute-start(bf16[168,256]{1,0:T(8,128)(2,1)S(1)} %fusion.8), channel_id=1, source_target_pairs={{0,8},{8,0},{1,9},{9,1},{2,10},{10,2},{3,11},{11,3},{4,12},{12,4},... | collective-permute-start | bytes 258056 | tf_op jit(solution)/shard_map/ppermute | solution.py:245
  82.7 15.9 %all-to-all-start.2 = ((bf16[8,208,256]{2,1,0:T(8,128)(2,1)}), bf16[8,208,256]{2,1,0:T(8,128)(2,1)S(1)}, u32[]{:S(2)}, u32[]{:S(2)}) async-start(bf16[8,208,256]{2,1,0:T(8,128)(2,1)} %broadcast_in_dim.32), calls=%async_computation.2 | async-start | bytes 1703936 | tf_op jit(solution)/shard_map/all_to_all | solution.py:298
  98.6 5.0 %copy-start = (bf16[2048,128]{1,0:T(8,128)(2,1)S(1)}, bf16[2048,128]{1,0:T(8,128)(2,1)}, u32[]{:S(2)}) copy-start(bf16[2048,128]{1,0:T(8,128)(2,1)} %refs_4_.1) | copy-start | bytes 1572868
  98.6 5.0 %copy-start.1 = (bf16[2048,128]{1,0:T(8,128)(2,1)S(1)}, bf16[2048,128]{1,0:T(8,128)(2,1)}, u32[]{:S(2)}) copy-start(bf16[2048,128]{1,0:T(8,128)(2,1)} %refs_5_.1) | copy-start | bytes 1572868
  98.6 5.0 %copy-start.2 = (bf16[2048,128]{1,0:T(8,128)(2,1)S(1)}, bf16[2048,128]{1,0:T(8,128)(2,1)}, u32[]{:S(2)}) copy-start(bf16[2048,128]{1,0:T(8,128)(2,1)} %refs_6_.1) | copy-start | bytes 1572868
  98.6 5.0 %copy-start.3 = (bf16[128,2048]{1,0:T(8,128)(2,1)S(1)}, bf16[128,2048]{1,0:T(8,128)(2,1)}, u32[]{:S(2)}) copy-start(bf16[128,2048]{1,0:T(8,128)(2,1)} %refs_7_.1) | copy-start | bytes 1572868
  109.5 39.2 %all-to-all-start.3 = ((bf16[64,64,128]{2,1,0:T(8,128)(2,1)}), bf16[64,64,128]{2,1,0:T(8,128)(2,1)S(1)}, u32[]{:S(2)}, u32[]{:S(2)}) async-start(bf16[64,64,128]{2,1,0:T(8,128)(2,1)} %get-tuple-element.18), calls=%async_computation.3 | async-start | bytes 2097152 | tf_op jit(solution)/shard_map/all_to_all | solution.py:316
  132.4 19.3 %copy-start.5 = (bf16[128,768]{1,0:T(8,128)(2,1)}, bf16[128,768]{1,0:T(8,128)(2,1)S(1)}, u32[]{:S(2)}) copy-start(bf16[128,768]{1,0:T(8,128)(2,1)S(1)} %slice_dynamic-update-slice_fusion) | copy-start | bytes 589828

commit v9 on v8

--- a/solution.py
+++ b/solution.py
@@ -13,6 +13,7 @@
 PLEN = 4
 CAPS = 2
 LANES = 128
+REACH = 4096
 IDX = ("z", "p", "q")
 M = ("x", "c")
 ALONG = ("z", "p", "q", "c")
@@ -191,9 +192,9 @@
     second_groups = at_y + [[i + 1 for i in group] for group in at_z]
     second = jnp.where(my_core == 0, my_y, my_z)
 
-    def places(owner):
+    def places(owner, core):
         z, y = owner // ny, owner % ny
-        return jnp.where(my_core == 0, z, y), jnp.where(my_core == 0, y, z)
+        return jnp.where(core == 0, z, y), jnp.where(core == 0, y, z)
 
     deep = vocab_table.shape[1]
     index_strip = my_strip(index_emb)
@@ -201,14 +202,26 @@
     message = jnp.concatenate(
         [vocab_table, jnp.concatenate([index_strip[:folded], index_strip[folded:]], axis=1)], axis=0
     )
-    held = message.shape[0]
+    asked = message.shape[0]
+    held = asked + 8
     stride = held + ny * CAPS
+    spare = -npass % 16
+    flat_ids = token_ids.reshape(-1)
+    row = jnp.concatenate([flat_ids % vocab_rows, vocab_rows + passage_row % folded])
+    row_first, row_second = places(
+        jnp.concatenate([flat_ids // vocab_rows, passage_owner[:, 0]]), 1 - my_core
+    )
+    code = row_second * REACH + row_first * stride + row
+    rows_here = count + npass + spare
+    code = jnp.pad(code, (0, deep - code.shape[0]), constant_values=ny * REACH - 1)
+    code = jnp.pad(jnp.stack([code // LANES, code % LANES]).astype(BF16), ((0, 6), (0, 0)))
+    message = jnp.concatenate([message, code], axis=0)
     slab_owner, slab_row = slab_ids // pass_rows, slab_ids % pass_rows
     earlier = (slab_owner[:, None] == slab_owner[None, :]) & (
         jnp.arange(slab)[:, None] > jnp.arange(slab)[None, :]
     )
     rank = jnp.sum(earlier.astype(jnp.int32), axis=1)
-    slab_first, slab_second = places(slab_owner)
+    slab_first, slab_second = places(slab_owner, my_core)
     slot = (slab_first * ny + slab_second) * CAPS + rank
     select = (jnp.arange(owners * CAPS)[:, None] == slot[None, :]).astype(BF16)
     slab_wide = jnp.concatenate(
@@ -227,12 +240,6 @@
         axis_index_groups=first_groups,
         tiled=True,
     )
-    wanted = jnp.concatenate([token_ids.reshape(-1), passage_owner[:, 0], passage_row])
-    wanted = jnp.pad(wanted[None], ((0, 0), (0, -wanted.shape[0] % LANES)))
-    wanted = lax.all_gather(
-        wanted, ALONG, axis=0, axis_index_groups=second_groups, tiled=True
-    )
-
     query_strips = query_emb.reshape(queries, strips, LANES).transpose(1, 0, 2)
     extra = jnp.concatenate(
         [
@@ -243,14 +250,9 @@
     )
     extra = jnp.pad(extra, ((0, -extra.shape[0] % 8), (0, 0)))
     other = lax.ppermute(jnp.concatenate([out_grad, extra], axis=0), "q", swap)
-    grads = lax.all_gather(jnp.concatenate([out_grad, other[:count]], axis=0), "x", axis=0)
-    grads = [
-        lax.all_gather(grads[i * grads.shape[0] // 2 : (i + 1) * grads.shape[0] // 2], "c", axis=0)
-        for i in range(2)
-    ]
+    got_first, other = lax.optimization_barrier((got_first, other))
+    along_x = lax.all_gather(jnp.concatenate([out_grad, other[:count]], axis=0), "x", axis=0)
     other_strips = other[count : count + strips].reshape(strips, queries, LANES)
-    spare = -npass % 16
-
     def per_passage(some):
         some = jnp.repeat(jnp.concatenate([some, some], axis=2), K, axis=1)
         return jnp.pad(some, ((0, 0), (0, spare), (0, 0)))
@@ -260,26 +262,16 @@
     high = jnp.concatenate([jnp.pad(passage_row, (0, spare)), jnp.pad(other_row, (0, spare))])
     high = (high[:, None] >= folded).astype(jnp.int32)
 
-    ids, place_owner, place_row = (
-        wanted[:, :count],
-        wanted[:, count : count + npass],
-        wanted[:, count + npass : count + 2 * npass],
-    )
-    token_first, token_second = places(ids // vocab_rows)
-    token_at = jnp.where(token_second == second, token_first * stride + ids % vocab_rows, -1)
-    place_first, place_second = places(place_owner)
-    place_at = jnp.where(
-        place_second == second, place_first * stride + vocab_rows + place_row % folded, -1
-    )
+    wanted = lax.ppermute(got_first[:, asked : asked + 2], "c", [(0, 1), (1, 0)])
+    wanted = wanted.astype(jnp.int32)[:, :, :rows_here]
+    rows_at = wanted[:, 0] * LANES + wanted[:, 1] - second * REACH
     slab_at = (
         held
         + jnp.arange(ny)[:, None, None] * CAPS
         + jnp.arange(nz)[None, :, None] * stride
         + jnp.arange(CAPS)[None, None, :]
     ).reshape(ny, nz * CAPS)
-    at = jnp.concatenate(
-        [token_at, place_at, jnp.full((ny, spare), -1, jnp.int32), slab_at], axis=1
-    )
+    at = jnp.concatenate([rows_at, slab_at], axis=1)
     one_hot = (at.reshape(-1)[:, None] == jnp.arange(nz * stride)[None, :]).astype(BF16)
     served = dot(one_hot, got_first.reshape(nz * stride, deep)).astype(BF16)
     got_second = lax.all_to_all(
@@ -290,14 +282,17 @@
         axis_index_groups=second_groups,
         tiled=True,
     )
-    got_second, grads = lax.optimization_barrier((got_second, grads))
-    rows_here = count + npass + spare
+    got_second, along_x = lax.optimization_barrier((got_second, along_x))
     part = jnp.sum(got_second[:, :rows_here].astype(F32), axis=0).astype(BF16)
 
     nx = lax.axis_size("x")
+    grads = [
+        lax.all_gather(along_x[i * nx // 2 : (i + 1) * nx // 2], "c", axis=0) for i in range(2)
+    ]
     near = lax.all_to_all(
         jnp.broadcast_to(part[None], (nq * nx, *part.shape)), ("q", "x"), 0, 0, tiled=True
     )
+    near, grads = lax.optimization_barrier((near, grads))
     tokens = [lax.all_gather(near[i * nx : (i + 1) * nx], "c", axis=0) for i in range(nq)]
 
     got_slab = got_second[:, rows_here:].reshape(-1, deep)

time: 153 us -> 140 us (0.915)
  blocking collectives: 55.4 us -> 36.1 us
  waiting for transfers between devices: 36.5 us -> 43.5 us
  starting transfers between devices: 35.4 us -> 33.7 us
    all_gather x3 -> x2, blocking collectives: 24.6 us -> 4.54 us  [shards(): lax.all_gather(along_x[i * nx // 2:(i + 1) * nx // 2], 'c', axis=0)]
    all_to_all x1, waiting for transfers between devices: 1.48 us -> 10.9 us  [shards(): lax.all_to_all(jnp.concatenate([jnp.broadcast_to(message[None], (nz, *mes...]
    all_to_all x1, waiting for transfers between devices: 8.23 us -> 3.48 us  [shards(): lax.all_to_all(jnp.broadcast_to(part[None], (nq * nx, *part.shape)), ('q'...]
    all_to_all x1, waiting for transfers between devices: 0.01 us -> 3.65 us  [shards(): lax.all_to_all(served.reshape(*at.shape, deep), ALONG, 0, 0, axis_index_g...]
    all_to_all x1, starting transfers between devices: 9.3 us -> 5.88 us  [shards(): terms = lax.all_to_all(terms, IDX, 0, 0, tiled=True)]
    ppermute x1, waiting for transfers between devices: 10.5 us -> 8.17 us  [shards(): other = lax.ppermute(jnp.concatenate([out_grad, extra], axis=0), 'q', swap)]
    ppermute x0 -> x1, starting transfers between devices: none -> 1.92 us  [shards(): wanted = lax.ppermute(got_first[:, asked:asked + 2], 'c', [(0, 1), (1, 0)])]
  transfers between devices with their start and end apart: 5 -> 6, of which waited for: 4 -> 6; matrix products, arithmetic and copies ran while one was open for 3% -> 2% of each run, Pallas kernels for 0% -> 0%
where the time goes in v9:
time: 140 us; the launch traced here: 138 us
  waiting for transfers between devices  43.5 us (31%)
  blocking collectives  36.1 us (26%)
  starting transfers between devices  33.7 us (24%)
  other arithmetic  8.13 us (6%)
  Pallas kernels  5.85 us (4%)
  matrix products  5.72 us (4%)
  local copies, waits for them, and re-layouts  4.27 us (3%)
    all_to_all x1, waiting for transfers between devices, shards(): terms = lax.all_to_all(terms, IDX, 0, 0, tiled=True)  16.3 us
    all_gather x1, blocking collectives, shards(): lax.all_gather(jnp.concatenate([out_grad, other[:count]], axis=0), 'x', a...  13.8 us
    all_gather x1, blocking collectives, shards(): refreshed = lax.all_gather(refreshed, M, axis=0)  12.8 us
    all_to_all x1, waiting for transfers between devices, shards(): lax.all_to_all(jnp.concatenate([jnp.broadcast_to(message[None], (nz, *mes...  10.9 us
    all_to_all x1, starting transfers between devices, shards(): lax.all_to_all(jnp.concatenate([jnp.broadcast_to(message[None], (nz, *mes...  10.5 us
    ppermute x1, waiting for transfers between devices, shards(): other = lax.ppermute(jnp.concatenate([out_grad, extra], axis=0), 'q', swap)  8.17 us
    all_to_all x1, starting transfers between devices, shards(): lax.all_to_all(served.reshape(*at.shape, deep), ALONG, 0, 0, axis_index_g...  7.23 us
    all_to_all x1, starting transfers between devices, shards(): terms = lax.all_to_all(terms, IDX, 0, 0, tiled=True)  5.88 us
  transfers between devices with their start and end apart: 6, of which 6 were waited for; matrix products, arithmetic and copies ran while one was open for 2% of the time, Pallas kernels for 0%

profile of v9, /device:TPU:6, one launch (start us, length us, event | category | flops | bytes accessed | tf_op | source)
XLA Modules:
  0.0 138.3 jit_solution(18419949906231344285)
XLA Ops:
  0.7 0.7 and_select_fusion.3
  1.3 0.2 convert_reduce_fusion.1
  1.5 0.7 convert_bitcast_fusion
  2.2 0.8 copy.44
  3.0 0.1 reshape.155
  3.1 0.7 add_add_fusion
  4.0 0.8 constant_dynamic-slice_fusion
  4.7 0.1 broadcast_in_dim.18
  4.8 0.1 convolution_convert_fusion
  5.0 0.9 pad_maximum_fusion.1
  5.9 0.1 broadcast_in_dim.17
  6.0 1.2 pad_maximum_fusion
  7.2 10.5 %all-to-all-start = ((bf16[8,344,256]{2,1,0:T(8,128)(2,1)}), bf16[8,344,256]{2,1,0:T(8,128)(2,1)S(1)}, u32[]{:S(2)}, u32[]{:S(2)}) async-start(bf16[8,344,256]{2,1,0:T(8,128)(2,1)} %pad_maximum_fusion), calls=%async_computation | async-start | bytes 2818048 | tf_op jit(solution)/shard_map/all_to_all | solution.py:235
  17.6 0.0 copy-done.6
  17.7 0.0 copy-done.4
  17.7 3.5 %collective-permute-start = (bf16[168,256]{1,0:T(8,128)(2,1)S(1)}, bf16[168,256]{1,0:T(8,128)(2,1)S(1)}, u32[]{:S(2)}, u32[]{:S(2)}) collective-permute-start(bf16[168,256]{1,0:T(8,128)(2,1)S(1)} %fusion.8), channel_id=1, source_target_pairs={{0,8},{8,0},{1,9},{9,1},{2,10},{10,2},{3,11},{11,3},{4,12},{12,4},... | collective-permute-start | bytes 258056 | tf_op jit(solution)/shard_map/ppermute | solution.py:252
  21.2 0.1 broadcast_add_fusion.1
  21.3 0.1 add.167
  21.3 8.2 %collective-permute-done = bf16[168,256]{1,0:T(8,128)(2,1)S(1)} collective-permute-done((bf16[168,256]{1,0:T(8,128)(2,1)S(1)}, bf16[168,256]{1,0:T(8,128)(2,1)S(1)}, u32[]{:S(2)}, u32[]{:S(2)}) %collective-permute-start) | collective-permute-done | bytes 86048 | tf_op jit(solution)/shard_map/ppermute | solution.py:252
  29.5 10.9 %all-to-all-done = bf16[8,344,256]{2,1,0:T(8,128)(2,1)S(1)} async-done(((bf16[8,344,256]{2,1,0:T(8,128)(2,1)}), bf16[8,344,256]{2,1,0:T(8,128)(2,1)S(1)}, u32[]{:S(2)}, u32[]{:S(2)}) %all-to-all-start) | async-done | bytes 1409056 | tf_op jit(solution)/shard_map/all_to_all | solution.py:235
  40.4 1.9 %collective-permute-start.1 = (bf16[8,2,256]{2,1,0:T(2,128)(2,1)S(1)}, bf16[8,2,256]{2,1,0:T(2,128)(2,1)S(1)}, u32[]{:S(2)}, u32[]{:S(2)}) collective-permute-start(bf16[8,2,256]{2,1,0:T(2,128)(2,1)S(1)} %slice.100), channel_id=1, source_target_pairs={{0,1},{1,0},{2,3},{3,2},{4,5},{5,4},{6,7},{7,6},{8,9},{9,8},{10,11... | collective-permute-start | bytes 24584 | tf_op jit(solution)/shard_map/ppermute | solution.py:265
  42.4 0.1 broadcast_add_fusion
  42.4 0.1 copy.46
  42.5 1.0 collective-permute-done.1
  43.5 0.1 pad_add_fusion
  43.6 0.1 eq.82
  43.7 4.7 %fusion.2 = bf16[1792,256]{1,0:T(8,128)(2,1)} fusion(bf16[2752,256]{1,0:T(8,128)(2,1)S(1)} %bitcast.54, s32[1792]{0:T(1024)S(1)} %eq.82), kind=kOutput, calls=%fused_computation.3 | convolution fusion | flops 2530361344 | bytes 2333696 | tf_op jit(solution)/shard_map/dot_general | solution.py:28
  48.4 7.2 %all-to-all-start.1 = ((bf16[8,224,256]{2,1,0:T(8,128)(2,1)}), bf16[8,224,256]{2,1,0:T(8,128)(2,1)S(1)}, u32[]{:S(2)}, u32[]{:S(2)}) async-start(bf16[8,224,256]{2,1,0:T(8,128)(2,1)} %bitcast.11), calls=%async_computation.1 | async-start | bytes 1835008 | tf_op jit(solution)/shard_map/all_to_all | solution.py:277
  55.7 0.0 copy-done.7
  55.7 13.8 %all-gather = bf16[1280,256]{1,0:T(8,128)(2,1)S(1)} all-gather(bf16[320,256]{1,0:T(8,128)(2,1)S(1)} %pad_maximum_fusion.2), channel_id=2, replica_groups=mesh['z'=8,'p'=4,'q'=2,'x'=4,'c'=2] {'x'}, dimensions={0}, use_global_device_ids=true | all-gather | bytes 819200 | tf_op jit(solution)/shard_map/all_gather | solution.py:254
  69.5 3.7 %all-to-all-done.1 = bf16[8,224,256]{2,1,0:T(8,128)(2,1)S(1)} async-done(((bf16[8,224,256]{2,1,0:T(8,128)(2,1)}), bf16[8,224,256]{2,1,0:T(8,128)(2,1)S(1)}, u32[]{:S(2)}, u32[]{:S(2)}) %all-to-all-start.1) | async-done | bytes 917536 | tf_op jit(solution)/shard_map/all_to_all | solution.py:277
  73.1 0.1 slice_reduce_fusion
  73.3 1.0 broadcast_in_dim.22
  74.2 4.8 %all-to-all-start.2 = ((bf16[8,208,256]{2,1,0:T(8,128)(2,1)}), bf16[8,208,256]{2,1,0:T(8,128)(2,1)S(1)}, u32[]{:S(2)}, u32[]{:S(2)}) async-start(bf16[8,208,256]{2,1,0:T(8,128)(2,1)} %broadcast_in_dim.22), calls=%async_computation.2 | async-start | bytes 1703936 | tf_op jit(solution)/shard_map/all_to_all | solution.py:292
  79.1 0.1 compare_convert_fusion
  79.1 0.1 copy.47.high_ref
  79.4 0.1 add_reduce_fusion
  79.5 0.1 fusion.9
  79.6 2.3 %all-gather.2 = bf16[4,320,256]{2,1,0:T(8,128)(2,1)S(1)} all-gather(bf16[2,320,256]{2,1,0:T(8,128)(2,1)S(1)} %get-tuple-element.30), channel_id=4, replica_groups=mesh['z'=8,'p'=4,'q'=2,'x'=4,'c'=2] {'c'}, dimensions={0}, use_global_device_ids=true | all-gather | bytes 983040 | tf_op jit(solution)/shard_map/all_gather | solution.py:290
  81.9 2.3 %all-gather.1 = bf16[4,320,256]{2,1,0:T(8,128)(2,1)S(1)} all-gather(bf16[2,320,256]{2,1,0:T(8,128)(2,1)S(1)} %get-tuple-element.31), channel_id=3, replica_groups=mesh['z'=8,'p'=4,'q'=2,'x'=4,'c'=2] {'c'}, dimensions={0}, use_global_device_ids=true | all-gather | bytes 983040 | tf_op jit(solution)/shard_map/all_gather | solution.py:290
  84.2 0.9 fusion.3
  85.1 3.5 %all-to-all-done.2 = bf16[8,208,256]{2,1,0:T(8,128)(2,1)S(1)} async-done(((bf16[8,208,256]{2,1,0:T(8,128)(2,1)}), bf16[8,208,256]{2,1,0:T(8,128)(2,1)S(1)}, u32[]{:S(2)}, u32[]{:S(2)}) %all-to-all-start.2) | async-done | bytes 852000 | tf_op jit(solution)/shard_map/all_to_all | solution.py:292
  88.6 0.1 fusion.32
  88.6 0.0 copy-start
  88.6 0.0 copy-start.1
  88.7 0.0 copy-start.2
  88.7 0.0 copy-start.3
  88.7 2.5 %all-gather.4 = bf16[8,208,256]{2,1,0:T(8,128)(2,1)S(1)} all-gather(bf16[4,208,256]{2,1,0:T(8,128)(2,1)S(1)} %get-tuple-element.28), channel_id=6, replica_groups=mesh['z'=8,'p'=4,'q'=2,'x'=4,'c'=2] {'c'}, dimensions={0}, use_global_device_ids=true | all-gather | bytes 1277952 | tf_op jit(solution)/shard_map/all_gather | solution.py:296
  91.2 2.4 %all-gather.3 = bf16[8,208,256]{2,1,0:T(8,128)(2,1)S(1)} all-gather(bf16[4,208,256]{2,1,0:T(8,128)(2,1)S(1)} %get-tuple-element.29), channel_id=5, replica_groups=mesh['z'=8,'p'=4,'q'=2,'x'=4,'c'=2] {'c'}, dimensions={0}, use_global_device_ids=true | all-gather | bytes 1277952 | tf_op jit(solution)/shard_map/all_gather | solution.py:296
  93.6 0.0 copy-done
  93.6 0.0 copy-done.1
  93.6 0.0 copy-done.3
  93.6 5.9 %reader.1 = (bf16[64,64,128]{2,1,0:T(8,128)(2,1)}, f32[1,96]{1,0:T(1,128)S(1)}) custom-call(s32[1]{0:T(128)} %bitcast.half_ref, s32[96,1]{1,0:T(8,128)S(1)} %copy.47.high_ref, bf16[6,96,256]{2,1,0:T(8,128)(2,1)S(1)} %fusion.6.query_ref, bf16[2,4,208,256]{3,2,1,0:T(8,128)(2,1)S(1)} %bitcast.49, bf16[2,4,208,256]{3,2,1,0:T(8,128)(2,1)S(1)} %bitcast.48, ...), custom_call_target="tpu_custom_call" | custom-call | tf_op jit(solution)/shard_map/reader/pallas_call | solution.py:136
  99.5 5.9 %all-to-all-start.3 = ((bf16[64,64,128]{2,1,0:T(8,128)(2,1)}), bf16[64,64,128]{2,1,0:T(8,128)(2,1)S(1)}, u32[]{:S(2)}, u32[]{:S(2)}) async-start(bf16[64,64,128]{2,1,0:T(8,128)(2,1)} %get-tuple-element.26), calls=%async_computation.3 | async-start | bytes 2097152 | tf_op jit(solution)/shard_map/all_to_all | solution.py:311
  105.4 0.6 reshape_squeeze.3
  106.1 12.8 %all-gather.5 = bf16[1024,128]{1,0:T(8,128)(2,1)S(1)} all-gather(bf16[128,128]{1,0:T(8,128)(2,1)S(1)} %fusion.3), channel_id=7, replica_groups=mesh['z'=8,'p'=4,'q'=2,'x'=4,'c'=2] {'x','c'}, dimensions={0}, use_global_device_ids=true | all-gather | bytes 294912 | tf_op jit(solution)/shard_map/all_gather | solution.py:309
  119.0 0.0 copy-start.5
  119.0 16.3 %all-to-all-done.3 = bf16[64,64,128]{2,1,0:T(8,128)(2,1)S(1)} async-done(((bf16[64,64,128]{2,1,0:T(8,128)(2,1)}), bf16[64,64,128]{2,1,0:T(8,128)(2,1)S(1)}, u32[]{:S(2)}, u32[]{:S(2)}) %all-to-all-start.3) | async-done | bytes 1048608 | tf_op jit(solution)/shard_map/all_to_all | solution.py:311
  135.3 0.2 convert_reduce_fusion
  135.4 0.1 slice_bitcast_fusion.1
  135.5 0.7 maximum_bitcast_fusion
  136.2 0.7 pad_maximum_fusion.5
  136.9 0.7 pad_maximum_fusion.4
  137.6 0.7 pad_maximum_fusion.3
  (45 shorter events, 0.5 us)
Async XLA Ops:
  7.2 10.5 %copy-start.6 = (bf16[2,768]{1,0:T(2,128)(2,1)S(1)}, bf16[2,768]{1,0:T(2,128)(2,1)}, u32[]{:S(2)}) copy-start(bf16[2,768]{1,0:T(2,128)(2,1)} %param.14) | copy-start | bytes 9220
  7.2 10.5 %copy-start.4 = (bf16[160,256]{1,0:T(8,128)(2,1)S(1)}, bf16[160,256]{1,0:T(8,128)(2,1)}, u32[]{:S(2)}) copy-start(bf16[160,256]{1,0:T(8,128)(2,1)} %param.23) | copy-start | bytes 245764
  7.2 33.2 %all-to-all-start = ((bf16[8,344,256]{2,1,0:T(8,128)(2,1)}), bf16[8,344,256]{2,1,0:T(8,128)(2,1)S(1)}, u32[]{:S(2)}, u32[]{:S(2)}) async-start(bf16[8,344,256]{2,1,0:T(8,128)(2,1)} %pad_maximum_fusion), calls=%async_computation | async-start | bytes 2818048 | tf_op jit(solution)/shard_map/all_to_all | solution.py:235
  17.7 11.8 %collective-permute-start = (bf16[168,256]{1,0:T(8,128)(2,1)S(1)}, bf16[168,256]{1,0:T(8,128)(2,1)S(1)}, u32[]{:S(2)}, u32[]{:S(2)}) collective-permute-start(bf16[168,256]{1,0:T(8,128)(2,1)S(1)} %fusion.8), channel_id=1, source_target_pairs={{0,8},{8,0},{1,9},{9,1},{2,10},{10,2},{3,11},{11,3},{4,12},{12,4},... | collective-permute-start | bytes 258056 | tf_op jit(solution)/shard_map/ppermute | solution.py:252
  40.4 3.1 %collective-permute-start.1 = (bf16[8,2,256]{2,1,0:T(2,128)(2,1)S(1)}, bf16[8,2,256]{2,1,0:T(2,128)(2,1)S(1)}, u32[]{:S(2)}, u32[]{:S(2)}) collective-permute-start(bf16[8,2,256]{2,1,0:T(2,128)(2,1)S(1)} %slice.100), channel_id=1, source_target_pairs={{0,1},{1,0},{2,3},{3,2},{4,5},{5,4},{6,7},{7,6},{8,9},{9,8},{10,11... | collective-permute-start | bytes 24584 | tf_op jit(solution)/shard_map/ppermute | solution.py:265
  48.4 7.3 %copy-start.7 = (s32[40]{0:T(128)S(1)}, s32[40]{0:T(128)}, u32[]{:S(2)}) copy-start(s32[40]{0:T(128)} %param.16) | copy-start | bytes 484
  48.4 24.8 %all-to-all-start.1 = ((bf16[8,224,256]{2,1,0:T(8,128)(2,1)}), bf16[8,224,256]{2,1,0:T(8,128)(2,1)S(1)}, u32[]{:S(2)}, u32[]{:S(2)}) async-start(bf16[8,224,256]{2,1,0:T(8,128)(2,1)} %bitcast.11), calls=%async_computation.1 | async-start | bytes 1835008 | tf_op jit(solution)/shard_map/all_to_all | solution.py:277
  74.2 14.3 %all-to-all-start.2 = ((bf16[8,208,256]{2,1,0:T(8,128)(2,1)}), bf16[8,208,256]{2,1,0:T(8,128)(2,1)S(1)}, u32[]{:S(2)}, u32[]{:S(2)}) async-start(bf16[8,208,256]{2,1,0:T(8,128)(2,1)} %broadcast_in_dim.22), calls=%async_computation.2 | async-start | bytes 1703936 | tf_op jit(solution)/shard_map/all_to_all | solution.py:292
  88.6 5.0 %copy-start = (bf16[2048,128]{1,0:T(8,128)(2,1)S(1)}, bf16[2048,128]{1,0:T(8,128)(2,1)}, u32[]{:S(2)}) copy-start(bf16[2048,128]{1,0:T(8,128)(2,1)} %refs_4_.1) | copy-start | bytes 1572868
  88.6 5.0 %copy-start.1 = (bf16[2048,128]{1,0:T(8,128)(2,1)S(1)}, bf16[2048,128]{1,0:T(8,128)(2,1)}, u32[]{:S(2)}) copy-start(bf16[2048,128]{1,0:T(8,128)(2,1)} %refs_5_.1) | copy-start | bytes 1572868
  88.7 5.0 %copy-start.2 = (bf16[2048,128]{1,0:T(8,128)(2,1)S(1)}, bf16[2048,128]{1,0:T(8,128)(2,1)}, u32[]{:S(2)}) copy-start(bf16[2048,128]{1,0:T(8,128)(2,1)} %refs_6_.1) | copy-start | bytes 1572868
  88.7 5.0 %copy-start.3 = (bf16[128,2048]{1,0:T(8,128)(2,1)S(1)}, bf16[128,2048]{1,0:T(8,128)(2,1)}, u32[]{:S(2)}) copy-start(bf16[128,2048]{1,0:T(8,128)(2,1)} %refs_7_.1) | copy-start | bytes 1572868
  99.5 35.8 %all-to-all-start.3 = ((bf16[64,64,128]{2,1,0:T(8,128)(2,1)}), bf16[64,64,128]{2,1,0:T(8,128)(2,1)S(1)}, u32[]{:S(2)}, u32[]{:S(2)}) async-start(bf16[64,64,128]{2,1,0:T(8,128)(2,1)} %get-tuple-element.26), calls=%async_computation.3 | async-start | bytes 2097152 | tf_op jit(solution)/shard_map/all_to_all | solution.py:311
  119.0 19.3 %copy-start.5 = (bf16[128,768]{1,0:T(8,128)(2,1)}, bf16[128,768]{1,0:T(8,128)(2,1)S(1)}, u32[]{:S(2)}) copy-start(bf16[128,768]{1,0:T(8,128)(2,1)S(1)} %slice_dynamic-update-slice_fusion) | copy-start | bytes 589828

commit v10 on v9

--- a/solution.py
+++ b/solution.py
@@ -31,11 +31,13 @@
 
 def reader_kernel(heads, half_ref, high_ref, query_ref, *refs):
     token_refs, grad_refs, hbm = refs[:2], refs[2:4], refs[4:8]
-    out_ref, rel_ref, vmem, sems = refs[8], refs[9], refs[10:14], refs[14]
-    copies = [pltpu.make_async_copy(hbm[i], vmem[i], sems.at[i]) for i in range(4)]
+    out_ref, rel_ref, vmem, sems = refs[8], refs[9], refs[10:12], refs[12]
+    states_ref, wo_ref = vmem
+    inner = wo_ref.shape[0]
+    targets = [states_ref.at[:, i * inner : (i + 1) * inner] for i in range(3)] + [wo_ref]
+    copies = [pltpu.make_async_copy(hbm[i], targets[i], sems.at[i]) for i in range(4)]
     for copy in copies:
         copy.start()
-    wq_ref, wk_ref, wv_ref, wo_ref = vmem
     nc, nx, count, deep = grad_refs[0].shape
     blocks = 2 * nx * nc
     strips, passages = query_ref.shape[:2]
@@ -88,19 +90,17 @@
     for copy in copies:
         copy.wait()
 
-    def projected(weight_ref):
-        total = dot(tokens[0], weight_ref[:deep])
-        for b in range(1, blocks):
-            total += dot(tokens[b], weight_ref[b * deep : (b + 1) * deep])
-        return total.astype(BF16)
-
     def own(states):
         kept = states[:, :HEAD_DIM]
         for head in range(1, heads):
             kept = jnp.where(mine == head, states[:, head * HEAD_DIM : (head + 1) * HEAD_DIM], kept)
         return kept
 
-    q, k, v = own(projected(wq_ref)), own(projected(wk_ref)), own(projected(wv_ref))
+    states = dot(tokens[0], states_ref[:deep])
+    for b in range(1, blocks):
+        states += dot(tokens[b], states_ref[b * deep : (b + 1) * deep])
+    states = states.astype(BF16)
+    q, k, v = (own(states[:, i * inner : (i + 1) * inner]) for i in range(3))
     total = dot(weighted[0], wo_ref[:, :deep], COLS)
     for b in range(1, blocks):
         total += dot(weighted[b], wo_ref[:, b * deep : (b + 1) * deep], COLS)
@@ -118,13 +118,14 @@
     key_grad = dot(score_grad, q, ROWS).astype(BF16)
     value_grad = dot(attn, c, ROWS).astype(BF16)
     context = dot(attn, v).astype(BF16)
-    query_key = jnp.concatenate([query_grad, key_grad], axis=1)
+    blank = jnp.zeros_like(context)
+    token_side = jnp.concatenate([query_grad, key_grad, value_grad, blank], axis=1)
+    weighted_side = jnp.concatenate([blank, context], axis=1)
     span = deep // rows
     for b in range(blocks):
-        upper = dot(tokens[b], query_key, ROWS).astype(BF16)
-        lower = jnp.concatenate(
-            [dot(tokens[b], value_grad, ROWS), dot(weighted[b], context, ROWS)], axis=1
-        ).astype(BF16)
+        term = dot(tokens[b], token_side, ROWS)
+        upper = term[:, : 2 * HEAD_DIM].astype(BF16)
+        lower = (term[:, 2 * HEAD_DIM :] + dot(weighted[b], weighted_side, ROWS)).astype(BF16)
         out_ref[b * span : (b + 1) * span, :rows, :] = upper.reshape(span, rows, -1)
         out_ref[b * span : (b + 1) * span, rows:, :] = lower.reshape(span, rows, -1)
 
@@ -143,11 +144,128 @@
         + [vmem] * 6
         + [pl.BlockSpec(memory_space=pl.ANY)] * 4,
         out_specs=(vmem, vmem),
-        scratch_shapes=[pltpu.VMEM((width, inner), BF16)] * 3
-        + [pltpu.VMEM((inner, width), BF16), pltpu.SemaphoreType.DMA((4,))],
+        scratch_shapes=[
+            pltpu.VMEM((width, 3 * inner), BF16),
+            pltpu.VMEM((inner, width), BF16),
+            pltpu.SemaphoreType.DMA((4,)),
+        ],
         compiler_params=pltpu.CompilerParams(vmem_limit_bytes=40 * 1024 * 1024),
         name="reader",
     )(half, high, query, *tokens, *out_grad, *weights)
+
+
+def exact(a, b):
+    return dot(a.astype(BF16), b.astype(BF16))
+
+
+def pack_kernel(
+    at_ref, vocab_ref, index_ref, slab_ref, slab_ids_ref, ids_ref, owner_ref, row_ref, out_ref
+):
+    core, strip = at_ref[0], at_ref[1]
+    peers, stride, deep = out_ref.shape
+    vocab_rows = vocab_ref.shape[0]
+    pass_rows = index_ref.shape[0]
+    folded = pass_rows // 2
+    asked = vocab_rows + folded
+    held = asked + 16
+    columns = pl.ds(pl.multiple_of(strip * LANES, LANES), LANES)
+    index = index_ref[:, columns]
+    slab, plen, npass = slab_ref.shape[0], ids_ref.shape[0], ids_ref.shape[1]
+
+    def places(owner, core):
+        z, y = owner // peers, lax.rem(owner, peers)
+        return jnp.where(core == 0, z, y), jnp.where(core == 0, y, z)
+
+    def coded(owner, row):
+        first, second = places(owner, 1 - core)
+        code = second * REACH + first * stride + row
+        return (code // LANES).astype(F32), lax.rem(code, LANES).astype(F32)
+
+    ids = ids_ref[...]
+    high, low = coded(ids // vocab_rows, lax.rem(ids, vocab_rows))
+    lane = lax.broadcasted_iota(jnp.int32, (npass, deep), 1)
+    passage = lax.broadcasted_iota(jnp.int32, (npass, deep), 0)
+    high_row, low_row = jnp.zeros((1, deep), F32), jnp.zeros((1, deep), F32)
+    for i in range(plen):
+        to = (lane == passage * plen + i).astype(F32)
+        high_row += exact(high[i : i + 1], to)
+        low_row += exact(low[i : i + 1], to)
+    high, low = coded(owner_ref[...], vocab_rows + lax.rem(row_ref[...], folded))
+    to = (lane == passage + plen * npass).astype(F32)
+    high_row += exact(high, to)
+    low_row += exact(low, to)
+    lane = lax.broadcasted_iota(jnp.int32, (1, deep), 1)
+    none = peers * REACH - 1
+    high_row = jnp.where(lane < (plen + 1) * npass, high_row, float(none // LANES))
+    low_row = jnp.where(lane < (plen + 1) * npass, low_row, float(none % LANES))
+    line = lax.broadcasted_iota(jnp.int32, (16, deep), 0)
+    wanted = jnp.where(line == 0, high_row, jnp.where(line == 1, low_row, 0.0)).astype(BF16)
+
+    slab_ids = slab_ids_ref[...]
+    owner, row = slab_ids // pass_rows, lax.rem(slab_ids, pass_rows)
+    i = lax.broadcasted_iota(jnp.int32, (slab, slab), 0)
+    j = lax.broadcasted_iota(jnp.int32, (slab, slab), 1)
+    owner_column = jnp.sum(jnp.where(i == j, owner.astype(F32), 0.0), axis=1, keepdims=True)
+    place_column = jnp.sum(jnp.where(i == j, (row + 1).astype(F32), 0.0), axis=1, keepdims=True)
+    before = jnp.where((owner_column == owner.astype(F32)) & (i < j), 1.0, 0.0)
+    first, second = places(owner, core)
+    slot = ((first * peers + second) * CAPS).astype(F32) + jnp.sum(before, axis=0, keepdims=True)
+    slots = lax.broadcasted_iota(jnp.int32, (peers * peers * CAPS, slab), 0).astype(F32)
+    select = jnp.where(slots == slot, 1.0, 0.0).astype(BF16)
+    place = jnp.broadcast_to(place_column, (slab, deep - LANES)).astype(BF16)
+    slab_out = dot(select, jnp.concatenate([slab_ref[:, columns], place], axis=1)).astype(BF16)
+
+    index = jnp.concatenate([index[:folded], index[folded:]], axis=1)
+    for peer in range(peers):
+        out_ref[peer, :vocab_rows, :] = vocab_ref[...]
+        out_ref[peer, vocab_rows:asked, :] = index
+        out_ref[peer, asked:held, :] = wanted
+        out_ref[peer, held:, :] = slab_out[peer * peers * CAPS : (peer + 1) * peers * CAPS]
+
+
+def pack(core, strip, vocab, index, slab, slab_ids, ids, owner, row, peers):
+    vmem = pl.BlockSpec(memory_space=pltpu.VMEM)
+    rows = vocab.shape[0] + index.shape[0] // 2 + 16 + peers * CAPS
+    return pl.pallas_call(
+        pack_kernel,
+        out_shape=jax.ShapeDtypeStruct((peers, rows, vocab.shape[1]), BF16),
+        in_specs=[pl.BlockSpec(memory_space=pltpu.SMEM)] + [vmem] * 7,
+        out_specs=vmem,
+        compiler_params=pltpu.CompilerParams(vmem_limit_bytes=32 * 1024 * 1024),
+        name="pack",
+    )(jnp.stack([core, strip]), vocab, index, slab, slab_ids, ids, owner, row)
+
+
+def total_kernel(terms_ref, *out_refs):
+    rows = terms_ref.shape[1] // 2
+    sums = []
+    for half in range(2):
+        acc = terms_ref[half].astype(F32)
+        for i in range(2 + half, terms_ref.shape[0], 2):
+            acc += terms_ref[i].astype(F32)
+        sums.append(acc)
+    for i, out_ref in enumerate(out_refs):
+        top, left = divmod(i, 2)
+        out_ref[...] = jnp.concatenate(
+            [
+                acc[top * rows : (top + 1) * rows, left * HEAD_DIM : (left + 1) * HEAD_DIM]
+                for acc in sums
+            ],
+            axis=1,
+        )
+
+
+def total(terms):
+    rows, width = terms.shape[1] // 2, terms.shape[2]
+    vmem = pl.BlockSpec(memory_space=pltpu.VMEM)
+    return pl.pallas_call(
+        total_kernel,
+        out_shape=(jax.ShapeDtypeStruct((rows, width), F32),) * 4,
+        in_specs=[vmem],
+        out_specs=(vmem,) * 4,
+        compiler_params=pltpu.CompilerParams(vmem_limit_bytes=32 * 1024 * 1024),
+        name="total",
+    )(terms)
 
 
 def shards(
@@ -177,7 +295,6 @@
     npass, plen = token_ids.shape
     count = npass * plen
     vocab_rows = vocab_table.shape[0]
-    slab = slab_ids.shape[0]
     strips = width // LANES
     strip = lax.rem(lax.axis_index(M), strips)
 
@@ -192,48 +309,28 @@
     second_groups = at_y + [[i + 1 for i in group] for group in at_z]
     second = jnp.where(my_core == 0, my_y, my_z)
 
-    def places(owner, core):
-        z, y = owner // ny, owner % ny
-        return jnp.where(core == 0, z, y), jnp.where(core == 0, y, z)
-
     deep = vocab_table.shape[1]
     index_strip = my_strip(index_emb)
     folded = pass_rows // 2
-    message = jnp.concatenate(
-        [vocab_table, jnp.concatenate([index_strip[:folded], index_strip[folded:]], axis=1)], axis=0
-    )
-    asked = message.shape[0]
-    held = asked + 8
+    asked = vocab_rows + folded
+    held = asked + 16
     stride = held + ny * CAPS
     spare = -npass % 16
-    flat_ids = token_ids.reshape(-1)
-    row = jnp.concatenate([flat_ids % vocab_rows, vocab_rows + passage_row % folded])
-    row_first, row_second = places(
-        jnp.concatenate([flat_ids // vocab_rows, passage_owner[:, 0]]), 1 - my_core
-    )
-    code = row_second * REACH + row_first * stride + row
     rows_here = count + npass + spare
-    code = jnp.pad(code, (0, deep - code.shape[0]), constant_values=ny * REACH - 1)
-    code = jnp.pad(jnp.stack([code // LANES, code % LANES]).astype(BF16), ((0, 6), (0, 0)))
-    message = jnp.concatenate([message, code], axis=0)
-    slab_owner, slab_row = slab_ids // pass_rows, slab_ids % pass_rows
-    earlier = (slab_owner[:, None] == slab_owner[None, :]) & (
-        jnp.arange(slab)[:, None] > jnp.arange(slab)[None, :]
-    )
-    rank = jnp.sum(earlier.astype(jnp.int32), axis=1)
-    slab_first, slab_second = places(slab_owner, my_core)
-    slot = (slab_first * ny + slab_second) * CAPS + rank
-    select = (jnp.arange(owners * CAPS)[:, None] == slot[None, :]).astype(BF16)
-    slab_wide = jnp.concatenate(
-        [
-            my_strip(slab_emb),
-            jnp.broadcast_to((slab_row + 1).astype(BF16)[:, None], (slab, deep - LANES)),
-        ],
-        axis=1,
-    )
-    slab_out = dot(select, slab_wide).astype(BF16).reshape(nz, ny * CAPS, deep)
+    message = pack(
+        my_core,
+        strip,
+        vocab_table,
+        index_emb,
+        slab_emb,
+        slab_ids[None],
+        token_ids.T,
+        passage_owner.T,
+        passage_row[None],
+        nz,
+    )
     got_first = lax.all_to_all(
-        jnp.concatenate([jnp.broadcast_to(message[None], (nz, *message.shape)), slab_out], axis=1),
+        message,
         ALONG,
         0,
         0,
@@ -309,26 +406,8 @@
     refreshed = lax.all_gather(refreshed, M, axis=0)
     refreshed = jnp.concatenate([refreshed[i] for i in range(strips)], axis=1)
     terms = lax.all_to_all(terms, IDX, 0, 0, tiled=True)
-    rows = terms.shape[1] // 2
-    sums = jnp.sum(terms.reshape(owners // nq, nq, *terms.shape[1:]).astype(F32), axis=0)
-
-    def whole(top, left):
-        return jnp.concatenate(
-            [
-                sums[h, top * rows : (top + 1) * rows, left * HEAD_DIM : (left + 1) * HEAD_DIM]
-                for h in range(nq)
-            ],
-            axis=1,
-        )
-
-    return (
-        relevance,
-        whole(0, 0),
-        whole(0, 1),
-        whole(1, 0),
-        whole(1, 1).T,
-        refreshed,
-    )
+    grad_query, grad_key, grad_value, grad_out = total(terms)
+    return (relevance, grad_query, grad_key, grad_value, grad_out.T, refreshed)
 
 
 def solution(mesh):

time: 140 us -> 139 us (level)
  other arithmetic: 8.13 us -> 0.74 us
  local copies, waits for them, and re-layouts: 4.27 us -> 7.74 us
  Pallas kernels: 5.85 us -> 8.58 us
    unnamed x23 -> x36, local copies, waits for them, and re-layouts: 0.87 us -> 5.47 us
    concatenate x5 -> x0, other arithmetic: 4.16 us -> none  [the longest x3 2.04 us: whole(): jnp.concatenate([sums[h, top * rows:(top + 1) * rows, left * HEAD_DIM:(le...]
    pallas_call x0 -> x2, Pallas kernels: none -> 2.74 us  [the longest x1 1.9 us: pack(): pl.pallas_call(pack_kernel, out_shape=jax.ShapeDtypeStruct((peers, rows,...]
    dot_general x3 -> x2, matrix products: 5.72 us -> 5.55 us  [dot(): return jnp.dot(a, b, preferred_element_type=F32)]
where the time goes in v10:
time: 139 us; the launch traced here: 137 us
  waiting for transfers between devices  43.9 us (32%)
  blocking collectives  36 us (26%)
  starting transfers between devices  33.8 us (24%)
  Pallas kernels  8.58 us (6%)
  local copies, waits for them, and re-layouts  7.74 us (6%)
  matrix products  5.55 us (4%)
    all_to_all x1, waiting for transfers between devices, shards(): terms = lax.all_to_all(terms, IDX, 0, 0, tiled=True)  16.3 us
    all_gather x1, blocking collectives, shards(): lax.all_gather(jnp.concatenate([out_grad, other[:count]], axis=0), 'x', a...  13.7 us
    all_gather x1, blocking collectives, shards(): refreshed = lax.all_gather(refreshed, M, axis=0)  12.8 us
    all_to_all x1, waiting for transfers between devices, shards(): lax.all_to_all(message, ALONG, 0, 0, axis_index_groups=first_groups, tile...  11.1 us
    all_to_all x1, starting transfers between devices, shards(): lax.all_to_all(message, ALONG, 0, 0, axis_index_groups=first_groups, tile...  10.4 us
    ppermute x1, waiting for transfers between devices, shards(): other = lax.ppermute(jnp.concatenate([out_grad, extra], axis=0), 'q', swap)  8.24 us
    all_to_all x1, starting transfers between devices, shards(): lax.all_to_all(served.reshape(*at.shape, deep), ALONG, 0, 0, axis_index_g...  7.1 us
    all_to_all x1, starting transfers between devices, shards(): terms = lax.all_to_all(terms, IDX, 0, 0, tiled=True)  6.03 us
  transfers between devices with their start and end apart: 6, of which 6 were waited for; matrix products, arithmetic and copies ran while one was open for 2% of the time, Pallas kernels for 0%

profile of v10, /device:TPU:6, one launch (start us, length us, event | category | flops | bytes accessed | tf_op | source)
XLA Modules:
  0.0 137.3 jit_solution(15417890935964745015)
XLA Ops:
  0.6 0.1 pad_add_fusion.1.at_ref
  0.7 0.0 copy-start.4
  0.7 0.9 copy-done.4
  1.6 0.0 copy-start.5
  1.7 0.9 copy-done.5
  2.6 0.0 copy-start.6
  2.6 0.9 copy-done.6
  3.4 0.0 copy-start.7
  3.4 0.7 copy-done.7
  4.1 0.0 copy-start.8
  4.1 0.7 copy-done.8
  4.8 0.0 copy-start.9
  4.8 0.7 copy-done.9
  5.4 0.0 copy-start.10
  5.4 0.7 copy-done.10
  6.1 1.9 %pack.1 = bf16[8,352,256]{2,1,0:T(8,128)(2,1)} custom-call(s32[2]{0:T(128)S(1)} %pad_add_fusion.1.at_ref, bf16[256,256]{1,0:T(8,128)(2,1)S(1)} %copy-done.5, bf16[128,768]{1,0:T(8,128)(2,1)S(1)} %copy-done.4, bf16[64,768]{1,0:T(8,128)(2,1)S(1)} %copy-done.6, s32[1,64]{1,0:T(1,128)S(1)} %bitcast.38, s32[4,40]{1,0:T(4,128)S(1)} %bitcast.37, ...), custom_call_target="tpu_custom_call" | custom-call | tf_op jit(solution)/shard_map/pack/pallas_call | solution.py:229
  8.0 10.4 %all-to-all-start = ((bf16[8,352,256]{2,1,0:T(8,128)(2,1)}), bf16[8,352,256]{2,1,0:T(8,128)(2,1)S(1)}, u32[]{:S(2)}, u32[]{:S(2)}) async-start(bf16[8,352,256]{2,1,0:T(8,128)(2,1)} %pack.1), calls=%async_computation | async-start | bytes 2883584 | tf_op jit(solution)/shard_map/all_to_all | solution.py:332
  18.5 0.0 copy-done.14
  18.5 0.0 copy-done.11
  18.5 0.0 copy-done.12
  18.5 3.5 %collective-permute-start = (bf16[168,256]{1,0:T(8,128)(2,1)S(1)}, bf16[168,256]{1,0:T(8,128)(2,1)S(1)}, u32[]{:S(2)}, u32[]{:S(2)}) collective-permute-start(bf16[168,256]{1,0:T(8,128)(2,1)S(1)} %fusion.8), channel_id=1, source_target_pairs={{0,8},{8,0},{1,9},{9,1},{2,10},{10,2},{3,11},{11,3},{4,12},{12,4},... | collective-permute-start | bytes 258056 | tf_op jit(solution)/shard_map/ppermute | solution.py:349
  22.0 0.1 broadcast_add_fusion.1
  22.1 0.1 copy.41
  22.2 0.1 add.87
  22.3 8.2 %collective-permute-done = bf16[168,256]{1,0:T(8,128)(2,1)S(1)} collective-permute-done((bf16[168,256]{1,0:T(8,128)(2,1)S(1)}, bf16[168,256]{1,0:T(8,128)(2,1)S(1)}, u32[]{:S(2)}, u32[]{:S(2)}) %collective-permute-start) | collective-permute-done | bytes 86048 | tf_op jit(solution)/shard_map/ppermute | solution.py:349
  30.5 11.1 %all-to-all-done = bf16[8,352,256]{2,1,0:T(8,128)(2,1)S(1)} async-done(((bf16[8,352,256]{2,1,0:T(8,128)(2,1)}), bf16[8,352,256]{2,1,0:T(8,128)(2,1)S(1)}, u32[]{:S(2)}, u32[]{:S(2)}) %all-to-all-start) | async-done | bytes 1441824 | tf_op jit(solution)/shard_map/all_to_all | solution.py:332
  41.6 1.9 %collective-permute-start.1 = (bf16[8,2,256]{2,1,0:T(2,128)(2,1)S(1)}, bf16[8,2,256]{2,1,0:T(2,128)(2,1)S(1)}, u32[]{:S(2)}, u32[]{:S(2)}) collective-permute-start(bf16[8,2,256]{2,1,0:T(2,128)(2,1)S(1)} %slice.68), channel_id=1, source_target_pairs={{0,1},{1,0},{2,3},{3,2},{4,5},{5,4},{6,7},{7,6},{8,9},{9,8},{10,11... | collective-permute-start | bytes 24584 | tf_op jit(solution)/shard_map/ppermute | solution.py:362
  43.6 1.1 collective-permute-done.1
  44.7 0.1 pad_add_fusion
  44.8 0.1 eq.32
  44.9 4.7 %fusion.2 = bf16[1792,256]{1,0:T(8,128)(2,1)} fusion(bf16[2816,256]{1,0:T(8,128)(2,1)S(1)} %bitcast.42, s32[1792]{0:T(1024)S(1)} %eq.32), kind=kOutput, calls=%fused_computation.3 | convolution fusion | flops 2589196288 | bytes 2366464 | tf_op jit(solution)/shard_map/dot_general | solution.py:28
  49.6 7.1 %all-to-all-start.1 = ((bf16[8,224,256]{2,1,0:T(8,128)(2,1)}), bf16[8,224,256]{2,1,0:T(8,128)(2,1)S(1)}, u32[]{:S(2)}, u32[]{:S(2)}) async-start(bf16[8,224,256]{2,1,0:T(8,128)(2,1)} %bitcast.15), calls=%async_computation.1 | async-start | bytes 1835008 | tf_op jit(solution)/shard_map/all_to_all | solution.py:374
  56.8 13.7 %all-gather = bf16[1280,256]{1,0:T(8,128)(2,1)S(1)} all-gather(bf16[320,256]{1,0:T(8,128)(2,1)S(1)} %pad_maximum_fusion), channel_id=2, replica_groups=mesh['z'=8,'p'=4,'q'=2,'x'=4,'c'=2] {'x'}, dimensions={0}, use_global_device_ids=true | all-gather | bytes 819200 | tf_op jit(solution)/shard_map/all_gather | solution.py:351
  70.5 3.7 %all-to-all-done.1 = bf16[8,224,256]{2,1,0:T(8,128)(2,1)S(1)} async-done(((bf16[8,224,256]{2,1,0:T(8,128)(2,1)}), bf16[8,224,256]{2,1,0:T(8,128)(2,1)S(1)}, u32[]{:S(2)}, u32[]{:S(2)}) %all-to-all-start.1) | async-done | bytes 917536 | tf_op jit(solution)/shard_map/all_to_all | solution.py:374
  74.2 0.1 slice_reduce_fusion
  74.3 1.0 broadcast_in_dim.42
  75.3 4.8 %all-to-all-start.2 = ((bf16[8,208,256]{2,1,0:T(8,128)(2,1)}), bf16[8,208,256]{2,1,0:T(8,128)(2,1)S(1)}, u32[]{:S(2)}, u32[]{:S(2)}) async-start(bf16[8,208,256]{2,1,0:T(8,128)(2,1)} %broadcast_in_dim.42), calls=%async_computation.2 | async-start | bytes 1703936 | tf_op jit(solution)/shard_map/all_to_all | solution.py:389
  80.1 0.1 compare_convert_fusion
  80.2 0.1 copy.42.high_ref
  80.4 0.1 add_reduce_fusion
  80.5 0.1 fusion.9
  80.7 2.3 %all-gather.2 = bf16[4,320,256]{2,1,0:T(8,128)(2,1)S(1)} all-gather(bf16[2,320,256]{2,1,0:T(8,128)(2,1)S(1)} %get-tuple-element.38), channel_id=4, replica_groups=mesh['z'=8,'p'=4,'q'=2,'x'=4,'c'=2] {'c'}, dimensions={0}, use_global_device_ids=true | all-gather | bytes 983040 | tf_op jit(solution)/shard_map/all_gather | solution.py:387
  83.0 2.3 %all-gather.1 = bf16[4,320,256]{2,1,0:T(8,128)(2,1)S(1)} all-gather(bf16[2,320,256]{2,1,0:T(8,128)(2,1)S(1)} %get-tuple-element.39), channel_id=3, replica_groups=mesh['z'=8,'p'=4,'q'=2,'x'=4,'c'=2] {'c'}, dimensions={0}, use_global_device_ids=true | all-gather | bytes 983040 | tf_op jit(solution)/shard_map/all_gather | solution.py:387
  85.2 0.9 fusion.3
  86.1 3.4 %all-to-all-done.2 = bf16[8,208,256]{2,1,0:T(8,128)(2,1)S(1)} async-done(((bf16[8,208,256]{2,1,0:T(8,128)(2,1)}), bf16[8,208,256]{2,1,0:T(8,128)(2,1)S(1)}, u32[]{:S(2)}, u32[]{:S(2)}) %all-to-all-start.2) | async-done | bytes 852000 | tf_op jit(solution)/shard_map/all_to_all | solution.py:389
  89.6 0.1 fusion.15
  89.6 0.0 copy-start
  89.6 0.0 copy-start.1
  89.7 0.0 copy-start.2
  89.7 0.0 copy-start.3
  89.7 2.5 %all-gather.4 = bf16[8,208,256]{2,1,0:T(8,128)(2,1)S(1)} all-gather(bf16[4,208,256]{2,1,0:T(8,128)(2,1)S(1)} %get-tuple-element.36), channel_id=6, replica_groups=mesh['z'=8,'p'=4,'q'=2,'x'=4,'c'=2] {'c'}, dimensions={0}, use_global_device_ids=true | all-gather | bytes 1277952 | tf_op jit(solution)/shard_map/all_gather | solution.py:393
  92.2 2.4 %all-gather.3 = bf16[8,208,256]{2,1,0:T(8,128)(2,1)S(1)} all-gather(bf16[4,208,256]{2,1,0:T(8,128)(2,1)S(1)} %get-tuple-element.37), channel_id=5, replica_groups=mesh['z'=8,'p'=4,'q'=2,'x'=4,'c'=2] {'c'}, dimensions={0}, use_global_device_ids=true | all-gather | bytes 1277952 | tf_op jit(solution)/shard_map/all_gather | solution.py:393
  94.6 0.0 copy-done
  94.6 0.0 copy-done.1
  94.6 0.0 copy-done.2
  94.6 0.0 copy-done.3
  94.7 5.8 %reader.1 = (bf16[64,64,128]{2,1,0:T(8,128)(2,1)}, f32[1,96]{1,0:T(1,128)S(1)}) custom-call(s32[1]{0:T(128)} %bitcast.half_ref, s32[96,1]{1,0:T(8,128)S(1)} %copy.42.high_ref, bf16[6,96,256]{2,1,0:T(8,128)(2,1)S(1)} %fusion.6.query_ref, bf16[2,4,208,256]{3,2,1,0:T(8,128)(2,1)S(1)} %bitcast.34, bf16[2,4,208,256]{3,2,1,0:T(8,128)(2,1)S(1)} %bitcast.33, ...), custom_call_target="tpu_custom_call" | custom-call | tf_op jit(solution)/shard_map/reader/pallas_call | solution.py:137
  100.5 6.0 %all-to-all-start.3 = ((bf16[64,64,128]{2,1,0:T(8,128)(2,1)}), bf16[64,64,128]{2,1,0:T(8,128)(2,1)S(1)}, u32[]{:S(2)}, u32[]{:S(2)}) async-start(bf16[64,64,128]{2,1,0:T(8,128)(2,1)} %get-tuple-element.30), calls=%async_computation.3 | async-start | bytes 2097152 | tf_op jit(solution)/shard_map/all_to_all | solution.py:408
  106.6 0.6 reshape_squeeze.3
  107.2 12.8 %all-gather.5 = bf16[1024,128]{1,0:T(8,128)(2,1)S(1)} all-gather(bf16[128,128]{1,0:T(8,128)(2,1)S(1)} %fusion.3), channel_id=7, replica_groups=mesh['z'=8,'p'=4,'q'=2,'x'=4,'c'=2] {'x','c'}, dimensions={0}, use_global_device_ids=true | all-gather | bytes 294912 | tf_op jit(solution)/shard_map/all_gather | solution.py:406
  120.1 0.0 copy-start.13
  120.1 16.3 %all-to-all-done.3.terms_ref = bf16[64,64,128]{2,1,0:T(8,128)(2,1)S(1)} async-done(((bf16[64,64,128]{2,1,0:T(8,128)(2,1)}), bf16[64,64,128]{2,1,0:T(8,128)(2,1)S(1)}, u32[]{:S(2)}, u32[]{:S(2)}) %all-to-all-start.3) | async-done | bytes 1048608 | tf_op jit(solution)/shard_map/all_to_all | solution.py:408
  136.4 0.8 total.1
  137.3 0.0 copy-done.13
  (39 shorter events, 0.4 us)
Async XLA Ops:
  0.7 0.9 copy-start.4
  1.6 0.9 copy-start.5
  2.6 0.9 copy-start.6
  3.4 0.7 copy-start.7
  4.1 0.7 copy-start.8
  4.8 0.7 copy-start.9
  5.4 0.7 copy-start.10
  8.0 10.5 %copy-start.14 = (bf16[2,768]{1,0:T(2,128)(2,1)S(1)}, bf16[2,768]{1,0:T(2,128)(2,1)}, u32[]{:S(2)}) copy-start(bf16[2,768]{1,0:T(2,128)(2,1)} %param.14) | copy-start | bytes 9220
  8.0 10.5 %copy-start.11 = (s32[40]{0:T(128)S(1)}, s32[40]{0:T(128)}, u32[]{:S(2)}) copy-start(s32[40]{0:T(128)} %param.16) | copy-start | bytes 484
  8.0 10.5 %copy-start.12 = (bf16[160,256]{1,0:T(8,128)(2,1)S(1)}, bf16[160,256]{1,0:T(8,128)(2,1)}, u32[]{:S(2)}) copy-start(bf16[160,256]{1,0:T(8,128)(2,1)} %param.23) | copy-start | bytes 245764
  8.0 33.6 %all-to-all-start = ((bf16[8,352,256]{2,1,0:T(8,128)(2,1)}), bf16[8,352,256]{2,1,0:T(8,128)(2,1)S(1)}, u32[]{:S(2)}, u32[]{:S(2)}) async-start(bf16[8,352,256]{2,1,0:T(8,128)(2,1)} %pack.1), calls=%async_computation | async-start | bytes 2883584 | tf_op jit(solution)/shard_map/all_to_all | solution.py:332
  18.5 12.0 %collective-permute-start = (bf16[168,256]{1,0:T(8,128)(2,1)S(1)}, bf16[168,256]{1,0:T(8,128)(2,1)S(1)}, u32[]{:S(2)}, u32[]{:S(2)}) collective-permute-start(bf16[168,256]{1,0:T(8,128)(2,1)S(1)} %fusion.8), channel_id=1, source_target_pairs={{0,8},{8,0},{1,9},{9,1},{2,10},{10,2},{3,11},{11,3},{4,12},{12,4},... | collective-permute-start | bytes 258056 | tf_op jit(solution)/shard_map/ppermute | solution.py:349
  41.6 3.1 %collective-permute-start.1 = (bf16[8,2,256]{2,1,0:T(2,128)(2,1)S(1)}, bf16[8,2,256]{2,1,0:T(2,128)(2,1)S(1)}, u32[]{:S(2)}, u32[]{:S(2)}) collective-permute-start(bf16[8,2,256]{2,1,0:T(2,128)(2,1)S(1)} %slice.68), channel_id=1, source_target_pairs={{0,1},{1,0},{2,3},{3,2},{4,5},{5,4},{6,7},{7,6},{8,9},{9,8},{10,11... | collective-permute-start | bytes 24584 | tf_op jit(solution)/shard_map/ppermute | solution.py:362
  49.6 24.6 %all-to-all-start.1 = ((bf16[8,224,256]{2,1,0:T(8,128)(2,1)}), bf16[8,224,256]{2,1,0:T(8,128)(2,1)S(1)}, u32[]{:S(2)}, u32[]{:S(2)}) async-start(bf16[8,224,256]{2,1,0:T(8,128)(2,1)} %bitcast.15), calls=%async_computation.1 | async-start | bytes 1835008 | tf_op jit(solution)/shard_map/all_to_all | solution.py:374
  75.3 14.3 %all-to-all-start.2 = ((bf16[8,208,256]{2,1,0:T(8,128)(2,1)}), bf16[8,208,256]{2,1,0:T(8,128)(2,1)S(1)}, u32[]{:S(2)}, u32[]{:S(2)}) async-start(bf16[8,208,256]{2,1,0:T(8,128)(2,1)} %broadcast_in_dim.42), calls=%async_computation.2 | async-start | bytes 1703936 | tf_op jit(solution)/shard_map/all_to_all | solution.py:389
  89.6 5.0 %copy-start = (bf16[2048,128]{1,0:T(8,128)(2,1)S(1)}, bf16[2048,128]{1,0:T(8,128)(2,1)}, u32[]{:S(2)}) copy-start(bf16[2048,128]{1,0:T(8,128)(2,1)} %refs_4_.1) | copy-start | bytes 1572868
  89.6 5.0 %copy-start.1 = (bf16[2048,128]{1,0:T(8,128)(2,1)S(1)}, bf16[2048,128]{1,0:T(8,128)(2,1)}, u32[]{:S(2)}) copy-start(bf16[2048,128]{1,0:T(8,128)(2,1)} %refs_5_.1) | copy-start | bytes 1572868
  89.7 5.0 %copy-start.2 = (bf16[2048,128]{1,0:T(8,128)(2,1)S(1)}, bf16[2048,128]{1,0:T(8,128)(2,1)}, u32[]{:S(2)}) copy-start(bf16[2048,128]{1,0:T(8,128)(2,1)} %refs_6_.1) | copy-start | bytes 1572868
  89.7 5.0 %copy-start.3 = (bf16[128,2048]{1,0:T(8,128)(2,1)S(1)}, bf16[128,2048]{1,0:T(8,128)(2,1)}, u32[]{:S(2)}) copy-start(bf16[128,2048]{1,0:T(8,128)(2,1)} %refs_7_.1) | copy-start | bytes 1572868
  100.5 35.9 %all-to-all-start.3 = ((bf16[64,64,128]{2,1,0:T(8,128)(2,1)}), bf16[64,64,128]{2,1,0:T(8,128)(2,1)S(1)}, u32[]{:S(2)}, u32[]{:S(2)}) async-start(bf16[64,64,128]{2,1,0:T(8,128)(2,1)} %get-tuple-element.30), calls=%async_computation.3 | async-start | bytes 2097152 | tf_op jit(solution)/shard_map/all_to_all | solution.py:408
  120.1 17.1 %copy-start.13 = (bf16[128,768]{1,0:T(8,128)(2,1)}, bf16[128,768]{1,0:T(8,128)(2,1)S(1)}, u32[]{:S(2)}) copy-start(bf16[128,768]{1,0:T(8,128)(2,1)S(1)} %slice_dynamic-update-slice_fusion) | copy-start | bytes 589828

commit v11 on v10

--- a/solution.py
+++ b/solution.py
@@ -30,14 +30,8 @@
 
 
 def reader_kernel(heads, half_ref, high_ref, query_ref, *refs):
-    token_refs, grad_refs, hbm = refs[:2], refs[2:4], refs[4:8]
-    out_ref, rel_ref, vmem, sems = refs[8], refs[9], refs[10:12], refs[12]
-    states_ref, wo_ref = vmem
-    inner = wo_ref.shape[0]
-    targets = [states_ref.at[:, i * inner : (i + 1) * inner] for i in range(3)] + [wo_ref]
-    copies = [pltpu.make_async_copy(hbm[i], targets[i], sems.at[i]) for i in range(4)]
-    for copy in copies:
-        copy.start()
+    token_refs, grad_refs, weight_refs, wo_ref = refs[:2], refs[2:4], refs[4:7], refs[7]
+    out_ref, rel_ref = refs[8:]
     nc, nx, count, deep = grad_refs[0].shape
     blocks = 2 * nx * nc
     strips, passages = query_ref.shape[:2]
@@ -87,20 +81,19 @@
     weighted = [
         (grad_block(b).astype(F32) * rel).astype(BF16) for b in range(blocks)
     ]
-    for copy in copies:
-        copy.wait()
-
     def own(states):
         kept = states[:, :HEAD_DIM]
         for head in range(1, heads):
             kept = jnp.where(mine == head, states[:, head * HEAD_DIM : (head + 1) * HEAD_DIM], kept)
         return kept
 
-    states = dot(tokens[0], states_ref[:deep])
-    for b in range(1, blocks):
-        states += dot(tokens[b], states_ref[b * deep : (b + 1) * deep])
-    states = states.astype(BF16)
-    q, k, v = (own(states[:, i * inner : (i + 1) * inner]) for i in range(3))
+    def projected(weight_ref):
+        states = dot(tokens[0], weight_ref[:deep])
+        for b in range(1, blocks):
+            states += dot(tokens[b], weight_ref[b * deep : (b + 1) * deep])
+        return own(states.astype(BF16))
+
+    q, k, v = (projected(weight_ref) for weight_ref in weight_refs)
     total = dot(weighted[0], wo_ref[:, :deep], COLS)
     for b in range(1, blocks):
         total += dot(weighted[b], wo_ref[:, b * deep : (b + 1) * deep], COLS)
@@ -141,14 +134,8 @@
             jax.ShapeDtypeStruct((1, passages), F32),
         ),
         in_specs=[pl.BlockSpec(memory_space=pltpu.SMEM)]
-        + [vmem] * 6
-        + [pl.BlockSpec(memory_space=pl.ANY)] * 4,
+        + [vmem] * 10,
         out_specs=(vmem, vmem),
-        scratch_shapes=[
-            pltpu.VMEM((width, 3 * inner), BF16),
-            pltpu.VMEM((inner, width), BF16),
-            pltpu.SemaphoreType.DMA((4,)),
-        ],
         compiler_params=pltpu.CompilerParams(vmem_limit_bytes=40 * 1024 * 1024),
         name="reader",
     )(half, high, query, *tokens, *out_grad, *weights)
@@ -158,10 +145,15 @@
     return dot(a.astype(BF16), b.astype(BF16))
 
 
-def pack_kernel(
-    at_ref, vocab_ref, index_ref, slab_ref, slab_ids_ref, ids_ref, owner_ref, row_ref, out_ref
-):
+def pack_kernel(at_ref, *refs):
+    hbm, out_ref, vmem, sems = refs[:7], refs[7], refs[8:15], refs[15]
+    copies = [pltpu.make_async_copy(hbm[i], vmem[i], sems.at[i]) for i in range(7)]
+    for copy in copies:
+        copy.start()
+    vocab_ref, index_ref, slab_ref, slab_ids_ref, ids_ref, owner_ref, row_ref = vmem
     core, strip = at_ref[0], at_ref[1]
+    for copy in copies:
+        copy.wait()
     peers, stride, deep = out_ref.shape
     vocab_rows = vocab_ref.shape[0]
     pass_rows = index_ref.shape[0]
@@ -224,16 +216,19 @@
 
 
 def pack(core, strip, vocab, index, slab, slab_ids, ids, owner, row, peers):
-    vmem = pl.BlockSpec(memory_space=pltpu.VMEM)
+    operands = (vocab, index, slab, slab_ids, ids, owner, row)
     rows = vocab.shape[0] + index.shape[0] // 2 + 16 + peers * CAPS
     return pl.pallas_call(
         pack_kernel,
         out_shape=jax.ShapeDtypeStruct((peers, rows, vocab.shape[1]), BF16),
-        in_specs=[pl.BlockSpec(memory_space=pltpu.SMEM)] + [vmem] * 7,
-        out_specs=vmem,
-        compiler_params=pltpu.CompilerParams(vmem_limit_bytes=32 * 1024 * 1024),
+        in_specs=[pl.BlockSpec(memory_space=pltpu.SMEM)]
+        + [pl.BlockSpec(memory_space=pltpu.HBM)] * 7,
+        out_specs=pl.BlockSpec(memory_space=pltpu.VMEM),
+        scratch_shapes=[pltpu.VMEM(operand.shape, operand.dtype) for operand in operands]
+        + [pltpu.SemaphoreType.DMA((7,))],
+        compiler_params=pltpu.CompilerParams(vmem_limit_bytes=60 * 1024 * 1024),
         name="pack",
-    )(jnp.stack([core, strip]), vocab, index, slab, slab_ids, ids, owner, row)
+    )(jnp.stack([core, strip]), *operands)
 
 
 def total_kernel(terms_ref, *out_refs):

time: 139 us -> 134 us (0.964)
  local copies, waits for them, and re-layouts: 7.74 us -> 2.39 us
    unnamed x36 -> x22, local copies, waits for them, and re-layouts: 5.47 us -> 0.11 us
where the time goes in v11:
time: 134 us; the launch traced here: 132 us
  waiting for transfers between devices  43.9 us (33%)
  blocking collectives  36 us (27%)
  starting transfers between devices  33.8 us (25%)
  Pallas kernels  8.63 us (6%)
  matrix products  5.53 us (4%)
  local copies, waits for them, and re-layouts  2.39 us (2%)
    all_to_all x1, waiting for transfers between devices, shards(): terms = lax.all_to_all(terms, IDX, 0, 0, tiled=True)  16.3 us
    all_gather x1, blocking collectives, shards(): lax.all_gather(jnp.concatenate([out_grad, other[:count]], axis=0), 'x', a...  13.7 us
    all_gather x1, blocking collectives, shards(): refreshed = lax.all_gather(refreshed, M, axis=0)  12.8 us
    all_to_all x1, waiting for transfers between devices, shards(): lax.all_to_all(message, ALONG, 0, 0, axis_index_groups=first_groups, tile...  11.1 us
    all_to_all x1, starting transfers between devices, shards(): lax.all_to_all(message, ALONG, 0, 0, axis_index_groups=first_groups, tile...  10.5 us
    ppermute x1, waiting for transfers between devices, shards(): other = lax.ppermute(jnp.concatenate([out_grad, extra], axis=0), 'q', swap)  8.24 us
    all_to_all x1, starting transfers between devices, shards(): lax.all_to_all(served.reshape(*at.shape, deep), ALONG, 0, 0, axis_index_g...  7.1 us
    all_to_all x1, starting transfers between devices, shards(): terms = lax.all_to_all(terms, IDX, 0, 0, tiled=True)  6.02 us
  transfers between devices with their start and end apart: 6, of which 6 were waited for; matrix products, arithmetic and copies ran while one was open for 2% of the time, Pallas kernels for 0%

profile of v11, /device:TPU:6, one launch (start us, length us, event | category | flops | bytes accessed | tf_op | source)
XLA Modules:
  0.0 132.5 jit_solution(811653769454888360)
XLA Ops:
  0.6 0.6 pad_add_fusion.1.at_ref
  1.2 3.2 %pack.1 = bf16[8,352,256]{2,1,0:T(8,128)(2,1)} custom-call(s32[2]{0:T(128)} %pad_add_fusion.1.at_ref, bf16[256,256]{1,0:T(8,128)(2,1)} %refs_0_.1, bf16[128,768]{1,0:T(8,128)(2,1)} %refs_1_.1, bf16[64,768]{1,0:T(8,128)(2,1)} %refs_2_.1, s32[1,64]{1,0:T(1,128)} %bitcast.46, s32[4,40]{1,0:T(4,128)} %bitcast.45, s32[1,40]{1,0:T(1,128)} %bitcast.47, ...), custom_call_target="tpu_custom_call" | custom-call | tf_op jit(solution)/shard_map/pack/pallas_call | solution.py:221
  4.4 0.0 copy-start.6
  4.4 0.0 copy-start.7
  4.4 0.0 copy-start.4
  4.4 10.5 %all-to-all-start = ((bf16[8,352,256]{2,1,0:T(8,128)(2,1)}), bf16[8,352,256]{2,1,0:T(8,128)(2,1)S(1)}, u32[]{:S(2)}, u32[]{:S(2)}) async-start(bf16[8,352,256]{2,1,0:T(8,128)(2,1)} %pack.1), calls=%async_computation | async-start | bytes 2883584 | tf_op jit(solution)/shard_map/all_to_all | solution.py:327
  14.9 0.0 copy-done.6
  14.9 0.0 copy-done.7
  15.0 0.0 copy-done.4
  15.0 3.5 %collective-permute-start = (bf16[168,256]{1,0:T(8,128)(2,1)S(1)}, bf16[168,256]{1,0:T(8,128)(2,1)S(1)}, u32[]{:S(2)}, u32[]{:S(2)}) collective-permute-start(bf16[168,256]{1,0:T(8,128)(2,1)S(1)} %fusion.8), channel_id=1, source_target_pairs={{0,8},{8,0},{1,9},{9,1},{2,10},{10,2},{3,11},{11,3},{4,12},{12,4},... | collective-permute-start | bytes 258056 | tf_op jit(solution)/shard_map/ppermute | solution.py:344
  18.5 0.1 broadcast_add_fusion.1
  18.6 0.1 copy.41
  18.6 0.1 add.87
  18.7 8.2 %collective-permute-done = bf16[168,256]{1,0:T(8,128)(2,1)S(1)} collective-permute-done((bf16[168,256]{1,0:T(8,128)(2,1)S(1)}, bf16[168,256]{1,0:T(8,128)(2,1)S(1)}, u32[]{:S(2)}, u32[]{:S(2)}) %collective-permute-start) | collective-permute-done | bytes 86048 | tf_op jit(solution)/shard_map/ppermute | solution.py:344
  27.0 11.1 %all-to-all-done = bf16[8,352,256]{2,1,0:T(8,128)(2,1)S(1)} async-done(((bf16[8,352,256]{2,1,0:T(8,128)(2,1)}), bf16[8,352,256]{2,1,0:T(8,128)(2,1)S(1)}, u32[]{:S(2)}, u32[]{:S(2)}) %all-to-all-start) | async-done | bytes 1441824 | tf_op jit(solution)/shard_map/all_to_all | solution.py:327
  38.1 1.9 %collective-permute-start.1 = (bf16[8,2,256]{2,1,0:T(2,128)(2,1)S(1)}, bf16[8,2,256]{2,1,0:T(2,128)(2,1)S(1)}, u32[]{:S(2)}, u32[]{:S(2)}) collective-permute-start(bf16[8,2,256]{2,1,0:T(2,128)(2,1)S(1)} %slice.68), channel_id=1, source_target_pairs={{0,1},{1,0},{2,3},{3,2},{4,5},{5,4},{6,7},{7,6},{8,9},{9,8},{10,11... | collective-permute-start | bytes 24584 | tf_op jit(solution)/shard_map/ppermute | solution.py:357
  40.0 1.1 collective-permute-done.1
  41.2 0.1 pad_add_fusion
  41.3 0.1 eq.32
  41.3 4.6 %fusion.2 = bf16[1792,256]{1,0:T(8,128)(2,1)} fusion(bf16[2816,256]{1,0:T(8,128)(2,1)S(1)} %bitcast.38, s32[1792]{0:T(1024)S(1)} %eq.32), kind=kOutput, calls=%fused_computation.3 | convolution fusion | flops 2589196288 | bytes 2366464 | tf_op jit(solution)/shard_map/dot_general | solution.py:28
  46.0 7.1 %all-to-all-start.1 = ((bf16[8,224,256]{2,1,0:T(8,128)(2,1)}), bf16[8,224,256]{2,1,0:T(8,128)(2,1)S(1)}, u32[]{:S(2)}, u32[]{:S(2)}) async-start(bf16[8,224,256]{2,1,0:T(8,128)(2,1)} %bitcast.15), calls=%async_computation.1 | async-start | bytes 1835008 | tf_op jit(solution)/shard_map/all_to_all | solution.py:369
  53.2 13.7 %all-gather = bf16[1280,256]{1,0:T(8,128)(2,1)S(1)} all-gather(bf16[320,256]{1,0:T(8,128)(2,1)S(1)} %pad_maximum_fusion), channel_id=2, replica_groups=mesh['z'=8,'p'=4,'q'=2,'x'=4,'c'=2] {'x'}, dimensions={0}, use_global_device_ids=true | all-gather | bytes 819200 | tf_op jit(solution)/shard_map/all_gather | solution.py:346
  66.9 3.7 %all-to-all-done.1 = bf16[8,224,256]{2,1,0:T(8,128)(2,1)S(1)} async-done(((bf16[8,224,256]{2,1,0:T(8,128)(2,1)}), bf16[8,224,256]{2,1,0:T(8,128)(2,1)S(1)}, u32[]{:S(2)}, u32[]{:S(2)}) %all-to-all-start.1) | async-done | bytes 917536 | tf_op jit(solution)/shard_map/all_to_all | solution.py:369
  70.6 0.1 slice_reduce_fusion
  70.7 1.0 broadcast_in_dim.42
  71.7 4.8 %all-to-all-start.2 = ((bf16[8,208,256]{2,1,0:T(8,128)(2,1)}), bf16[8,208,256]{2,1,0:T(8,128)(2,1)S(1)}, u32[]{:S(2)}, u32[]{:S(2)}) async-start(bf16[8,208,256]{2,1,0:T(8,128)(2,1)} %broadcast_in_dim.42), calls=%async_computation.2 | async-start | bytes 1703936 | tf_op jit(solution)/shard_map/all_to_all | solution.py:384
  76.5 0.1 compare_convert_fusion
  76.6 0.1 copy.42.high_ref
  76.8 0.1 add_reduce_fusion
  76.9 0.1 fusion.9
  77.1 2.3 %all-gather.2 = bf16[4,320,256]{2,1,0:T(8,128)(2,1)S(1)} all-gather(bf16[2,320,256]{2,1,0:T(8,128)(2,1)S(1)} %get-tuple-element.38), channel_id=4, replica_groups=mesh['z'=8,'p'=4,'q'=2,'x'=4,'c'=2] {'c'}, dimensions={0}, use_global_device_ids=true | all-gather | bytes 983040 | tf_op jit(solution)/shard_map/all_gather | solution.py:382
  79.4 2.3 %all-gather.1 = bf16[4,320,256]{2,1,0:T(8,128)(2,1)S(1)} all-gather(bf16[2,320,256]{2,1,0:T(8,128)(2,1)S(1)} %get-tuple-element.39), channel_id=3, replica_groups=mesh['z'=8,'p'=4,'q'=2,'x'=4,'c'=2] {'c'}, dimensions={0}, use_global_device_ids=true | all-gather | bytes 983040 | tf_op jit(solution)/shard_map/all_gather | solution.py:382
  81.7 0.9 fusion.3
  82.6 3.4 %all-to-all-done.2 = bf16[8,208,256]{2,1,0:T(8,128)(2,1)S(1)} async-done(((bf16[8,208,256]{2,1,0:T(8,128)(2,1)}), bf16[8,208,256]{2,1,0:T(8,128)(2,1)S(1)}, u32[]{:S(2)}, u32[]{:S(2)}) %all-to-all-start.2) | async-done | bytes 852000 | tf_op jit(solution)/shard_map/all_to_all | solution.py:384
  86.0 0.1 fusion.15
  86.1 0.0 copy-start
  86.1 0.0 copy-start.1
  86.1 0.0 copy-start.2
  86.1 0.0 copy-start.3
  86.1 2.5 %all-gather.4 = bf16[8,208,256]{2,1,0:T(8,128)(2,1)S(1)} all-gather(bf16[4,208,256]{2,1,0:T(8,128)(2,1)S(1)} %get-tuple-element.36), channel_id=6, replica_groups=mesh['z'=8,'p'=4,'q'=2,'x'=4,'c'=2] {'c'}, dimensions={0}, use_global_device_ids=true | all-gather | bytes 1277952 | tf_op jit(solution)/shard_map/all_gather | solution.py:388
  88.7 2.4 %all-gather.3 = bf16[8,208,256]{2,1,0:T(8,128)(2,1)S(1)} all-gather(bf16[4,208,256]{2,1,0:T(8,128)(2,1)S(1)} %get-tuple-element.37), channel_id=5, replica_groups=mesh['z'=8,'p'=4,'q'=2,'x'=4,'c'=2] {'c'}, dimensions={0}, use_global_device_ids=true | all-gather | bytes 1277952 | tf_op jit(solution)/shard_map/all_gather | solution.py:388
  91.1 0.0 copy-done
  91.1 0.0 copy-done.1
  91.1 0.0 copy-done.2
  91.1 0.0 copy-done.3
  91.1 4.6 %reader.1 = (bf16[64,64,128]{2,1,0:T(8,128)(2,1)}, f32[1,96]{1,0:T(1,128)S(1)}) custom-call(s32[1]{0:T(128)} %bitcast.half_ref, s32[96,1]{1,0:T(8,128)S(1)} %copy.42.high_ref, bf16[6,96,256]{2,1,0:T(8,128)(2,1)S(1)} %fusion.6.query_ref, bf16[2,4,208,256]{3,2,1,0:T(8,128)(2,1)S(1)} %bitcast.34, bf16[2,4,208,256]{3,2,1,0:T(8,128)(2,1)S(1)} %bitcast.33, ...), custom_call_target="tpu_custom_call" | custom-call | tf_op jit(solution)/shard_map/reader/pallas_call | solution.py:130
  95.7 6.0 %all-to-all-start.3 = ((bf16[64,64,128]{2,1,0:T(8,128)(2,1)}), bf16[64,64,128]{2,1,0:T(8,128)(2,1)S(1)}, u32[]{:S(2)}, u32[]{:S(2)}) async-start(bf16[64,64,128]{2,1,0:T(8,128)(2,1)} %get-tuple-element.30), calls=%async_computation.3 | async-start | bytes 2097152 | tf_op jit(solution)/shard_map/all_to_all | solution.py:403
  101.8 0.6 reshape_squeeze.3
  102.4 12.8 %all-gather.5 = bf16[1024,128]{1,0:T(8,128)(2,1)S(1)} all-gather(bf16[128,128]{1,0:T(8,128)(2,1)S(1)} %fusion.3), channel_id=7, replica_groups=mesh['z'=8,'p'=4,'q'=2,'x'=4,'c'=2] {'x','c'}, dimensions={0}, use_global_device_ids=true | all-gather | bytes 294912 | tf_op jit(solution)/shard_map/all_gather | solution.py:401
  115.3 0.0 copy-start.5
  115.3 16.3 %all-to-all-done.3.terms_ref = bf16[64,64,128]{2,1,0:T(8,128)(2,1)S(1)} async-done(((bf16[64,64,128]{2,1,0:T(8,128)(2,1)}), bf16[64,64,128]{2,1,0:T(8,128)(2,1)S(1)}, u32[]{:S(2)}, u32[]{:S(2)}) %all-to-all-start.3) | async-done | bytes 1048608 | tf_op jit(solution)/shard_map/all_to_all | solution.py:403
  131.6 0.8 total.1
  132.5 0.0 copy-done.5
  (36 shorter events, 0.4 us)
Async XLA Ops:
  4.4 10.5 %copy-start.6 = (bf16[2,768]{1,0:T(2,128)(2,1)S(1)}, bf16[2,768]{1,0:T(2,128)(2,1)}, u32[]{:S(2)}) copy-start(bf16[2,768]{1,0:T(2,128)(2,1)} %param.14) | copy-start | bytes 9220
  4.4 10.5 %copy-start.7 = (s32[40]{0:T(128)S(1)}, s32[40]{0:T(128)}, u32[]{:S(2)}) copy-start(s32[40]{0:T(128)} %param.16) | copy-start | bytes 484
  4.4 10.5 %copy-start.4 = (bf16[160,256]{1,0:T(8,128)(2,1)S(1)}, bf16[160,256]{1,0:T(8,128)(2,1)}, u32[]{:S(2)}) copy-start(bf16[160,256]{1,0:T(8,128)(2,1)} %param.23) | copy-start | bytes 245764
  4.4 33.6 %all-to-all-start = ((bf16[8,352,256]{2,1,0:T(8,128)(2,1)}), bf16[8,352,256]{2,1,0:T(8,128)(2,1)S(1)}, u32[]{:S(2)}, u32[]{:S(2)}) async-start(bf16[8,352,256]{2,1,0:T(8,128)(2,1)} %pack.1), calls=%async_computation | async-start | bytes 2883584 | tf_op jit(solution)/shard_map/all_to_all | solution.py:327
  15.0 12.0 %collective-permute-start = (bf16[168,256]{1,0:T(8,128)(2,1)S(1)}, bf16[168,256]{1,0:T(8,128)(2,1)S(1)}, u32[]{:S(2)}, u32[]{:S(2)}) collective-permute-start(bf16[168,256]{1,0:T(8,128)(2,1)S(1)} %fusion.8), channel_id=1, source_target_pairs={{0,8},{8,0},{1,9},{9,1},{2,10},{10,2},{3,11},{11,3},{4,12},{12,4},... | collective-permute-start | bytes 258056 | tf_op jit(solution)/shard_map/ppermute | solution.py:344
  38.1 3.1 %collective-permute-start.1 = (bf16[8,2,256]{2,1,0:T(2,128)(2,1)S(1)}, bf16[8,2,256]{2,1,0:T(2,128)(2,1)S(1)}, u32[]{:S(2)}, u32[]{:S(2)}) collective-permute-start(bf16[8,2,256]{2,1,0:T(2,128)(2,1)S(1)} %slice.68), channel_id=1, source_target_pairs={{0,1},{1,0},{2,3},{3,2},{4,5},{5,4},{6,7},{7,6},{8,9},{9,8},{10,11... | collective-permute-start | bytes 24584 | tf_op jit(solution)/shard_map/ppermute | solution.py:357
  46.0 24.7 %all-to-all-start.1 = ((bf16[8,224,256]{2,1,0:T(8,128)(2,1)}), bf16[8,224,256]{2,1,0:T(8,128)(2,1)S(1)}, u32[]{:S(2)}, u32[]{:S(2)}) async-start(bf16[8,224,256]{2,1,0:T(8,128)(2,1)} %bitcast.15), calls=%async_computation.1 | async-start | bytes 1835008 | tf_op jit(solution)/shard_map/all_to_all | solution.py:369
  71.7 14.3 %all-to-all-start.2 = ((bf16[8,208,256]{2,1,0:T(8,128)(2,1)}), bf16[8,208,256]{2,1,0:T(8,128)(2,1)S(1)}, u32[]{:S(2)}, u32[]{:S(2)}) async-start(bf16[8,208,256]{2,1,0:T(8,128)(2,1)} %broadcast_in_dim.42), calls=%async_computation.2 | async-start | bytes 1703936 | tf_op jit(solution)/shard_map/all_to_all | solution.py:384
  86.1 5.0 %copy-start = (bf16[2048,128]{1,0:T(8,128)(2,1)S(1)}, bf16[2048,128]{1,0:T(8,128)(2,1)}, u32[]{:S(2)}) copy-start(bf16[2048,128]{1,0:T(8,128)(2,1)} %refs_4_.1) | copy-start | bytes 1572868
  86.1 5.0 %copy-start.1 = (bf16[2048,128]{1,0:T(8,128)(2,1)S(1)}, bf16[2048,128]{1,0:T(8,128)(2,1)}, u32[]{:S(2)}) copy-start(bf16[2048,128]{1,0:T(8,128)(2,1)} %refs_5_.1) | copy-start | bytes 1572868
  86.1 5.0 %copy-start.2 = (bf16[2048,128]{1,0:T(8,128)(2,1)S(1)}, bf16[2048,128]{1,0:T(8,128)(2,1)}, u32[]{:S(2)}) copy-start(bf16[2048,128]{1,0:T(8,128)(2,1)} %refs_6_.1) | copy-start | bytes 1572868
  86.1 5.0 %copy-start.3 = (bf16[128,2048]{1,0:T(8,128)(2,1)S(1)}, bf16[128,2048]{1,0:T(8,128)(2,1)}, u32[]{:S(2)}) copy-start(bf16[128,2048]{1,0:T(8,128)(2,1)} %refs_7_.1) | copy-start | bytes 1572868
  95.7 35.9 %all-to-all-start.3 = ((bf16[64,64,128]{2,1,0:T(8,128)(2,1)}), bf16[64,64,128]{2,1,0:T(8,128)(2,1)S(1)}, u32[]{:S(2)}, u32[]{:S(2)}) async-start(bf16[64,64,128]{2,1,0:T(8,128)(2,1)} %get-tuple-element.30), calls=%async_computation.3 | async-start | bytes 2097152 | tf_op jit(solution)/shard_map/all_to_all | solution.py:403
  115.3 17.1 %copy-start.5 = (bf16[128,768]{1,0:T(8,128)(2,1)}, bf16[128,768]{1,0:T(8,128)(2,1)S(1)}, u32[]{:S(2)}) copy-start(bf16[128,768]{1,0:T(8,128)(2,1)S(1)} %slice_dynamic-update-slice_fusion) | copy-start | bytes 589828

commit v12 on v11

--- a/solution.py
+++ b/solution.py
@@ -29,12 +29,11 @@
     return lax.dot_general(a, b, dims, preferred_element_type=F32)
 
 
-def reader_kernel(heads, half_ref, high_ref, query_ref, *refs):
+def reader_kernel(heads, strips, half_ref, *refs):
     token_refs, grad_refs, weight_refs, wo_ref = refs[:2], refs[2:4], refs[4:7], refs[7]
     out_ref, rel_ref = refs[8:]
     nc, nx, count, deep = grad_refs[0].shape
     blocks = 2 * nx * nc
-    strips, passages = query_ref.shape[:2]
     rows = out_ref.shape[1] // 2
     mine = half_ref[0]
 
@@ -48,34 +47,33 @@
         ordered = [jnp.where(mine == 0, both[0], both[1]), jnp.where(mine == 0, both[1], both[0])]
         return jnp.concatenate(ordered, axis=0)
 
-    acc = jnp.zeros((passages, deep), F32)
-    for s in range(strips):
-        fetched = token_block(s, count // 2, (count + passages) // 2)
-        acc += fetched.astype(F32) * query_ref[s].astype(F32)
-    low = jnp.sum(acc[:, :LANES], axis=1, keepdims=True)
-    high = jnp.sum(acc[:, LANES:], axis=1, keepdims=True)
-    scores = jnp.where(high_ref[...] > 0, high, low)
-    each, valid = passages // 2, count // 2 // PLEN
-    queries = valid // K
-    p = lax.broadcasted_iota(jnp.int32, (passages, 2 * queries), 0)
-    g = lax.broadcasted_iota(jnp.int32, (passages, 2 * queries), 1)
-    first = jnp.where(g >= queries, each + (g - queries) * K, g * K)
-    group = (p >= first) & (p < first + K)
-    top = jnp.max(jnp.where(group, scores, -jnp.inf), axis=0, keepdims=True)
-    exps = jnp.where(group, jnp.exp(scores - top), 0.0)
-    rel_column = jnp.sum(exps / jnp.sum(exps, axis=0, keepdims=True), axis=1, keepdims=True)
-    same = lax.broadcasted_iota(jnp.int32, (passages, passages), 0) == lax.broadcasted_iota(
-        jnp.int32, (passages, passages), 1
-    )
-    rel_row = jnp.sum(jnp.where(same, rel_column, 0.0), axis=0, keepdims=True)
-    rel_ref[...] = rel_row
-    token = lax.broadcasted_iota(jnp.int32, (count, passages), 0)
-    p = lax.broadcasted_iota(jnp.int32, (count, passages), 1)
-    at = jnp.where(p >= each, p - each, p)
-    begin = jnp.where(p >= each, count // 2, 0) + at * PLEN
-    begin = jnp.where(at < valid, begin, count)
+    valid = count // 2 // PLEN
+    sums = []
+    for ref in token_refs:
+        acc = jnp.zeros((16, LANES), F32)
+        for b in range(strips):
+            x, c = divmod(b, nc)
+            acc += ref[c, x, count // 2 :, :LANES].astype(F32)
+        sums.append(jnp.sum(acc, axis=0, keepdims=True))
+    lane = lax.broadcasted_iota(jnp.int32, (1, LANES), 1)
+    token = lax.broadcasted_iota(jnp.int32, (count // 2, LANES), 0)
+    begin = lax.broadcasted_iota(jnp.int32, (count // 2, LANES), 1) * PLEN
     of_token = (token >= begin) & (token < begin + PLEN)
-    rel = jnp.sum(jnp.where(of_token, rel_row, 0.0), axis=1, keepdims=True)
+    rel = []
+    for scores in (
+        jnp.where(mine == 0, sums[0], sums[1]),
+        jnp.where(mine == 0, sums[1], sums[0]),
+    ):
+        share = jnp.zeros((1, LANES), F32)
+        for first in range(0, valid, K):
+            group = (lane >= first) & (lane < first + K)
+            top = jnp.max(jnp.where(group, scores, -jnp.inf), axis=1, keepdims=True)
+            exps = jnp.where(group, jnp.exp(scores - top), 0.0)
+            share += exps / jnp.sum(exps, axis=1, keepdims=True)
+        if not rel:
+            rel_ref[...] = share
+        rel.append(jnp.sum(jnp.where(of_token, share, 0.0), axis=1, keepdims=True))
+    rel = jnp.concatenate(rel, axis=0)
 
     tokens = [token_block(b, 0, count // 2) for b in range(blocks)]
     weighted = [
@@ -123,22 +121,21 @@
         out_ref[b * span : (b + 1) * span, rows:, :] = lower.reshape(span, rows, -1)
 
 
-def reader(half, high, query, tokens, out_grad, weights, owners):
+def reader(half, tokens, out_grad, weights, strips, owners):
     width, inner = weights[0].shape
-    passages = query.shape[1]
     vmem = pl.BlockSpec(memory_space=pltpu.VMEM)
     return pl.pallas_call(
-        functools.partial(reader_kernel, inner // HEAD_DIM),
+        functools.partial(reader_kernel, inner // HEAD_DIM, strips),
         out_shape=(
             jax.ShapeDtypeStruct((owners, 2 * width // owners, 2 * HEAD_DIM), BF16),
-            jax.ShapeDtypeStruct((1, passages), F32),
+            jax.ShapeDtypeStruct((1, LANES), F32),
         ),
         in_specs=[pl.BlockSpec(memory_space=pltpu.SMEM)]
-        + [vmem] * 10,
+        + [vmem] * 8,
         out_specs=(vmem, vmem),
         compiler_params=pltpu.CompilerParams(vmem_limit_bytes=40 * 1024 * 1024),
         name="reader",
-    )(half, high, query, *tokens, *out_grad, *weights)
+    )(half, *tokens, *out_grad, *weights)
 
 
 def exact(a, b):
@@ -229,6 +226,49 @@
         compiler_params=pltpu.CompilerParams(vmem_limit_bytes=60 * 1024 * 1024),
         name="pack",
     )(jnp.stack([core, strip]), *operands)
+
+
+def spread_kernel(got_ref, query_ref, high_ref, out_ref):
+    count, passages = out_ref.shape[1] - 16, query_ref.shape[0]
+
+    def summed(low, high):
+        acc = got_ref[0, low:high, :].astype(F32)
+        for source in range(1, got_ref.shape[0]):
+            acc += got_ref[source, low:high, :].astype(F32)
+        return acc.astype(BF16)
+
+    rows = summed(0, count)
+    products = summed(count, count + passages).astype(F32) * query_ref[...].astype(F32)
+    low = jnp.sum(products[:, :LANES], axis=1, keepdims=True)
+    high = jnp.sum(products[:, LANES:], axis=1, keepdims=True)
+    scores = jnp.where(high_ref[...] > 0, high, low)
+    p = lax.broadcasted_iota(jnp.int32, (passages, out_ref.shape[2]), 0)
+    lane = lax.broadcasted_iota(jnp.int32, (passages, out_ref.shape[2]), 1)
+    scores = jnp.sum(jnp.where(p == lane, scores, 0.0), axis=0, keepdims=True)
+    parts = []
+    for _ in range(3):
+        parts.append(scores.astype(BF16).astype(F32))
+        scores = scores - parts[-1]
+    line = lax.broadcasted_iota(jnp.int32, (16, out_ref.shape[2]), 0)
+    block = jnp.zeros((16, out_ref.shape[2]), F32)
+    for i, part in enumerate(parts):
+        block = jnp.where(line == i, part, block)
+    block = block.astype(BF16)
+    for peer in range(out_ref.shape[0]):
+        out_ref[peer, :count, :] = rows
+        out_ref[peer, count:, :] = block
+
+
+def spread(got, query, high, count, peers):
+    vmem = pl.BlockSpec(memory_space=pltpu.VMEM)
+    return pl.pallas_call(
+        spread_kernel,
+        out_shape=jax.ShapeDtypeStruct((peers, count + 16, got.shape[2]), BF16),
+        in_specs=[vmem] * 3,
+        out_specs=vmem,
+        compiler_params=pltpu.CompilerParams(vmem_limit_bytes=32 * 1024 * 1024),
+        name="spread",
+    )(got, query, high)
 
 
 def total_kernel(terms_ref, *out_refs):
@@ -332,28 +372,9 @@
         axis_index_groups=first_groups,
         tiled=True,
     )
-    query_strips = query_emb.reshape(queries, strips, LANES).transpose(1, 0, 2)
-    extra = jnp.concatenate(
-        [
-            query_strips.reshape(strips, queries * LANES),
-            jnp.pad(passage_row.astype(BF16)[None], ((0, 0), (0, deep - npass))),
-        ],
-        axis=0,
-    )
-    extra = jnp.pad(extra, ((0, -extra.shape[0] % 8), (0, 0)))
-    other = lax.ppermute(jnp.concatenate([out_grad, extra], axis=0), "q", swap)
+    other = lax.ppermute(out_grad, "q", swap)
     got_first, other = lax.optimization_barrier((got_first, other))
-    along_x = lax.all_gather(jnp.concatenate([out_grad, other[:count]], axis=0), "x", axis=0)
-    other_strips = other[count : count + strips].reshape(strips, queries, LANES)
-    def per_passage(some):
-        some = jnp.repeat(jnp.concatenate([some, some], axis=2), K, axis=1)
-        return jnp.pad(some, ((0, 0), (0, spare), (0, 0)))
-
-    pair_query = jnp.concatenate([per_passage(query_strips), per_passage(other_strips)], axis=1)
-    other_row = other[count + strips, :npass].astype(jnp.int32)
-    high = jnp.concatenate([jnp.pad(passage_row, (0, spare)), jnp.pad(other_row, (0, spare))])
-    high = (high[:, None] >= folded).astype(jnp.int32)
-
+    along_x = lax.all_gather(jnp.concatenate([out_grad, other], axis=0), "x", axis=0)
     wanted = lax.ppermute(got_first[:, asked : asked + 2], "c", [(0, 1), (1, 0)])
     wanted = wanted.astype(jnp.int32)[:, :, :rows_here]
     rows_at = wanted[:, 0] * LANES + wanted[:, 1] - second * REACH
@@ -375,15 +396,17 @@
         tiled=True,
     )
     got_second, along_x = lax.optimization_barrier((got_second, along_x))
-    part = jnp.sum(got_second[:, :rows_here].astype(F32), axis=0).astype(BF16)
-
+
+    query = my_strip(query_emb)
+    query = jnp.repeat(jnp.concatenate([query, query], axis=1), K, axis=0)
+    query = jnp.pad(query, ((0, spare), (0, 0)))
+    high = jnp.pad((passage_row >= folded).astype(jnp.int32), (0, spare))[:, None]
     nx = lax.axis_size("x")
+    part = spread(got_second, query, high, count, nq * nx)
     grads = [
         lax.all_gather(along_x[i * nx // 2 : (i + 1) * nx // 2], "c", axis=0) for i in range(2)
     ]
-    near = lax.all_to_all(
-        jnp.broadcast_to(part[None], (nq * nx, *part.shape)), ("q", "x"), 0, 0, tiled=True
-    )
+    near = lax.all_to_all(part, ("q", "x"), 0, 0, tiled=True)
     near, grads = lax.optimization_barrier((near, grads))
     tokens = [lax.all_gather(near[i * nx : (i + 1) * nx], "c", axis=0) for i in range(nq)]
 
@@ -394,7 +417,7 @@
     refreshed = jnp.where(jnp.any(put, axis=1)[:, None], placed, index_strip)
 
     terms, pair_relevance = reader(
-        my_half.reshape(1), high, pair_query, tokens, grads, (w_query, w_key, w_value, w_out), owners
+        my_half.reshape(1), tokens, grads, (w_query, w_key, w_value, w_out), strips, owners
     )
     relevance = pair_relevance[0, :npass].reshape(queries, K)
     refreshed, terms = lax.optimization_barrier((refreshed, terms))

time: 134 us -> 133 us (level)
    pallas_call x1 -> x2, Pallas kernels: 4.64 us -> 5.81 us  [the longest x1 4.65 us: reader(): pl.pallas_call(functools.partial(reader_kernel, inner // HEAD_DIM, strips...]
where the time goes in v12:
time: 133 us; the launch traced here: 131 us
  waiting for transfers between devices  42.7 us (32%)
  blocking collectives  35.8 us (27%)
  starting transfers between devices  34.1 us (26%)
  Pallas kernels  9.78 us (7%)
  matrix products  5.53 us (4%)
    all_to_all x1, waiting for transfers between devices, shards(): terms = lax.all_to_all(terms, IDX, 0, 0, tiled=True)  16.3 us
    all_gather x1, blocking collectives, shards(): lax.all_gather(jnp.concatenate([out_grad, other], axis=0), 'x', axis=0)  13.7 us
    all_gather x1, blocking collectives, shards(): refreshed = lax.all_gather(refreshed, M, axis=0)  12.8 us
    all_to_all x1, waiting for transfers between devices, shards(): lax.all_to_all(message, ALONG, 0, 0, axis_index_groups=first_groups, tile...  11.1 us
    all_to_all x1, starting transfers between devices, shards(): lax.all_to_all(message, ALONG, 0, 0, axis_index_groups=first_groups, tile...  10.5 us
    ppermute x1, waiting for transfers between devices, shards(): other = lax.ppermute(out_grad, 'q', swap)  8.28 us
    all_to_all x1, starting transfers between devices, shards(): lax.all_to_all(served.reshape(*at.shape, deep), ALONG, 0, 0, axis_index_g...  7.23 us
    all_to_all x1, starting transfers between devices, shards(): terms = lax.all_to_all(terms, IDX, 0, 0, tiled=True)  6.25 us
  transfers between devices with their start and end apart: 6, of which 6 were waited for; matrix products, arithmetic and copies ran while one was open for 2% of the time, Pallas kernels for 0%

profile of v12, /device:TPU:6, one launch (start us, length us, event | category | flops | bytes accessed | tf_op | source)
XLA Modules:
  0.0 131.1 jit_solution(12836342984508062971)
XLA Ops:
  0.6 0.0 copy-start
  0.7 0.6 pad_add_fusion.1.at_ref
  1.2 3.1 %pack.1 = bf16[8,352,256]{2,1,0:T(8,128)(2,1)} custom-call(s32[2]{0:T(128)} %pad_add_fusion.1.at_ref, bf16[256,256]{1,0:T(8,128)(2,1)} %refs_0_.1, bf16[128,768]{1,0:T(8,128)(2,1)} %refs_1_.1, bf16[64,768]{1,0:T(8,128)(2,1)} %refs_2_.1, s32[1,64]{1,0:T(1,128)} %bitcast.35, s32[4,40]{1,0:T(4,128)} %bitcast.34, s32[1,40]{1,0:T(1,128)} %bitcast.36, ...), custom_call_target="tpu_custom_call" | custom-call | tf_op jit(solution)/shard_map/pack/pallas_call | solution.py:218
  4.4 0.0 copy-start.5
  4.4 10.5 %all-to-all-start = ((bf16[8,352,256]{2,1,0:T(8,128)(2,1)}), bf16[8,352,256]{2,1,0:T(8,128)(2,1)S(1)}, u32[]{:S(2)}, u32[]{:S(2)}) async-start(bf16[8,352,256]{2,1,0:T(8,128)(2,1)} %pack.1), calls=%async_computation | async-start | bytes 2883584 | tf_op jit(solution)/shard_map/all_to_all | solution.py:367
  14.9 0.0 copy-done.5
  14.9 3.5 %collective-permute-start = (bf16[160,256]{1,0:T(8,128)(2,1)S(1)}, bf16[160,256]{1,0:T(8,128)(2,1)S(1)}, u32[]{:S(2)}, u32[]{:S(2)}) collective-permute-start(bf16[160,256]{1,0:T(8,128)(2,1)S(1)} %copy-done.5), channel_id=1, source_target_pairs={{0,8},{8,0},{1,9},{9,1},{2,10},{10,2},{3,11},{11,3},{4,12},{12,4},... | collective-permute-start | bytes 245768 | tf_op jit(solution)/shard_map/ppermute | solution.py:375
  18.4 0.1 broadcast_add_fusion.1
  18.5 0.1 copy.28
  18.5 0.1 add.78
  18.6 8.3 %collective-permute-done = bf16[160,256]{1,0:T(8,128)(2,1)S(1)} collective-permute-done((bf16[160,256]{1,0:T(8,128)(2,1)S(1)}, bf16[160,256]{1,0:T(8,128)(2,1)S(1)}, u32[]{:S(2)}, u32[]{:S(2)}) %collective-permute-start) | collective-permute-done | bytes 81952 | tf_op jit(solution)/shard_map/ppermute | solution.py:375
  26.9 11.1 %all-to-all-done = bf16[8,352,256]{2,1,0:T(8,128)(2,1)S(1)} async-done(((bf16[8,352,256]{2,1,0:T(8,128)(2,1)}), bf16[8,352,256]{2,1,0:T(8,128)(2,1)S(1)}, u32[]{:S(2)}, u32[]{:S(2)}) %all-to-all-start) | async-done | bytes 1441824 | tf_op jit(solution)/shard_map/all_to_all | solution.py:367
  38.0 1.9 %collective-permute-start.1 = (bf16[8,2,256]{2,1,0:T(2,128)(2,1)S(1)}, bf16[8,2,256]{2,1,0:T(2,128)(2,1)S(1)}, u32[]{:S(2)}, u32[]{:S(2)}) collective-permute-start(bf16[8,2,256]{2,1,0:T(2,128)(2,1)S(1)} %slice.54), channel_id=1, source_target_pairs={{0,1},{1,0},{2,3},{3,2},{4,5},{5,4},{6,7},{7,6},{8,9},{9,8},{10,11... | collective-permute-start | bytes 24584 | tf_op jit(solution)/shard_map/ppermute | solution.py:378
  40.0 1.1 collective-permute-done.1
  41.2 0.1 pad_add_fusion
  41.2 0.1 eq.32
  41.3 4.6 %fusion.2 = bf16[1792,256]{1,0:T(8,128)(2,1)} fusion(bf16[2816,256]{1,0:T(8,128)(2,1)S(1)} %bitcast.29, s32[1792]{0:T(1024)S(1)} %eq.32), kind=kOutput, calls=%fused_computation.3 | convolution fusion | flops 2589196288 | bytes 2366464 | tf_op jit(solution)/shard_map/dot_general | solution.py:28
  45.9 0.0 copy-start.7
  45.9 7.2 %all-to-all-start.1 = ((bf16[8,224,256]{2,1,0:T(8,128)(2,1)}), bf16[8,224,256]{2,1,0:T(8,128)(2,1)S(1)}, u32[]{:S(2)}, u32[]{:S(2)}) async-start(bf16[8,224,256]{2,1,0:T(8,128)(2,1)} %bitcast.9), calls=%async_computation.1 | async-start | bytes 1835008 | tf_op jit(solution)/shard_map/all_to_all | solution.py:390
  53.2 0.0 copy-done
  53.2 0.0 copy-done.7
  53.3 0.1 copy.29.high_ref
  53.4 13.7 %all-gather = bf16[1280,256]{1,0:T(8,128)(2,1)S(1)} all-gather(bf16[320,256]{1,0:T(8,128)(2,1)S(1)} %pad_maximum_fusion), channel_id=2, replica_groups=mesh['z'=8,'p'=4,'q'=2,'x'=4,'c'=2] {'x'}, dimensions={0}, use_global_device_ids=true | all-gather | bytes 819200 | tf_op jit(solution)/shard_map/all_gather | solution.py:377
  67.1 3.7 %all-to-all-done.1.got_ref = bf16[8,224,256]{2,1,0:T(8,128)(2,1)S(1)} async-done(((bf16[8,224,256]{2,1,0:T(8,128)(2,1)}), bf16[8,224,256]{2,1,0:T(8,128)(2,1)S(1)}, u32[]{:S(2)}, u32[]{:S(2)}) %all-to-all-start.1) | async-done | bytes 917536 | tf_op jit(solution)/shard_map/all_to_all | solution.py:390
  70.7 1.2 spread.1
  71.9 4.8 %all-to-all-start.2 = ((bf16[8,176,256]{2,1,0:T(8,128)(2,1)}), bf16[8,176,256]{2,1,0:T(8,128)(2,1)S(1)}, u32[]{:S(2)}, u32[]{:S(2)}) async-start(bf16[8,176,256]{2,1,0:T(8,128)(2,1)} %spread.1), calls=%async_computation.2 | async-start | bytes 1441792 | tf_op jit(solution)/shard_map/all_to_all | solution.py:409
  76.7 0.1 copy.33
  76.7 0.1 fusion.4
  76.9 2.3 %all-gather.2 = bf16[4,320,256]{2,1,0:T(8,128)(2,1)S(1)} all-gather(bf16[2,320,256]{2,1,0:T(8,128)(2,1)S(1)} %get-tuple-element.38), channel_id=4, replica_groups=mesh['z'=8,'p'=4,'q'=2,'x'=4,'c'=2] {'c'}, dimensions={0}, use_global_device_ids=true | all-gather | bytes 983040 | tf_op jit(solution)/shard_map/all_gather | solution.py:407
  79.2 2.3 %all-gather.1 = bf16[4,320,256]{2,1,0:T(8,128)(2,1)S(1)} all-gather(bf16[2,320,256]{2,1,0:T(8,128)(2,1)S(1)} %get-tuple-element.39), channel_id=3, replica_groups=mesh['z'=8,'p'=4,'q'=2,'x'=4,'c'=2] {'c'}, dimensions={0}, use_global_device_ids=true | all-gather | bytes 983040 | tf_op jit(solution)/shard_map/all_gather | solution.py:407
  81.5 0.9 fusion.3
  82.4 2.2 %all-to-all-done.2 = bf16[8,176,256]{2,1,0:T(8,128)(2,1)S(1)} async-done(((bf16[8,176,256]{2,1,0:T(8,128)(2,1)}), bf16[8,176,256]{2,1,0:T(8,128)(2,1)S(1)}, u32[]{:S(2)}, u32[]{:S(2)}) %all-to-all-start.2) | async-done | bytes 720928 | tf_op jit(solution)/shard_map/all_to_all | solution.py:409
  84.6 0.0 copy-start.1
  84.7 0.0 copy-start.2
  84.7 0.0 copy-start.3
  84.7 0.0 copy-start.4
  84.7 2.5 %all-gather.4 = bf16[8,176,256]{2,1,0:T(8,128)(2,1)S(1)} all-gather(bf16[4,176,256]{2,1,0:T(8,128)(2,1)S(1)} %get-tuple-element.36), channel_id=6, replica_groups=mesh['z'=8,'p'=4,'q'=2,'x'=4,'c'=2] {'c'}, dimensions={0}, use_global_device_ids=true | all-gather | bytes 1081344 | tf_op jit(solution)/shard_map/all_gather | solution.py:411
  87.1 2.3 %all-gather.3 = bf16[8,176,256]{2,1,0:T(8,128)(2,1)S(1)} all-gather(bf16[4,176,256]{2,1,0:T(8,128)(2,1)S(1)} %get-tuple-element.37), channel_id=5, replica_groups=mesh['z'=8,'p'=4,'q'=2,'x'=4,'c'=2] {'c'}, dimensions={0}, use_global_device_ids=true | all-gather | bytes 1081344 | tf_op jit(solution)/shard_map/all_gather | solution.py:411
  89.5 0.0 copy-done.1
  89.5 0.0 copy-done.2
  89.5 0.0 copy-done.3
  89.5 0.0 copy-done.4
  89.5 4.6 %reader.1 = (bf16[64,64,128]{2,1,0:T(8,128)(2,1)}, f32[1,128]{1,0:T(1,128)S(1)}) custom-call(s32[1]{0:T(128)} %bitcast.half_ref, bf16[2,4,176,256]{3,2,1,0:T(8,128)(2,1)S(1)} %bitcast.25, bf16[2,4,176,256]{3,2,1,0:T(8,128)(2,1)S(1)} %bitcast.24, bf16[2,2,320,256]{3,2,1,0:T(8,128)(2,1)S(1)} %bitcast.27, bf16[2,2,320,256]{3,2,1,0:T(8,128)(2,1)S(1)} %bitcast.26, ...), custom_call_target="tpu_custom_call" | custom-call | tf_op jit(solution)/shard_map/reader/pallas_call | solution.py:127
  94.1 6.2 %all-to-all-start.3 = ((bf16[64,64,128]{2,1,0:T(8,128)(2,1)}), bf16[64,64,128]{2,1,0:T(8,128)(2,1)S(1)}, u32[]{:S(2)}, u32[]{:S(2)}) async-start(bf16[64,64,128]{2,1,0:T(8,128)(2,1)} %get-tuple-element.30), calls=%async_computation.3 | async-start | bytes 2097152 | tf_op jit(solution)/shard_map/all_to_all | solution.py:426
  100.4 0.6 reshape_squeeze.3
  101.0 12.8 %all-gather.5 = bf16[1024,128]{1,0:T(8,128)(2,1)S(1)} all-gather(bf16[128,128]{1,0:T(8,128)(2,1)S(1)} %fusion.3), channel_id=7, replica_groups=mesh['z'=8,'p'=4,'q'=2,'x'=4,'c'=2] {'x','c'}, dimensions={0}, use_global_device_ids=true | all-gather | bytes 294912 | tf_op jit(solution)/shard_map/all_gather | solution.py:424
  114.0 0.0 copy-start.6
  114.0 16.3 %all-to-all-done.3.terms_ref = bf16[64,64,128]{2,1,0:T(8,128)(2,1)S(1)} async-done(((bf16[64,64,128]{2,1,0:T(8,128)(2,1)}), bf16[64,64,128]{2,1,0:T(8,128)(2,1)S(1)}, u32[]{:S(2)}, u32[]{:S(2)}) %all-to-all-start.3) | async-done | bytes 1048608 | tf_op jit(solution)/shard_map/all_to_all | solution.py:426
  130.3 0.8 total.1
  131.1 0.0 copy-done.6
  (27 shorter events, 0.3 us)
Async XLA Ops:
  0.6 52.5 %copy-start = (bf16[2,768]{1,0:T(2,128)(2,1)S(1)}, bf16[2,768]{1,0:T(2,128)(2,1)}, u32[]{:S(2)}) copy-start(bf16[2,768]{1,0:T(2,128)(2,1)} %param.14) | copy-start | bytes 9220
  4.4 10.5 %copy-start.5 = (bf16[160,256]{1,0:T(8,128)(2,1)S(1)}, bf16[160,256]{1,0:T(8,128)(2,1)}, u32[]{:S(2)}) copy-start(bf16[160,256]{1,0:T(8,128)(2,1)} %param.23) | copy-start | bytes 245764
  4.4 33.6 %all-to-all-start = ((bf16[8,352,256]{2,1,0:T(8,128)(2,1)}), bf16[8,352,256]{2,1,0:T(8,128)(2,1)S(1)}, u32[]{:S(2)}, u32[]{:S(2)}) async-start(bf16[8,352,256]{2,1,0:T(8,128)(2,1)} %pack.1), calls=%async_computation | async-start | bytes 2883584 | tf_op jit(solution)/shard_map/all_to_all | solution.py:367
  14.9 12.0 %collective-permute-start = (bf16[160,256]{1,0:T(8,128)(2,1)S(1)}, bf16[160,256]{1,0:T(8,128)(2,1)S(1)}, u32[]{:S(2)}, u32[]{:S(2)}) collective-permute-start(bf16[160,256]{1,0:T(8,128)(2,1)S(1)} %copy-done.5), channel_id=1, source_target_pairs={{0,8},{8,0},{1,9},{9,1},{2,10},{10,2},{3,11},{11,3},{4,12},{12,4},... | collective-permute-start | bytes 245768 | tf_op jit(solution)/shard_map/ppermute | solution.py:375
  38.0 3.1 %collective-permute-start.1 = (bf16[8,2,256]{2,1,0:T(2,128)(2,1)S(1)}, bf16[8,2,256]{2,1,0:T(2,128)(2,1)S(1)}, u32[]{:S(2)}, u32[]{:S(2)}) collective-permute-start(bf16[8,2,256]{2,1,0:T(2,128)(2,1)S(1)} %slice.54), channel_id=1, source_target_pairs={{0,1},{1,0},{2,3},{3,2},{4,5},{5,4},{6,7},{7,6},{8,9},{9,8},{10,11... | collective-permute-start | bytes 24584 | tf_op jit(solution)/shard_map/ppermute | solution.py:378
  45.9 7.3 %copy-start.7 = (s32[40]{0:T(128)S(1)}, s32[40]{0:T(128)}, u32[]{:S(2)}) copy-start(s32[40]{0:T(128)} %param.16) | copy-start | bytes 484
  45.9 24.8 %all-to-all-start.1 = ((bf16[8,224,256]{2,1,0:T(8,128)(2,1)}), bf16[8,224,256]{2,1,0:T(8,128)(2,1)S(1)}, u32[]{:S(2)}, u32[]{:S(2)}) async-start(bf16[8,224,256]{2,1,0:T(8,128)(2,1)} %bitcast.9), calls=%async_computation.1 | async-start | bytes 1835008 | tf_op jit(solution)/shard_map/all_to_all | solution.py:390
  71.9 12.7 %all-to-all-start.2 = ((bf16[8,176,256]{2,1,0:T(8,128)(2,1)}), bf16[8,176,256]{2,1,0:T(8,128)(2,1)S(1)}, u32[]{:S(2)}, u32[]{:S(2)}) async-start(bf16[8,176,256]{2,1,0:T(8,128)(2,1)} %spread.1), calls=%async_computation.2 | async-start | bytes 1441792 | tf_op jit(solution)/shard_map/all_to_all | solution.py:409
  84.6 4.8 %copy-start.1 = (bf16[2048,128]{1,0:T(8,128)(2,1)S(1)}, bf16[2048,128]{1,0:T(8,128)(2,1)}, u32[]{:S(2)}) copy-start(bf16[2048,128]{1,0:T(8,128)(2,1)} %refs_4_.1) | copy-start | bytes 1572868
  84.7 4.8 %copy-start.2 = (bf16[2048,128]{1,0:T(8,128)(2,1)S(1)}, bf16[2048,128]{1,0:T(8,128)(2,1)}, u32[]{:S(2)}) copy-start(bf16[2048,128]{1,0:T(8,128)(2,1)} %refs_5_.1) | copy-start | bytes 1572868
  84.7 4.8 %copy-start.3 = (bf16[2048,128]{1,0:T(8,128)(2,1)S(1)}, bf16[2048,128]{1,0:T(8,128)(2,1)}, u32[]{:S(2)}) copy-start(bf16[2048,128]{1,0:T(8,128)(2,1)} %refs_6_.1) | copy-start | bytes 1572868
  84.7 4.8 %copy-start.4 = (bf16[128,2048]{1,0:T(8,128)(2,1)S(1)}, bf16[128,2048]{1,0:T(8,128)(2,1)}, u32[]{:S(2)}) copy-start(bf16[128,2048]{1,0:T(8,128)(2,1)} %refs_7_.1) | copy-start | bytes 1572868
  94.1 36.1 %all-to-all-start.3 = ((bf16[64,64,128]{2,1,0:T(8,128)(2,1)}), bf16[64,64,128]{2,1,0:T(8,128)(2,1)S(1)}, u32[]{:S(2)}, u32[]{:S(2)}) async-start(bf16[64,64,128]{2,1,0:T(8,128)(2,1)} %get-tuple-element.30), calls=%async_computation.3 | async-start | bytes 2097152 | tf_op jit(solution)/shard_map/all_to_all | solution.py:426
  114.0 17.2 %copy-start.6 = (bf16[128,768]{1,0:T(8,128)(2,1)}, bf16[128,768]{1,0:T(8,128)(2,1)S(1)}, u32[]{:S(2)}) copy-start(bf16[128,768]{1,0:T(8,128)(2,1)S(1)} %slice_dynamic-update-slice_fusion) | copy-start | bytes 589828

commit v13 on v12

--- a/solution.py
+++ b/solution.py
@@ -111,12 +111,12 @@
     context = dot(attn, v).astype(BF16)
     blank = jnp.zeros_like(context)
     token_side = jnp.concatenate([query_grad, key_grad, value_grad, blank], axis=1)
-    weighted_side = jnp.concatenate([blank, context], axis=1)
+    weighted_side = jnp.concatenate([blank, blank, blank, context], axis=1)
+    sides = jnp.concatenate([token_side, weighted_side], axis=0)
     span = deep // rows
     for b in range(blocks):
-        term = dot(tokens[b], token_side, ROWS)
-        upper = term[:, : 2 * HEAD_DIM].astype(BF16)
-        lower = (term[:, 2 * HEAD_DIM :] + dot(weighted[b], weighted_side, ROWS)).astype(BF16)
+        term = dot(jnp.concatenate([tokens[b], weighted[b]], axis=0), sides, ROWS).astype(BF16)
+        upper, lower = term[:, : 2 * HEAD_DIM], term[:, 2 * HEAD_DIM :]
         out_ref[b * span : (b + 1) * span, :rows, :] = upper.reshape(span, rows, -1)
         out_ref[b * span : (b + 1) * span, rows:, :] = lower.reshape(span, rows, -1)
 
@@ -143,20 +143,26 @@
 
 
 def pack_kernel(at_ref, *refs):
-    hbm, out_ref, vmem, sems = refs[:7], refs[7], refs[8:15], refs[15]
+    hbm, out_ref, vmem, rest_ref, sems = refs[:7], refs[7], refs[8:15], refs[15], refs[16]
     copies = [pltpu.make_async_copy(hbm[i], vmem[i], sems.at[i]) for i in range(7)]
     for copy in copies:
         copy.start()
     vocab_ref, index_ref, slab_ref, slab_ids_ref, ids_ref, owner_ref, row_ref = vmem
     core, strip = at_ref[0], at_ref[1]
-    for copy in copies:
-        copy.wait()
     peers, stride, deep = out_ref.shape
     vocab_rows = vocab_ref.shape[0]
+    copies[0].wait()
+    sends = [
+        pltpu.make_async_copy(vocab_ref, out_ref.at[peer, :vocab_rows, :], sems.at[7 + peer])
+        for peer in range(peers)
+    ]
+    for send in sends:
+        send.start()
+    for copy in copies[1:]:
+        copy.wait()
     pass_rows = index_ref.shape[0]
     folded = pass_rows // 2
     asked = vocab_rows + folded
-    held = asked + 16
     columns = pl.ds(pl.multiple_of(strip * LANES, LANES), LANES)
     index = index_ref[:, columns]
     slab, plen, npass = slab_ref.shape[0], ids_ref.shape[0], ids_ref.shape[1]
@@ -206,10 +212,16 @@
 
     index = jnp.concatenate([index[:folded], index[folded:]], axis=1)
     for peer in range(peers):
-        out_ref[peer, :vocab_rows, :] = vocab_ref[...]
-        out_ref[peer, vocab_rows:asked, :] = index
-        out_ref[peer, asked:held, :] = wanted
-        out_ref[peer, held:, :] = slab_out[peer * peers * CAPS : (peer + 1) * peers * CAPS]
+        rest_ref[peer, :folded, :] = index
+        rest_ref[peer, folded : folded + 16, :] = wanted
+        rest_ref[peer, folded + 16 :, :] = slab_out[
+            peer * peers * CAPS : (peer + 1) * peers * CAPS
+        ]
+    last = pltpu.make_async_copy(rest_ref, out_ref.at[:, vocab_rows:, :], sems.at[7 + peers])
+    last.start()
+    for send in sends:
+        send.wait()
+    last.wait()
 
 
 def pack(core, strip, vocab, index, slab, slab_ids, ids, owner, row, peers):
@@ -220,9 +232,12 @@
         out_shape=jax.ShapeDtypeStruct((peers, rows, vocab.shape[1]), BF16),
         in_specs=[pl.BlockSpec(memory_space=pltpu.SMEM)]
         + [pl.BlockSpec(memory_space=pltpu.HBM)] * 7,
-        out_specs=pl.BlockSpec(memory_space=pltpu.VMEM),
+        out_specs=pl.BlockSpec(memory_space=pltpu.HBM),
         scratch_shapes=[pltpu.VMEM(operand.shape, operand.dtype) for operand in operands]
-        + [pltpu.SemaphoreType.DMA((7,))],
+        + [
+            pltpu.VMEM((peers, rows - vocab.shape[0], vocab.shape[1]), BF16),
+            pltpu.SemaphoreType.DMA((8 + peers,)),
+        ],
         compiler_params=pltpu.CompilerParams(vmem_limit_bytes=60 * 1024 * 1024),
         name="pack",
     )(jnp.stack([core, strip]), *operands)
@@ -375,8 +390,9 @@
     other = lax.ppermute(out_grad, "q", swap)
     got_first, other = lax.optimization_barrier((got_first, other))
     along_x = lax.all_gather(jnp.concatenate([out_grad, other], axis=0), "x", axis=0)
-    wanted = lax.ppermute(got_first[:, asked : asked + 2], "c", [(0, 1), (1, 0)])
-    wanted = wanted.astype(jnp.int32)[:, :, :rows_here]
+    wanted = lax.all_gather(got_first[:, asked : asked + 2].reshape(1, -1, deep), "c", axis=0, tiled=True)
+    wanted = lax.dynamic_index_in_dim(wanted, 1 - my_core, axis=0, keepdims=False)
+    wanted = wanted.reshape(ny, 2, deep).astype(jnp.int32)[:, :, :rows_here]
     rows_at = wanted[:, 0] * LANES + wanted[:, 1] - second * REACH
     slab_at = (
         held

time: 133 us -> 131 us (0.985)
  starting transfers between devices: 34.1 us -> 32.2 us
  blocking collectives: 35.8 us -> 37.6 us
    ppermute x1 -> x0, starting transfers between devices: 1.92 us -> none  [shards(): wanted = lax.ppermute(got_first[:, asked:asked + 2], 'c', [(0, 1), (1, 0)])]
    all_gather x0 -> x1, blocking collectives: none -> 1.81 us  [shards(): lax.all_gather(got_first[:, asked:asked + 2].reshape(1, -1, deep), 'c', a...]
  transfers between devices with their start and end apart: 6 -> 5, of which waited for: 6 -> 5; matrix products, arithmetic and copies ran while one was open for 2% -> 2% of each run, Pallas kernels for 0% -> 0%
where the time goes in v13:
time: 131 us; the launch traced here: 129 us
  waiting for transfers between devices  41.5 us (32%)
  blocking collectives  37.6 us (29%)
  starting transfers between devices  32.2 us (25%)
  Pallas kernels  9.29 us (7%)
  matrix products  5.53 us (4%)
  local copies, waits for them, and re-layouts  1.35 us (1%)
    all_to_all x1, waiting for transfers between devices, shards(): terms = lax.all_to_all(terms, IDX, 0, 0, tiled=True)  16.3 us
    all_gather x1, blocking collectives, shards(): lax.all_gather(jnp.concatenate([out_grad, other], axis=0), 'x', axis=0)  13.7 us
    all_gather x1, blocking collectives, shards(): refreshed = lax.all_gather(refreshed, M, axis=0)  12.8 us
    all_to_all x1, waiting for transfers between devices, shards(): lax.all_to_all(message, ALONG, 0, 0, axis_index_groups=first_groups, tile...  11.1 us
    all_to_all x1, starting transfers between devices, shards(): lax.all_to_all(message, ALONG, 0, 0, axis_index_groups=first_groups, tile...  10.5 us
    ppermute x1, waiting for transfers between devices, shards(): other = lax.ppermute(out_grad, 'q', swap)  8.21 us
    all_to_all x1, starting transfers between devices, shards(): lax.all_to_all(served.reshape(*at.shape, deep), ALONG, 0, 0, axis_index_g...  7.23 us
    all_to_all x1, starting transfers between devices, shards(): terms = lax.all_to_all(terms, IDX, 0, 0, tiled=True)  6.27 us
  transfers between devices with their start and end apart: 5, of which 5 were waited for; matrix products, arithmetic and copies ran while one was open for 2% of the time, Pallas kernels for 0%

profile of v13, /device:TPU:6, one launch (start us, length us, event | category | flops | bytes accessed | tf_op | source)
XLA Modules:
  0.0 129.4 jit_solution(10555167469352007236)
XLA Ops:
  0.6 0.0 copy-start
  0.7 0.6 pad_add_fusion.1.at_ref
  1.2 2.9 %pack.1 = bf16[8,352,256]{2,1,0:T(8,128)(2,1)} custom-call(s32[2]{0:T(128)} %pad_add_fusion.1.at_ref, bf16[256,256]{1,0:T(8,128)(2,1)} %refs_0_.1, bf16[128,768]{1,0:T(8,128)(2,1)} %refs_1_.1, bf16[64,768]{1,0:T(8,128)(2,1)} %refs_2_.1, s32[1,64]{1,0:T(1,128)} %bitcast.35, s32[4,40]{1,0:T(4,128)} %bitcast.34, s32[1,40]{1,0:T(1,128)} %bitcast.36, ...), custom_call_target="tpu_custom_call" | custom-call | tf_op jit(solution)/shard_map/pack/pallas_call | solution.py:230
  4.1 0.0 copy-start.5
  4.1 10.5 %all-to-all-start = ((bf16[8,352,256]{2,1,0:T(8,128)(2,1)}), bf16[8,352,256]{2,1,0:T(8,128)(2,1)S(1)}, u32[]{:S(2)}, u32[]{:S(2)}) async-start(bf16[8,352,256]{2,1,0:T(8,128)(2,1)} %pack.1), calls=%async_computation | async-start | bytes 2883584 | tf_op jit(solution)/shard_map/all_to_all | solution.py:382
  14.6 0.0 copy-done.5
  14.6 3.5 %collective-permute-start = (bf16[160,256]{1,0:T(8,128)(2,1)S(1)}, bf16[160,256]{1,0:T(8,128)(2,1)S(1)}, u32[]{:S(2)}, u32[]{:S(2)}) collective-permute-start(bf16[160,256]{1,0:T(8,128)(2,1)S(1)} %copy-done.5), channel_id=1, source_target_pairs={{0,8},{8,0},{1,9},{9,1},{2,10},{10,2},{3,11},{11,3},{4,12},{12,4},... | collective-permute-start | bytes 245768 | tf_op jit(solution)/shard_map/ppermute | solution.py:390
  18.1 0.1 add.84
  18.2 0.1 broadcast_add_fusion.1
  18.3 0.1 broadcast_add_fusion
  18.3 0.1 copy.28
  18.4 8.2 %collective-permute-done = bf16[160,256]{1,0:T(8,128)(2,1)S(1)} collective-permute-done((bf16[160,256]{1,0:T(8,128)(2,1)S(1)}, bf16[160,256]{1,0:T(8,128)(2,1)S(1)}, u32[]{:S(2)}, u32[]{:S(2)}) %collective-permute-start) | collective-permute-done | bytes 81952 | tf_op jit(solution)/shard_map/ppermute | solution.py:390
  26.6 11.1 %all-to-all-done = bf16[8,352,256]{2,1,0:T(8,128)(2,1)S(1)} async-done(((bf16[8,352,256]{2,1,0:T(8,128)(2,1)}), bf16[8,352,256]{2,1,0:T(8,128)(2,1)S(1)}, u32[]{:S(2)}, u32[]{:S(2)}) %all-to-all-start) | async-done | bytes 1441824 | tf_op jit(solution)/shard_map/all_to_all | solution.py:382
  37.8 1.8 %all_gather.39 = bf16[2,16,256]{2,1,0:T(8,128)(2,1)S(1)} all-gather(bf16[1,16,256]{2,1,0:T(8,128)(2,1)S(1)} %reshape.98), channel_id=1, replica_groups=mesh['z'=8,'p'=4,'q'=2,'x'=4,'c'=2] {'c'}, dimensions={0}, use_global_device_ids=true | all-gather | bytes 24576 | tf_op jit(solution)/shard_map/all_gather | solution.py:393
  39.6 0.1 pad_add_fusion
  39.7 0.1 eq.32
  39.8 4.6 %fusion.2 = bf16[1792,256]{1,0:T(8,128)(2,1)} fusion(bf16[2816,256]{1,0:T(8,128)(2,1)S(1)} %bitcast.29, s32[1792]{0:T(1024)S(1)} %eq.32), kind=kOutput, calls=%fused_computation.3 | convolution fusion | flops 2589196288 | bytes 2366464 | tf_op jit(solution)/shard_map/dot_general | solution.py:28
  44.4 0.0 copy-start.7
  44.4 7.2 %all-to-all-start.1 = ((bf16[8,224,256]{2,1,0:T(8,128)(2,1)}), bf16[8,224,256]{2,1,0:T(8,128)(2,1)S(1)}, u32[]{:S(2)}, u32[]{:S(2)}) async-start(bf16[8,224,256]{2,1,0:T(8,128)(2,1)} %bitcast.9), calls=%async_computation.1 | async-start | bytes 1835008 | tf_op jit(solution)/shard_map/all_to_all | solution.py:406
  51.7 0.0 copy-done
  51.7 0.0 copy-done.7
  51.8 0.1 copy.29.high_ref
  51.9 13.7 %all-gather = bf16[1280,256]{1,0:T(8,128)(2,1)S(1)} all-gather(bf16[320,256]{1,0:T(8,128)(2,1)S(1)} %pad_maximum_fusion), channel_id=2, replica_groups=mesh['z'=8,'p'=4,'q'=2,'x'=4,'c'=2] {'x'}, dimensions={0}, use_global_device_ids=true | all-gather | bytes 819200 | tf_op jit(solution)/shard_map/all_gather | solution.py:392
  65.6 3.7 %all-to-all-done.1.got_ref = bf16[8,224,256]{2,1,0:T(8,128)(2,1)S(1)} async-done(((bf16[8,224,256]{2,1,0:T(8,128)(2,1)}), bf16[8,224,256]{2,1,0:T(8,128)(2,1)S(1)}, u32[]{:S(2)}, u32[]{:S(2)}) %all-to-all-start.1) | async-done | bytes 917536 | tf_op jit(solution)/shard_map/all_to_all | solution.py:406
  69.2 1.1 spread.1
  70.4 4.8 %all-to-all-start.2 = ((bf16[8,176,256]{2,1,0:T(8,128)(2,1)}), bf16[8,176,256]{2,1,0:T(8,128)(2,1)S(1)}, u32[]{:S(2)}, u32[]{:S(2)}) async-start(bf16[8,176,256]{2,1,0:T(8,128)(2,1)} %spread.1), calls=%async_computation.2 | async-start | bytes 1441792 | tf_op jit(solution)/shard_map/all_to_all | solution.py:425
  75.2 0.1 copy.33
  75.2 0.1 fusion.4
  75.4 2.3 %all-gather.2 = bf16[4,320,256]{2,1,0:T(8,128)(2,1)S(1)} all-gather(bf16[2,320,256]{2,1,0:T(8,128)(2,1)S(1)} %get-tuple-element.38), channel_id=4, replica_groups=mesh['z'=8,'p'=4,'q'=2,'x'=4,'c'=2] {'c'}, dimensions={0}, use_global_device_ids=true | all-gather | bytes 983040 | tf_op jit(solution)/shard_map/all_gather | solution.py:423
  77.7 2.3 %all-gather.1 = bf16[4,320,256]{2,1,0:T(8,128)(2,1)S(1)} all-gather(bf16[2,320,256]{2,1,0:T(8,128)(2,1)S(1)} %get-tuple-element.39), channel_id=3, replica_groups=mesh['z'=8,'p'=4,'q'=2,'x'=4,'c'=2] {'c'}, dimensions={0}, use_global_device_ids=true | all-gather | bytes 983040 | tf_op jit(solution)/shard_map/all_gather | solution.py:423
  80.0 0.9 fusion.3
  80.9 2.2 %all-to-all-done.2 = bf16[8,176,256]{2,1,0:T(8,128)(2,1)S(1)} async-done(((bf16[8,176,256]{2,1,0:T(8,128)(2,1)}), bf16[8,176,256]{2,1,0:T(8,128)(2,1)S(1)}, u32[]{:S(2)}, u32[]{:S(2)}) %all-to-all-start.2) | async-done | bytes 720928 | tf_op jit(solution)/shard_map/all_to_all | solution.py:425
  83.1 0.0 copy-start.1
  83.1 0.0 copy-start.2
  83.1 0.0 copy-start.3
  83.2 0.0 copy-start.4
  83.2 2.5 %all-gather.4 = bf16[8,176,256]{2,1,0:T(8,128)(2,1)S(1)} all-gather(bf16[4,176,256]{2,1,0:T(8,128)(2,1)S(1)} %get-tuple-element.36), channel_id=6, replica_groups=mesh['z'=8,'p'=4,'q'=2,'x'=4,'c'=2] {'c'}, dimensions={0}, use_global_device_ids=true | all-gather | bytes 1081344 | tf_op jit(solution)/shard_map/all_gather | solution.py:427
  85.6 2.3 %all-gather.3 = bf16[8,176,256]{2,1,0:T(8,128)(2,1)S(1)} all-gather(bf16[4,176,256]{2,1,0:T(8,128)(2,1)S(1)} %get-tuple-element.37), channel_id=5, replica_groups=mesh['z'=8,'p'=4,'q'=2,'x'=4,'c'=2] {'c'}, dimensions={0}, use_global_device_ids=true | all-gather | bytes 1081344 | tf_op jit(solution)/shard_map/all_gather | solution.py:427
  87.9 0.0 copy-done.1
  87.9 0.0 copy-done.2
  87.9 0.0 copy-done.3
  87.9 0.0 copy-done.4
  88.0 4.5 %reader.1 = (bf16[64,64,128]{2,1,0:T(8,128)(2,1)}, f32[1,128]{1,0:T(1,128)S(1)}) custom-call(s32[1]{0:T(128)} %bitcast.half_ref, bf16[2,4,176,256]{3,2,1,0:T(8,128)(2,1)S(1)} %bitcast.25, bf16[2,4,176,256]{3,2,1,0:T(8,128)(2,1)S(1)} %bitcast.24, bf16[2,2,320,256]{3,2,1,0:T(8,128)(2,1)S(1)} %bitcast.27, bf16[2,2,320,256]{3,2,1,0:T(8,128)(2,1)S(1)} %bitcast.26, ...), custom_call_target="tpu_custom_call" | custom-call | tf_op jit(solution)/shard_map/reader/pallas_call | solution.py:127
  92.4 6.3 %all-to-all-start.3 = ((bf16[64,64,128]{2,1,0:T(8,128)(2,1)}), bf16[64,64,128]{2,1,0:T(8,128)(2,1)S(1)}, u32[]{:S(2)}, u32[]{:S(2)}) async-start(bf16[64,64,128]{2,1,0:T(8,128)(2,1)} %get-tuple-element.30), calls=%async_computation.3 | async-start | bytes 2097152 | tf_op jit(solution)/shard_map/all_to_all | solution.py:442
  98.7 0.6 reshape_squeeze.3
  99.4 12.8 %all-gather.5 = bf16[1024,128]{1,0:T(8,128)(2,1)S(1)} all-gather(bf16[128,128]{1,0:T(8,128)(2,1)S(1)} %fusion.3), channel_id=7, replica_groups=mesh['z'=8,'p'=4,'q'=2,'x'=4,'c'=2] {'x','c'}, dimensions={0}, use_global_device_ids=true | all-gather | bytes 294912 | tf_op jit(solution)/shard_map/all_gather | solution.py:440
  112.3 0.0 copy-start.6
  112.3 16.3 %all-to-all-done.3.terms_ref = bf16[64,64,128]{2,1,0:T(8,128)(2,1)S(1)} async-done(((bf16[64,64,128]{2,1,0:T(8,128)(2,1)}), bf16[64,64,128]{2,1,0:T(8,128)(2,1)S(1)}, u32[]{:S(2)}, u32[]{:S(2)}) %all-to-all-start.3) | async-done | bytes 1048608 | tf_op jit(solution)/shard_map/all_to_all | solution.py:442
  128.6 0.8 total.1
  129.4 0.0 copy-done.6
  (28 shorter events, 0.3 us)
Async XLA Ops:
  0.6 51.0 %copy-start = (bf16[2,768]{1,0:T(2,128)(2,1)S(1)}, bf16[2,768]{1,0:T(2,128)(2,1)}, u32[]{:S(2)}) copy-start(bf16[2,768]{1,0:T(2,128)(2,1)} %param.14) | copy-start | bytes 9220
  4.1 10.5 %copy-start.5 = (bf16[160,256]{1,0:T(8,128)(2,1)S(1)}, bf16[160,256]{1,0:T(8,128)(2,1)}, u32[]{:S(2)}) copy-start(bf16[160,256]{1,0:T(8,128)(2,1)} %param.23) | copy-start | bytes 245764
  4.1 33.6 %all-to-all-start = ((bf16[8,352,256]{2,1,0:T(8,128)(2,1)}), bf16[8,352,256]{2,1,0:T(8,128)(2,1)S(1)}, u32[]{:S(2)}, u32[]{:S(2)}) async-start(bf16[8,352,256]{2,1,0:T(8,128)(2,1)} %pack.1), calls=%async_computation | async-start | bytes 2883584 | tf_op jit(solution)/shard_map/all_to_all | solution.py:382
  14.6 12.0 %collective-permute-start = (bf16[160,256]{1,0:T(8,128)(2,1)S(1)}, bf16[160,256]{1,0:T(8,128)(2,1)S(1)}, u32[]{:S(2)}, u32[]{:S(2)}) collective-permute-start(bf16[160,256]{1,0:T(8,128)(2,1)S(1)} %copy-done.5), channel_id=1, source_target_pairs={{0,8},{8,0},{1,9},{9,1},{2,10},{10,2},{3,11},{11,3},{4,12},{12,4},... | collective-permute-start | bytes 245768 | tf_op jit(solution)/shard_map/ppermute | solution.py:390
  44.4 7.3 %copy-start.7 = (s32[40]{0:T(128)S(1)}, s32[40]{0:T(128)}, u32[]{:S(2)}) copy-start(s32[40]{0:T(128)} %param.16) | copy-start | bytes 484
  44.4 24.8 %all-to-all-start.1 = ((bf16[8,224,256]{2,1,0:T(8,128)(2,1)}), bf16[8,224,256]{2,1,0:T(8,128)(2,1)S(1)}, u32[]{:S(2)}, u32[]{:S(2)}) async-start(bf16[8,224,256]{2,1,0:T(8,128)(2,1)} %bitcast.9), calls=%async_computation.1 | async-start | bytes 1835008 | tf_op jit(solution)/shard_map/all_to_all | solution.py:406
  70.4 12.7 %all-to-all-start.2 = ((bf16[8,176,256]{2,1,0:T(8,128)(2,1)}), bf16[8,176,256]{2,1,0:T(8,128)(2,1)S(1)}, u32[]{:S(2)}, u32[]{:S(2)}) async-start(bf16[8,176,256]{2,1,0:T(8,128)(2,1)} %spread.1), calls=%async_computation.2 | async-start | bytes 1441792 | tf_op jit(solution)/shard_map/all_to_all | solution.py:425
  83.1 4.8 %copy-start.1 = (bf16[2048,128]{1,0:T(8,128)(2,1)S(1)}, bf16[2048,128]{1,0:T(8,128)(2,1)}, u32[]{:S(2)}) copy-start(bf16[2048,128]{1,0:T(8,128)(2,1)} %refs_4_.1) | copy-start | bytes 1572868
  83.1 4.8 %copy-start.2 = (bf16[2048,128]{1,0:T(8,128)(2,1)S(1)}, bf16[2048,128]{1,0:T(8,128)(2,1)}, u32[]{:S(2)}) copy-start(bf16[2048,128]{1,0:T(8,128)(2,1)} %refs_5_.1) | copy-start | bytes 1572868
  83.1 4.8 %copy-start.3 = (bf16[2048,128]{1,0:T(8,128)(2,1)S(1)}, bf16[2048,128]{1,0:T(8,128)(2,1)}, u32[]{:S(2)}) copy-start(bf16[2048,128]{1,0:T(8,128)(2,1)} %refs_6_.1) | copy-start | bytes 1572868
  83.2 4.8 %copy-start.4 = (bf16[128,2048]{1,0:T(8,128)(2,1)S(1)}, bf16[128,2048]{1,0:T(8,128)(2,1)}, u32[]{:S(2)}) copy-start(bf16[128,2048]{1,0:T(8,128)(2,1)} %refs_7_.1) | copy-start | bytes 1572868
  92.4 36.1 %all-to-all-start.3 = ((bf16[64,64,128]{2,1,0:T(8,128)(2,1)}), bf16[64,64,128]{2,1,0:T(8,128)(2,1)S(1)}, u32[]{:S(2)}, u32[]{:S(2)}) async-start(bf16[64,64,128]{2,1,0:T(8,128)(2,1)} %get-tuple-element.30), calls=%async_computation.3 | async-start | bytes 2097152 | tf_op jit(solution)/shard_map/all_to_all | solution.py:442
  112.3 17.1 %copy-start.6 = (bf16[128,768]{1,0:T(8,128)(2,1)}, bf16[128,768]{1,0:T(8,128)(2,1)S(1)}, u32[]{:S(2)}) copy-start(bf16[128,768]{1,0:T(8,128)(2,1)S(1)} %slice_dynamic-update-slice_fusion) | copy-start | bytes 589828

commit v14 on v13

--- a/solution.py
+++ b/solution.py
@@ -366,7 +366,7 @@
     held = asked + 16
     stride = held + ny * CAPS
     spare = -npass % 16
-    rows_here = count + npass + spare
+    rows_here = count + npass
     message = pack(
         my_core,
         strip,

time: 131 us -> 131 us (level)
  no operation moved by 1% of the time
where the time goes in v14:
time: 131 us; the launch traced here: 129 us
  waiting for transfers between devices  41.2 us (31%)
  blocking collectives  37.6 us (29%)
  starting transfers between devices  32.6 us (25%)
  Pallas kernels  9.28 us (7%)
  matrix products  5.39 us (4%)
  local copies, waits for them, and re-layouts  1.35 us (1%)
    all_to_all x1, waiting for transfers between devices, shards(): terms = lax.all_to_all(terms, IDX, 0, 0, tiled=True)  16.3 us
    all_gather x1, blocking collectives, shards(): lax.all_gather(jnp.concatenate([out_grad, other], axis=0), 'x', axis=0)  13.7 us
    all_gather x1, blocking collectives, shards(): refreshed = lax.all_gather(refreshed, M, axis=0)  12.8 us
    all_to_all x1, waiting for transfers between devices, shards(): lax.all_to_all(message, ALONG, 0, 0, axis_index_groups=first_groups, tile...  11.1 us
    all_to_all x1, starting transfers between devices, shards(): lax.all_to_all(message, ALONG, 0, 0, axis_index_groups=first_groups, tile...  10.5 us
    ppermute x1, waiting for transfers between devices, shards(): other = lax.ppermute(out_grad, 'q', swap)  8.21 us
    all_to_all x1, starting transfers between devices, shards(): lax.all_to_all(served.reshape(*at.shape, deep), ALONG, 0, 0, axis_index_g...  7.23 us
    all_to_all x1, starting transfers between devices, shards(): terms = lax.all_to_all(terms, IDX, 0, 0, tiled=True)  6.61 us
  transfers between devices with their start and end apart: 5, of which 5 were waited for; matrix products, arithmetic and copies ran while one was open for 2% of the time, Pallas kernels for 0%

profile of v14, /device:TPU:6, one launch (start us, length us, event | category | flops | bytes accessed | tf_op | source)
XLA Modules:
  0.0 129.3 jit_solution(20965723123914393)
XLA Ops:
  0.6 0.0 copy-start
  0.7 0.6 pad_add_fusion.1.at_ref
  1.2 2.9 %pack.1 = bf16[8,352,256]{2,1,0:T(8,128)(2,1)} custom-call(s32[2]{0:T(128)} %pad_add_fusion.1.at_ref, bf16[256,256]{1,0:T(8,128)(2,1)} %refs_0_.1, bf16[128,768]{1,0:T(8,128)(2,1)} %refs_1_.1, bf16[64,768]{1,0:T(8,128)(2,1)} %refs_2_.1, s32[1,64]{1,0:T(1,128)} %bitcast.35, s32[4,40]{1,0:T(4,128)} %bitcast.34, s32[1,40]{1,0:T(1,128)} %bitcast.36, ...), custom_call_target="tpu_custom_call" | custom-call | tf_op jit(solution)/shard_map/pack/pallas_call | solution.py:230
  4.1 0.0 copy-start.5
  4.1 10.5 %all-to-all-start = ((bf16[8,352,256]{2,1,0:T(8,128)(2,1)}), bf16[8,352,256]{2,1,0:T(8,128)(2,1)S(1)}, u32[]{:S(2)}, u32[]{:S(2)}) async-start(bf16[8,352,256]{2,1,0:T(8,128)(2,1)} %pack.1), calls=%async_computation | async-start | bytes 2883584 | tf_op jit(solution)/shard_map/all_to_all | solution.py:382
  14.6 0.0 copy-done.5
  14.6 3.5 %collective-permute-start = (bf16[160,256]{1,0:T(8,128)(2,1)S(1)}, bf16[160,256]{1,0:T(8,128)(2,1)S(1)}, u32[]{:S(2)}, u32[]{:S(2)}) collective-permute-start(bf16[160,256]{1,0:T(8,128)(2,1)S(1)} %copy-done.5), channel_id=1, source_target_pairs={{0,8},{8,0},{1,9},{9,1},{2,10},{10,2},{3,11},{11,3},{4,12},{12,4},... | collective-permute-start | bytes 245768 | tf_op jit(solution)/shard_map/ppermute | solution.py:390
  18.1 0.1 add.84
  18.2 0.1 broadcast_add_fusion.1
  18.3 0.1 broadcast_add_fusion
  18.3 0.1 copy.28
  18.4 8.2 %collective-permute-done = bf16[160,256]{1,0:T(8,128)(2,1)S(1)} collective-permute-done((bf16[160,256]{1,0:T(8,128)(2,1)S(1)}, bf16[160,256]{1,0:T(8,128)(2,1)S(1)}, u32[]{:S(2)}, u32[]{:S(2)}) %collective-permute-start) | collective-permute-done | bytes 81952 | tf_op jit(solution)/shard_map/ppermute | solution.py:390
  26.6 11.1 %all-to-all-done = bf16[8,352,256]{2,1,0:T(8,128)(2,1)S(1)} async-done(((bf16[8,352,256]{2,1,0:T(8,128)(2,1)}), bf16[8,352,256]{2,1,0:T(8,128)(2,1)S(1)}, u32[]{:S(2)}, u32[]{:S(2)}) %all-to-all-start) | async-done | bytes 1441824 | tf_op jit(solution)/shard_map/all_to_all | solution.py:382
  37.8 1.8 %all_gather.39 = bf16[2,16,256]{2,1,0:T(8,128)(2,1)S(1)} all-gather(bf16[1,16,256]{2,1,0:T(8,128)(2,1)S(1)} %reshape.98), channel_id=1, replica_groups=mesh['z'=8,'p'=4,'q'=2,'x'=4,'c'=2] {'c'}, dimensions={0}, use_global_device_ids=true | all-gather | bytes 24576 | tf_op jit(solution)/shard_map/all_gather | solution.py:393
  39.6 0.1 pad_add_fusion
  39.7 0.1 eq.32
  39.8 4.5 %fusion.2 = bf16[1728,256]{1,0:T(8,128)(2,1)} fusion(bf16[2816,256]{1,0:T(8,128)(2,1)S(1)} %bitcast.29, s32[1728]{0:T(1024)S(1)} %eq.32), kind=kOutput, calls=%fused_computation.3 | convolution fusion | flops 2496724992 | bytes 2333440 | tf_op jit(solution)/shard_map/dot_general | solution.py:28
  44.3 0.0 copy-start.7
  44.3 7.2 %all-to-all-start.1 = ((bf16[8,216,256]{2,1,0:T(8,128)(2,1)}), bf16[8,216,256]{2,1,0:T(8,128)(2,1)S(1)}, u32[]{:S(2)}, u32[]{:S(2)}) async-start(bf16[8,216,256]{2,1,0:T(8,128)(2,1)} %bitcast.9), calls=%async_computation.1 | async-start | bytes 1769472 | tf_op jit(solution)/shard_map/all_to_all | solution.py:406
  51.5 0.0 copy-done
  51.6 0.0 copy-done.7
  51.6 0.1 copy.29.high_ref
  51.8 13.7 %all-gather = bf16[1280,256]{1,0:T(8,128)(2,1)S(1)} all-gather(bf16[320,256]{1,0:T(8,128)(2,1)S(1)} %pad_maximum_fusion), channel_id=2, replica_groups=mesh['z'=8,'p'=4,'q'=2,'x'=4,'c'=2] {'x'}, dimensions={0}, use_global_device_ids=true | all-gather | bytes 819200 | tf_op jit(solution)/shard_map/all_gather | solution.py:392
  65.4 3.3 %all-to-all-done.1.got_ref = bf16[8,216,256]{2,1,0:T(8,128)(2,1)S(1)} async-done(((bf16[8,216,256]{2,1,0:T(8,128)(2,1)}), bf16[8,216,256]{2,1,0:T(8,128)(2,1)S(1)}, u32[]{:S(2)}, u32[]{:S(2)}) %all-to-all-start.1) | async-done | bytes 884768 | tf_op jit(solution)/shard_map/all_to_all | solution.py:406
  68.7 1.1 spread.1
  69.9 4.8 %all-to-all-start.2 = ((bf16[8,176,256]{2,1,0:T(8,128)(2,1)}), bf16[8,176,256]{2,1,0:T(8,128)(2,1)S(1)}, u32[]{:S(2)}, u32[]{:S(2)}) async-start(bf16[8,176,256]{2,1,0:T(8,128)(2,1)} %spread.1), calls=%async_computation.2 | async-start | bytes 1441792 | tf_op jit(solution)/shard_map/all_to_all | solution.py:425
  74.7 0.1 copy.33
  74.8 0.1 fusion.4
  74.9 2.3 %all-gather.2 = bf16[4,320,256]{2,1,0:T(8,128)(2,1)S(1)} all-gather(bf16[2,320,256]{2,1,0:T(8,128)(2,1)S(1)} %get-tuple-element.38), channel_id=4, replica_groups=mesh['z'=8,'p'=4,'q'=2,'x'=4,'c'=2] {'c'}, dimensions={0}, use_global_device_ids=true | all-gather | bytes 983040 | tf_op jit(solution)/shard_map/all_gather | solution.py:423
  77.2 2.3 %all-gather.1 = bf16[4,320,256]{2,1,0:T(8,128)(2,1)S(1)} all-gather(bf16[2,320,256]{2,1,0:T(8,128)(2,1)S(1)} %get-tuple-element.39), channel_id=3, replica_groups=mesh['z'=8,'p'=4,'q'=2,'x'=4,'c'=2] {'c'}, dimensions={0}, use_global_device_ids=true | all-gather | bytes 983040 | tf_op jit(solution)/shard_map/all_gather | solution.py:423
  79.5 0.9 fusion.3
  80.4 2.2 %all-to-all-done.2 = bf16[8,176,256]{2,1,0:T(8,128)(2,1)S(1)} async-done(((bf16[8,176,256]{2,1,0:T(8,128)(2,1)}), bf16[8,176,256]{2,1,0:T(8,128)(2,1)S(1)}, u32[]{:S(2)}, u32[]{:S(2)}) %all-to-all-start.2) | async-done | bytes 720928 | tf_op jit(solution)/shard_map/all_to_all | solution.py:425
  82.6 0.0 copy-start.1
  82.7 0.0 copy-start.2
  82.7 0.0 copy-start.3
  82.7 0.0 copy-start.4
  82.7 2.5 %all-gather.4 = bf16[8,176,256]{2,1,0:T(8,128)(2,1)S(1)} all-gather(bf16[4,176,256]{2,1,0:T(8,128)(2,1)S(1)} %get-tuple-element.36), channel_id=6, replica_groups=mesh['z'=8,'p'=4,'q'=2,'x'=4,'c'=2] {'c'}, dimensions={0}, use_global_device_ids=true | all-gather | bytes 1081344 | tf_op jit(solution)/shard_map/all_gather | solution.py:427
  85.1 2.3 %all-gather.3 = bf16[8,176,256]{2,1,0:T(8,128)(2,1)S(1)} all-gather(bf16[4,176,256]{2,1,0:T(8,128)(2,1)S(1)} %get-tuple-element.37), channel_id=5, replica_groups=mesh['z'=8,'p'=4,'q'=2,'x'=4,'c'=2] {'c'}, dimensions={0}, use_global_device_ids=true | all-gather | bytes 1081344 | tf_op jit(solution)/shard_map/all_gather | solution.py:427
  87.5 0.0 copy-done.1
  87.5 0.0 copy-done.2
  87.5 0.0 copy-done.3
  87.5 0.0 copy-done.4
  87.5 4.5 %reader.1 = (bf16[64,64,128]{2,1,0:T(8,128)(2,1)}, f32[1,128]{1,0:T(1,128)S(1)}) custom-call(s32[1]{0:T(128)} %bitcast.half_ref, bf16[2,4,176,256]{3,2,1,0:T(8,128)(2,1)S(1)} %bitcast.25, bf16[2,4,176,256]{3,2,1,0:T(8,128)(2,1)S(1)} %bitcast.24, bf16[2,2,320,256]{3,2,1,0:T(8,128)(2,1)S(1)} %bitcast.27, bf16[2,2,320,256]{3,2,1,0:T(8,128)(2,1)S(1)} %bitcast.26, ...), custom_call_target="tpu_custom_call" | custom-call | tf_op jit(solution)/shard_map/reader/pallas_call | solution.py:127
  91.9 6.6 %all-to-all-start.3 = ((bf16[64,64,128]{2,1,0:T(8,128)(2,1)}), bf16[64,64,128]{2,1,0:T(8,128)(2,1)S(1)}, u32[]{:S(2)}, u32[]{:S(2)}) async-start(bf16[64,64,128]{2,1,0:T(8,128)(2,1)} %get-tuple-element.30), calls=%async_computation.3 | async-start | bytes 2097152 | tf_op jit(solution)/shard_map/all_to_all | solution.py:442
  98.6 0.6 reshape_squeeze.3
  99.2 12.8 %all-gather.5 = bf16[1024,128]{1,0:T(8,128)(2,1)S(1)} all-gather(bf16[128,128]{1,0:T(8,128)(2,1)S(1)} %fusion.3), channel_id=7, replica_groups=mesh['z'=8,'p'=4,'q'=2,'x'=4,'c'=2] {'x','c'}, dimensions={0}, use_global_device_ids=true | all-gather | bytes 294912 | tf_op jit(solution)/shard_map/all_gather | solution.py:440
  112.1 0.0 copy-start.6
  112.1 16.3 %all-to-all-done.3.terms_ref = bf16[64,64,128]{2,1,0:T(8,128)(2,1)S(1)} async-done(((bf16[64,64,128]{2,1,0:T(8,128)(2,1)}), bf16[64,64,128]{2,1,0:T(8,128)(2,1)S(1)}, u32[]{:S(2)}, u32[]{:S(2)}) %all-to-all-start.3) | async-done | bytes 1048608 | tf_op jit(solution)/shard_map/all_to_all | solution.py:442
  128.4 0.8 total.1
  129.3 0.0 copy-done.6
  (28 shorter events, 0.3 us)
Async XLA Ops:
  0.6 50.9 %copy-start = (bf16[2,768]{1,0:T(2,128)(2,1)S(1)}, bf16[2,768]{1,0:T(2,128)(2,1)}, u32[]{:S(2)}) copy-start(bf16[2,768]{1,0:T(2,128)(2,1)} %param.14) | copy-start | bytes 9220
  4.1 10.5 %copy-start.5 = (bf16[160,256]{1,0:T(8,128)(2,1)S(1)}, bf16[160,256]{1,0:T(8,128)(2,1)}, u32[]{:S(2)}) copy-start(bf16[160,256]{1,0:T(8,128)(2,1)} %param.23) | copy-start | bytes 245764
  4.1 33.6 %all-to-all-start = ((bf16[8,352,256]{2,1,0:T(8,128)(2,1)}), bf16[8,352,256]{2,1,0:T(8,128)(2,1)S(1)}, u32[]{:S(2)}, u32[]{:S(2)}) async-start(bf16[8,352,256]{2,1,0:T(8,128)(2,1)} %pack.1), calls=%async_computation | async-start | bytes 2883584 | tf_op jit(solution)/shard_map/all_to_all | solution.py:382
  14.6 12.0 %collective-permute-start = (bf16[160,256]{1,0:T(8,128)(2,1)S(1)}, bf16[160,256]{1,0:T(8,128)(2,1)S(1)}, u32[]{:S(2)}, u32[]{:S(2)}) collective-permute-start(bf16[160,256]{1,0:T(8,128)(2,1)S(1)} %copy-done.5), channel_id=1, source_target_pairs={{0,8},{8,0},{1,9},{9,1},{2,10},{10,2},{3,11},{11,3},{4,12},{12,4},... | collective-permute-start | bytes 245768 | tf_op jit(solution)/shard_map/ppermute | solution.py:390
  44.3 7.3 %copy-start.7 = (s32[40]{0:T(128)S(1)}, s32[40]{0:T(128)}, u32[]{:S(2)}) copy-start(s32[40]{0:T(128)} %param.16) | copy-start | bytes 484
  44.3 24.4 %all-to-all-start.1 = ((bf16[8,216,256]{2,1,0:T(8,128)(2,1)}), bf16[8,216,256]{2,1,0:T(8,128)(2,1)S(1)}, u32[]{:S(2)}, u32[]{:S(2)}) async-start(bf16[8,216,256]{2,1,0:T(8,128)(2,1)} %bitcast.9), calls=%async_computation.1 | async-start | bytes 1769472 | tf_op jit(solution)/shard_map/all_to_all | solution.py:406
  69.9 12.7 %all-to-all-start.2 = ((bf16[8,176,256]{2,1,0:T(8,128)(2,1)}), bf16[8,176,256]{2,1,0:T(8,128)(2,1)S(1)}, u32[]{:S(2)}, u32[]{:S(2)}) async-start(bf16[8,176,256]{2,1,0:T(8,128)(2,1)} %spread.1), calls=%async_computation.2 | async-start | bytes 1441792 | tf_op jit(solution)/shard_map/all_to_all | solution.py:425
  82.6 4.8 %copy-start.1 = (bf16[2048,128]{1,0:T(8,128)(2,1)S(1)}, bf16[2048,128]{1,0:T(8,128)(2,1)}, u32[]{:S(2)}) copy-start(bf16[2048,128]{1,0:T(8,128)(2,1)} %refs_4_.1) | copy-start | bytes 1572868
  82.7 4.8 %copy-start.2 = (bf16[2048,128]{1,0:T(8,128)(2,1)S(1)}, bf16[2048,128]{1,0:T(8,128)(2,1)}, u32[]{:S(2)}) copy-start(bf16[2048,128]{1,0:T(8,128)(2,1)} %refs_5_.1) | copy-start | bytes 1572868
  82.7 4.8 %copy-start.3 = (bf16[2048,128]{1,0:T(8,128)(2,1)S(1)}, bf16[2048,128]{1,0:T(8,128)(2,1)}, u32[]{:S(2)}) copy-start(bf16[2048,128]{1,0:T(8,128)(2,1)} %refs_6_.1) | copy-start | bytes 1572868
  82.7 4.8 %copy-start.4 = (bf16[128,2048]{1,0:T(8,128)(2,1)S(1)}, bf16[128,2048]{1,0:T(8,128)(2,1)}, u32[]{:S(2)}) copy-start(bf16[128,2048]{1,0:T(8,128)(2,1)} %refs_7_.1) | copy-start | bytes 1572868
  91.9 36.5 %all-to-all-start.3 = ((bf16[64,64,128]{2,1,0:T(8,128)(2,1)}), bf16[64,64,128]{2,1,0:T(8,128)(2,1)S(1)}, u32[]{:S(2)}, u32[]{:S(2)}) async-start(bf16[64,64,128]{2,1,0:T(8,128)(2,1)} %get-tuple-element.30), calls=%async_computation.3 | async-start | bytes 2097152 | tf_op jit(solution)/shard_map/all_to_all | solution.py:442
  112.1 17.2 %copy-start.6 = (bf16[128,768]{1,0:T(8,128)(2,1)}, bf16[128,768]{1,0:T(8,128)(2,1)S(1)}, u32[]{:S(2)}) copy-start(bf16[128,768]{1,0:T(8,128)(2,1)S(1)} %slice_dynamic-update-slice_fusion) | copy-start | bytes 589828

commit v15 on v13

--- a/solution.py
+++ b/solution.py
@@ -355,9 +355,9 @@
     my_core = lax.axis_index("c")
     at_z = [[(z * ny + y) * cores for z in range(nz)] for y in range(ny)]
     at_y = [[(z * ny + y) * cores for y in range(ny)] for z in range(nz)]
-    first_groups = at_z + [[i + 1 for i in group] for group in at_y]
-    second_groups = at_y + [[i + 1 for i in group] for group in at_z]
-    second = jnp.where(my_core == 0, my_y, my_z)
+    first_groups = at_y + [[i + 1 for i in group] for group in at_z]
+    second_groups = at_z + [[i + 1 for i in group] for group in at_y]
+    second = jnp.where(my_core == 0, my_z, my_y)
 
     deep = vocab_table.shape[1]
     index_strip = my_strip(index_emb)
@@ -368,7 +368,7 @@
     spare = -npass % 16
     rows_here = count + npass + spare
     message = pack(
-        my_core,
+        1 - my_core,
         strip,
         vocab_table,
         index_emb,

time: 131 us -> 132 us (level)
    ppermute x1, waiting for transfers between devices: 8.21 us -> 16.7 us  [shards(): other = lax.ppermute(out_grad, 'q', swap)]
    all_to_all x1, waiting for transfers between devices: 11.1 us -> 3.08 us  [shards(): lax.all_to_all(message, ALONG, 0, 0, axis_index_groups=first_groups, tile...]
    all_to_all x1, starting transfers between devices: 10.5 us -> 7.24 us  [shards(): lax.all_to_all(message, ALONG, 0, 0, axis_index_groups=first_groups, tile...]
    all_to_all x1, starting transfers between devices: 7.23 us -> 10 us  [shards(): lax.all_to_all(served.reshape(*at.shape, deep), ALONG, 0, 0, axis_index_g...]
where the time goes in v15:
time: 132 us; the launch traced here: 130 us
  waiting for transfers between devices  41.8 us (32%)
  blocking collectives  37.4 us (28%)
  starting transfers between devices  33 us (25%)
  Pallas kernels  9.29 us (7%)
  matrix products  5.53 us (4%)
  local copies, waits for them, and re-layouts  1.35 us (1%)
    ppermute x1, waiting for transfers between devices, shards(): other = lax.ppermute(out_grad, 'q', swap)  16.7 us
    all_to_all x1, waiting for transfers between devices, shards(): terms = lax.all_to_all(terms, IDX, 0, 0, tiled=True)  16.3 us
    all_gather x1, blocking collectives, shards(): lax.all_gather(jnp.concatenate([out_grad, other], axis=0), 'x', axis=0)  13 us
    all_gather x1, blocking collectives, shards(): refreshed = lax.all_gather(refreshed, M, axis=0)  12.8 us
    all_to_all x1, starting transfers between devices, shards(): lax.all_to_all(served.reshape(*at.shape, deep), ALONG, 0, 0, axis_index_g...  10 us
    all_to_all x1, starting transfers between devices, shards(): lax.all_to_all(message, ALONG, 0, 0, axis_index_groups=first_groups, tile...  7.24 us
    all_to_all x1, starting transfers between devices, shards(): terms = lax.all_to_all(terms, IDX, 0, 0, tiled=True)  7.01 us
    dot_general x2, matrix products, dot(): return jnp.dot(a, b, preferred_element_type=F32)  5.53 us
  transfers between devices with their start and end apart: 5, of which 5 were waited for; matrix products, arithmetic and copies ran while one was open for 2% of the time, Pallas kernels for 0%

profile of v15, /device:TPU:6, one launch (start us, length us, event | category | flops | bytes accessed | tf_op | source)
XLA Modules:
  0.0 130.2 jit_solution(2113207775305202665)
XLA Ops:
  0.6 0.0 copy-start
  0.7 0.6 pad_add_fusion.1.at_ref
  1.2 2.9 %pack.1 = bf16[8,352,256]{2,1,0:T(8,128)(2,1)} custom-call(s32[2]{0:T(128)} %pad_add_fusion.1.at_ref, bf16[256,256]{1,0:T(8,128)(2,1)} %refs_0_.1, bf16[128,768]{1,0:T(8,128)(2,1)} %refs_1_.1, bf16[64,768]{1,0:T(8,128)(2,1)} %refs_2_.1, s32[1,64]{1,0:T(1,128)} %bitcast.35, s32[4,40]{1,0:T(4,128)} %bitcast.34, s32[1,40]{1,0:T(1,128)} %bitcast.36, ...), custom_call_target="tpu_custom_call" | custom-call | tf_op jit(solution)/shard_map/pack/pallas_call | solution.py:230
  4.1 0.0 copy-start.5
  4.1 7.2 %all-to-all-start = ((bf16[8,352,256]{2,1,0:T(8,128)(2,1)}), bf16[8,352,256]{2,1,0:T(8,128)(2,1)S(1)}, u32[]{:S(2)}, u32[]{:S(2)}) async-start(bf16[8,352,256]{2,1,0:T(8,128)(2,1)} %pack.1), calls=%async_computation | async-start | bytes 2883584 | tf_op jit(solution)/shard_map/all_to_all | solution.py:382
  11.4 0.0 copy-done.5
  11.4 3.9 %collective-permute-start = (bf16[160,256]{1,0:T(8,128)(2,1)S(1)}, bf16[160,256]{1,0:T(8,128)(2,1)S(1)}, u32[]{:S(2)}, u32[]{:S(2)}) collective-permute-start(bf16[160,256]{1,0:T(8,128)(2,1)S(1)} %copy-done.5), channel_id=1, source_target_pairs={{0,8},{8,0},{1,9},{9,1},{2,10},{10,2},{3,11},{11,3},{4,12},{12,4},... | collective-permute-start | bytes 245768 | tf_op jit(solution)/shard_map/ppermute | solution.py:390
  15.3 0.1 add.84
  15.4 0.1 broadcast_add_fusion.1
  15.5 0.1 broadcast_add_fusion
  15.5 0.1 copy.28
  15.6 16.7 %collective-permute-done = bf16[160,256]{1,0:T(8,128)(2,1)S(1)} collective-permute-done((bf16[160,256]{1,0:T(8,128)(2,1)S(1)}, bf16[160,256]{1,0:T(8,128)(2,1)S(1)}, u32[]{:S(2)}, u32[]{:S(2)}) %collective-permute-start) | collective-permute-done | bytes 81952 | tf_op jit(solution)/shard_map/ppermute | solution.py:390
  32.3 3.1 %all-to-all-done = bf16[8,352,256]{2,1,0:T(8,128)(2,1)S(1)} async-done(((bf16[8,352,256]{2,1,0:T(8,128)(2,1)}), bf16[8,352,256]{2,1,0:T(8,128)(2,1)S(1)}, u32[]{:S(2)}, u32[]{:S(2)}) %all-to-all-start) | async-done | bytes 1441824 | tf_op jit(solution)/shard_map/all_to_all | solution.py:382
  35.4 2.2 %all_gather.39 = bf16[2,16,256]{2,1,0:T(8,128)(2,1)S(1)} all-gather(bf16[1,16,256]{2,1,0:T(8,128)(2,1)S(1)} %reshape.98), channel_id=1, replica_groups=mesh['z'=8,'p'=4,'q'=2,'x'=4,'c'=2] {'c'}, dimensions={0}, use_global_device_ids=true | all-gather | bytes 24576 | tf_op jit(solution)/shard_map/all_gather | solution.py:393
  37.7 0.1 pad_add_fusion
  37.8 0.1 eq.32
  37.9 4.6 %fusion.2 = bf16[1792,256]{1,0:T(8,128)(2,1)} fusion(bf16[2816,256]{1,0:T(8,128)(2,1)S(1)} %bitcast.29, s32[1792]{0:T(1024)S(1)} %eq.32), kind=kOutput, calls=%fused_computation.3 | convolution fusion | flops 2589196288 | bytes 2366464 | tf_op jit(solution)/shard_map/dot_general | solution.py:28
  42.5 0.0 copy-start.7
  42.5 10.0 %all-to-all-start.1 = ((bf16[8,224,256]{2,1,0:T(8,128)(2,1)}), bf16[8,224,256]{2,1,0:T(8,128)(2,1)S(1)}, u32[]{:S(2)}, u32[]{:S(2)}) async-start(bf16[8,224,256]{2,1,0:T(8,128)(2,1)} %bitcast.9), calls=%async_computation.1 | async-start | bytes 1835008 | tf_op jit(solution)/shard_map/all_to_all | solution.py:406
  52.6 0.0 copy-done
  52.6 0.0 copy-done.7
  52.7 0.1 copy.29.high_ref
  52.8 13.0 %all-gather = bf16[1280,256]{1,0:T(8,128)(2,1)S(1)} all-gather(bf16[320,256]{1,0:T(8,128)(2,1)S(1)} %pad_maximum_fusion), channel_id=2, replica_groups=mesh['z'=8,'p'=4,'q'=2,'x'=4,'c'=2] {'x'}, dimensions={0}, use_global_device_ids=true | all-gather | bytes 819200 | tf_op jit(solution)/shard_map/all_gather | solution.py:392
  65.8 4.3 %all-to-all-done.1.got_ref = bf16[8,224,256]{2,1,0:T(8,128)(2,1)S(1)} async-done(((bf16[8,224,256]{2,1,0:T(8,128)(2,1)}), bf16[8,224,256]{2,1,0:T(8,128)(2,1)S(1)}, u32[]{:S(2)}, u32[]{:S(2)}) %all-to-all-start.1) | async-done | bytes 917536 | tf_op jit(solution)/shard_map/all_to_all | solution.py:406
  70.1 1.1 spread.1
  71.3 4.8 %all-to-all-start.2 = ((bf16[8,176,256]{2,1,0:T(8,128)(2,1)}), bf16[8,176,256]{2,1,0:T(8,128)(2,1)S(1)}, u32[]{:S(2)}, u32[]{:S(2)}) async-start(bf16[8,176,256]{2,1,0:T(8,128)(2,1)} %spread.1), calls=%async_computation.2 | async-start | bytes 1441792 | tf_op jit(solution)/shard_map/all_to_all | solution.py:425
  76.1 0.1 copy.33
  76.1 0.1 fusion.4
  76.3 2.3 %all-gather.2 = bf16[4,320,256]{2,1,0:T(8,128)(2,1)S(1)} all-gather(bf16[2,320,256]{2,1,0:T(8,128)(2,1)S(1)} %get-tuple-element.38), channel_id=4, replica_groups=mesh['z'=8,'p'=4,'q'=2,'x'=4,'c'=2] {'c'}, dimensions={0}, use_global_device_ids=true | all-gather | bytes 983040 | tf_op jit(solution)/shard_map/all_gather | solution.py:423
  78.6 2.3 %all-gather.1 = bf16[4,320,256]{2,1,0:T(8,128)(2,1)S(1)} all-gather(bf16[2,320,256]{2,1,0:T(8,128)(2,1)S(1)} %get-tuple-element.39), channel_id=3, replica_groups=mesh['z'=8,'p'=4,'q'=2,'x'=4,'c'=2] {'c'}, dimensions={0}, use_global_device_ids=true | all-gather | bytes 983040 | tf_op jit(solution)/shard_map/all_gather | solution.py:423
  80.9 0.9 fusion.3
  81.8 1.4 %all-to-all-done.2 = bf16[8,176,256]{2,1,0:T(8,128)(2,1)S(1)} async-done(((bf16[8,176,256]{2,1,0:T(8,128)(2,1)}), bf16[8,176,256]{2,1,0:T(8,128)(2,1)S(1)}, u32[]{:S(2)}, u32[]{:S(2)}) %all-to-all-start.2) | async-done | bytes 720928 | tf_op jit(solution)/shard_map/all_to_all | solution.py:425
  83.2 0.0 copy-start.1
  83.2 0.0 copy-start.2
  83.2 0.0 copy-start.3
  83.2 0.0 copy-start.4
  83.3 2.5 %all-gather.4 = bf16[8,176,256]{2,1,0:T(8,128)(2,1)S(1)} all-gather(bf16[4,176,256]{2,1,0:T(8,128)(2,1)S(1)} %get-tuple-element.36), channel_id=6, replica_groups=mesh['z'=8,'p'=4,'q'=2,'x'=4,'c'=2] {'c'}, dimensions={0}, use_global_device_ids=true | all-gather | bytes 1081344 | tf_op jit(solution)/shard_map/all_gather | solution.py:427
  85.7 2.3 %all-gather.3 = bf16[8,176,256]{2,1,0:T(8,128)(2,1)S(1)} all-gather(bf16[4,176,256]{2,1,0:T(8,128)(2,1)S(1)} %get-tuple-element.37), channel_id=5, replica_groups=mesh['z'=8,'p'=4,'q'=2,'x'=4,'c'=2] {'c'}, dimensions={0}, use_global_device_ids=true | all-gather | bytes 1081344 | tf_op jit(solution)/shard_map/all_gather | solution.py:427
  88.0 0.0 copy-done.1
  88.0 0.0 copy-done.2
  88.0 0.0 copy-done.3
  88.0 0.0 copy-done.4
  88.0 4.5 %reader.1 = (bf16[64,64,128]{2,1,0:T(8,128)(2,1)}, f32[1,128]{1,0:T(1,128)S(1)}) custom-call(s32[1]{0:T(128)} %bitcast.half_ref, bf16[2,4,176,256]{3,2,1,0:T(8,128)(2,1)S(1)} %bitcast.25, bf16[2,4,176,256]{3,2,1,0:T(8,128)(2,1)S(1)} %bitcast.24, bf16[2,2,320,256]{3,2,1,0:T(8,128)(2,1)S(1)} %bitcast.27, bf16[2,2,320,256]{3,2,1,0:T(8,128)(2,1)S(1)} %bitcast.26, ...), custom_call_target="tpu_custom_call" | custom-call | tf_op jit(solution)/shard_map/reader/pallas_call | solution.py:127
  92.5 7.0 %all-to-all-start.3 = ((bf16[64,64,128]{2,1,0:T(8,128)(2,1)}), bf16[64,64,128]{2,1,0:T(8,128)(2,1)S(1)}, u32[]{:S(2)}, u32[]{:S(2)}) async-start(bf16[64,64,128]{2,1,0:T(8,128)(2,1)} %get-tuple-element.30), calls=%async_computation.3 | async-start | bytes 2097152 | tf_op jit(solution)/shard_map/all_to_all | solution.py:442
  99.5 0.6 reshape_squeeze.3
  100.2 12.8 %all-gather.5 = bf16[1024,128]{1,0:T(8,128)(2,1)S(1)} all-gather(bf16[128,128]{1,0:T(8,128)(2,1)S(1)} %fusion.3), channel_id=7, replica_groups=mesh['z'=8,'p'=4,'q'=2,'x'=4,'c'=2] {'x','c'}, dimensions={0}, use_global_device_ids=true | all-gather | bytes 294912 | tf_op jit(solution)/shard_map/all_gather | solution.py:440
  113.1 0.0 copy-start.6
  113.1 16.3 %all-to-all-done.3.terms_ref = bf16[64,64,128]{2,1,0:T(8,128)(2,1)S(1)} async-done(((bf16[64,64,128]{2,1,0:T(8,128)(2,1)}), bf16[64,64,128]{2,1,0:T(8,128)(2,1)S(1)}, u32[]{:S(2)}, u32[]{:S(2)}) %all-to-all-start.3) | async-done | bytes 1048608 | tf_op jit(solution)/shard_map/all_to_all | solution.py:442
  129.4 0.8 total.1
  130.2 0.0 copy-done.6
  (28 shorter events, 0.3 us)
Async XLA Ops:
  0.6 51.9 %copy-start = (bf16[2,768]{1,0:T(2,128)(2,1)S(1)}, bf16[2,768]{1,0:T(2,128)(2,1)}, u32[]{:S(2)}) copy-start(bf16[2,768]{1,0:T(2,128)(2,1)} %param.14) | copy-start | bytes 9220
  4.1 7.3 %copy-start.5 = (bf16[160,256]{1,0:T(8,128)(2,1)S(1)}, bf16[160,256]{1,0:T(8,128)(2,1)}, u32[]{:S(2)}) copy-start(bf16[160,256]{1,0:T(8,128)(2,1)} %param.23) | copy-start | bytes 245764
  4.1 31.3 %all-to-all-start = ((bf16[8,352,256]{2,1,0:T(8,128)(2,1)}), bf16[8,352,256]{2,1,0:T(8,128)(2,1)S(1)}, u32[]{:S(2)}, u32[]{:S(2)}) async-start(bf16[8,352,256]{2,1,0:T(8,128)(2,1)} %pack.1), calls=%async_computation | async-start | bytes 2883584 | tf_op jit(solution)/shard_map/all_to_all | solution.py:382
  11.4 21.0 %collective-permute-start = (bf16[160,256]{1,0:T(8,128)(2,1)S(1)}, bf16[160,256]{1,0:T(8,128)(2,1)S(1)}, u32[]{:S(2)}, u32[]{:S(2)}) collective-permute-start(bf16[160,256]{1,0:T(8,128)(2,1)S(1)} %copy-done.5), channel_id=1, source_target_pairs={{0,8},{8,0},{1,9},{9,1},{2,10},{10,2},{3,11},{11,3},{4,12},{12,4},... | collective-permute-start | bytes 245768 | tf_op jit(solution)/shard_map/ppermute | solution.py:390
  42.5 10.1 %copy-start.7 = (s32[40]{0:T(128)S(1)}, s32[40]{0:T(128)}, u32[]{:S(2)}) copy-start(s32[40]{0:T(128)} %param.16) | copy-start | bytes 484
  42.5 27.6 %all-to-all-start.1 = ((bf16[8,224,256]{2,1,0:T(8,128)(2,1)}), bf16[8,224,256]{2,1,0:T(8,128)(2,1)S(1)}, u32[]{:S(2)}, u32[]{:S(2)}) async-start(bf16[8,224,256]{2,1,0:T(8,128)(2,1)} %bitcast.9), calls=%async_computation.1 | async-start | bytes 1835008 | tf_op jit(solution)/shard_map/all_to_all | solution.py:406
  71.3 11.9 %all-to-all-start.2 = ((bf16[8,176,256]{2,1,0:T(8,128)(2,1)}), bf16[8,176,256]{2,1,0:T(8,128)(2,1)S(1)}, u32[]{:S(2)}, u32[]{:S(2)}) async-start(bf16[8,176,256]{2,1,0:T(8,128)(2,1)} %spread.1), calls=%async_computation.2 | async-start | bytes 1441792 | tf_op jit(solution)/shard_map/all_to_all | solution.py:425
  83.2 4.8 %copy-start.1 = (bf16[2048,128]{1,0:T(8,128)(2,1)S(1)}, bf16[2048,128]{1,0:T(8,128)(2,1)}, u32[]{:S(2)}) copy-start(bf16[2048,128]{1,0:T(8,128)(2,1)} %refs_4_.1) | copy-start | bytes 1572868
  83.2 4.8 %copy-start.2 = (bf16[2048,128]{1,0:T(8,128)(2,1)S(1)}, bf16[2048,128]{1,0:T(8,128)(2,1)}, u32[]{:S(2)}) copy-start(bf16[2048,128]{1,0:T(8,128)(2,1)} %refs_5_.1) | copy-start | bytes 1572868
  83.2 4.8 %copy-start.3 = (bf16[2048,128]{1,0:T(8,128)(2,1)S(1)}, bf16[2048,128]{1,0:T(8,128)(2,1)}, u32[]{:S(2)}) copy-start(bf16[2048,128]{1,0:T(8,128)(2,1)} %refs_6_.1) | copy-start | bytes 1572868
  83.2 4.8 %copy-start.4 = (bf16[128,2048]{1,0:T(8,128)(2,1)S(1)}, bf16[128,2048]{1,0:T(8,128)(2,1)}, u32[]{:S(2)}) copy-start(bf16[128,2048]{1,0:T(8,128)(2,1)} %refs_7_.1) | copy-start | bytes 1572868
  92.5 36.9 %all-to-all-start.3 = ((bf16[64,64,128]{2,1,0:T(8,128)(2,1)}), bf16[64,64,128]{2,1,0:T(8,128)(2,1)S(1)}, u32[]{:S(2)}, u32[]{:S(2)}) async-start(bf16[64,64,128]{2,1,0:T(8,128)(2,1)} %get-tuple-element.30), calls=%async_computation.3 | async-start | bytes 2097152 | tf_op jit(solution)/shard_map/all_to_all | solution.py:442
  113.1 17.1 %copy-start.6 = (bf16[128,768]{1,0:T(8,128)(2,1)}, bf16[128,768]{1,0:T(8,128)(2,1)S(1)}, u32[]{:S(2)}) copy-start(bf16[128,768]{1,0:T(8,128)(2,1)S(1)} %slice_dynamic-update-slice_fusion) | copy-start | bytes 589828
